TPU v7x, 32 devices: a whole 2x2x4 slice. The times are simulated.
32 devices in a mesh: frames: 4 (over z), mp: 4 (over x, core), dp: 2 (over y).
Axes of the slice: x: 2, y: 2, z: 4, core: 2. Of those that a mesh axis runs over, the one named last changes fastest.
Arguments:
- projections: bfloat16 [2, 8, 96, 3, 3584], P('dp', 'frames', None, None, 'mp'), may hold values from -18 to 18
- perturbation: bfloat16 [2, 8, 96, 3, 3584], P('dp', 'frames', None, None, 'mp'), may hold values from -44 to 44
- out_weight: bfloat16 [3584, 3584], P('frames', 'mp'), may hold values from -0.09375 to 0.09375
- norm_gain: float32 [3584], P('mp'), may hold values from 0.25 to 1.75
- live_counts: int32 [2, 8], P('dp'), may hold values from 72 to 96, as said below
Outputs:
- features: bfloat16 [2, 8, 96, 3584], P('dp', 'frames', None, 'mp')
- penalty: float32 [2], P('dp')
- gain_grad: float32 [3584], P('mp')
Inputs may be any that keep to these rules, and one draw needn't show every extreme that they name: `live_counts`: in each clip one slot has all 96 tokens live and another has 72 live.
All inputs are finite; a program needn't handle non-finite values.
Results may differ from a plain program's by a relative error of at most 0.0057.
Values may be sent and summed in bfloat16 or wider, within the bound.
No kernel may reach another device: no remote copies, remote signals or barrier semaphores. Data moves between devices by JAX's collectives and lax.ppermute only.
A program may use at most 64 MiB of HBM per device.

v0:
```python
import math

import jax
import jax.numpy as jnp
from jax import lax
from jax.experimental import pallas as pl
from jax.experimental.pallas import tpu as pltpu
from jax.sharding import PartitionSpec as P

HEAD_DIM = 128
HEADS_AT_ONCE = 1
LANES = 128


sigma_noise = 0.25
epsilon = 1e-06


def perturb(clean, noise):
    return (clean.astype(jnp.float32) + sigma_noise * noise.astype(jnp.float32)).astype(jnp.bfloat16)


def attend_kernel(counts_ref, own_ref, left_ref, right_ref, out_ref):
    slots, _, tile_len, width = own_ref.shape
    key_pos = lax.broadcasted_iota(jnp.int32, (1, 2 * tile_len), 1)
    live = []
    for slot in range(slots):
        own_count = counts_ref[slot + 1]
        far_count = counts_ref[0 if slot == 0 else slots + 1]
        live.append((key_pos < own_count) | ((key_pos >= tile_len) & (key_pos < tile_len + far_count)))
    row_pos = lax.broadcasted_iota(jnp.int32, (tile_len, 1), 0)
    units = [(slot, head) for head in range(width // HEAD_DIM) for slot in range(slots)]

    scores = []
    for slot, head in units:
        cols = pl.ds(head * HEAD_DIM, HEAD_DIM)
        halo_ref = left_ref if slot == 0 else right_ref
        keys = jnp.concatenate([own_ref[slot, 1, :, cols], halo_ref[0, :, cols]], axis=0)
        raw = lax.dot_general(
            own_ref[slot, 0, :, cols],
            keys,
            (((1,), (1,)), ((), ())),
            preferred_element_type=jnp.float32,
        )
        scores.append(jnp.where(live[slot], raw * (1.0 / math.sqrt(HEAD_DIM)), jnp.float32(-1e30)))
    largest = [jnp.max(s, axis=-1, keepdims=True) for s in scores]
    weights = [jnp.exp(s - top) for s, top in zip(scores, largest)]
    totals = [jnp.sum(w, axis=-1, keepdims=True) for w in weights]
    for (slot, head), weight, total in zip(units, weights, totals):
        cols = pl.ds(head * HEAD_DIM, HEAD_DIM)
        halo_ref = left_ref if slot == 0 else right_ref
        values = jnp.concatenate([own_ref[slot, 2, :, cols], halo_ref[1, :, cols]], axis=0)
        probabilities = (weight * (1.0 / total)).astype(jnp.bfloat16)
        mixed = jnp.dot(probabilities, values, preferred_element_type=jnp.float32)
        out_ref[slot, :, cols] = jnp.where(row_pos < counts_ref[slot + 1], mixed, 0.0).astype(
            jnp.bfloat16
        )


def attention(nearby, own, left, right, stream):
    slots, _, tile_len, width = own.shape
    block = HEADS_AT_ONCE * HEAD_DIM
    own_spec = pl.BlockSpec((slots, 3, tile_len, block), lambda h, c: (0, 0, 0, h))
    halo_spec = pl.BlockSpec((None, 2, tile_len, block), lambda h, c: (stream, 0, 0, h))
    return pl.pallas_call(
        attend_kernel,
        grid_spec=pltpu.PrefetchScalarGridSpec(
            num_scalar_prefetch=1,
            grid=(width // block,),
            in_specs=[own_spec, halo_spec, halo_spec],
            out_specs=pl.BlockSpec((slots, tile_len, block), lambda h, c: (0, 0, h)),
        ),
        out_shape=jax.ShapeDtypeStruct((slots, tile_len, width), jnp.bfloat16),
        compiler_params=pltpu.CompilerParams(vmem_limit_bytes=48 * 1024 * 1024),
        cost_estimate=pl.CostEstimate(
            flops=0 * slots * tile_len * tile_len * width,
            bytes_accessed=0 * slots * tile_len * width,
            transcendentals=0,
        ),
        name="attention",
    )(nearby, own, left, right)


def whole_lanes(columns):
    return -(-columns // LANES) * LANES


def on_diagonal():
    row = lax.broadcasted_iota(jnp.int32, (LANES, LANES), 0)
    return row == lax.broadcasted_iota(jnp.int32, (LANES, LANES), 1)


def project(places, valid, clip_index, gathered, weights, total, peers):
    stream_count = len(gathered)
    keys = gathered[0][0]
    clip_count = 1 + max(clip for _, clip in keys)
    place_count = 1 + max(place for place, _ in keys)
    _, block_rows, depth = gathered[0][1][0].shape
    columns = sum(part.shape[0] for part in weights[0])
    lanes = whole_lanes(columns)
    row_count = stream_count * block_rows
    shard_total = len(weights)
    part_total = sum(len(parts) for parts in weights)
    scalars = jnp.stack([jnp.int32(n) for n in (*places, *valid, clip_index)])
    flat = [stack for _, stacks in gathered for stack in stacks]

    def kernel(scalars_ref, *refs):
        block_refs = refs[: len(flat)]
        weight_refs = refs[len(flat) : len(flat) + part_total]
        total_ref = refs[len(flat) + part_total] if total is not None else None
        rows, held, row_sem, weight_sem, total_sem = refs[-5:]
        out_ref = refs[len(operands)]
        squares_ref = refs[len(operands) + 1]

        def weight_copies(shard):
            parts = len(weights[shard])
            for n in range(parts):
                size = columns // parts
                yield pltpu.make_async_copy(
                    weight_refs[sum(len(p) for p in weights[:shard]) + n],
                    held.at[shard, pl.ds(n * size, size)],
                    weight_sem.at[shard, n],
                )

        def row_copy(place, shard, clip, stream):
            at = gathered[stream][0].index((place, clip))
            near = gathered[stream][1][0].shape[0]
            source = block_refs[2 * stream + at // near].at[at % near]
            first = pl.multiple_of(
                (clip ^ scalars_ref[2 * shard_total]) * row_count + stream * block_rows, 16
            )
            return pltpu.make_async_copy(
                source,
                rows.at[shard, pl.ds(first, block_rows)],
                row_sem.at[shard, clip, stream],
            )

        if total is not None:
            pltpu.make_async_copy(total_ref, out_ref, total_sem).start()
        for shard in range(shard_total):

            @pl.when(scalars_ref[shard_total + shard] == 1)
            def _():
                for copy in weight_copies(shard):
                    copy.start()
                for place in range(place_count):

                    @pl.when(scalars_ref[shard] == place)
                    def _():
                        for clip in range(clip_count):
                            for stream in range(stream_count):
                                row_copy(place, shard, clip, stream).start()

        if total is not None:
            pltpu.make_async_copy(total_ref, out_ref, total_sem).wait()
        else:
            out_ref[...] = jnp.zeros_like(out_ref)

        for shard in range(shard_total):

            @pl.when(scalars_ref[shard_total + shard] == 1)
            def _():
                for copy in weight_copies(shard):
                    copy.wait()
                for clip in range(clip_count):
                    for stream in range(stream_count):
                        row_copy(0, shard, clip, stream).wait()
                if lanes > columns:
                    held[shard, columns:] = jnp.zeros((lanes - columns, depth), held.dtype)
                for clip in range(clip_count):
                    out_ref[clip] += lax.dot_general(
                        rows[shard, pl.ds(clip * row_count, row_count)],
                        held[shard],
                        (((1,), (1,)), ((), ())),
                        preferred_element_type=jnp.float32,
                    )

        if peers:
            diagonal = on_diagonal()
            for clip in range(clip_count):
                for first in range(0, row_count, LANES):
                    piece = out_ref[clip, pl.ds(first, LANES)]
                    sums = jnp.sum(piece * piece, axis=1, keepdims=True)
                    sums = jnp.sum(jnp.where(diagonal, sums, 0.0), axis=0, keepdims=True)
                    squares_ref[:, pl.ds(clip * row_count + first, LANES)] = jnp.broadcast_to(
                        sums, (peers, LANES)
                    )

    operands = [*flat, *(part for parts in weights for part in parts)]
    if total is not None:
        operands.append(total)
    in_specs = [pl.BlockSpec(memory_space=pl.ANY) for _ in operands]
    out_shape = [jax.ShapeDtypeStruct((clip_count, row_count, lanes), jnp.float32)]
    if peers:
        out_shape.append(jax.ShapeDtypeStruct((peers, clip_count * row_count), jnp.float32))
    return pl.pallas_call(
        kernel,
        in_specs=[pl.BlockSpec(memory_space=pltpu.SMEM)] + in_specs,
        out_specs=[pl.BlockSpec(memory_space=pltpu.VMEM)] * len(out_shape),
        out_shape=out_shape,
        scratch_shapes=[
            pltpu.VMEM((shard_total, clip_count * row_count, depth), jnp.bfloat16),
            pltpu.VMEM((shard_total, lanes, depth), jnp.bfloat16),
            pltpu.SemaphoreType.DMA((shard_total, clip_count, stream_count)),
            pltpu.SemaphoreType.DMA((shard_total, max(len(parts) for parts in weights))),
            pltpu.SemaphoreType.DMA,
        ],
        compiler_params=pltpu.CompilerParams(vmem_limit_bytes=56 * 1024 * 1024),
        cost_estimate=pl.CostEstimate(
            flops=2 * clip_count * row_count * depth * columns * shard_total,
            bytes_accessed=shard_total * depth * (clip_count * row_count + columns) * 2,
            transcendentals=0,
        ),
        name="project",
    )(scalars, *operands)


def finish(total, squares, gain, model_width, devices):
    clip_count, row_count, lanes = total.shape
    columns = gain.shape[0]
    near_rows = row_count // 2
    gain = jnp.pad(gain, (0, lanes - columns))[None]

    def kernel(total_ref, squares_ref, gain_ref, features_ref, row_ref):
        clip = pl.program_id(0)
        diagonal = on_diagonal()
        scales = []
        for first in range(0, row_count, LANES):
            at = pl.ds(pl.multiple_of(clip * row_count + first, LANES), LANES)
            mean = jnp.sum(squares_ref[:, at], axis=0, keepdims=True) / model_width
            scale = jnp.broadcast_to(lax.rsqrt(mean + epsilon), (LANES, LANES))
            scales.append(jnp.sum(jnp.where(diagonal, scale, 0.0), axis=1, keepdims=True))
        scale = jnp.concatenate(scales, axis=0)
        clean = total_ref[0, :near_rows] * scale[:near_rows]
        features_ref[0] = (clean * gain_ref[...]).astype(jnp.bfloat16)
        difference = total_ref[0, near_rows:] * scale[near_rows:] - clean
        sums = jnp.sum(difference * difference, axis=0, keepdims=True)
        penalty = jnp.sum(sums * gain_ref[...] * gain_ref[...], axis=1, keepdims=True)
        lane = lax.broadcasted_iota(jnp.int32, (1, lanes), 1)
        sums = sums + jnp.where(lane == columns + clip, penalty, 0.0)
        sums = jnp.broadcast_to(sums, row_ref.shape)

        @pl.when(clip == 0)
        def _():
            row_ref[...] = sums

        @pl.when(clip > 0)
        def _():
            row_ref[...] += sums

    return pl.pallas_call(
        kernel,
        grid=(clip_count,),
        in_specs=[
            pl.BlockSpec((1, row_count, lanes), lambda c: (c, 0, 0)),
            pl.BlockSpec(squares.shape, lambda c: (0, 0)),
            pl.BlockSpec((1, lanes), lambda c: (0, 0)),
        ],
        out_specs=[
            pl.BlockSpec((1, near_rows, lanes), lambda c: (c, 0, 0)),
            pl.BlockSpec((devices, lanes), lambda c: (0, 0)),
        ],
        out_shape=[
            jax.ShapeDtypeStruct((clip_count, near_rows, lanes), jnp.bfloat16),
            jax.ShapeDtypeStruct((devices, lanes), jnp.float32),
        ],
        compiler_params=pltpu.CompilerParams(vmem_limit_bytes=32 * 1024 * 1024),
        name="finish",
    )(total, squares, gain)


def conclude(rows, gain, model_index, clip_index, model_count, clip_count, tokens, model_width):
    devices, lanes = rows.shape
    columns = gain.shape[0] // clip_count

    def kernel(index_ref, rows_ref, gain_ref, penalty_ref, grad_ref):
        row = lax.broadcasted_iota(jnp.int32, (devices, lanes), 0)
        model = (row // clip_count) % model_count
        sums = []
        for clip in range(clip_count):
            mine = (model == index_ref[0]) & (row % clip_count == clip)
            sums.append(
                jnp.sum(jnp.where(mine, rows_ref[...], 0.0), axis=0, keepdims=True)[:, :columns]
            )
        sums = jnp.concatenate(sums, axis=1)
        grad_ref[...] = gain_ref[...] * sums / (sigma_noise * sigma_noise * tokens)
        lane = lax.broadcasted_iota(jnp.int32, (devices, lanes), 1)
        own = jnp.where(lane == columns + index_ref[1], rows_ref[...], 0.0)
        total = jnp.sum(jnp.sum(own, axis=0, keepdims=True), axis=1, keepdims=True)
        penalty_ref[...] = total / (sigma_noise * sigma_noise * tokens * model_width)

    penalty, grad = pl.pallas_call(
        kernel,
        in_specs=[pl.BlockSpec(memory_space=pltpu.SMEM)]
        + [pl.BlockSpec(memory_space=pltpu.VMEM)] * 2,
        out_specs=[pl.BlockSpec(memory_space=pltpu.VMEM)] * 2,
        out_shape=[
            jax.ShapeDtypeStruct((1, 1), jnp.float32),
            jax.ShapeDtypeStruct((1, gain.shape[0]), jnp.float32),
        ],
        name="conclude",
    )(jnp.stack([model_index, clip_index]).astype(jnp.int32), rows, gain[None])
    return penalty[0], grad[0]


def swap(array, axis, distance):
    count = lax.axis_size(axis)
    return lax.ppermute(array, axis, [(i, i ^ distance) for i in range(count)])


def distances(axis):
    count = lax.axis_size(axis)
    return [(axis, 1 << bit) for bit in reversed(range(count.bit_length() - 1))]


def spread(block, order, before_step):
    keys = [(0, 0)]
    held = block[None]
    received = held[:0]
    for step, (axis, distance) in enumerate(order):
        held = jnp.concatenate([held, received]) if received.shape[0] else held
        held = before_step(step, held)
        received = swap(held, axis, distance)
        keys += [(m ^ distance, c) if axis == "mp" else (m, c ^ distance) for m, c in keys]
    return keys, (held, received)


def collect(rows, axes):
    return lax.all_to_all(rows, axes, split_axis=0, concat_axis=0, tiled=True)


def pick(options, index):
    return lax.select_n(index, *options) if len(options) > 1 else options[0]


def local(projections, perturbation, out_weight, norm_gain, live_counts):
    tile_len = projections.shape[2]
    local_width = projections.shape[4]
    slots = projections.shape[1]
    slab_count = lax.axis_size("frames")
    slab_index = lax.axis_index("frames")
    model_count = lax.axis_size("mp")
    model_index = lax.axis_index("mp")
    clip_count = lax.axis_size("dp")
    clip_index = lax.axis_index("dp")
    model_width = local_width * model_count
    token_total = slots * slab_count * tile_len
    half = local_width // clip_count
    near_rows = slots * tile_len

    def own_columns(array):
        return pick(
            [array[..., n * half : (n + 1) * half] for n in range(clip_count)], clip_index
        )

    clean = projections[0].transpose(0, 2, 1, 3)
    noise = perturbation[0].transpose(0, 2, 1, 3)
    perturbed = perturb(clean, noise)
    up = [(i, i + 1) for i in range(slab_count - 1)]
    down = [(i + 1, i) for i in range(slab_count - 1)]

    streams = (clean, perturbed)
    tail = jnp.stack([stream[slots - 1, 1:] for stream in streams])
    head = jnp.stack([stream[0, 1:] for stream in streams])
    tail, head, out_weight = lax.optimization_barrier((tail, head, out_weight))
    left = lax.ppermute(tail, "frames", up)
    right = lax.ppermute(head, "frames", down)

    own_weight = own_columns(out_weight).T
    line = slab_count == model_count and slab_count == 4
    last = slab_count - 1
    part = half // 2
    near, passed, across = [], [], []

    if line:
        near = [lax.ppermute(own_weight, "frames", up), lax.ppermute(own_weight, "frames", down)]

    def before_step(stream, step, value):
        nonlocal near, passed, across
        if line and stream == 0 and step == 1:
            value, near = lax.optimization_barrier((value, near))
            passed = [
                lax.ppermute(near[0], "frames", up[1:]),
                lax.ppermute(near[1], "frames", down[:2]),
            ]
            across = [
                lax.ppermute(block, "frames", [(0, last), (last, 0)])
                for block in (own_weight[:part], own_weight[part:])
            ]
        if line and stream == 1 and step == 2:
            value, passed, across[0] = lax.optimization_barrier((value, passed, across[0]))
        return value

    counts = jnp.pad(live_counts[0], (1, 1))
    nearby = lax.dynamic_slice_in_dim(counts, slots * slab_index, slots + 2)

    gathered = []
    orders = (
        distances("dp") + distances("mp"),
        distances("mp")[:1] + distances("dp") + distances("mp")[1:],
    )
    for n, order in enumerate(orders):
        attended = attention(nearby, streams[n], left, right, n).reshape(near_rows, local_width)
        gathered.append(
            spread(attended, order, lambda step, value, n=n: before_step(n, step, value))
        )

    if line:
        at_end = (slab_index == 0) | (slab_index == last)
        far = (slab_index + 2) % slab_count
        shards = [
            ([own_weight], slab_index, jnp.int32(1)),
            ([near[0]], jnp.maximum(slab_index - 1, 0), slab_index > 0),
            ([near[1]], jnp.minimum(slab_index + 1, last), slab_index < last),
            ([passed[0]], far, slab_index >= 2),
            ([passed[1]], far, slab_index < 2),
            (across, last - slab_index, at_end),
        ]

    peers = model_count * clip_count

    def project_shards(some, total, peers):
        return project(
            [place ^ model_index for _, place, _ in some],
            [exists for _, _, exists in some],
            clip_index,
            gathered,
            [weight for weight, _, _ in some],
            total,
            peers,
        )

    if line:
        (total,) = project_shards(shards[:5], None, 0)
        total, squares = project_shards(shards[5:], total, peers)
    else:
        weight = lax.all_gather(own_weight, "frames", axis=1, tiled=True)
        shards = [
            (
                [lax.dynamic_slice_in_dim(weight, m * local_width, local_width, axis=1)],
                jnp.int32(m),
                jnp.int32(1),
            )
            for m in range(model_count)
        ]
        total, squares = project_shards(shards, None, peers)

    squares = collect(squares, ("mp", "dp"))
    features, sums = finish(
        total, squares, own_columns(norm_gain), model_width, slab_count * model_count * clip_count
    )
    sums = collect(sums, ("frames", "mp", "dp"))

    features = features[..., :half].reshape(clip_count, slots, tile_len, half)
    columns = [pick([features[d] for d in range(clip_count)], clip_index)]
    for distance in range(1, clip_count):
        sent = pick([features[d ^ distance] for d in range(clip_count)], clip_index)
        columns.append(swap(sent, "dp", distance))
    features = jnp.concatenate(
        [
            pick([columns[n ^ d] for d in range(clip_count)], clip_index)
            for n in range(clip_count)
        ],
        axis=-1,
    )[None]
    sums, features = lax.optimization_barrier((sums, features))
    penalty, gain_grad = conclude(
        sums,
        norm_gain,
        model_index,
        clip_index,
        model_count,
        clip_count,
        token_total,
        model_width,
    )
    return (features, penalty, gain_grad)


def solution(mesh):
    placed = (
        P("dp", "frames", None, None, "mp"),
        P("dp", "frames", None, None, "mp"),
        P("frames", "mp"),
        P("mp"),
        P("dp", None),
    )
    return jax.shard_map(
        local,
        mesh=mesh,
        in_specs=placed,
        out_specs=(P("dp", "frames", None, "mp"), P("dp"), P("mp")),
        check_vma=False,
    )
```

profile of v0, /device:TPU:0, one launch (start us, length us, event | category | flops | bytes accessed | tf_op | source)
XLA Modules:
  0.0 128.9 jit_solution(14640683102462323824)
XLA Ops:
  0.6 1.8 %fusion.own_ref = bf16[2,3,96,896]{3,2,1,0:T(8,128)(2,1)S(1)} fusion(bf16[1,2,96,3,896]{4,2,3,1,0:T(8,128)(2,1)} %param.6, bf16[1,2,96,3,896]{4,2,3,1,0:T(8,128)(2,1)} %param.5), kind=kLoop, calls=%fused_computation.1 | loop fusion | flops 2580480 | bytes 3096576 | tf_op jit(solution)/shard_map/convert_element_type | solution.py:20
  5.0 5.0 %collective-permute-start = (bf16[2,2,96,896]{3,2,1,0:T(8,128)(2,1)}, bf16[2,2,96,896]{3,2,1,0:T(8,128)(2,1)S(1)}, u32[]{:S(2)}, u32[]{:S(2)}) collective-permute-start(bf16[2,2,96,896]{3,2,1,0:T(8,128)(2,1)} %get-tuple-element.21), channel_id=1, source_target_pairs={{0,8},{8,16},{16,24},{1,9},{9,17},{17,25},{2,10},{10,18},{18,26},{... | collective-permute-start | bytes 2064392 | tf_op jit(solution)/shard_map/ppermute | solution.py:366
  11.3 3.6 %copy.10 = bf16[896,896]{0,1:T(8,128)(2,1)} copy(bf16[896,896]{1,0:T(8,128)(2,1)} %param.7) | data formatting | bytes 3211264 | tf_op jit(solution)/shard_map/optimization_barrier | solution.py:365
  14.9 2.4 %fusion.1.refs_4_ = bf16[448,896]{1,0:T(8,128)(2,1)} fusion(bf16[896,896]{0,1:T(8,128)(2,1)} %copy.10, pred[]{:T(512)S(6)} %select_n.57), kind=kLoop, calls=%fused_computation.4 | loop fusion | flops 401408 | bytes 2408449 | tf_op jit(solution)/shard_map/transpose | solution.py:369
  17.2 5.4 %collective-permute-start.3 = (bf16[448,896]{1,0:T(8,128)(2,1)}, bf16[448,896]{1,0:T(8,128)(2,1)}, u32[]{:S(2)}, u32[]{:S(2)}) collective-permute-start(bf16[448,896]{1,0:T(8,128)(2,1)} %fusion.1.refs_4_), channel_id=1, source_target_pairs={{0,8},{8,16},{16,24},{1,9},{9,17},{17,25},{2,10},{10,18},{18,26},{... | collective-permute-start | bytes 2408456 | tf_op jit(solution)/shard_map/ppermute | solution.py:376
  24.0 2.0 %collective-permute-done.left_ref = bf16[2,2,96,896]{3,2,1,0:T(8,128)(2,1)S(1)} collective-permute-done((bf16[2,2,96,896]{3,2,1,0:T(8,128)(2,1)}, bf16[2,2,96,896]{3,2,1,0:T(8,128)(2,1)S(1)}, u32[]{:S(2)}, u32[]{:S(2)}) %collective-permute-start) | collective-permute-done | bytes 688160 | tf_op jit(solution)/shard_map/ppermute | solution.py:366
  26.0 4.4 %collective-permute-done.1.right_ref = bf16[2,2,96,896]{3,2,1,0:T(8,128)(2,1)S(1)} collective-permute-done((bf16[2,2,96,896]{3,2,1,0:T(8,128)(2,1)}, bf16[2,2,96,896]{3,2,1,0:T(8,128)(2,1)S(1)}, u32[]{:S(2)}, u32[]{:S(2)}) %collective-permute-start.1) | collective-permute-done | bytes 688160 | tf_op jit(solution)/shard_map/ppermute | solution.py:367
  30.4 4.5 %attention.2 = bf16[2,96,896]{2,1,0:T(8,128)(2,1)S(1)} custom-call(s32[4]{0:T(128)S(1)} %pad_dynamic-slice_fusion.counts_ref, bf16[2,3,96,896]{3,2,1,0:T(8,128)(2,1)S(1)} %bitcast.42, bf16[2,2,96,896]{3,2,1,0:T(8,128)(2,1)S(1)} %collective-permute-done.left_ref, bf16[2,2,96,896]{3,2,1,0:T(8,128)(2,1)S(1)} %collective-permute-done.1.right_ref), custom_call_target="tpu_custom_call" | custom-call | tf_op jit(solution)/shard_map/attention/pallas_call | solution.py:65
  34.9 1.6 %collective-permute-start.2 = (bf16[1,192,896]{2,1,0:T(8,128)(2,1)S(1)}, bf16[1,192,896]{2,1,0:T(8,128)(2,1)S(1)}, u32[]{:S(2)}, u32[]{:S(2)}) collective-permute-start(bf16[1,192,896]{2,1,0:T(8,128)(2,1)S(1)} %bitcast.46), channel_id=1, source_target_pairs={{0,1},{1,0},{2,3},{3,2},{4,5},{5,4},{6,7},{7,6},{8,9},{9,8},{10,11... | collective-permute-start | bytes 1032200 | tf_op jit(solution)/shard_map/ppermute | solution.py:308
  36.5 4.5 %attention.3 = bf16[2,96,896]{2,1,0:T(8,128)(2,1)S(1)} custom-call(s32[4]{0:T(128)S(1)} %pad_dynamic-slice_fusion.counts_ref, bf16[2,3,96,896]{3,2,1,0:T(8,128)(2,1)S(1)} %fusion.own_ref, bf16[2,2,96,896]{3,2,1,0:T(8,128)(2,1)S(1)} %collective-permute-done.left_ref, bf16[2,2,96,896]{3,2,1,0:T(8,128)(2,1)S(1)} %collective-permute-done.1.right_ref), custom_call_target="tpu_custom_call" | custom-call | tf_op jit(solution)/shard_map/attention/pallas_call | solution.py:65
  41.0 1.6 %collective-permute-start.7 = (bf16[1,192,896]{2,1,0:T(8,128)(2,1)S(1)}, bf16[1,192,896]{2,1,0:T(8,128)(2,1)S(1)}, u32[]{:S(2)}, u32[]{:S(2)}) collective-permute-start(bf16[1,192,896]{2,1,0:T(8,128)(2,1)S(1)} %bitcast.43), channel_id=1, source_target_pairs={{0,4},{2,6},{4,0},{6,2},{1,5},{3,7},{5,1},{7,3},{8,12},{10,14},{12... | collective-permute-start | bytes 1032200 | tf_op jit(solution)/shard_map/ppermute | solution.py:308
  42.7 3.6 %collective-permute-done.4.refs_6_ = bf16[448,896]{1,0:T(8,128)(2,1)} collective-permute-done((bf16[448,896]{1,0:T(8,128)(2,1)}, bf16[448,896]{1,0:T(8,128)(2,1)}, u32[]{:S(2)}, u32[]{:S(2)}) %collective-permute-start.4) | collective-permute-done | bytes 802848 | tf_op jit(solution)/shard_map/ppermute | solution.py:376
  52.6 3.5 %collective-permute-start.11 = (bf16[224,896]{1,0:T(8,128)(2,1)S(1)}, bf16[224,896]{1,0:T(8,128)(2,1)S(1)}, u32[]{:S(2)}, u32[]{:S(2)}) collective-permute-start(bf16[224,896]{1,0:T(8,128)(2,1)S(1)} %get-tuple-element.44), channel_id=1, source_target_pairs={{0,24},{24,0},{1,25},{25,1},{2,26},{26,2},{3,27},{27,3},{4,28},{28... | collective-permute-start | bytes 1204232 | tf_op jit(solution)/shard_map/ppermute | solution.py:387
  57.1 6.0 %collective-permute-done.5 = bf16[2,192,896]{2,1,0:T(8,128)(2,1)S(1)} collective-permute-done((bf16[2,192,896]{2,1,0:T(8,128)(2,1)S(1)}, bf16[2,192,896]{2,1,0:T(8,128)(2,1)S(1)}, u32[]{:S(2)}, u32[]{:S(2)}) %collective-permute-start.5) | collective-permute-done | bytes 688160 | tf_op jit(solution)/shard_map/ppermute | solution.py:308
  65.8 15.3 %collective-permute-done.10.refs_8_ = bf16[448,896]{1,0:T(8,128)(2,1)S(1)} collective-permute-done((bf16[448,896]{1,0:T(8,128)(2,1)}, bf16[448,896]{1,0:T(8,128)(2,1)S(1)}, u32[]{:S(2)}, u32[]{:S(2)}) %collective-permute-start.10) | collective-permute-done | bytes 802848 | tf_op jit(solution)/shard_map/ppermute | solution.py:384
  82.0 1.9 %collective-permute-start.13 = (bf16[224,896]{1,0:T(8,128)(2,1)S(1)}, bf16[224,896]{1,0:T(8,128)(2,1)}, u32[]{:S(2)}, u32[]{:S(2)}) collective-permute-start(bf16[224,896]{1,0:T(8,128)(2,1)S(1)} %get-tuple-element.43), channel_id=1, source_target_pairs={{0,24},{24,0},{1,25},{25,1},{2,26},{26,2},{3,27},{27,3},{4,28},{28... | collective-permute-start | bytes 1204232 | tf_op jit(solution)/shard_map/ppermute | solution.py:387
  86.3 6.7 %project.2.refs_6_ = f32[2,384,512]{2,1,0:T(8,128)} custom-call(s32[11]{0:T(128)} %stack.88.scalars_ref, bf16[4,192,896]{2,1,0:T(8,128)(2,1)} %constant_dynamic-update-slice_fusion.refs_0_, bf16[4,192,896]{2,1,0:T(8,128)(2,1)} %copy-done.3, bf16[4,192,896]{2,1,0:T(8,128)(2,1)} %copy-done.2, bf16[4,192,896]{2,1,0:T(8,128)(2,1)} %collective-permute-done.12.refs_3_, ...), custom_call_target="tpu_custom_call" | custom-call | flops 3082813440 | bytes 10895360 | tf_op jit(solution)/shard_map/project/pallas_call | solution.py:196
  93.1 3.5 %collective-permute-done.13.refs_5_ = bf16[224,896]{1,0:T(8,128)(2,1)} collective-permute-done((bf16[224,896]{1,0:T(8,128)(2,1)S(1)}, bf16[224,896]{1,0:T(8,128)(2,1)}, u32[]{:S(2)}, u32[]{:S(2)}) %collective-permute-start.13) | collective-permute-done | bytes 401440 | tf_op jit(solution)/shard_map/ppermute | solution.py:387
  96.6 4.9 %project.3 = (f32[2,384,512]{2,1,0:T(8,128)}, f32[8,768]{1,0:T(8,128)}) custom-call(s32[3]{0:T(128)} %pad_add_fusion.scalars_ref, bf16[4,192,896]{2,1,0:T(8,128)(2,1)} %constant_dynamic-update-slice_fusion.refs_0_, bf16[4,192,896]{2,1,0:T(8,128)(2,1)} %copy-done.3, bf16[4,192,896]{2,1,0:T(8,128)(2,1)} %copy-done.2, ...), custom_call_target="tpu_custom_call" | custom-call | flops 616562688 | bytes 2179072 | tf_op jit(solution)/shard_map/project/pallas_call | solution.py:196
  102.8 3.3 %all-to-all-start = ((f32[8,1,768]{2,1,0:T(1,128)}), f32[8,1,768]{2,1,0:T(1,128)S(1)}, u32[]{:S(2)}, u32[]{:S(2)}) async-start(f32[8,1,768]{2,1,0:T(1,128)} %copy.12), calls=%async_computation | async-start | bytes 49152 | tf_op jit(solution)/shard_map/all_to_all | solution.py:329
  106.3 4.5 %all-to-all-done = f32[8,1,768]{2,1,0:T(1,128)S(1)} async-done(((f32[8,1,768]{2,1,0:T(1,128)}), f32[8,1,768]{2,1,0:T(1,128)S(1)}, u32[]{:S(2)}, u32[]{:S(2)}) %all-to-all-start) | async-done | bytes 24608 | tf_op jit(solution)/shard_map/all_to_all | solution.py:329
  114.4 2.6 %all-to-all-start.1 = ((f32[32,1,512]{2,1,0:T(1,128)}), f32[32,1,512]{2,1,0:T(1,128)S(1)}, u32[]{:S(2)}, u32[]{:S(2)}) async-start(f32[32,1,512]{2,1,0:T(1,128)} %copy.13), calls=%async_computation.1 | async-start | bytes 131072 | tf_op jit(solution)/shard_map/all_to_all | solution.py:329
  118.1 6.4 %all-to-all-done.1 = f32[32,1,512]{2,1,0:T(1,128)S(1)} async-done(((f32[32,1,512]{2,1,0:T(1,128)}), f32[32,1,512]{2,1,0:T(1,128)S(1)}, u32[]{:S(2)}, u32[]{:S(2)}) %all-to-all-start.1) | async-done | bytes 65568 | tf_op jit(solution)/shard_map/all_to_all | solution.py:329
  126.1 1.5 %conclude.1 = (f32[1,1]{1,0:T(1,128)}, f32[1,896]{1,0:T(1,128)}) custom-call(s32[2]{0:T(128)} %pad_add_fusion.1.index_ref, f32[32,512]{1,0:T(8,128)} %bitcast.52, f32[1,896]{1,0:T(1,128)} %broadcast_in_dim.11.gain_ref), custom_call_target="tpu_custom_call" | custom-call | tf_op jit(solution)/shard_map/conclude/pallas_call | solution.py:292
  (61 shorter events, 27.4 us)
Async XLA Ops:
  2.5 1.2 copy-start
  5.0 21.1 %collective-permute-start = (bf16[2,2,96,896]{3,2,1,0:T(8,128)(2,1)}, bf16[2,2,96,896]{3,2,1,0:T(8,128)(2,1)S(1)}, u32[]{:S(2)}, u32[]{:S(2)}) collective-permute-start(bf16[2,2,96,896]{3,2,1,0:T(8,128)(2,1)} %get-tuple-element.21), channel_id=1, source_target_pairs={{0,8},{8,16},{16,24},{1,9},{9,17},{17,25},{2,10},{10,18},{18,26},{... | collective-permute-start | bytes 2064392 | tf_op jit(solution)/shard_map/ppermute | solution.py:366
  9.9 20.5 %collective-permute-start.1 = (bf16[2,2,96,896]{3,2,1,0:T(8,128)(2,1)}, bf16[2,2,96,896]{3,2,1,0:T(8,128)(2,1)S(1)}, u32[]{:S(2)}, u32[]{:S(2)}) collective-permute-start(bf16[2,2,96,896]{3,2,1,0:T(8,128)(2,1)} %get-tuple-element.22), channel_id=1, source_target_pairs={{8,0},{16,8},{24,16},{9,1},{17,9},{25,17},{10,2},{18,10},{26,18},{... | collective-permute-start | bytes 2064392 | tf_op jit(solution)/shard_map/ppermute | solution.py:367
  14.9 9.1 %copy-start.8 = (s32[1,8]{1,0:T(1,128)S(1)}, s32[1,8]{1,0:T(1,128)}, u32[]{:S(2)}) copy-start(s32[1,8]{1,0:T(1,128)} %param.9) | copy-start | bytes 100
  17.2 25.4 %collective-permute-start.3 = (bf16[448,896]{1,0:T(8,128)(2,1)}, bf16[448,896]{1,0:T(8,128)(2,1)}, u32[]{:S(2)}, u32[]{:S(2)}) collective-permute-start(bf16[448,896]{1,0:T(8,128)(2,1)} %fusion.1.refs_4_), channel_id=1, source_target_pairs={{0,8},{8,16},{16,24},{1,9},{9,17},{17,25},{2,10},{10,18},{18,26},{... | collective-permute-start | bytes 2408456 | tf_op jit(solution)/shard_map/ppermute | solution.py:376
  22.7 23.6 %collective-permute-start.4 = (bf16[448,896]{1,0:T(8,128)(2,1)}, bf16[448,896]{1,0:T(8,128)(2,1)}, u32[]{:S(2)}, u32[]{:S(2)}) collective-permute-start(bf16[448,896]{1,0:T(8,128)(2,1)} %fusion.1.refs_4_), channel_id=1, source_target_pairs={{8,0},{16,8},{24,16},{9,1},{17,9},{25,17},{10,2},{18,10},{26,18},{... | collective-permute-start | bytes 2408456 | tf_op jit(solution)/shard_map/ppermute | solution.py:376
  34.9 7.7 %collective-permute-start.2 = (bf16[1,192,896]{2,1,0:T(8,128)(2,1)S(1)}, bf16[1,192,896]{2,1,0:T(8,128)(2,1)S(1)}, u32[]{:S(2)}, u32[]{:S(2)}) collective-permute-start(bf16[1,192,896]{2,1,0:T(8,128)(2,1)S(1)} %bitcast.46), channel_id=1, source_target_pairs={{0,1},{1,0},{2,3},{3,2},{4,5},{5,4},{6,7},{7,6},{8,9},{9,8},{10,11... | collective-permute-start | bytes 1032200 | tf_op jit(solution)/shard_map/ppermute | solution.py:308
  41.0 8.1 %collective-permute-start.7 = (bf16[1,192,896]{2,1,0:T(8,128)(2,1)S(1)}, bf16[1,192,896]{2,1,0:T(8,128)(2,1)S(1)}, u32[]{:S(2)}, u32[]{:S(2)}) collective-permute-start(bf16[1,192,896]{2,1,0:T(8,128)(2,1)S(1)} %bitcast.43), channel_id=1, source_target_pairs={{0,4},{2,6},{4,0},{6,2},{1,5},{3,7},{5,1},{7,3},{8,12},{10,14},{12... | collective-permute-start | bytes 1032200 | tf_op jit(solution)/shard_map/ppermute | solution.py:308
  46.3 16.9 %collective-permute-start.5 = (bf16[2,192,896]{2,1,0:T(8,128)(2,1)S(1)}, bf16[2,192,896]{2,1,0:T(8,128)(2,1)S(1)}, u32[]{:S(2)}, u32[]{:S(2)}) collective-permute-start(bf16[2,192,896]{2,1,0:T(8,128)(2,1)S(1)} %pad_maximum_fusion.3), channel_id=1, source_target_pairs={{0,4},{2,6},{4,0},{6,2},{1,5},{3,7},{5,1},{7,3},{8,12},{10,14},{12... | collective-permute-start | bytes 2064392 | tf_op jit(solution)/shard_map/ppermute | solution.py:308
  49.2 14.8 %collective-permute-start.8 = (bf16[2,192,896]{2,1,0:T(8,128)(2,1)S(1)}, bf16[2,192,896]{2,1,0:T(8,128)(2,1)S(1)}, u32[]{:S(2)}, u32[]{:S(2)}) collective-permute-start(bf16[2,192,896]{2,1,0:T(8,128)(2,1)S(1)} %pad_maximum_fusion.4), channel_id=1, source_target_pairs={{0,1},{1,0},{2,3},{3,2},{4,5},{5,4},{6,7},{7,6},{8,9},{9,8},{10,11... | collective-permute-start | bytes 2064392 | tf_op jit(solution)/shard_map/ppermute | solution.py:308
  49.4 16.3 %collective-permute-start.9 = (bf16[448,896]{1,0:T(8,128)(2,1)}, bf16[448,896]{1,0:T(8,128)(2,1)S(1)}, u32[]{:S(2)}, u32[]{:S(2)}) collective-permute-start(bf16[448,896]{1,0:T(8,128)(2,1)} %collective-permute-done.3.refs_5_), channel_id=1, source_target_pairs={{8,16},{16,24},{9,17},{17,25},{10,18},{18,26},{11,19},{19,27},{12,... | collective-permute-start | bytes 2408456 | tf_op jit(solution)/shard_map/ppermute | solution.py:383
  50.1 30.9 %collective-permute-start.10 = (bf16[448,896]{1,0:T(8,128)(2,1)}, bf16[448,896]{1,0:T(8,128)(2,1)S(1)}, u32[]{:S(2)}, u32[]{:S(2)}) collective-permute-start(bf16[448,896]{1,0:T(8,128)(2,1)} %collective-permute-done.4.refs_6_), channel_id=1, source_target_pairs={{8,0},{16,8},{9,1},{17,9},{10,2},{18,10},{11,3},{19,11},{12,4},{20... | collective-permute-start | bytes 2408456 | tf_op jit(solution)/shard_map/ppermute | solution.py:384
  52.6 13.1 %collective-permute-start.11 = (bf16[224,896]{1,0:T(8,128)(2,1)S(1)}, bf16[224,896]{1,0:T(8,128)(2,1)S(1)}, u32[]{:S(2)}, u32[]{:S(2)}) collective-permute-start(bf16[224,896]{1,0:T(8,128)(2,1)S(1)} %get-tuple-element.44), channel_id=1, source_target_pairs={{0,24},{24,0},{1,25},{25,1},{2,26},{26,2},{3,27},{27,3},{4,28},{28... | collective-permute-start | bytes 1204232 | tf_op jit(solution)/shard_map/ppermute | solution.py:387
  64.1 21.2 %collective-permute-start.6 = (bf16[4,192,896]{2,1,0:T(8,128)(2,1)}, bf16[4,192,896]{2,1,0:T(8,128)(2,1)S(1)}, u32[]{:S(2)}, u32[]{:S(2)}) collective-permute-start(bf16[4,192,896]{2,1,0:T(8,128)(2,1)} %constant_dynamic-update-slice_fusion.refs_0_), channel_id=1, source_target_pairs={{0,2},{2,0},{4,6},{6,4},{1,3},{3,1},{5,7},{7,5},{8,10},{10,8},{12,... | collective-permute-start | bytes 4128776 | tf_op jit(solution)/shard_map/ppermute | solution.py:308
  64.2 21.0 %copy-start.2 = (bf16[4,192,896]{2,1,0:T(8,128)(2,1)}, bf16[4,192,896]{2,1,0:T(8,128)(2,1)S(1)}, u32[]{:S(2)}) copy-start(bf16[4,192,896]{2,1,0:T(8,128)(2,1)S(1)} %pad_maximum_fusion.refs_2_) | copy-start | bytes 4128772
  65.7 15.3 %copy-start.4 = (bf16[224,896]{1,0:T(8,128)(2,1)}, bf16[224,896]{1,0:T(8,128)(2,1)S(1)}, u32[]{:S(2)}) copy-start(bf16[224,896]{1,0:T(8,128)(2,1)S(1)} %collective-permute-done.11.refs_4_) | copy-start | bytes 1204228
  65.7 15.3 %copy-start.6 = (bf16[448,896]{1,0:T(8,128)(2,1)}, bf16[448,896]{1,0:T(8,128)(2,1)S(1)}, u32[]{:S(2)}) copy-start(bf16[448,896]{1,0:T(8,128)(2,1)S(1)} %collective-permute-done.9.refs_7_) | copy-start | bytes 2408452
  81.1 4.2 %collective-permute-start.12 = (bf16[4,192,896]{2,1,0:T(8,128)(2,1)S(1)}, bf16[4,192,896]{2,1,0:T(8,128)(2,1)}, u32[]{:S(2)}, u32[]{:S(2)}) collective-permute-start(bf16[4,192,896]{2,1,0:T(8,128)(2,1)S(1)} %pad_maximum_fusion.refs_2_), channel_id=1, source_target_pairs={{0,2},{2,0},{4,6},{6,4},{1,3},{3,1},{5,7},{7,5},{8,10},{10,8},{12,... | collective-permute-start | bytes 4128776 | tf_op jit(solution)/shard_map/ppermute | solution.py:308
  82.0 14.5 %collective-permute-start.13 = (bf16[224,896]{1,0:T(8,128)(2,1)S(1)}, bf16[224,896]{1,0:T(8,128)(2,1)}, u32[]{:S(2)}, u32[]{:S(2)}) collective-permute-start(bf16[224,896]{1,0:T(8,128)(2,1)S(1)} %get-tuple-element.43), channel_id=1, source_target_pairs={{0,24},{24,0},{1,25},{25,1},{2,26},{26,2},{3,27},{27,3},{4,28},{28... | collective-permute-start | bytes 1204232 | tf_op jit(solution)/shard_map/ppermute | solution.py:387
  93.0 13.2 %copy-start.5 = (f32[896]{0:T(1024)S(1)}, f32[896]{0:T(1024)}, u32[]{:S(2)}) copy-start(f32[896]{0:T(1024)} %param.8) | copy-start | bytes 10756
  102.8 8.0 %all-to-all-start = ((f32[8,1,768]{2,1,0:T(1,128)}), f32[8,1,768]{2,1,0:T(1,128)S(1)}, u32[]{:S(2)}, u32[]{:S(2)}) async-start(f32[8,1,768]{2,1,0:T(1,128)} %copy.12), calls=%async_computation | async-start | bytes 49152 | tf_op jit(solution)/shard_map/all_to_all | solution.py:329
  110.8 1.4 %copy-start.1 = (f32[2,384,512]{2,1,0:T(8,128)S(1)}, f32[2,384,512]{2,1,0:T(8,128)}, u32[]{:S(2)}) copy-start(f32[2,384,512]{2,1,0:T(8,128)} %get-tuple-element.31.total_ref) | copy-start | bytes 4718596
  113.0 12.2 %collective-permute-start.14 = (bf16[2,96,448]{2,1,0:T(8,128)(2,1)S(1)}, bf16[2,96,448]{2,1,0:T(8,128)(2,1)S(1)}, u32[]{:S(2)}, u32[]{:S(2)}) collective-permute-start(bf16[2,96,448]{2,1,0:T(8,128)(2,1)S(1)} %bitcast.53), channel_id=1, source_target_pairs={{0,1},{1,0},{2,3},{3,2},{4,5},{5,4},{6,7},{7,6},{8,9},{9,8},{10,11... | collective-permute-start | bytes 516104 | tf_op jit(solution)/shard_map/ppermute | solution.py:308
  114.4 10.2 %all-to-all-start.1 = ((f32[32,1,512]{2,1,0:T(1,128)}), f32[32,1,512]{2,1,0:T(1,128)S(1)}, u32[]{:S(2)}, u32[]{:S(2)}) async-start(f32[32,1,512]{2,1,0:T(1,128)} %copy.13), calls=%async_computation.1 | async-start | bytes 131072 | tf_op jit(solution)/shard_map/all_to_all | solution.py:329
  (2 other events, 2.1 us)
where the time goes:
time: 130 us; the launch traced here: 129 us
  waiting for transfers between devices  48.7 us (37%)
  starting transfers between devices  31.9 us (25%)
  Pallas kernels  22.9 us (18%)
  local copies, waits for them, and re-layouts  15.4 us (12%)
  other arithmetic  9.19 us (7%)
    ppermute x1, waiting for transfers between devices, before_step(): lax.ppermute(near[1], 'frames', down[:2])  15.3 us
    pallas_call x2, Pallas kernels, project(): pl.pallas_call(kernel, in_specs=[pl.BlockSpec(memory_space=pltpu.SMEM)] +...  11.6 us
    all_to_all x2, waiting for transfers between devices, collect(): return lax.all_to_all(rows, axes, split_axis=0, concat_axis=0, tiled=True)  11 us
    pallas_call x2, Pallas kernels, attention(): pl.pallas_call(attend_kernel, grid_spec=pltpu.PrefetchScalarGridSpec(num_...  9.03 us
    ppermute x7, waiting for transfers between devices, swap(): return lax.ppermute(array, axis, [(i, i ^ distance) for i in range(count)])  7.46 us
    unnamed x21, local copies, waits for them, and re-layouts  6.15 us
    all_to_all x2, starting transfers between devices, collect(): return lax.all_to_all(rows, axes, split_axis=0, concat_axis=0, tiled=True)  5.91 us
    ppermute x7, starting transfers between devices, swap(): return lax.ppermute(array, axis, [(i, i ^ distance) for i in range(count)])  5.54 us
  transfers between devices with their start and end apart: 17, of which 10 were waited for; matrix products, arithmetic and copies ran while one was open for 10% of the time, Pallas kernels for 12%

commit v1 on v0

--- a/solution.py
+++ b/solution.py
@@ -90,42 +90,39 @@
     return row == lax.broadcasted_iota(jnp.int32, (LANES, LANES), 1)
 
 
-def project(places, valid, clip_index, gathered, weights, total, peers):
+def project(places, valid, clip_index, gathered, weights, total, columns, peers):
     stream_count = len(gathered)
-    keys = gathered[0][0]
-    clip_count = 1 + max(clip for _, clip in keys)
-    place_count = 1 + max(place for place, _ in keys)
-    _, block_rows, depth = gathered[0][1][0].shape
-    columns = sum(part.shape[0] for part in weights[0])
+    home = [
+        {key: (n, at) for n, (keys, _) in enumerate(stacks) for at, key in enumerate(keys)}
+        for stacks in gathered
+    ]
+    clip_count = 1 + max(clip for _, clip in home[0])
+    place_count = 1 + max(place for place, _ in home[0])
+    _, block_rows, depth = gathered[0][0][1].shape
     lanes = whole_lanes(columns)
     row_count = stream_count * block_rows
     shard_total = len(weights)
-    part_total = sum(len(parts) for parts in weights)
-    scalars = jnp.stack([jnp.int32(n) for n in (*places, *valid, clip_index)])
-    flat = [stack for _, stacks in gathered for stack in stacks]
+    scalars = jnp.stack([jnp.int32(n) for n in (*places, *valid, clip_index)]).astype(jnp.int32)
+    flat = [array for stacks in gathered for _, array in stacks]
+    base = [sum(len(stacks) for stacks in gathered[:n]) for n in range(stream_count)]
 
     def kernel(scalars_ref, *refs):
         block_refs = refs[: len(flat)]
-        weight_refs = refs[len(flat) : len(flat) + part_total]
-        total_ref = refs[len(flat) + part_total] if total is not None else None
+        weight_refs = refs[len(flat) : len(flat) + shard_total]
+        total_ref = refs[len(flat) + shard_total] if total is not None else None
         rows, held, row_sem, weight_sem, total_sem = refs[-5:]
         out_ref = refs[len(operands)]
         squares_ref = refs[len(operands) + 1]
 
-        def weight_copies(shard):
-            parts = len(weights[shard])
-            for n in range(parts):
-                size = columns // parts
-                yield pltpu.make_async_copy(
-                    weight_refs[sum(len(p) for p in weights[:shard]) + n],
-                    held.at[shard, pl.ds(n * size, size)],
-                    weight_sem.at[shard, n],
-                )
+        def weight_copy(shard):
+            size = weights[shard][1].shape[0]
+            return pltpu.make_async_copy(
+                weight_refs[shard], held.at[shard, pl.ds(0, size)], weight_sem.at[shard]
+            )
 
         def row_copy(place, shard, clip, stream):
-            at = gathered[stream][0].index((place, clip))
-            near = gathered[stream][1][0].shape[0]
-            source = block_refs[2 * stream + at // near].at[at % near]
+            stack, at = home[stream][place, clip]
+            source = block_refs[base[stream] + stack].at[at]
             first = pl.multiple_of(
                 (clip ^ scalars_ref[2 * shard_total]) * row_count + stream * block_rows, 16
             )
@@ -141,8 +138,7 @@
 
             @pl.when(scalars_ref[shard_total + shard] == 1)
             def _():
-                for copy in weight_copies(shard):
-                    copy.start()
+                weight_copy(shard).start()
                 for place in range(place_count):
 
                     @pl.when(scalars_ref[shard] == place)
@@ -160,17 +156,19 @@
 
             @pl.when(scalars_ref[shard_total + shard] == 1)
             def _():
-                for copy in weight_copies(shard):
-                    copy.wait()
+                weight_copy(shard).wait()
                 for clip in range(clip_count):
                     for stream in range(stream_count):
                         row_copy(0, shard, clip, stream).wait()
-                if lanes > columns:
-                    held[shard, columns:] = jnp.zeros((lanes - columns, depth), held.dtype)
+                first, array = weights[shard]
+                size = array.shape[0]
+                wide = whole_lanes(size)
+                if wide > size:
+                    held[shard, size:wide] = jnp.zeros((wide - size, depth), held.dtype)
                 for clip in range(clip_count):
-                    out_ref[clip] += lax.dot_general(
+                    out_ref[clip, :, pl.ds(first, wide)] += lax.dot_general(
                         rows[shard, pl.ds(clip * row_count, row_count)],
-                        held[shard],
+                        held[shard, pl.ds(0, wide)],
                         (((1,), (1,)), ((), ())),
                         preferred_element_type=jnp.float32,
                     )
@@ -182,17 +180,17 @@
                     piece = out_ref[clip, pl.ds(first, LANES)]
                     sums = jnp.sum(piece * piece, axis=1, keepdims=True)
                     sums = jnp.sum(jnp.where(diagonal, sums, 0.0), axis=0, keepdims=True)
-                    squares_ref[:, pl.ds(clip * row_count + first, LANES)] = jnp.broadcast_to(
-                        sums, (peers, LANES)
+                    squares_ref[:, :, pl.ds(clip * row_count + first, LANES)] = jnp.broadcast_to(
+                        sums[None], (peers, 1, LANES)
                     )
 
-    operands = [*flat, *(part for parts in weights for part in parts)]
+    operands = [*flat, *(array for _, array in weights)]
     if total is not None:
         operands.append(total)
     in_specs = [pl.BlockSpec(memory_space=pl.ANY) for _ in operands]
     out_shape = [jax.ShapeDtypeStruct((clip_count, row_count, lanes), jnp.float32)]
     if peers:
-        out_shape.append(jax.ShapeDtypeStruct((peers, clip_count * row_count), jnp.float32))
+        out_shape.append(jax.ShapeDtypeStruct((peers, 1, clip_count * row_count), jnp.float32))
     return pl.pallas_call(
         kernel,
         in_specs=[pl.BlockSpec(memory_space=pltpu.SMEM)] + in_specs,
@@ -202,7 +200,7 @@
             pltpu.VMEM((shard_total, clip_count * row_count, depth), jnp.bfloat16),
             pltpu.VMEM((shard_total, lanes, depth), jnp.bfloat16),
             pltpu.SemaphoreType.DMA((shard_total, clip_count, stream_count)),
-            pltpu.SemaphoreType.DMA((shard_total, max(len(parts) for parts in weights))),
+            pltpu.SemaphoreType.DMA((shard_total,)),
             pltpu.SemaphoreType.DMA,
         ],
         compiler_params=pltpu.CompilerParams(vmem_limit_bytes=56 * 1024 * 1024),
@@ -227,7 +225,7 @@
         scales = []
         for first in range(0, row_count, LANES):
             at = pl.ds(pl.multiple_of(clip * row_count + first, LANES), LANES)
-            mean = jnp.sum(squares_ref[:, at], axis=0, keepdims=True) / model_width
+            mean = jnp.sum(squares_ref[:, :, at], axis=0) / model_width
             scale = jnp.broadcast_to(lax.rsqrt(mean + epsilon), (LANES, LANES))
             scales.append(jnp.sum(jnp.where(diagonal, scale, 0.0), axis=1, keepdims=True))
         scale = jnp.concatenate(scales, axis=0)
@@ -238,7 +236,7 @@
         penalty = jnp.sum(sums * gain_ref[...] * gain_ref[...], axis=1, keepdims=True)
         lane = lax.broadcasted_iota(jnp.int32, (1, lanes), 1)
         sums = sums + jnp.where(lane == columns + clip, penalty, 0.0)
-        sums = jnp.broadcast_to(sums, row_ref.shape)
+        sums = jnp.broadcast_to(sums[None], row_ref.shape)
 
         @pl.when(clip == 0)
         def _():
@@ -253,16 +251,16 @@
         grid=(clip_count,),
         in_specs=[
             pl.BlockSpec((1, row_count, lanes), lambda c: (c, 0, 0)),
-            pl.BlockSpec(squares.shape, lambda c: (0, 0)),
+            pl.BlockSpec(squares.shape, lambda c: (0, 0, 0)),
             pl.BlockSpec((1, lanes), lambda c: (0, 0)),
         ],
         out_specs=[
             pl.BlockSpec((1, near_rows, lanes), lambda c: (c, 0, 0)),
-            pl.BlockSpec((devices, lanes), lambda c: (0, 0)),
+            pl.BlockSpec((devices, 1, lanes), lambda c: (0, 0, 0)),
         ],
         out_shape=[
             jax.ShapeDtypeStruct((clip_count, near_rows, lanes), jnp.bfloat16),
-            jax.ShapeDtypeStruct((devices, lanes), jnp.float32),
+            jax.ShapeDtypeStruct((devices, 1, lanes), jnp.float32),
         ],
         compiler_params=pltpu.CompilerParams(vmem_limit_bytes=32 * 1024 * 1024),
         name="finish",
@@ -270,23 +268,23 @@
 
 
 def conclude(rows, gain, model_index, clip_index, model_count, clip_count, tokens, model_width):
-    devices, lanes = rows.shape
+    devices, _, lanes = rows.shape
     columns = gain.shape[0] // clip_count
 
     def kernel(index_ref, rows_ref, gain_ref, penalty_ref, grad_ref):
-        row = lax.broadcasted_iota(jnp.int32, (devices, lanes), 0)
+        row = lax.broadcasted_iota(jnp.int32, (devices, 1, lanes), 0)
         model = (row // clip_count) % model_count
         sums = []
         for clip in range(clip_count):
             mine = (model == index_ref[0]) & (row % clip_count == clip)
             sums.append(
-                jnp.sum(jnp.where(mine, rows_ref[...], 0.0), axis=0, keepdims=True)[:, :columns]
+                jnp.sum(jnp.where(mine, rows_ref[...], 0.0), axis=0)[:, :columns]
             )
         sums = jnp.concatenate(sums, axis=1)
         grad_ref[...] = gain_ref[...] * sums / (sigma_noise * sigma_noise * tokens)
-        lane = lax.broadcasted_iota(jnp.int32, (devices, lanes), 1)
+        lane = lax.broadcasted_iota(jnp.int32, (devices, 1, lanes), 2)
         own = jnp.where(lane == columns + index_ref[1], rows_ref[...], 0.0)
-        total = jnp.sum(jnp.sum(own, axis=0, keepdims=True), axis=1, keepdims=True)
+        total = jnp.sum(jnp.sum(own, axis=0), axis=1, keepdims=True)
         penalty_ref[...] = total / (sigma_noise * sigma_noise * tokens * model_width)
 
     penalty, grad = pl.pallas_call(
@@ -300,7 +298,7 @@
         ],
         name="conclude",
     )(jnp.stack([model_index, clip_index]).astype(jnp.int32), rows, gain[None])
-    return penalty[0], grad[0]
+    return penalty.reshape(1), grad.reshape(-1)
 
 
 def swap(array, axis, distance):
@@ -314,15 +312,17 @@
 
 
 def spread(block, order, before_step):
-    keys = [(0, 0)]
-    held = block[None]
-    received = held[:0]
+    stacks = [([(0, 0)], block[None])]
     for step, (axis, distance) in enumerate(order):
-        held = jnp.concatenate([held, received]) if received.shape[0] else held
-        held = before_step(step, held)
-        received = swap(held, axis, distance)
-        keys += [(m ^ distance, c) if axis == "mp" else (m, c ^ distance) for m, c in keys]
-    return keys, (held, received)
+        if step < len(order) - 1 and len(stacks) > 1:
+            keys = [key for some, _ in stacks for key in some]
+            stacks = [(keys, jnp.concatenate([array for _, array in stacks]))]
+        received = []
+        for part, (keys, array) in enumerate(stacks):
+            keys = [(m ^ distance, c) if axis == "mp" else (m, c ^ distance) for m, c in keys]
+            received.append((keys, swap(before_step(step, part, array), axis, distance)))
+        stacks = stacks + received
+    return stacks
 
 
 def collect(rows, axes):
@@ -355,40 +355,46 @@
 
     clean = projections[0].transpose(0, 2, 1, 3)
     noise = perturbation[0].transpose(0, 2, 1, 3)
-    perturbed = perturb(clean, noise)
     up = [(i, i + 1) for i in range(slab_count - 1)]
     down = [(i + 1, i) for i in range(slab_count - 1)]
 
-    streams = (clean, perturbed)
-    tail = jnp.stack([stream[slots - 1, 1:] for stream in streams])
-    head = jnp.stack([stream[0, 1:] for stream in streams])
-    tail, head, out_weight = lax.optimization_barrier((tail, head, out_weight))
+    def keys_and_values(slot):
+        keep = clean[slot, 1:]
+        return jnp.stack([keep, perturb(keep, noise[slot, 1:])])
+
+    tail, head = keys_and_values(slots - 1), keys_and_values(0)
+    tail, head, clean, noise, out_weight = lax.optimization_barrier(
+        (tail, head, clean, noise, out_weight)
+    )
+    streams = (clean, perturb(clean, noise))
     left = lax.ppermute(tail, "frames", up)
     right = lax.ppermute(head, "frames", down)
 
     own_weight = own_columns(out_weight).T
     line = slab_count == model_count and slab_count == 4
     last = slab_count - 1
-    part = half // 2
+    cut = whole_lanes(half) // 2
     near, passed, across = [], [], []
 
     if line:
         near = [lax.ppermute(own_weight, "frames", up), lax.ppermute(own_weight, "frames", down)]
-
-    def before_step(stream, step, value):
-        nonlocal near, passed, across
+        across = [
+            lax.ppermute(block, "frames", [(0, last), (last, 0)])
+            for block in (own_weight[:cut], own_weight[cut:])
+        ]
+
+    def before_step(stream, step, part, value):
+        nonlocal near, passed
         if line and stream == 0 and step == 1:
             value, near = lax.optimization_barrier((value, near))
             passed = [
                 lax.ppermute(near[0], "frames", up[1:]),
                 lax.ppermute(near[1], "frames", down[:2]),
             ]
-            across = [
-                lax.ppermute(block, "frames", [(0, last), (last, 0)])
-                for block in (own_weight[:part], own_weight[part:])
-            ]
-        if line and stream == 1 and step == 2:
-            value, passed, across[0] = lax.optimization_barrier((value, passed, across[0]))
+        if line and stream == 1 and step == 1:
+            value, across[0] = lax.optimization_barrier((value, across[0]))
+        if line and stream == 1 and step == 2 and part == 1:
+            value, passed = lax.optimization_barrier((value, passed))
         return value
 
     counts = jnp.pad(live_counts[0], (1, 1))
@@ -402,42 +408,45 @@
     for n, order in enumerate(orders):
         attended = attention(nearby, streams[n], left, right, n).reshape(near_rows, local_width)
         gathered.append(
-            spread(attended, order, lambda step, value, n=n: before_step(n, step, value))
+            spread(attended, order, lambda *at, n=n: before_step(n, *at))
         )
 
     if line:
         at_end = (slab_index == 0) | (slab_index == last)
         far = (slab_index + 2) % slab_count
         shards = [
-            ([own_weight], slab_index, jnp.int32(1)),
-            ([near[0]], jnp.maximum(slab_index - 1, 0), slab_index > 0),
-            ([near[1]], jnp.minimum(slab_index + 1, last), slab_index < last),
-            ([passed[0]], far, slab_index >= 2),
-            ([passed[1]], far, slab_index < 2),
-            (across, last - slab_index, at_end),
+            (0, own_weight, slab_index, jnp.int32(1)),
+            (0, near[0], jnp.maximum(slab_index - 1, 0), slab_index > 0),
+            (0, near[1], jnp.minimum(slab_index + 1, last), slab_index < last),
+            (0, passed[0], far, slab_index >= 2),
+            (0, passed[1], far, slab_index < 2),
+            (0, across[0], last - slab_index, at_end),
+            (cut, across[1], last - slab_index, at_end),
         ]
 
     peers = model_count * clip_count
 
     def project_shards(some, total, peers):
         return project(
-            [place ^ model_index for _, place, _ in some],
-            [exists for _, _, exists in some],
+            [place ^ model_index for _, _, place, _ in some],
+            [exists for _, _, _, exists in some],
             clip_index,
             gathered,
-            [weight for weight, _, _ in some],
+            [(first, weight) for first, weight, _, _ in some],
             total,
+            half,
             peers,
         )
 
     if line:
-        (total,) = project_shards(shards[:5], None, 0)
-        total, squares = project_shards(shards[5:], total, peers)
+        (total,) = project_shards(shards[:-1], None, 0)
+        total, squares = project_shards(shards[-1:], total, peers)
     else:
         weight = lax.all_gather(own_weight, "frames", axis=1, tiled=True)
         shards = [
             (
-                [lax.dynamic_slice_in_dim(weight, m * local_width, local_width, axis=1)],
+                0,
+                lax.dynamic_slice_in_dim(weight, m * local_width, local_width, axis=1),
                 jnp.int32(m),
                 jnp.int32(1),
             )

time: 130 us -> 123 us (0.946)
  local copies, waits for them, and re-layouts: 15.4 us -> 10.1 us
  waiting for transfers between devices: 48.7 us -> 45.4 us
  starting transfers between devices: 31.9 us -> 33.8 us
    ppermute x1, waiting for transfers between devices: 15.3 us -> 0.01 us  [before_step(): lax.ppermute(near[1], 'frames', down[:2])]
    ppermute x7 -> x9, waiting for transfers between devices: 7.46 us -> 16.7 us  [swap(): return lax.ppermute(array, axis, [(i, i ^ distance) for i in range(count)])]
    ppermute x2, waiting for transfers between devices: 5.01 us -> 12.8 us  [local(): lax.ppermute(block, 'frames', [(0, last), (last, 0)])]
    ppermute x1, waiting for transfers between devices: 3.56 us -> 0.01 us  [local(): lax.ppermute(own_weight, 'frames', down)]
    unnamed x21 -> x30, local copies, waits for them, and re-layouts: 6.15 us -> 3 us
    all_to_all x2, waiting for transfers between devices: 11 us -> 8.67 us  [collect(): return lax.all_to_all(rows, axes, split_axis=0, concat_axis=0, tiled=True)]
    all_to_all x2 -> x0, local copies, waits for them, and re-layouts: 2.06 us -> none  [collect(): return lax.all_to_all(rows, axes, split_axis=0, concat_axis=0, tiled=True)]
    ppermute x7 -> x9, starting transfers between devices: 5.54 us -> 7.44 us  [swap(): return lax.ppermute(array, axis, [(i, i ^ distance) for i in range(count)])]
  transfers between devices with their start and end apart: 17 -> 19, of which waited for: 10 -> 9; matrix products, arithmetic and copies ran while one was open for 10% -> 8% of each run, Pallas kernels for 12% -> 13%
where the time goes in v1:
time: 123 us; the launch traced here: 122 us
  waiting for transfers between devices  45.4 us (37%)
  starting transfers between devices  33.8 us (27%)
  Pallas kernels  23.7 us (19%)
  local copies, waits for them, and re-layouts  10.1 us (8%)
  other arithmetic  7.97 us (6%)
    ppermute x9, waiting for transfers between devices, swap(): return lax.ppermute(array, axis, [(i, i ^ distance) for i in range(count)])  16.7 us
    ppermute x2, waiting for transfers between devices, local(): lax.ppermute(block, 'frames', [(0, last), (last, 0)])  12.8 us
    pallas_call x2, Pallas kernels, project(): pl.pallas_call(kernel, in_specs=[pl.BlockSpec(memory_space=pltpu.SMEM)] +...  11.7 us
    pallas_call x2, Pallas kernels, attention(): pl.pallas_call(attend_kernel, grid_spec=pltpu.PrefetchScalarGridSpec(num_...  9.04 us
    all_to_all x2, waiting for transfers between devices, collect(): return lax.all_to_all(rows, axes, split_axis=0, concat_axis=0, tiled=True)  8.67 us
    ppermute x9, starting transfers between devices, swap(): return lax.ppermute(array, axis, [(i, i ^ distance) for i in range(count)])  7.44 us
    all_to_all x2, starting transfers between devices, collect(): return lax.all_to_all(rows, axes, split_axis=0, concat_axis=0, tiled=True)  5.89 us
    ppermute x1, starting transfers between devices, local(): lax.ppermute(own_weight, 'frames', up)  5.46 us
  transfers between devices with their start and end apart: 19, of which 9 were waited for; matrix products, arithmetic and copies ran while one was open for 8% of the time, Pallas kernels for 13%

profile of v1, /device:TPU:0, one launch (start us, length us, event | category | flops | bytes accessed | tf_op | source)
XLA Modules:
  0.0 121.9 jit_solution(6182719902355014966)
XLA Ops:
  4.6 5.0 %collective-permute-start = (bf16[2,2,96,896]{3,2,1,0:T(8,128)(2,1)}, bf16[2,2,96,896]{3,2,1,0:T(8,128)(2,1)S(1)}, u32[]{:S(2)}, u32[]{:S(2)}) collective-permute-start(bf16[2,2,96,896]{3,2,1,0:T(8,128)(2,1)} %get-tuple-element.25), channel_id=1, source_target_pairs={{0,8},{8,16},{16,24},{1,9},{9,17},{17,25},{2,10},{10,18},{18,26},{... | collective-permute-start | bytes 2064392 | tf_op jit(solution)/shard_map/ppermute | solution.py:370
  10.9 3.6 %copy.8 = bf16[896,896]{0,1:T(8,128)(2,1)} copy(bf16[896,896]{1,0:T(8,128)(2,1)} %param.7) | data formatting | bytes 3211264 | tf_op jit(solution)/shard_map/optimization_barrier | solution.py:366
  16.0 5.5 %collective-permute-start.3 = (bf16[448,896]{1,0:T(8,128)(2,1)S(1)}, bf16[448,896]{1,0:T(8,128)(2,1)}, u32[]{:S(2)}, u32[]{:S(2)}) collective-permute-start(bf16[448,896]{1,0:T(8,128)(2,1)S(1)} %fusion.refs_8_), channel_id=1, source_target_pairs={{0,8},{8,16},{16,24},{1,9},{9,17},{17,25},{2,10},{10,18},{18,26},{... | collective-permute-start | bytes 2408456 | tf_op jit(solution)/shard_map/ppermute | solution.py:380
  22.8 2.8 %collective-permute-done.left_ref = bf16[2,2,96,896]{3,2,1,0:T(8,128)(2,1)S(1)} collective-permute-done((bf16[2,2,96,896]{3,2,1,0:T(8,128)(2,1)}, bf16[2,2,96,896]{3,2,1,0:T(8,128)(2,1)S(1)}, u32[]{:S(2)}, u32[]{:S(2)}) %collective-permute-start) | collective-permute-done | bytes 688160 | tf_op jit(solution)/shard_map/ppermute | solution.py:370
  25.7 4.4 %collective-permute-done.1.right_ref = bf16[2,2,96,896]{3,2,1,0:T(8,128)(2,1)S(1)} collective-permute-done((bf16[2,2,96,896]{3,2,1,0:T(8,128)(2,1)}, bf16[2,2,96,896]{3,2,1,0:T(8,128)(2,1)S(1)}, u32[]{:S(2)}, u32[]{:S(2)}) %collective-permute-start.1) | collective-permute-done | bytes 688160 | tf_op jit(solution)/shard_map/ppermute | solution.py:371
  30.0 4.5 %attention.2 = bf16[2,96,896]{2,1,0:T(8,128)(2,1)S(1)} custom-call(s32[4]{0:T(128)S(1)} %pad_dynamic-slice_fusion.counts_ref, bf16[2,3,96,896]{3,2,1,0:T(8,128)(2,1)S(1)} %bitcast.31, bf16[2,2,96,896]{3,2,1,0:T(8,128)(2,1)S(1)} %collective-permute-done.left_ref, bf16[2,2,96,896]{3,2,1,0:T(8,128)(2,1)S(1)} %collective-permute-done.1.right_ref), custom_call_target="tpu_custom_call" | custom-call | tf_op jit(solution)/shard_map/attention/pallas_call | solution.py:65
  34.6 1.6 %collective-permute-start.2 = (bf16[1,192,896]{2,1,0:T(8,128)(2,1)S(1)}, bf16[1,192,896]{2,1,0:T(8,128)(2,1)S(1)}, u32[]{:S(2)}, u32[]{:S(2)}) collective-permute-start(bf16[1,192,896]{2,1,0:T(8,128)(2,1)S(1)} %bitcast.35), channel_id=1, source_target_pairs={{0,1},{1,0},{2,3},{3,2},{4,5},{5,4},{6,7},{7,6},{8,9},{9,8},{10,11... | collective-permute-start | bytes 1032200 | tf_op jit(solution)/shard_map/ppermute | solution.py:306
  36.5 4.5 %attention.3 = bf16[2,96,896]{2,1,0:T(8,128)(2,1)S(1)} custom-call(s32[4]{0:T(128)S(1)} %pad_dynamic-slice_fusion.counts_ref, bf16[2,3,96,896]{3,2,1,0:T(8,128)(2,1)S(1)} %add_convert_fusion.own_ref, bf16[2,2,96,896]{3,2,1,0:T(8,128)(2,1)S(1)} %collective-permute-done.left_ref, bf16[2,2,96,896]{3,2,1,0:T(8,128)(2,1)S(1)} %collective-permute-done.1.right_ref), custom_call_target="tpu_custom_call" | custom-call | tf_op jit(solution)/shard_map/attention/pallas_call | solution.py:65
  41.0 1.6 %collective-permute-start.8 = (bf16[1,192,896]{2,1,0:T(8,128)(2,1)S(1)}, bf16[1,192,896]{2,1,0:T(8,128)(2,1)S(1)}, u32[]{:S(2)}, u32[]{:S(2)}) collective-permute-start(bf16[1,192,896]{2,1,0:T(8,128)(2,1)S(1)} %bitcast.33), channel_id=1, source_target_pairs={{0,4},{2,6},{4,0},{6,2},{1,5},{3,7},{5,1},{7,3},{8,12},{10,14},{12... | collective-permute-start | bytes 1032200 | tf_op jit(solution)/shard_map/ppermute | solution.py:306
  42.6 3.5 %collective-permute-start.9 = (bf16[256,896]{1,0:T(8,128)(2,1)S(1)}, bf16[256,896]{1,0:T(8,128)(2,1)S(1)}, u32[]{:S(2)}, u32[]{:S(2)}) collective-permute-start(bf16[256,896]{1,0:T(8,128)(2,1)S(1)} %slice.61), channel_id=1, source_target_pairs={{0,24},{24,0},{1,25},{25,1},{2,26},{26,2},{3,27},{27,3},{4,28},{28... | collective-permute-start | bytes 1376264 | tf_op jit(solution)/shard_map/ppermute | solution.py:382
  48.4 9.4 %collective-permute-done.9.refs_13_ = bf16[256,896]{1,0:T(8,128)(2,1)S(1)} collective-permute-done((bf16[256,896]{1,0:T(8,128)(2,1)S(1)}, bf16[256,896]{1,0:T(8,128)(2,1)S(1)}, u32[]{:S(2)}, u32[]{:S(2)}) %collective-permute-start.9) | collective-permute-done | bytes 458784 | tf_op jit(solution)/shard_map/ppermute | solution.py:382
  57.8 1.5 %collective-permute-start.10 = (bf16[2,192,896]{2,1,0:T(8,128)(2,1)S(1)}, bf16[2,192,896]{2,1,0:T(8,128)(2,1)S(1)}, u32[]{:S(2)}, u32[]{:S(2)}) collective-permute-start(bf16[2,192,896]{2,1,0:T(8,128)(2,1)S(1)} %pad_maximum_fusion.3.refs_4_), channel_id=1, source_target_pairs={{0,1},{1,0},{2,3},{3,2},{4,5},{5,4},{6,7},{7,6},{8,9},{9,8},{10,11... | collective-permute-start | bytes 2064392 | tf_op jit(solution)/shard_map/ppermute | solution.py:306
  59.3 1.5 %collective-permute-start.5 = (bf16[2,192,896]{2,1,0:T(8,128)(2,1)S(1)}, bf16[2,192,896]{2,1,0:T(8,128)(2,1)S(1)}, u32[]{:S(2)}, u32[]{:S(2)}) collective-permute-start(bf16[2,192,896]{2,1,0:T(8,128)(2,1)S(1)} %pad_maximum_fusion.2.refs_0_), channel_id=1, source_target_pairs={{0,4},{2,6},{4,0},{6,2},{1,5},{3,7},{5,1},{7,3},{8,12},{10,14},{12... | collective-permute-start | bytes 2064392 | tf_op jit(solution)/shard_map/ppermute | solution.py:306
  60.8 12.6 %collective-permute-done.10.refs_5_ = bf16[2,192,896]{2,1,0:T(8,128)(2,1)S(1)} collective-permute-done((bf16[2,192,896]{2,1,0:T(8,128)(2,1)S(1)}, bf16[2,192,896]{2,1,0:T(8,128)(2,1)S(1)}, u32[]{:S(2)}, u32[]{:S(2)}) %collective-permute-start.10) | collective-permute-done | bytes 688160 | tf_op jit(solution)/shard_map/ppermute | solution.py:306
  76.4 1.9 %collective-permute-start.15 = (bf16[192,896]{1,0:T(8,128)(2,1)}, bf16[192,896]{1,0:T(8,128)(2,1)S(1)}, u32[]{:S(2)}, u32[]{:S(2)}) collective-permute-start(bf16[192,896]{1,0:T(8,128)(2,1)} %slice.62), channel_id=1, source_target_pairs={{0,24},{24,0},{1,25},{25,1},{2,26},{26,2},{3,27},{27,3},{4,28},{28... | collective-permute-start | bytes 1032200 | tf_op jit(solution)/shard_map/ppermute | solution.py:382
  79.7 7.3 %project.2.refs_9_ = f32[2,384,512]{2,1,0:T(8,128)} custom-call(s32[13]{0:T(128)} %stack.92.scalars_ref, bf16[2,192,896]{2,1,0:T(8,128)(2,1)} %copy-done.4, bf16[2,192,896]{2,1,0:T(8,128)(2,1)} %copy-done.7, bf16[2,192,896]{2,1,0:T(8,128)(2,1)} %collective-permute-done.6.refs_2_, bf16[2,192,896]{2,1,0:T(8,128)(2,1)} %collective-permute-done.7.refs_3_, ...), custom_call_target="tpu_custom_call" | custom-call | flops 3699376128 | bytes 13074432 | tf_op jit(solution)/shard_map/project/pallas_call | solution.py:194
  87.1 3.5 %collective-permute-done.15.refs_8_ = bf16[192,896]{1,0:T(8,128)(2,1)S(1)} collective-permute-done((bf16[192,896]{1,0:T(8,128)(2,1)}, bf16[192,896]{1,0:T(8,128)(2,1)S(1)}, u32[]{:S(2)}, u32[]{:S(2)}) %collective-permute-start.15) | collective-permute-done | bytes 344096 | tf_op jit(solution)/shard_map/ppermute | solution.py:382
  91.3 4.4 %project.3 = (f32[2,384,512]{2,1,0:T(8,128)}, f32[8,1,768]{2,1,0:T(1,128)}) custom-call(s32[3]{0:T(128)} %pad_add_fusion.scalars_ref, bf16[2,192,896]{2,1,0:T(8,128)(2,1)} %copy-done.4, bf16[2,192,896]{2,1,0:T(8,128)(2,1)} %copy-done.7, bf16[2,192,896]{2,1,0:T(8,128)(2,1)} %collective-permute-done.6.refs_2_, ...), custom_call_target="tpu_custom_call" | custom-call | flops 616562688 | bytes 2179072 | tf_op jit(solution)/shard_map/project/pallas_call | solution.py:194
  95.6 3.3 %all-to-all-start = ((f32[8,1,768]{2,1,0:T(1,128)}), f32[8,1,768]{2,1,0:T(1,128)S(1)}, u32[]{:S(2)}, u32[]{:S(2)}) async-start(f32[8,1,768]{2,1,0:T(1,128)} %get-tuple-element.38), calls=%async_computation | async-start | bytes 49152 | tf_op jit(solution)/shard_map/all_to_all | solution.py:329
  99.1 4.5 %all-to-all-done.squares_ref = f32[8,1,768]{2,1,0:T(1,128)S(1)} async-done(((f32[8,1,768]{2,1,0:T(1,128)}), f32[8,1,768]{2,1,0:T(1,128)S(1)}, u32[]{:S(2)}, u32[]{:S(2)}) %all-to-all-start) | async-done | bytes 24608 | tf_op jit(solution)/shard_map/all_to_all | solution.py:329
  108.3 2.5 %all-to-all-start.1 = ((f32[32,1,512]{2,1,0:T(1,128)}), f32[32,1,512]{2,1,0:T(1,128)S(1)}, u32[]{:S(2)}, u32[]{:S(2)}) async-start(f32[32,1,512]{2,1,0:T(1,128)} %get-tuple-element.39), calls=%async_computation.1 | async-start | bytes 131072 | tf_op jit(solution)/shard_map/all_to_all | solution.py:329
  110.8 2.6 %collective-permute-done.16 = bf16[2,96,448]{2,1,0:T(8,128)(2,1)S(1)} collective-permute-done((bf16[2,96,448]{2,1,0:T(8,128)(2,1)S(1)}, bf16[2,96,448]{2,1,0:T(8,128)(2,1)S(1)}, u32[]{:S(2)}, u32[]{:S(2)}) %collective-permute-start.16) | collective-permute-done | bytes 172064 | tf_op jit(solution)/shard_map/ppermute | solution.py:306
  114.3 4.1 %all-to-all-done.1.rows_ref = f32[32,1,512]{2,1,0:T(1,128)S(1)} async-done(((f32[32,1,512]{2,1,0:T(1,128)}), f32[32,1,512]{2,1,0:T(1,128)S(1)}, u32[]{:S(2)}, u32[]{:S(2)}) %all-to-all-start.1) | async-done | bytes 65568 | tf_op jit(solution)/shard_map/all_to_all | solution.py:329
  119.1 1.6 %conclude.1 = (f32[1,1]{1,0:T(1,128)}, f32[1,896]{1,0:T(1,128)}) custom-call(s32[2]{0:T(128)} %pad_add_fusion.1.index_ref, f32[32,1,512]{2,1,0:T(1,128)} %copy-done.9, f32[1,896]{1,0:T(1,128)} %broadcast_in_dim.11.gain_ref), custom_call_target="tpu_custom_call" | custom-call | tf_op jit(solution)/shard_map/conclude/pallas_call | solution.py:290
  (71 shorter events, 23.2 us)
Async XLA Ops:
  4.6 21.1 %collective-permute-start = (bf16[2,2,96,896]{3,2,1,0:T(8,128)(2,1)}, bf16[2,2,96,896]{3,2,1,0:T(8,128)(2,1)S(1)}, u32[]{:S(2)}, u32[]{:S(2)}) collective-permute-start(bf16[2,2,96,896]{3,2,1,0:T(8,128)(2,1)} %get-tuple-element.25), channel_id=1, source_target_pairs={{0,8},{8,16},{16,24},{1,9},{9,17},{17,25},{2,10},{10,18},{18,26},{... | collective-permute-start | bytes 2064392 | tf_op jit(solution)/shard_map/ppermute | solution.py:370
  9.6 20.5 %collective-permute-start.1 = (bf16[2,2,96,896]{3,2,1,0:T(8,128)(2,1)}, bf16[2,2,96,896]{3,2,1,0:T(8,128)(2,1)S(1)}, u32[]{:S(2)}, u32[]{:S(2)}) collective-permute-start(bf16[2,2,96,896]{3,2,1,0:T(8,128)(2,1)} %get-tuple-element.26), channel_id=1, source_target_pairs={{8,0},{16,8},{24,16},{9,1},{17,9},{25,17},{10,2},{18,10},{26,18},{... | collective-permute-start | bytes 2064392 | tf_op jit(solution)/shard_map/ppermute | solution.py:371
  16.0 59.5 %copy-start.2 = (bf16[448,896]{1,0:T(8,128)(2,1)}, bf16[448,896]{1,0:T(8,128)(2,1)S(1)}, u32[]{:S(2)}) copy-start(bf16[448,896]{1,0:T(8,128)(2,1)S(1)} %fusion.refs_8_) | copy-start | bytes 2408452
  16.0 30.3 %collective-permute-start.3 = (bf16[448,896]{1,0:T(8,128)(2,1)S(1)}, bf16[448,896]{1,0:T(8,128)(2,1)}, u32[]{:S(2)}, u32[]{:S(2)}) collective-permute-start(bf16[448,896]{1,0:T(8,128)(2,1)S(1)} %fusion.refs_8_), channel_id=1, source_target_pairs={{0,8},{8,16},{16,24},{1,9},{9,17},{17,25},{2,10},{10,18},{18,26},{... | collective-permute-start | bytes 2408456 | tf_op jit(solution)/shard_map/ppermute | solution.py:380
  21.4 24.8 %collective-permute-start.4 = (bf16[448,896]{1,0:T(8,128)(2,1)S(1)}, bf16[448,896]{1,0:T(8,128)(2,1)}, u32[]{:S(2)}, u32[]{:S(2)}) collective-permute-start(bf16[448,896]{1,0:T(8,128)(2,1)S(1)} %fusion.refs_8_), channel_id=1, source_target_pairs={{8,0},{16,8},{24,16},{9,1},{17,9},{25,17},{10,2},{18,10},{26,18},{... | collective-permute-start | bytes 2408456 | tf_op jit(solution)/shard_map/ppermute | solution.py:380
  22.7 13.4 %copy-start.3 = (bf16[1,2,96,3,896]{4,2,3,1,0:T(8,128)(2,1)S(1)}, bf16[1,2,96,3,896]{4,2,3,1,0:T(8,128)(2,1)}, u32[]{:S(2)}) copy-start(bf16[1,2,96,3,896]{4,2,3,1,0:T(8,128)(2,1)} %param.6) | copy-start | bytes 3096580
  34.6 11.6 %collective-permute-start.2 = (bf16[1,192,896]{2,1,0:T(8,128)(2,1)S(1)}, bf16[1,192,896]{2,1,0:T(8,128)(2,1)S(1)}, u32[]{:S(2)}, u32[]{:S(2)}) collective-permute-start(bf16[1,192,896]{2,1,0:T(8,128)(2,1)S(1)} %bitcast.35), channel_id=1, source_target_pairs={{0,1},{1,0},{2,3},{3,2},{4,5},{5,4},{6,7},{7,6},{8,9},{9,8},{10,11... | collective-permute-start | bytes 1032200 | tf_op jit(solution)/shard_map/ppermute | solution.py:306
  41.0 7.3 %collective-permute-start.8 = (bf16[1,192,896]{2,1,0:T(8,128)(2,1)S(1)}, bf16[1,192,896]{2,1,0:T(8,128)(2,1)S(1)}, u32[]{:S(2)}, u32[]{:S(2)}) collective-permute-start(bf16[1,192,896]{2,1,0:T(8,128)(2,1)S(1)} %bitcast.33), channel_id=1, source_target_pairs={{0,4},{2,6},{4,0},{6,2},{1,5},{3,7},{5,1},{7,3},{8,12},{10,14},{12... | collective-permute-start | bytes 1032200 | tf_op jit(solution)/shard_map/ppermute | solution.py:306
  42.6 15.2 %collective-permute-start.9 = (bf16[256,896]{1,0:T(8,128)(2,1)S(1)}, bf16[256,896]{1,0:T(8,128)(2,1)S(1)}, u32[]{:S(2)}, u32[]{:S(2)}) collective-permute-start(bf16[256,896]{1,0:T(8,128)(2,1)S(1)} %slice.61), channel_id=1, source_target_pairs={{0,24},{24,0},{1,25},{25,1},{2,26},{26,2},{3,27},{27,3},{4,28},{28... | collective-permute-start | bytes 1376264 | tf_op jit(solution)/shard_map/ppermute | solution.py:382
  46.2 33.4 %copy-start.4 = (bf16[2,192,896]{2,1,0:T(8,128)(2,1)}, bf16[2,192,896]{2,1,0:T(8,128)(2,1)S(1)}, u32[]{:S(2)}) copy-start(bf16[2,192,896]{2,1,0:T(8,128)(2,1)S(1)} %pad_maximum_fusion.2.refs_0_) | copy-start | bytes 2064388
  46.3 28.6 %collective-permute-start.12 = (bf16[448,896]{1,0:T(8,128)(2,1)}, bf16[448,896]{1,0:T(8,128)(2,1)S(1)}, u32[]{:S(2)}, u32[]{:S(2)}) collective-permute-start(bf16[448,896]{1,0:T(8,128)(2,1)} %collective-permute-done.3.refs_9_), channel_id=1, source_target_pairs={{8,16},{16,24},{9,17},{17,25},{10,18},{18,26},{11,19},{19,27},{12,... | collective-permute-start | bytes 2408456 | tf_op jit(solution)/shard_map/ppermute | solution.py:391
  47.0 27.9 %collective-permute-start.13 = (bf16[448,896]{1,0:T(8,128)(2,1)}, bf16[448,896]{1,0:T(8,128)(2,1)S(1)}, u32[]{:S(2)}, u32[]{:S(2)}) collective-permute-start(bf16[448,896]{1,0:T(8,128)(2,1)} %collective-permute-done.4.refs_10_), channel_id=1, source_target_pairs={{8,0},{16,8},{9,1},{17,9},{10,2},{18,10},{11,3},{19,11},{12,4},{20... | collective-permute-start | bytes 2408456 | tf_op jit(solution)/shard_map/ppermute | solution.py:392
  48.4 31.3 %copy-start.5 = (bf16[2,192,896]{2,1,0:T(8,128)(2,1)}, bf16[2,192,896]{2,1,0:T(8,128)(2,1)S(1)}, u32[]{:S(2)}) copy-start(bf16[2,192,896]{2,1,0:T(8,128)(2,1)S(1)} %pad_maximum_fusion.3.refs_4_) | copy-start | bytes 2064388
  57.8 18.6 %copy-start.13 = (bf16[256,896]{1,0:T(8,128)(2,1)}, bf16[256,896]{1,0:T(8,128)(2,1)S(1)}, u32[]{:S(2)}) copy-start(bf16[256,896]{1,0:T(8,128)(2,1)S(1)} %collective-permute-done.9.refs_13_) | copy-start | bytes 1376260
  57.8 15.6 %collective-permute-start.10 = (bf16[2,192,896]{2,1,0:T(8,128)(2,1)S(1)}, bf16[2,192,896]{2,1,0:T(8,128)(2,1)S(1)}, u32[]{:S(2)}, u32[]{:S(2)}) collective-permute-start(bf16[2,192,896]{2,1,0:T(8,128)(2,1)S(1)} %pad_maximum_fusion.3.refs_4_), channel_id=1, source_target_pairs={{0,1},{1,0},{2,3},{3,2},{4,5},{5,4},{6,7},{7,6},{8,9},{9,8},{10,11... | collective-permute-start | bytes 2064392 | tf_op jit(solution)/shard_map/ppermute | solution.py:306
  59.3 15.6 %collective-permute-start.5 = (bf16[2,192,896]{2,1,0:T(8,128)(2,1)S(1)}, bf16[2,192,896]{2,1,0:T(8,128)(2,1)S(1)}, u32[]{:S(2)}, u32[]{:S(2)}) collective-permute-start(bf16[2,192,896]{2,1,0:T(8,128)(2,1)S(1)} %pad_maximum_fusion.2.refs_0_), channel_id=1, source_target_pairs={{0,4},{2,6},{4,0},{6,2},{1,5},{3,7},{5,1},{7,3},{8,12},{10,14},{12... | collective-permute-start | bytes 2064392 | tf_op jit(solution)/shard_map/ppermute | solution.py:306
  60.8 18.9 %collective-permute-start.11 = (bf16[2,192,896]{2,1,0:T(8,128)(2,1)S(1)}, bf16[2,192,896]{2,1,0:T(8,128)(2,1)}, u32[]{:S(2)}, u32[]{:S(2)}) collective-permute-start(bf16[2,192,896]{2,1,0:T(8,128)(2,1)S(1)} %pad_maximum_fusion.3.refs_4_), channel_id=1, source_target_pairs={{0,2},{2,0},{4,6},{6,4},{1,3},{3,1},{5,7},{7,5},{8,10},{10,8},{12,... | collective-permute-start | bytes 2064392 | tf_op jit(solution)/shard_map/ppermute | solution.py:306
  73.4 6.2 %collective-permute-start.6 = (bf16[2,192,896]{2,1,0:T(8,128)(2,1)S(1)}, bf16[2,192,896]{2,1,0:T(8,128)(2,1)}, u32[]{:S(2)}, u32[]{:S(2)}) collective-permute-start(bf16[2,192,896]{2,1,0:T(8,128)(2,1)S(1)} %pad_maximum_fusion.2.refs_0_), channel_id=1, source_target_pairs={{0,2},{2,0},{4,6},{6,4},{1,3},{3,1},{5,7},{7,5},{8,10},{10,8},{12,... | collective-permute-start | bytes 2064392 | tf_op jit(solution)/shard_map/ppermute | solution.py:306
  74.9 4.8 %collective-permute-start.7 = (bf16[2,192,896]{2,1,0:T(8,128)(2,1)S(1)}, bf16[2,192,896]{2,1,0:T(8,128)(2,1)}, u32[]{:S(2)}, u32[]{:S(2)}) collective-permute-start(bf16[2,192,896]{2,1,0:T(8,128)(2,1)S(1)} %collective-permute-done.5.refs_1_), channel_id=1, source_target_pairs={{0,2},{2,0},{4,6},{6,4},{1,3},{3,1},{5,7},{7,5},{8,10},{10,8},{12,... | collective-permute-start | bytes 2064392 | tf_op jit(solution)/shard_map/ppermute | solution.py:306
  74.9 4.7 %collective-permute-start.14 = (bf16[2,192,896]{2,1,0:T(8,128)(2,1)S(1)}, bf16[2,192,896]{2,1,0:T(8,128)(2,1)}, u32[]{:S(2)}, u32[]{:S(2)}) collective-permute-start(bf16[2,192,896]{2,1,0:T(8,128)(2,1)S(1)} %collective-permute-done.10.refs_5_), channel_id=1, source_target_pairs={{0,2},{2,0},{4,6},{6,4},{1,3},{3,1},{5,7},{7,5},{8,10},{10,8},{12,... | collective-permute-start | bytes 2064392 | tf_op jit(solution)/shard_map/ppermute | solution.py:306
  76.4 14.2 %collective-permute-start.15 = (bf16[192,896]{1,0:T(8,128)(2,1)}, bf16[192,896]{1,0:T(8,128)(2,1)S(1)}, u32[]{:S(2)}, u32[]{:S(2)}) collective-permute-start(bf16[192,896]{1,0:T(8,128)(2,1)} %slice.62), channel_id=1, source_target_pairs={{0,24},{24,0},{1,25},{25,1},{2,26},{26,2},{3,27},{27,3},{4,28},{28... | collective-permute-start | bytes 1032200 | tf_op jit(solution)/shard_map/ppermute | solution.py:382
  95.6 8.0 %all-to-all-start = ((f32[8,1,768]{2,1,0:T(1,128)}), f32[8,1,768]{2,1,0:T(1,128)S(1)}, u32[]{:S(2)}, u32[]{:S(2)}) async-start(f32[8,1,768]{2,1,0:T(1,128)} %get-tuple-element.38), calls=%async_computation | async-start | bytes 49152 | tf_op jit(solution)/shard_map/all_to_all | solution.py:329
  106.4 7.0 %collective-permute-start.16 = (bf16[2,96,448]{2,1,0:T(8,128)(2,1)S(1)}, bf16[2,96,448]{2,1,0:T(8,128)(2,1)S(1)}, u32[]{:S(2)}, u32[]{:S(2)}) collective-permute-start(bf16[2,96,448]{2,1,0:T(8,128)(2,1)S(1)} %bitcast.41), channel_id=1, source_target_pairs={{0,1},{1,0},{2,3},{3,2},{4,5},{5,4},{6,7},{7,6},{8,9},{9,8},{10,11... | collective-permute-start | bytes 516104 | tf_op jit(solution)/shard_map/ppermute | solution.py:306
  108.3 10.2 %all-to-all-start.1 = ((f32[32,1,512]{2,1,0:T(1,128)}), f32[32,1,512]{2,1,0:T(1,128)S(1)}, u32[]{:S(2)}, u32[]{:S(2)}) async-start(f32[32,1,512]{2,1,0:T(1,128)} %get-tuple-element.39), calls=%async_computation.1 | async-start | bytes 131072 | tf_op jit(solution)/shard_map/all_to_all | solution.py:329
  (10 other events, 38.4 us)

commit v2 on v1

--- a/solution.py
+++ b/solution.py
@@ -20,13 +20,13 @@
     return (clean.astype(jnp.float32) + sigma_noise * noise.astype(jnp.float32)).astype(jnp.bfloat16)
 
 
-def attend_kernel(counts_ref, own_ref, left_ref, right_ref, out_ref):
+def attend_kernel(where_ref, own_ref, left_ref, right_ref, out_ref):
     slots, _, tile_len, width = own_ref.shape
     key_pos = lax.broadcasted_iota(jnp.int32, (1, 2 * tile_len), 1)
     live = []
     for slot in range(slots):
-        own_count = counts_ref[slot + 1]
-        far_count = counts_ref[0 if slot == 0 else slots + 1]
+        own_count = where_ref[4 + slot]
+        far_count = where_ref[3 if slot == 0 else slots + 4]
         live.append((key_pos < own_count) | ((key_pos >= tile_len) & (key_pos < tile_len + far_count)))
     row_pos = lax.broadcasted_iota(jnp.int32, (tile_len, 1), 0)
     units = [(slot, head) for head in range(width // HEAD_DIM) for slot in range(slots)]
@@ -52,16 +52,16 @@
         values = jnp.concatenate([own_ref[slot, 2, :, cols], halo_ref[1, :, cols]], axis=0)
         probabilities = (weight * (1.0 / total)).astype(jnp.bfloat16)
         mixed = jnp.dot(probabilities, values, preferred_element_type=jnp.float32)
-        out_ref[slot, :, cols] = jnp.where(row_pos < counts_ref[slot + 1], mixed, 0.0).astype(
+        out_ref[slot, :, cols] = jnp.where(row_pos < where_ref[4 + slot], mixed, 0.0).astype(
             jnp.bfloat16
         )
 
 
-def attention(nearby, own, left, right, stream):
+def attention(where, own, left, right):
     slots, _, tile_len, width = own.shape
     block = HEADS_AT_ONCE * HEAD_DIM
     own_spec = pl.BlockSpec((slots, 3, tile_len, block), lambda h, c: (0, 0, 0, h))
-    halo_spec = pl.BlockSpec((None, 2, tile_len, block), lambda h, c: (stream, 0, 0, h))
+    halo_spec = pl.BlockSpec((2, tile_len, block), lambda h, c: (0, 0, h))
     return pl.pallas_call(
         attend_kernel,
         grid_spec=pltpu.PrefetchScalarGridSpec(
@@ -78,7 +78,7 @@
             transcendentals=0,
         ),
         name="attention",
-    )(nearby, own, left, right)
+    )(where, own, left, right)
 
 
 def whole_lanes(columns):
@@ -90,7 +90,7 @@
     return row == lax.broadcasted_iota(jnp.int32, (LANES, LANES), 1)
 
 
-def project(places, valid, clip_index, gathered, weights, total, columns, peers):
+def project(where, gathered, shards, total, columns, peers):
     stream_count = len(gathered)
     home = [
         {key: (n, at) for n, (keys, _) in enumerate(stacks) for at, key in enumerate(keys)}
@@ -101,21 +101,21 @@
     _, block_rows, depth = gathered[0][0][1].shape
     lanes = whole_lanes(columns)
     row_count = stream_count * block_rows
-    shard_total = len(weights)
-    scalars = jnp.stack([jnp.int32(n) for n in (*places, *valid, clip_index)]).astype(jnp.int32)
+    shard_total = len(shards)
     flat = [array for stacks in gathered for _, array in stacks]
     base = [sum(len(stacks) for stacks in gathered[:n]) for n in range(stream_count)]
 
-    def kernel(scalars_ref, *refs):
+    def kernel(where_ref, *refs):
+        slab, model, own_clip = where_ref[0], where_ref[1], where_ref[2]
         block_refs = refs[: len(flat)]
         weight_refs = refs[len(flat) : len(flat) + shard_total]
         total_ref = refs[len(flat) + shard_total] if total is not None else None
-        rows, held, row_sem, weight_sem, total_sem = refs[-5:]
+        rows, held, row_sem, weight_sem = refs[-4:]
         out_ref = refs[len(operands)]
         squares_ref = refs[len(operands) + 1]
 
         def weight_copy(shard):
-            size = weights[shard][1].shape[0]
+            size = shards[shard][1].shape[0]
             return pltpu.make_async_copy(
                 weight_refs[shard], held.at[shard, pl.ds(0, size)], weight_sem.at[shard]
             )
@@ -124,7 +124,7 @@
             stack, at = home[stream][place, clip]
             source = block_refs[base[stream] + stack].at[at]
             first = pl.multiple_of(
-                (clip ^ scalars_ref[2 * shard_total]) * row_count + stream * block_rows, 16
+                (clip ^ own_clip) * row_count + stream * block_rows, 16
             )
             return pltpu.make_async_copy(
                 source,
@@ -132,35 +132,33 @@
                 row_sem.at[shard, clip, stream],
             )
 
-        if total is not None:
-            pltpu.make_async_copy(total_ref, out_ref, total_sem).start()
         for shard in range(shard_total):
 
-            @pl.when(scalars_ref[shard_total + shard] == 1)
+            @pl.when(shards[shard][3](slab))
             def _():
                 weight_copy(shard).start()
                 for place in range(place_count):
 
-                    @pl.when(scalars_ref[shard] == place)
+                    @pl.when((shards[shard][2](slab) ^ model) == place)
                     def _():
                         for clip in range(clip_count):
                             for stream in range(stream_count):
                                 row_copy(place, shard, clip, stream).start()
 
-        if total is not None:
-            pltpu.make_async_copy(total_ref, out_ref, total_sem).wait()
+        if total is None:
+            out_ref[...] = jnp.zeros_like(out_ref)
         else:
-            out_ref[...] = jnp.zeros_like(out_ref)
+            out_ref[...] = total_ref[...]
 
         for shard in range(shard_total):
 
-            @pl.when(scalars_ref[shard_total + shard] == 1)
+            @pl.when(shards[shard][3](slab))
             def _():
                 weight_copy(shard).wait()
                 for clip in range(clip_count):
                     for stream in range(stream_count):
                         row_copy(0, shard, clip, stream).wait()
-                first, array = weights[shard]
+                first, array = shards[shard][:2]
                 size = array.shape[0]
                 wide = whole_lanes(size)
                 if wide > size:
@@ -184,10 +182,13 @@
                         sums[None], (peers, 1, LANES)
                     )
 
-    operands = [*flat, *(array for _, array in weights)]
+    operands = [*flat, *(array for _, array, _, _ in shards)]
+    in_specs = [pl.BlockSpec(memory_space=pl.ANY) for _ in operands]
+    aliases = {}
     if total is not None:
         operands.append(total)
-    in_specs = [pl.BlockSpec(memory_space=pl.ANY) for _ in operands]
+        in_specs.append(pl.BlockSpec(memory_space=pltpu.VMEM))
+        aliases = {len(operands): 0}
     out_shape = [jax.ShapeDtypeStruct((clip_count, row_count, lanes), jnp.float32)]
     if peers:
         out_shape.append(jax.ShapeDtypeStruct((peers, 1, clip_count * row_count), jnp.float32))
@@ -201,23 +202,21 @@
             pltpu.VMEM((shard_total, lanes, depth), jnp.bfloat16),
             pltpu.SemaphoreType.DMA((shard_total, clip_count, stream_count)),
             pltpu.SemaphoreType.DMA((shard_total,)),
-            pltpu.SemaphoreType.DMA,
-        ],
-        compiler_params=pltpu.CompilerParams(vmem_limit_bytes=56 * 1024 * 1024),
+        ],
+        input_output_aliases=aliases,
+        compiler_params=pltpu.CompilerParams(vmem_limit_bytes=(8 + 4 * shard_total) * 1024 * 1024),
         cost_estimate=pl.CostEstimate(
             flops=2 * clip_count * row_count * depth * columns * shard_total,
             bytes_accessed=shard_total * depth * (clip_count * row_count + columns) * 2,
             transcendentals=0,
         ),
         name="project",
-    )(scalars, *operands)
-
-
-def finish(total, squares, gain, model_width, devices):
+    )(where, *operands)
+
+
+def finish(total, squares, gain, columns, model_width, devices):
     clip_count, row_count, lanes = total.shape
-    columns = gain.shape[0]
     near_rows = row_count // 2
-    gain = jnp.pad(gain, (0, lanes - columns))[None]
 
     def kernel(total_ref, squares_ref, gain_ref, features_ref, row_ref):
         clip = pl.program_id(0)
@@ -262,43 +261,44 @@
             jax.ShapeDtypeStruct((clip_count, near_rows, lanes), jnp.bfloat16),
             jax.ShapeDtypeStruct((devices, 1, lanes), jnp.float32),
         ],
-        compiler_params=pltpu.CompilerParams(vmem_limit_bytes=32 * 1024 * 1024),
+        compiler_params=pltpu.CompilerParams(vmem_limit_bytes=16 * 1024 * 1024),
         name="finish",
     )(total, squares, gain)
 
 
-def conclude(rows, gain, model_index, clip_index, model_count, clip_count, tokens, model_width):
+def conclude(rows, where, gain, model_count, clip_count, tokens):
     devices, _, lanes = rows.shape
-    columns = gain.shape[0] // clip_count
-
-    def kernel(index_ref, rows_ref, gain_ref, penalty_ref, grad_ref):
+    columns = gain.shape[1] // clip_count
+    model_width = gain.shape[1] * model_count
+
+    def kernel(where_ref, rows_ref, gain_ref, penalty_ref, grad_ref):
         row = lax.broadcasted_iota(jnp.int32, (devices, 1, lanes), 0)
         model = (row // clip_count) % model_count
         sums = []
         for clip in range(clip_count):
-            mine = (model == index_ref[0]) & (row % clip_count == clip)
-            sums.append(
-                jnp.sum(jnp.where(mine, rows_ref[...], 0.0), axis=0)[:, :columns]
-            )
+            mine = (model == where_ref[1]) & (row % clip_count == clip)
+            sums.append(jnp.sum(jnp.where(mine, rows_ref[...], 0.0), axis=0)[:, :columns])
         sums = jnp.concatenate(sums, axis=1)
-        grad_ref[...] = gain_ref[...] * sums / (sigma_noise * sigma_noise * tokens)
+        grad = gain_ref[...] * sums / (sigma_noise * sigma_noise * tokens)
+        grad_ref[...] = grad.reshape(grad_ref.shape)
         lane = lax.broadcasted_iota(jnp.int32, (devices, 1, lanes), 2)
-        own = jnp.where(lane == columns + index_ref[1], rows_ref[...], 0.0)
-        total = jnp.sum(jnp.sum(own, axis=0), axis=1, keepdims=True)
-        penalty_ref[...] = total / (sigma_noise * sigma_noise * tokens * model_width)
-
-    penalty, grad = pl.pallas_call(
+        own = jnp.where(lane == columns + where_ref[2], rows_ref[...], 0.0)
+        penalty_ref[0] = jnp.sum(own) / (sigma_noise * sigma_noise * tokens * model_width)
+
+    return pl.pallas_call(
         kernel,
         in_specs=[pl.BlockSpec(memory_space=pltpu.SMEM)]
         + [pl.BlockSpec(memory_space=pltpu.VMEM)] * 2,
-        out_specs=[pl.BlockSpec(memory_space=pltpu.VMEM)] * 2,
+        out_specs=[
+            pl.BlockSpec(memory_space=pltpu.SMEM),
+            pl.BlockSpec(memory_space=pltpu.VMEM),
+        ],
         out_shape=[
-            jax.ShapeDtypeStruct((1, 1), jnp.float32),
-            jax.ShapeDtypeStruct((1, gain.shape[0]), jnp.float32),
+            jax.ShapeDtypeStruct((1,), jnp.float32),
+            jax.ShapeDtypeStruct((gain.shape[1],), jnp.float32),
         ],
         name="conclude",
-    )(jnp.stack([model_index, clip_index]).astype(jnp.int32), rows, gain[None])
-    return penalty.reshape(1), grad.reshape(-1)
+    )(where, rows, gain)
 
 
 def swap(array, axis, distance):
@@ -358,47 +358,49 @@
     up = [(i, i + 1) for i in range(slab_count - 1)]
     down = [(i + 1, i) for i in range(slab_count - 1)]
 
-    def keys_and_values(slot):
-        keep = clean[slot, 1:]
-        return jnp.stack([keep, perturb(keep, noise[slot, 1:])])
-
-    tail, head = keys_and_values(slots - 1), keys_and_values(0)
-    tail, head, clean, noise, out_weight = lax.optimization_barrier(
-        (tail, head, clean, noise, out_weight)
-    )
+    halo = []
+    edges = (slots - 1, 0)
+    for noisy in (False, True):
+        sent = [
+            perturb(clean[slot, 1:], noise[slot, 1:]) if noisy else clean[slot, 1:]
+            for slot in edges
+        ]
+        sent, clean, noise, out_weight = lax.optimization_barrier((sent, clean, noise, out_weight))
+        halo.append(
+            (lax.ppermute(sent[0], "frames", up), lax.ppermute(sent[1], "frames", down))
+        )
     streams = (clean, perturb(clean, noise))
-    left = lax.ppermute(tail, "frames", up)
-    right = lax.ppermute(head, "frames", down)
+    counts = jnp.pad(live_counts[0], (1, 1))
+    nearby = lax.dynamic_slice_in_dim(counts, slots * slab_index, slots + 2)
+    where = jnp.concatenate(
+        [jnp.stack([slab_index, model_index, clip_index]).astype(jnp.int32), nearby]
+    )
+    gain_row = jnp.pad(own_columns(norm_gain), (0, whole_lanes(half) - half))[None]
+    gain_all = norm_gain[None]
 
     own_weight = own_columns(out_weight).T
+    own_weight, halo[0] = lax.optimization_barrier((own_weight, halo[0]))
     line = slab_count == model_count and slab_count == 4
     last = slab_count - 1
-    cut = whole_lanes(half) // 2
-    near, passed, across = [], [], []
+    near, passed, across = [], [], None
 
     if line:
         near = [lax.ppermute(own_weight, "frames", up), lax.ppermute(own_weight, "frames", down)]
-        across = [
-            lax.ppermute(block, "frames", [(0, last), (last, 0)])
-            for block in (own_weight[:cut], own_weight[cut:])
-        ]
+        across = lax.ppermute(own_weight, "frames", [(0, last), (last, 0)])
 
     def before_step(stream, step, part, value):
-        nonlocal near, passed
+        nonlocal near, passed, gain_row, gain_all
         if line and stream == 0 and step == 1:
-            value, near = lax.optimization_barrier((value, near))
+            value, near, gain_row, gain_all = lax.optimization_barrier(
+                (value, near, gain_row, gain_all)
+            )
             passed = [
                 lax.ppermute(near[0], "frames", up[1:]),
                 lax.ppermute(near[1], "frames", down[:2]),
             ]
-        if line and stream == 1 and step == 1:
-            value, across[0] = lax.optimization_barrier((value, across[0]))
         if line and stream == 1 and step == 2 and part == 1:
             value, passed = lax.optimization_barrier((value, passed))
         return value
-
-    counts = jnp.pad(live_counts[0], (1, 1))
-    nearby = lax.dynamic_slice_in_dim(counts, slots * slab_index, slots + 2)
 
     gathered = []
     orders = (
@@ -406,57 +408,39 @@
         distances("mp")[:1] + distances("dp") + distances("mp")[1:],
     )
     for n, order in enumerate(orders):
-        attended = attention(nearby, streams[n], left, right, n).reshape(near_rows, local_width)
+        attended = attention(where, streams[n], *halo[n]).reshape(near_rows, local_width)
         gathered.append(
             spread(attended, order, lambda *at, n=n: before_step(n, *at))
         )
 
+    peers = model_count * clip_count
     if line:
-        at_end = (slab_index == 0) | (slab_index == last)
-        far = (slab_index + 2) % slab_count
         shards = [
-            (0, own_weight, slab_index, jnp.int32(1)),
-            (0, near[0], jnp.maximum(slab_index - 1, 0), slab_index > 0),
-            (0, near[1], jnp.minimum(slab_index + 1, last), slab_index < last),
-            (0, passed[0], far, slab_index >= 2),
-            (0, passed[1], far, slab_index < 2),
-            (0, across[0], last - slab_index, at_end),
-            (cut, across[1], last - slab_index, at_end),
+            (0, own_weight, lambda slab: slab, lambda slab: slab >= 0),
+            (0, near[0], lambda slab: jnp.maximum(slab - 1, 0), lambda slab: slab > 0),
+            (0, near[1], lambda slab: jnp.minimum(slab + 1, last), lambda slab: slab < last),
+            (0, passed[0], lambda slab: jnp.maximum(slab - 2, 0), lambda slab: slab >= 2),
+            (0, passed[1], lambda slab: jnp.minimum(slab + 2, last), lambda slab: slab < 2),
+            (0, across, lambda slab: last - slab, lambda slab: (slab == 0) | (slab == last)),
         ]
-
-    peers = model_count * clip_count
-
-    def project_shards(some, total, peers):
-        return project(
-            [place ^ model_index for _, _, place, _ in some],
-            [exists for _, _, _, exists in some],
-            clip_index,
-            gathered,
-            [(first, weight) for first, weight, _, _ in some],
-            total,
-            half,
-            peers,
-        )
-
-    if line:
-        (total,) = project_shards(shards[:-1], None, 0)
-        total, squares = project_shards(shards[-1:], total, peers)
+        (total,) = project(where, gathered, shards[:-1], None, half, 0)
+        total, squares = project(where, gathered, shards[-1:], total, half, peers)
     else:
         weight = lax.all_gather(own_weight, "frames", axis=1, tiled=True)
         shards = [
             (
                 0,
                 lax.dynamic_slice_in_dim(weight, m * local_width, local_width, axis=1),
-                jnp.int32(m),
-                jnp.int32(1),
+                lambda slab, m=m: m,
+                lambda slab: slab >= 0,
             )
             for m in range(model_count)
         ]
-        total, squares = project_shards(shards, None, peers)
+        total, squares = project(where, gathered, shards, None, half, peers)
 
     squares = collect(squares, ("mp", "dp"))
     features, sums = finish(
-        total, squares, own_columns(norm_gain), model_width, slab_count * model_count * clip_count
+        total, squares, gain_row, half, model_width, slab_count * model_count * clip_count
     )
     sums = collect(sums, ("frames", "mp", "dp"))
 
@@ -474,14 +458,7 @@
     )[None]
     sums, features = lax.optimization_barrier((sums, features))
     penalty, gain_grad = conclude(
-        sums,
-        norm_gain,
-        model_index,
-        clip_index,
-        model_count,
-        clip_count,
-        token_total,
-        model_width,
+        sums, where, gain_all, model_count, clip_count, token_total
     )
     return (features, penalty, gain_grad)
 

time: 123 us -> 119 us (0.967)
  blocking collectives: 0 us -> 8.22 us
  Pallas kernels: 23.7 us -> 20.4 us
  other arithmetic: 7.97 us -> 5.14 us
  local copies, waits for them, and re-layouts: 10.1 us -> 7.51 us
  starting transfers between devices: 33.8 us -> 32.2 us
    all_to_all x0 -> x1, blocking collectives: none -> 8.22 us  [collect(): return lax.all_to_all(rows, axes, split_axis=0, concat_axis=0, tiled=True)]
    all_to_all x2 -> x1, waiting for transfers between devices: 8.67 us -> 2.97 us  [collect(): return lax.all_to_all(rows, axes, split_axis=0, concat_axis=0, tiled=True)]
    ppermute x1, waiting for transfers between devices: 0.01 us -> 4.8 us  [local(): lax.ppermute(own_weight, 'frames', down)]
    ppermute x4 -> x5, waiting for transfers between devices: 20 us -> 16.2 us  [the longest x1 16.1 us: local(): across = lax.ppermute(own_weight, 'frames', [(0, last), (last, 0)])]
    pallas_call x2, Pallas kernels: 11.7 us -> 8.3 us  [project(): pl.pallas_call(kernel, in_specs=[pl.BlockSpec(memory_space=pltpu.SMEM)] +...]
    ppermute x1, waiting for transfers between devices: 0.01 us -> 3.35 us  [before_step(): lax.ppermute(near[1], 'frames', down[:2])]
    all_to_all x2 -> x1, starting transfers between devices: 5.89 us -> 2.57 us  [collect(): return lax.all_to_all(rows, axes, split_axis=0, concat_axis=0, tiled=True)]
    another operation x3 -> x0, other arithmetic: 2.48 us -> none  [the longest x1 1.27 us: keys_and_values(): return jnp.stack([keep, perturb(keep, noise[slot, 1:])])]
  transfers between devices with their start and end apart: 19 -> 19, of which waited for: 9 -> 8; matrix products, arithmetic and copies ran while one was open for 8% -> 8% of each run, Pallas kernels for 13% -> 12%
where the time goes in v2:
time: 119 us
  waiting for transfers between devices  44.3 us (37%)
  starting transfers between devices  32.2 us (27%)
  Pallas kernels  20.4 us (17%)
  blocking collectives  8.22 us (7%)
  local copies, waits for them, and re-layouts  7.51 us (6%)
  other arithmetic  5.14 us (4%)
    ppermute x9, waiting for transfers between devices, swap(): return lax.ppermute(array, axis, [(i, i ^ distance) for i in range(count)])  17 us
    ppermute x1, waiting for transfers between devices, local(): across = lax.ppermute(own_weight, 'frames', [(0, last), (last, 0)])  16.1 us
    ppermute x2, starting transfers between devices, local(): lax.ppermute(sent[0], 'frames', up)  9.49 us
    pallas_call x2, Pallas kernels, attention(): pl.pallas_call(attend_kernel, grid_spec=pltpu.PrefetchScalarGridSpec(num_...  9.04 us
    pallas_call x2, Pallas kernels, project(): pl.pallas_call(kernel, in_specs=[pl.BlockSpec(memory_space=pltpu.SMEM)] +...  8.3 us
    all_to_all x1, blocking collectives, collect(): return lax.all_to_all(rows, axes, split_axis=0, concat_axis=0, tiled=True)  8.22 us
    ppermute x9, starting transfers between devices, swap(): return lax.ppermute(array, axis, [(i, i ^ distance) for i in range(count)])  6.95 us
    ppermute x1, starting transfers between devices, local(): lax.ppermute(own_weight, 'frames', up)  5.45 us
  transfers between devices with their start and end apart: 19, of which 8 were waited for; matrix products, arithmetic and copies ran while one was open for 8% of the time, Pallas kernels for 12%

profile of v2, /device:TPU:0, one launch (start us, length us, event | category | flops | bytes accessed | tf_op | source)
XLA Modules:
  0.0 118.6 jit_solution(7343050978829876008)
XLA Ops:
  0.6 2.0 %slice_bitcast_fusion = (bf16[2,96,896]{2,1,0:T(8,128)(2,1)S(1)}, bf16[2,96,896]{2,1,0:T(8,128)(2,1)}) fusion(bf16[2,3,96,896]{3,2,1,0:T(8,128)(2,1)} %bitcast.27), kind=kLoop, calls=%fused_computation.9 | loop fusion | bytes 1376256 | tf_op jit(solution)/shard_map/squeeze | solution.py:365
  2.6 4.9 %collective-permute-start = (bf16[2,96,896]{2,1,0:T(8,128)(2,1)}, bf16[2,96,896]{2,1,0:T(8,128)(2,1)S(1)}, u32[]{:S(2)}, u32[]{:S(2)}) collective-permute-start(bf16[2,96,896]{2,1,0:T(8,128)(2,1)} %get-tuple-element.37), channel_id=1, source_target_pairs={{0,8},{8,16},{16,24},{1,9},{9,17},{17,25},{2,10},{10,18},{18,26},{... | collective-permute-start | bytes 1032200 | tf_op jit(solution)/shard_map/ppermute | solution.py:370
  8.8 2.1 %fusion.2 = (bf16[2,96,896]{2,1,0:T(8,128)(2,1)}, bf16[2,96,896]{2,1,0:T(8,128)(2,1)}) fusion(bf16[2,3,96,896]{3,2,1,0:T(8,128)(2,1)} %bitcast.36, bf16[2,3,96,896]{3,2,1,0:T(8,128)(2,1)S(1)} %bitcast.28), kind=kLoop, calls=%fused_computation.8 | loop fusion | flops 1720320 | bytes 2064384 | tf_op jit(solution)/shard_map/convert_element_type | solution.py:20
  11.0 4.6 %collective-permute-start.8 = (bf16[2,96,896]{2,1,0:T(8,128)(2,1)}, bf16[2,96,896]{2,1,0:T(8,128)(2,1)S(1)}, u32[]{:S(2)}, u32[]{:S(2)}) collective-permute-start(bf16[2,96,896]{2,1,0:T(8,128)(2,1)} %get-tuple-element.44), channel_id=1, source_target_pairs={{0,8},{8,16},{16,24},{1,9},{9,17},{17,25},{2,10},{10,18},{18,26},{... | collective-permute-start | bytes 1032200 | tf_op jit(solution)/shard_map/ppermute | solution.py:370
  16.9 3.6 %copy.9 = bf16[896,896]{0,1:T(8,128)(2,1)} copy(bf16[896,896]{1,0:T(8,128)(2,1)} %param.7) | data formatting | bytes 3211264 | tf_op jit(solution)/shard_map/optimization_barrier | solution.py:368
  21.9 5.5 %collective-permute-start.3 = (bf16[448,896]{1,0:T(8,128)(2,1)S(1)}, bf16[448,896]{1,0:T(8,128)(2,1)}, u32[]{:S(2)}, u32[]{:S(2)}) collective-permute-start(bf16[448,896]{1,0:T(8,128)(2,1)S(1)} %fusion.refs_8_), channel_id=1, source_target_pairs={{0,8},{8,16},{16,24},{1,9},{9,17},{17,25},{2,10},{10,18},{18,26},{... | collective-permute-start | bytes 2408456 | tf_op jit(solution)/shard_map/ppermute | solution.py:388
  29.5 4.5 %attention.2 = bf16[2,96,896]{2,1,0:T(8,128)(2,1)S(1)} custom-call(s32[7]{0:T(128)S(1)} %pad_add_fusion.where_ref, bf16[2,3,96,896]{3,2,1,0:T(8,128)(2,1)S(1)} %bitcast.29, bf16[2,96,896]{2,1,0:T(8,128)(2,1)S(1)} %collective-permute-done.left_ref, bf16[2,96,896]{2,1,0:T(8,128)(2,1)S(1)} %collective-permute-done.1.right_ref), custom_call_target="tpu_custom_call" | custom-call | tf_op jit(solution)/shard_map/attention/pallas_call | solution.py:65
  34.0 1.6 %collective-permute-start.2 = (bf16[1,192,896]{2,1,0:T(8,128)(2,1)S(1)}, bf16[1,192,896]{2,1,0:T(8,128)(2,1)S(1)}, u32[]{:S(2)}, u32[]{:S(2)}) collective-permute-start(bf16[1,192,896]{2,1,0:T(8,128)(2,1)S(1)} %bitcast.33), channel_id=1, source_target_pairs={{0,1},{1,0},{2,3},{3,2},{4,5},{5,4},{6,7},{7,6},{8,9},{9,8},{10,11... | collective-permute-start | bytes 1032200 | tf_op jit(solution)/shard_map/ppermute | solution.py:306
  36.5 4.5 %attention.3 = bf16[2,96,896]{2,1,0:T(8,128)(2,1)S(1)} custom-call(s32[7]{0:T(128)S(1)} %pad_add_fusion.where_ref, bf16[2,3,96,896]{3,2,1,0:T(8,128)(2,1)S(1)} %add_convert_fusion.own_ref, bf16[2,96,896]{2,1,0:T(8,128)(2,1)S(1)} %collective-permute-done.8.left_ref, bf16[2,96,896]{2,1,0:T(8,128)(2,1)S(1)} %collective-permute-done.9.right_ref), custom_call_target="tpu_custom_call" | custom-call | tf_op jit(solution)/shard_map/attention/pallas_call | solution.py:65
  41.1 1.6 %collective-permute-start.10 = (bf16[1,192,896]{2,1,0:T(8,128)(2,1)S(1)}, bf16[1,192,896]{2,1,0:T(8,128)(2,1)S(1)}, u32[]{:S(2)}, u32[]{:S(2)}) collective-permute-start(bf16[1,192,896]{2,1,0:T(8,128)(2,1)S(1)} %bitcast.31), channel_id=1, source_target_pairs={{0,4},{2,6},{4,0},{6,2},{1,5},{3,7},{5,1},{7,3},{8,12},{10,14},{12... | collective-permute-start | bytes 1032200 | tf_op jit(solution)/shard_map/ppermute | solution.py:306
  42.8 4.8 %collective-permute-done.4.refs_10_ = bf16[448,896]{1,0:T(8,128)(2,1)} collective-permute-done((bf16[448,896]{1,0:T(8,128)(2,1)S(1)}, bf16[448,896]{1,0:T(8,128)(2,1)}, u32[]{:S(2)}, u32[]{:S(2)}) %collective-permute-start.4) | collective-permute-done | bytes 802848 | tf_op jit(solution)/shard_map/ppermute | solution.py:388
  49.7 1.6 %collective-permute-start.11 = (bf16[2,192,896]{2,1,0:T(8,128)(2,1)S(1)}, bf16[2,192,896]{2,1,0:T(8,128)(2,1)S(1)}, u32[]{:S(2)}, u32[]{:S(2)}) collective-permute-start(bf16[2,192,896]{2,1,0:T(8,128)(2,1)S(1)} %pad_maximum_fusion.1.refs_4_), channel_id=1, source_target_pairs={{0,1},{1,0},{2,3},{3,2},{4,5},{5,4},{6,7},{7,6},{8,9},{9,8},{10,11... | collective-permute-start | bytes 2064392 | tf_op jit(solution)/shard_map/ppermute | solution.py:306
  51.3 1.5 %collective-permute-start.5 = (bf16[2,192,896]{2,1,0:T(8,128)(2,1)S(1)}, bf16[2,192,896]{2,1,0:T(8,128)(2,1)S(1)}, u32[]{:S(2)}, u32[]{:S(2)}) collective-permute-start(bf16[2,192,896]{2,1,0:T(8,128)(2,1)S(1)} %pad_maximum_fusion.refs_0_), channel_id=1, source_target_pairs={{0,4},{2,6},{4,0},{6,2},{1,5},{3,7},{5,1},{7,3},{8,12},{10,14},{12... | collective-permute-start | bytes 2064392 | tf_op jit(solution)/shard_map/ppermute | solution.py:306
  52.8 11.8 %collective-permute-done.11.refs_5_ = bf16[2,192,896]{2,1,0:T(8,128)(2,1)S(1)} collective-permute-done((bf16[2,192,896]{2,1,0:T(8,128)(2,1)S(1)}, bf16[2,192,896]{2,1,0:T(8,128)(2,1)S(1)}, u32[]{:S(2)}, u32[]{:S(2)}) %collective-permute-start.11) | collective-permute-done | bytes 688160 | tf_op jit(solution)/shard_map/ppermute | solution.py:306
  65.9 3.4 %collective-permute-done.14.refs_12_ = bf16[448,896]{1,0:T(8,128)(2,1)S(1)} collective-permute-done((bf16[448,896]{1,0:T(8,128)(2,1)}, bf16[448,896]{1,0:T(8,128)(2,1)S(1)}, u32[]{:S(2)}, u32[]{:S(2)}) %collective-permute-start.14) | collective-permute-done | bytes 802848 | tf_op jit(solution)/shard_map/ppermute | solution.py:399
  69.2 1.9 %collective-permute-start.16 = (bf16[448,896]{1,0:T(8,128)(2,1)S(1)}, bf16[448,896]{1,0:T(8,128)(2,1)S(1)}, u32[]{:S(2)}, u32[]{:S(2)}) collective-permute-start(bf16[448,896]{1,0:T(8,128)(2,1)S(1)} %fusion.refs_8_), channel_id=1, source_target_pairs={{0,24},{24,0},{1,25},{25,1},{2,26},{26,2},{3,27},{27,3},{4,28},{28... | collective-permute-start | bytes 2408456 | tf_op jit(solution)/shard_map/ppermute | solution.py:389
  71.4 5.7 %project.2.refs_9_ = f32[2,384,512]{2,1,0:T(8,128)S(1)} custom-call(s32[7]{0:T(128)S(1)} %pad_add_fusion.where_ref, bf16[2,192,896]{2,1,0:T(8,128)(2,1)S(1)} %pad_maximum_fusion.refs_0_, bf16[2,192,896]{2,1,0:T(8,128)(2,1)S(1)} %collective-permute-done.5.refs_1_, bf16[2,192,896]{2,1,0:T(8,128)(2,1)S(1)} %collective-permute-done.6.refs_2_, ...), custom_call_target="tpu_custom_call" | custom-call | flops 3082813440 | bytes 10895360 | tf_op jit(solution)/shard_map/project/pallas_call | solution.py:195
  77.1 16.1 %collective-permute-done.16.refs_8_ = bf16[448,896]{1,0:T(8,128)(2,1)S(1)} collective-permute-done((bf16[448,896]{1,0:T(8,128)(2,1)S(1)}, bf16[448,896]{1,0:T(8,128)(2,1)S(1)}, u32[]{:S(2)}, u32[]{:S(2)}) %collective-permute-start.16) | collective-permute-done | bytes 802848 | tf_op jit(solution)/shard_map/ppermute | solution.py:389
  93.2 2.6 %project.3 = (f32[2,384,512]{2,1,0:T(8,128)S(1)}, f32[8,1,768]{2,1,0:T(1,128)S(1)}) custom-call(s32[7]{0:T(128)S(1)} %pad_add_fusion.where_ref, bf16[2,192,896]{2,1,0:T(8,128)(2,1)S(1)} %pad_maximum_fusion.refs_0_, bf16[2,192,896]{2,1,0:T(8,128)(2,1)S(1)} %collective-permute-done.5.refs_1_, ...), custom_call_target="tpu_custom_call", output_to_operand_aliasing={{0}: (10, {})} | custom-call | flops 616562688 | bytes 2179072 | tf_op jit(solution)/shard_map/project/pallas_call | solution.py:195
  95.8 8.2 %all_to_all.10.squares_ref = f32[8,1,768]{2,1,0:T(1,128)S(1)} all-to-all(f32[8,1,768]{2,1,0:T(1,128)S(1)} %get-tuple-element.52), channel_id=1, replica_groups=mesh['frames'=4,'mp'=4,'dp'=2] {'mp','dp'}, dimensions={0} | all-to-all | bytes 49152 | tf_op jit(solution)/shard_map/all_to_all | solution.py:329
  106.2 2.6 %all-to-all-start.1 = ((f32[32,1,512]{2,1,0:T(1,128)}), f32[32,1,512]{2,1,0:T(1,128)S(1)}, u32[]{:S(2)}, u32[]{:S(2)}) async-start(f32[32,1,512]{2,1,0:T(1,128)} %get-tuple-element.54), calls=%async_computation.1 | async-start | bytes 131072 | tf_op jit(solution)/shard_map/all_to_all | solution.py:329
  108.7 3.7 %collective-permute-done.17 = bf16[2,96,448]{2,1,0:T(8,128)(2,1)S(1)} collective-permute-done((bf16[2,96,448]{2,1,0:T(8,128)(2,1)S(1)}, bf16[2,96,448]{2,1,0:T(8,128)(2,1)S(1)}, u32[]{:S(2)}, u32[]{:S(2)}) %collective-permute-start.17) | collective-permute-done | bytes 172064 | tf_op jit(solution)/shard_map/ppermute | solution.py:306
  113.4 3.0 %all-to-all-done.1.rows_ref = f32[32,1,512]{2,1,0:T(1,128)S(1)} async-done(((f32[32,1,512]{2,1,0:T(1,128)}), f32[32,1,512]{2,1,0:T(1,128)S(1)}, u32[]{:S(2)}, u32[]{:S(2)}) %all-to-all-start.1) | async-done | bytes 65568 | tf_op jit(solution)/shard_map/all_to_all | solution.py:329
  117.0 1.7 %conclude.1 = (f32[1]{0:T(128)}, f32[896]{0:T(1024)}) custom-call(s32[7]{0:T(128)} %copy-done.1, f32[32,1,512]{2,1,0:T(1,128)} %copy-done.3, f32[1,896]{1,0:T(1,128)} %broadcast_in_dim.10.gain_ref), custom_call_target="tpu_custom_call" | custom-call | tf_op jit(solution)/shard_map/conclude/pallas_call | solution.py:288
  (46 shorter events, 14.4 us)
Async XLA Ops:
  0.6 8.2 %copy-start = (bf16[1,2,96,3,896]{4,2,3,1,0:T(8,128)(2,1)S(1)}, bf16[1,2,96,3,896]{4,2,3,1,0:T(8,128)(2,1)}, u32[]{:S(2)}) copy-start(bf16[1,2,96,3,896]{4,2,3,1,0:T(8,128)(2,1)} %param.5) | copy-start | bytes 3096580
  2.6 19.3 %collective-permute-start = (bf16[2,96,896]{2,1,0:T(8,128)(2,1)}, bf16[2,96,896]{2,1,0:T(8,128)(2,1)S(1)}, u32[]{:S(2)}, u32[]{:S(2)}) collective-permute-start(bf16[2,96,896]{2,1,0:T(8,128)(2,1)} %get-tuple-element.37), channel_id=1, source_target_pairs={{0,8},{8,16},{16,24},{1,9},{9,17},{17,25},{2,10},{10,18},{18,26},{... | collective-permute-start | bytes 1032200 | tf_op jit(solution)/shard_map/ppermute | solution.py:370
  7.5 14.4 %collective-permute-start.1 = (bf16[2,96,896]{2,1,0:T(8,128)(2,1)S(1)}, bf16[2,96,896]{2,1,0:T(8,128)(2,1)S(1)}, u32[]{:S(2)}, u32[]{:S(2)}) collective-permute-start(bf16[2,96,896]{2,1,0:T(8,128)(2,1)S(1)} %get-tuple-element.38), channel_id=1, source_target_pairs={{8,0},{16,8},{24,16},{9,1},{17,9},{25,17},{10,2},{18,10},{26,18},{... | collective-permute-start | bytes 1032200 | tf_op jit(solution)/shard_map/ppermute | solution.py:370
  11.0 25.6 %collective-permute-start.8 = (bf16[2,96,896]{2,1,0:T(8,128)(2,1)}, bf16[2,96,896]{2,1,0:T(8,128)(2,1)S(1)}, u32[]{:S(2)}, u32[]{:S(2)}) collective-permute-start(bf16[2,96,896]{2,1,0:T(8,128)(2,1)} %get-tuple-element.44), channel_id=1, source_target_pairs={{0,8},{8,16},{16,24},{1,9},{9,17},{17,25},{2,10},{10,18},{18,26},{... | collective-permute-start | bytes 1032200 | tf_op jit(solution)/shard_map/ppermute | solution.py:370
  15.6 21.0 %collective-permute-start.9 = (bf16[2,96,896]{2,1,0:T(8,128)(2,1)}, bf16[2,96,896]{2,1,0:T(8,128)(2,1)S(1)}, u32[]{:S(2)}, u32[]{:S(2)}) collective-permute-start(bf16[2,96,896]{2,1,0:T(8,128)(2,1)} %get-tuple-element.45), channel_id=1, source_target_pairs={{8,0},{16,8},{24,16},{9,1},{17,9},{25,17},{10,2},{18,10},{26,18},{... | collective-permute-start | bytes 1032200 | tf_op jit(solution)/shard_map/ppermute | solution.py:370
  21.9 20.9 %collective-permute-start.3 = (bf16[448,896]{1,0:T(8,128)(2,1)S(1)}, bf16[448,896]{1,0:T(8,128)(2,1)}, u32[]{:S(2)}, u32[]{:S(2)}) collective-permute-start(bf16[448,896]{1,0:T(8,128)(2,1)S(1)} %fusion.refs_8_), channel_id=1, source_target_pairs={{0,8},{8,16},{16,24},{1,9},{9,17},{17,25},{2,10},{10,18},{18,26},{... | collective-permute-start | bytes 2408456 | tf_op jit(solution)/shard_map/ppermute | solution.py:388
  27.4 20.2 %collective-permute-start.4 = (bf16[448,896]{1,0:T(8,128)(2,1)S(1)}, bf16[448,896]{1,0:T(8,128)(2,1)}, u32[]{:S(2)}, u32[]{:S(2)}) collective-permute-start(bf16[448,896]{1,0:T(8,128)(2,1)S(1)} %fusion.refs_8_), channel_id=1, source_target_pairs={{8,0},{16,8},{24,16},{9,1},{17,9},{25,17},{10,2},{18,10},{26,18},{... | collective-permute-start | bytes 2408456 | tf_op jit(solution)/shard_map/ppermute | solution.py:388
  29.4 6.2 %copy-start.2 = (bf16[1,2,96,3,896]{4,2,3,1,0:T(8,128)(2,1)S(1)}, bf16[1,2,96,3,896]{4,2,3,1,0:T(8,128)(2,1)}, u32[]{:S(2)}) copy-start(bf16[1,2,96,3,896]{4,2,3,1,0:T(8,128)(2,1)} %param.6) | copy-start | bytes 3096580
  29.5 63.7 %copy-start.1 = (s32[7]{0:T(128)}, s32[7]{0:T(128)S(1)}, u32[]{:S(2)}) copy-start(s32[7]{0:T(128)S(1)} %pad_add_fusion.where_ref) | copy-start | bytes 88
  34.0 1.9 %copy-start.4 = (f32[896]{0:T(1024)S(1)}, f32[896]{0:T(1024)}, u32[]{:S(2)}) copy-start(f32[896]{0:T(1024)} %param.8) | copy-start | bytes 10756
  34.0 8.7 %collective-permute-start.2 = (bf16[1,192,896]{2,1,0:T(8,128)(2,1)S(1)}, bf16[1,192,896]{2,1,0:T(8,128)(2,1)S(1)}, u32[]{:S(2)}, u32[]{:S(2)}) collective-permute-start(bf16[1,192,896]{2,1,0:T(8,128)(2,1)S(1)} %bitcast.33), channel_id=1, source_target_pairs={{0,1},{1,0},{2,3},{3,2},{4,5},{5,4},{6,7},{7,6},{8,9},{9,8},{10,11... | collective-permute-start | bytes 1032200 | tf_op jit(solution)/shard_map/ppermute | solution.py:306
  41.1 8.5 %collective-permute-start.10 = (bf16[1,192,896]{2,1,0:T(8,128)(2,1)S(1)}, bf16[1,192,896]{2,1,0:T(8,128)(2,1)S(1)}, u32[]{:S(2)}, u32[]{:S(2)}) collective-permute-start(bf16[1,192,896]{2,1,0:T(8,128)(2,1)S(1)} %bitcast.31), channel_id=1, source_target_pairs={{0,4},{2,6},{4,0},{6,2},{1,5},{3,7},{5,1},{7,3},{8,12},{10,14},{12... | collective-permute-start | bytes 1032200 | tf_op jit(solution)/shard_map/ppermute | solution.py:306
  47.6 18.3 %collective-permute-start.13 = (bf16[448,896]{1,0:T(8,128)(2,1)}, bf16[448,896]{1,0:T(8,128)(2,1)S(1)}, u32[]{:S(2)}, u32[]{:S(2)}) collective-permute-start(bf16[448,896]{1,0:T(8,128)(2,1)} %collective-permute-done.3.refs_9_), channel_id=1, source_target_pairs={{8,16},{16,24},{9,17},{17,25},{10,18},{18,26},{11,19},{19,27},{12,... | collective-permute-start | bytes 2408456 | tf_op jit(solution)/shard_map/ppermute | solution.py:398
  48.3 20.9 %collective-permute-start.14 = (bf16[448,896]{1,0:T(8,128)(2,1)}, bf16[448,896]{1,0:T(8,128)(2,1)S(1)}, u32[]{:S(2)}, u32[]{:S(2)}) collective-permute-start(bf16[448,896]{1,0:T(8,128)(2,1)} %collective-permute-done.4.refs_10_), channel_id=1, source_target_pairs={{8,0},{16,8},{9,1},{17,9},{10,2},{18,10},{11,3},{19,11},{12,4},{20... | collective-permute-start | bytes 2408456 | tf_op jit(solution)/shard_map/ppermute | solution.py:399
  49.7 14.9 %collective-permute-start.11 = (bf16[2,192,896]{2,1,0:T(8,128)(2,1)S(1)}, bf16[2,192,896]{2,1,0:T(8,128)(2,1)S(1)}, u32[]{:S(2)}, u32[]{:S(2)}) collective-permute-start(bf16[2,192,896]{2,1,0:T(8,128)(2,1)S(1)} %pad_maximum_fusion.1.refs_4_), channel_id=1, source_target_pairs={{0,1},{1,0},{2,3},{3,2},{4,5},{5,4},{6,7},{7,6},{8,9},{9,8},{10,11... | collective-permute-start | bytes 2064392 | tf_op jit(solution)/shard_map/ppermute | solution.py:306
  51.3 14.6 %collective-permute-start.5 = (bf16[2,192,896]{2,1,0:T(8,128)(2,1)S(1)}, bf16[2,192,896]{2,1,0:T(8,128)(2,1)S(1)}, u32[]{:S(2)}, u32[]{:S(2)}) collective-permute-start(bf16[2,192,896]{2,1,0:T(8,128)(2,1)S(1)} %pad_maximum_fusion.refs_0_), channel_id=1, source_target_pairs={{0,4},{2,6},{4,0},{6,2},{1,5},{3,7},{5,1},{7,3},{8,12},{10,14},{12... | collective-permute-start | bytes 2064392 | tf_op jit(solution)/shard_map/ppermute | solution.py:306
  52.8 18.4 %collective-permute-start.12 = (bf16[2,192,896]{2,1,0:T(8,128)(2,1)S(1)}, bf16[2,192,896]{2,1,0:T(8,128)(2,1)S(1)}, u32[]{:S(2)}, u32[]{:S(2)}) collective-permute-start(bf16[2,192,896]{2,1,0:T(8,128)(2,1)S(1)} %pad_maximum_fusion.1.refs_4_), channel_id=1, source_target_pairs={{0,2},{2,0},{4,6},{6,4},{1,3},{3,1},{5,7},{7,5},{8,10},{10,8},{12,... | collective-permute-start | bytes 2064392 | tf_op jit(solution)/shard_map/ppermute | solution.py:306
  64.6 6.5 %collective-permute-start.6 = (bf16[2,192,896]{2,1,0:T(8,128)(2,1)S(1)}, bf16[2,192,896]{2,1,0:T(8,128)(2,1)S(1)}, u32[]{:S(2)}, u32[]{:S(2)}) collective-permute-start(bf16[2,192,896]{2,1,0:T(8,128)(2,1)S(1)} %pad_maximum_fusion.refs_0_), channel_id=1, source_target_pairs={{0,2},{2,0},{4,6},{6,4},{1,3},{3,1},{5,7},{7,5},{8,10},{10,8},{12,... | collective-permute-start | bytes 2064392 | tf_op jit(solution)/shard_map/ppermute | solution.py:306
  65.9 5.3 %collective-permute-start.7 = (bf16[2,192,896]{2,1,0:T(8,128)(2,1)S(1)}, bf16[2,192,896]{2,1,0:T(8,128)(2,1)S(1)}, u32[]{:S(2)}, u32[]{:S(2)}) collective-permute-start(bf16[2,192,896]{2,1,0:T(8,128)(2,1)S(1)} %collective-permute-done.5.refs_1_), channel_id=1, source_target_pairs={{0,2},{2,0},{4,6},{6,4},{1,3},{3,1},{5,7},{7,5},{8,10},{10,8},{12,... | collective-permute-start | bytes 2064392 | tf_op jit(solution)/shard_map/ppermute | solution.py:306
  69.2 2.1 %collective-permute-start.15 = (bf16[2,192,896]{2,1,0:T(8,128)(2,1)S(1)}, bf16[2,192,896]{2,1,0:T(8,128)(2,1)S(1)}, u32[]{:S(2)}, u32[]{:S(2)}) collective-permute-start(bf16[2,192,896]{2,1,0:T(8,128)(2,1)S(1)} %collective-permute-done.11.refs_5_), channel_id=1, source_target_pairs={{0,2},{2,0},{4,6},{6,4},{1,3},{3,1},{5,7},{7,5},{8,10},{10,8},{12,... | collective-permute-start | bytes 2064392 | tf_op jit(solution)/shard_map/ppermute | solution.py:306
  69.2 24.0 %collective-permute-start.16 = (bf16[448,896]{1,0:T(8,128)(2,1)S(1)}, bf16[448,896]{1,0:T(8,128)(2,1)S(1)}, u32[]{:S(2)}, u32[]{:S(2)}) collective-permute-start(bf16[448,896]{1,0:T(8,128)(2,1)S(1)} %fusion.refs_8_), channel_id=1, source_target_pairs={{0,24},{24,0},{1,25},{25,1},{2,26},{26,2},{3,27},{27,3},{4,28},{28... | collective-permute-start | bytes 2408456 | tf_op jit(solution)/shard_map/ppermute | solution.py:389
  105.4 7.0 %collective-permute-start.17 = (bf16[2,96,448]{2,1,0:T(8,128)(2,1)S(1)}, bf16[2,96,448]{2,1,0:T(8,128)(2,1)S(1)}, u32[]{:S(2)}, u32[]{:S(2)}) collective-permute-start(bf16[2,96,448]{2,1,0:T(8,128)(2,1)S(1)} %bitcast.39), channel_id=1, source_target_pairs={{0,1},{1,0},{2,3},{3,2},{4,5},{5,4},{6,7},{7,6},{8,9},{9,8},{10,11... | collective-permute-start | bytes 516104 | tf_op jit(solution)/shard_map/ppermute | solution.py:306
  106.2 10.2 %all-to-all-start.1 = ((f32[32,1,512]{2,1,0:T(1,128)}), f32[32,1,512]{2,1,0:T(1,128)S(1)}, u32[]{:S(2)}, u32[]{:S(2)}) async-start(f32[32,1,512]{2,1,0:T(1,128)} %get-tuple-element.54), calls=%async_computation.1 | async-start | bytes 131072 | tf_op jit(solution)/shard_map/all_to_all | solution.py:329
  116.4 0.6 copy-start.3

commit v3 on v2

--- a/solution.py
+++ b/solution.py
@@ -20,7 +20,71 @@
     return (clean.astype(jnp.float32) + sigma_noise * noise.astype(jnp.float32)).astype(jnp.bfloat16)
 
 
-def attend_kernel(where_ref, own_ref, left_ref, right_ref, out_ref):
+def prepare_halo(clean, noise, slots):
+    _, _, tile_len, width = clean.shape
+
+    def kernel(clean_ref, noise_ref, *refs):
+        out_refs, (keep, add, sems) = refs[: len(slots)], refs[len(slots) :]
+        copies = []
+        for n, slot in enumerate(slots):
+            for m, (source, target) in enumerate(((clean_ref, keep), (noise_ref, add))):
+                copies.append(
+                    pltpu.make_async_copy(
+                        source.at[slot, pl.ds(1, 2)], target.at[n], sems.at[n, m]
+                    )
+                )
+                copies[-1].start()
+        for n in range(len(slots)):
+            copies[2 * n].wait()
+            copies[2 * n + 1].wait()
+            out_refs[n][0] = keep[n]
+            out_refs[n][1] = perturb(keep[n], add[n])
+
+    block = (2, 2, tile_len, width)
+    return pl.pallas_call(
+        kernel,
+        in_specs=[pl.BlockSpec(memory_space=pl.ANY)] * 2,
+        out_specs=[pl.BlockSpec(memory_space=pltpu.VMEM)] * len(slots),
+        out_shape=[jax.ShapeDtypeStruct(block, jnp.bfloat16)] * len(slots),
+        scratch_shapes=[
+            pltpu.VMEM((len(slots), 2, tile_len, width), jnp.bfloat16),
+            pltpu.VMEM((len(slots), 2, tile_len, width), jnp.bfloat16),
+            pltpu.SemaphoreType.DMA((len(slots), 2)),
+        ],
+        compiler_params=pltpu.CompilerParams(vmem_limit_bytes=16 * 1024 * 1024),
+        name="prepare_halo",
+    )(clean, noise)
+
+
+def prepare_weight(where, weight, clip_count):
+    depth, width = weight.shape
+    half = width // clip_count
+
+    def kernel(where_ref, weight_ref, out_ref):
+        for clip in range(clip_count):
+
+            @pl.when(where_ref[2] == clip)
+            def _():
+                begin, end = clip * half, (clip + 1) * half
+                for first in range(begin // LANES * LANES, end, LANES):
+                    low, high = max(first, begin), min(first + LANES, end)
+                    turned = weight_ref[:, pl.ds(first, LANES)].T
+                    out_ref[pl.ds(low - begin, high - low)] = turned[low - first : high - first]
+
+    return pl.pallas_call(
+        kernel,
+        in_specs=[
+            pl.BlockSpec(memory_space=pltpu.SMEM),
+            pl.BlockSpec(memory_space=pltpu.VMEM),
+        ],
+        out_specs=pl.BlockSpec(memory_space=pltpu.VMEM),
+        out_shape=jax.ShapeDtypeStruct((half, depth), weight.dtype),
+        compiler_params=pltpu.CompilerParams(vmem_limit_bytes=16 * 1024 * 1024),
+        name="prepare_weight",
+    )(where, weight)
+
+
+def attend_kernel(where_ref, own_ref, right_ref, left_ref, out_ref):
     slots, _, tile_len, width = own_ref.shape
     key_pos = lax.broadcasted_iota(jnp.int32, (1, 2 * tile_len), 1)
     live = []
@@ -57,11 +121,11 @@
         )
 
 
-def attention(where, own, left, right):
+def attention(where, own, left, right, stream):
     slots, _, tile_len, width = own.shape
     block = HEADS_AT_ONCE * HEAD_DIM
     own_spec = pl.BlockSpec((slots, 3, tile_len, block), lambda h, c: (0, 0, 0, h))
-    halo_spec = pl.BlockSpec((2, tile_len, block), lambda h, c: (0, 0, h))
+    halo_spec = pl.BlockSpec((None, 2, tile_len, block), lambda h, c: (stream, 0, 0, h))
     return pl.pallas_call(
         attend_kernel,
         grid_spec=pltpu.PrefetchScalarGridSpec(
@@ -73,12 +137,12 @@
         out_shape=jax.ShapeDtypeStruct((slots, tile_len, width), jnp.bfloat16),
         compiler_params=pltpu.CompilerParams(vmem_limit_bytes=48 * 1024 * 1024),
         cost_estimate=pl.CostEstimate(
-            flops=0 * slots * tile_len * tile_len * width,
-            bytes_accessed=0 * slots * tile_len * width,
+            flops=0,
+            bytes_accessed=0,
             transcendentals=0,
         ),
         name="attention",
-    )(where, own, left, right)
+    )(where, own, right, left)
 
 
 def whole_lanes(columns):
@@ -206,8 +270,8 @@
         input_output_aliases=aliases,
         compiler_params=pltpu.CompilerParams(vmem_limit_bytes=(8 + 4 * shard_total) * 1024 * 1024),
         cost_estimate=pl.CostEstimate(
-            flops=2 * clip_count * row_count * depth * columns * shard_total,
-            bytes_accessed=shard_total * depth * (clip_count * row_count + columns) * 2,
+            flops=0,
+            bytes_accessed=0,
             transcendentals=0,
         ),
         name="project",
@@ -358,17 +422,12 @@
     up = [(i, i + 1) for i in range(slab_count - 1)]
     down = [(i + 1, i) for i in range(slab_count - 1)]
 
-    halo = []
-    edges = (slots - 1, 0)
-    for noisy in (False, True):
-        sent = [
-            perturb(clean[slot, 1:], noise[slot, 1:]) if noisy else clean[slot, 1:]
-            for slot in edges
-        ]
-        sent, clean, noise, out_weight = lax.optimization_barrier((sent, clean, noise, out_weight))
-        halo.append(
-            (lax.ppermute(sent[0], "frames", up), lax.ppermute(sent[1], "frames", down))
-        )
+    tail, head = prepare_halo(clean, noise, (slots - 1, 0))
+    tail, head, clean, noise, out_weight = lax.optimization_barrier(
+        (tail, head, clean, noise, out_weight)
+    )
+    right = lax.ppermute(head, "frames", down)
+    left = lax.ppermute(tail, "frames", up)
     streams = (clean, perturb(clean, noise))
     counts = jnp.pad(live_counts[0], (1, 1))
     nearby = lax.dynamic_slice_in_dim(counts, slots * slab_index, slots + 2)
@@ -378,15 +437,18 @@
     gain_row = jnp.pad(own_columns(norm_gain), (0, whole_lanes(half) - half))[None]
     gain_all = norm_gain[None]
 
-    own_weight = own_columns(out_weight).T
-    own_weight, halo[0] = lax.optimization_barrier((own_weight, halo[0]))
+    own_weight = prepare_weight(where, out_weight, clip_count)
     line = slab_count == model_count and slab_count == 4
     last = slab_count - 1
-    near, passed, across = [], [], None
+    cut = min(LANES, half)
+    near, passed, across = [], [], []
 
     if line:
-        near = [lax.ppermute(own_weight, "frames", up), lax.ppermute(own_weight, "frames", down)]
-        across = lax.ppermute(own_weight, "frames", [(0, last), (last, 0)])
+        near = [lax.ppermute(own_weight, "frames", pairs) for pairs in (down, up)]
+        across = [
+            lax.ppermute(block, "frames", [(0, last), (last, 0)])
+            for block in (own_weight[:cut], own_weight[cut:])
+        ]
 
     def before_step(stream, step, part, value):
         nonlocal near, passed, gain_row, gain_all
@@ -395,9 +457,11 @@
                 (value, near, gain_row, gain_all)
             )
             passed = [
-                lax.ppermute(near[0], "frames", up[1:]),
-                lax.ppermute(near[1], "frames", down[:2]),
+                lax.ppermute(near[0], "frames", down[:2]),
+                lax.ppermute(near[1], "frames", up[1:]),
             ]
+        if line and stream == 1 and step == 1:
+            value, across[0] = lax.optimization_barrier((value, across[0]))
         if line and stream == 1 and step == 2 and part == 1:
             value, passed = lax.optimization_barrier((value, passed))
         return value
@@ -408,7 +472,7 @@
         distances("mp")[:1] + distances("dp") + distances("mp")[1:],
     )
     for n, order in enumerate(orders):
-        attended = attention(where, streams[n], *halo[n]).reshape(near_rows, local_width)
+        attended = attention(where, streams[n], left, right, n).reshape(near_rows, local_width)
         gathered.append(
             spread(attended, order, lambda *at, n=n: before_step(n, *at))
         )
@@ -417,12 +481,15 @@
     if line:
         shards = [
             (0, own_weight, lambda slab: slab, lambda slab: slab >= 0),
-            (0, near[0], lambda slab: jnp.maximum(slab - 1, 0), lambda slab: slab > 0),
-            (0, near[1], lambda slab: jnp.minimum(slab + 1, last), lambda slab: slab < last),
-            (0, passed[0], lambda slab: jnp.maximum(slab - 2, 0), lambda slab: slab >= 2),
-            (0, passed[1], lambda slab: jnp.minimum(slab + 2, last), lambda slab: slab < 2),
-            (0, across, lambda slab: last - slab, lambda slab: (slab == 0) | (slab == last)),
+            (0, near[0], lambda slab: jnp.minimum(slab + 1, last), lambda slab: slab < last),
+            (0, near[1], lambda slab: jnp.maximum(slab - 1, 0), lambda slab: slab > 0),
+            (0, passed[0], lambda slab: jnp.minimum(slab + 2, last), lambda slab: slab < 2),
+            (0, passed[1], lambda slab: jnp.maximum(slab - 2, 0), lambda slab: slab >= 2),
         ]
+        for first, block in zip((0, cut), across):
+            shards.append(
+                (first, block, lambda slab: last - slab, lambda slab: (slab == 0) | (slab == last))
+            )
         (total,) = project(where, gathered, shards[:-1], None, half, 0)
         total, squares = project(where, gathered, shards[-1:], total, half, peers)
     else:

time: 119 us -> 115 us (0.966)
  waiting for transfers between devices: 44.3 us -> 32.7 us
  starting transfers between devices: 32.2 us -> 36.7 us
  Pallas kernels: 20.4 us -> 24.7 us
  other arithmetic: 5.14 us -> 2.61 us
    ppermute x9 -> x8, waiting for transfers between devices: 24.3 us -> 9.07 us  [the longest x2 6.73 us: local(): lax.ppermute(block, 'frames', [(0, last), (last, 0)])]
    unnamed x10 -> x24, local copies, waits for them, and re-layouts: 0.64 us -> 6.27 us
    optimization_barrier x1 -> x0, local copies, waits for them, and re-layouts: 3.58 us -> none  [local(): lax.optimization_barrier((sent, clean, noise, out_weight))]
    pallas_call x0 -> x2, Pallas kernels: none -> 2.58 us  [the longest x1 1.76 us: prepare_halo(): pl.pallas_call(kernel, in_specs=[pl.BlockSpec(memory_space=pl.ANY)] * 2,...]
    all_to_all x1, waiting for transfers between devices: 2.97 us -> 5.19 us  [collect(): return lax.all_to_all(rows, axes, split_axis=0, concat_axis=0, tiled=True)]
    all_to_all x1, starting transfers between devices: 2.57 us -> 4.73 us  [collect(): return lax.all_to_all(rows, axes, split_axis=0, concat_axis=0, tiled=True)]
    convert_element_type x2 -> x1, other arithmetic: 2.46 us -> 0.32 us  [perturb(): (clean.astype(jnp.float32) + sigma_noise * noise.astype(jnp.float32)).ast...]
    ppermute x9 -> x8, starting transfers between devices: 22.7 us -> 24.7 us  [the longest x2 8.76 us: local(): lax.ppermute(block, 'frames', [(0, last), (last, 0)])]
  transfers between devices with their start and end apart: 19 -> 18, of which waited for: 8 -> 8; matrix products, arithmetic and copies ran while one was open for 8% -> 4% of each run, Pallas kernels for 12% -> 15%
where the time goes in v3:
time: 115 us; the launch traced here: 114 us
  starting transfers between devices  36.7 us (32%)
  waiting for transfers between devices  32.7 us (28%)
  Pallas kernels  24.7 us (21%)
  local copies, waits for them, and re-layouts  8.44 us (7%)
  blocking collectives  7.86 us (7%)
  other arithmetic  2.61 us (2%)
    ppermute x9, waiting for transfers between devices, swap(): return lax.ppermute(array, axis, [(i, i ^ distance) for i in range(count)])  18.4 us
    pallas_call x2, Pallas kernels, attention(): pl.pallas_call(attend_kernel, grid_spec=pltpu.PrefetchScalarGridSpec(num_...  9.74 us
    pallas_call x2, Pallas kernels, project(): pl.pallas_call(kernel, in_specs=[pl.BlockSpec(memory_space=pltpu.SMEM)] +...  9.36 us
    ppermute x2, starting transfers between devices, local(): lax.ppermute(block, 'frames', [(0, last), (last, 0)])  8.76 us
    all_to_all x1, blocking collectives, collect(): return lax.all_to_all(rows, axes, split_axis=0, concat_axis=0, tiled=True)  7.86 us
    ppermute x9, starting transfers between devices, swap(): return lax.ppermute(array, axis, [(i, i ^ distance) for i in range(count)])  7.3 us
    ppermute x2, starting transfers between devices, local(): near = [lax.ppermute(own_weight, 'frames', pairs) for pairs in (down, up)]  6.91 us
    ppermute x2, waiting for transfers between devices, local(): lax.ppermute(block, 'frames', [(0, last), (last, 0)])  6.73 us
  transfers between devices with their start and end apart: 18, of which 8 were waited for; matrix products, arithmetic and copies ran while one was open for 4% of the time, Pallas kernels for 15%

profile of v3, /device:TPU:0, one launch (start us, length us, event | category | flops | bytes accessed | tf_op | source)
XLA Modules:
  0.0 113.9 jit_solution(14715425626088659545)
XLA Ops:
  3.1 1.8 %prepare_halo.1 = (bf16[2,2,96,896]{3,2,1,0:T(8,128)(2,1)}, bf16[2,2,96,896]{3,2,1,0:T(8,128)(2,1)}) custom-call(bf16[2,3,96,896]{3,2,1,0:T(8,128)(2,1)S(1)} %bitcast.17, bf16[2,3,96,896]{3,2,1,0:T(8,128)(2,1)S(1)} %bitcast.20), custom_call_target="tpu_custom_call" | custom-call | tf_op jit(solution)/shard_map/prepare_halo/pallas_call | solution.py:44
  4.9 1.4 %collective-permute-start = (bf16[2,2,96,896]{3,2,1,0:T(8,128)(2,1)}, bf16[2,2,96,896]{3,2,1,0:T(8,128)(2,1)S(1)}, u32[]{:S(2)}, u32[]{:S(2)}) collective-permute-start(bf16[2,2,96,896]{3,2,1,0:T(8,128)(2,1)} %get-tuple-element.31), channel_id=1, source_target_pairs={{8,0},{16,8},{24,16},{9,1},{17,9},{25,17},{10,2},{18,10},{26,18},{... | collective-permute-start | bytes 2064392 | tf_op jit(solution)/shard_map/ppermute | solution.py:429
  6.3 5.6 %collective-permute-start.1 = (bf16[2,2,96,896]{3,2,1,0:T(8,128)(2,1)}, bf16[2,2,96,896]{3,2,1,0:T(8,128)(2,1)S(1)}, u32[]{:S(2)}, u32[]{:S(2)}) collective-permute-start(bf16[2,2,96,896]{3,2,1,0:T(8,128)(2,1)} %get-tuple-element.32), channel_id=1, source_target_pairs={{0,8},{8,16},{16,24},{1,9},{9,17},{17,25},{2,10},{10,18},{18,26},{... | collective-permute-start | bytes 2064392 | tf_op jit(solution)/shard_map/ppermute | solution.py:430
  12.1 1.4 %copy-done.6 = bf16[896,896]{1,0:T(8,128)(2,1)S(1)} copy-done((bf16[896,896]{1,0:T(8,128)(2,1)S(1)}, bf16[896,896]{1,0:T(8,128)(2,1)}, u32[]{:S(2)}) %copy-start.6) | copy-done | bytes 1605656
  14.3 1.4 %collective-permute-start.3 = (bf16[448,896]{1,0:T(8,128)(2,1)S(1)}, bf16[448,896]{1,0:T(8,128)(2,1)}, u32[]{:S(2)}, u32[]{:S(2)}) collective-permute-start(bf16[448,896]{1,0:T(8,128)(2,1)S(1)} %prepare_weight.1.refs_8_), channel_id=1, source_target_pairs={{8,0},{16,8},{24,16},{9,1},{17,9},{25,17},{10,2},{18,10},{26,18},{... | collective-permute-start | bytes 2408456 | tf_op jit(solution)/shard_map/ppermute | solution.py:447
  15.8 5.5 %collective-permute-start.4 = (bf16[448,896]{1,0:T(8,128)(2,1)S(1)}, bf16[448,896]{1,0:T(8,128)(2,1)}, u32[]{:S(2)}, u32[]{:S(2)}) collective-permute-start(bf16[448,896]{1,0:T(8,128)(2,1)S(1)} %prepare_weight.1.refs_8_), channel_id=1, source_target_pairs={{0,8},{8,16},{16,24},{1,9},{9,17},{17,25},{2,10},{10,18},{18,26},{... | collective-permute-start | bytes 2408456 | tf_op jit(solution)/shard_map/ppermute | solution.py:447
  22.0 3.7 %collective-permute-start.9 = (bf16[128,896]{1,0:T(8,128)(2,1)}, bf16[128,896]{1,0:T(8,128)(2,1)}, u32[]{:S(2)}, u32[]{:S(2)}) collective-permute-start(bf16[128,896]{1,0:T(8,128)(2,1)} %slice.31), channel_id=1, source_target_pairs={{0,24},{24,0},{1,25},{25,1},{2,26},{26,2},{3,27},{27,3},{4,28},{28... | collective-permute-start | bytes 688136 | tf_op jit(solution)/shard_map/ppermute | solution.py:449
  26.4 1.6 %collective-permute-done.1.left_ref = bf16[2,2,96,896]{3,2,1,0:T(8,128)(2,1)S(1)} collective-permute-done((bf16[2,2,96,896]{3,2,1,0:T(8,128)(2,1)}, bf16[2,2,96,896]{3,2,1,0:T(8,128)(2,1)S(1)}, u32[]{:S(2)}, u32[]{:S(2)}) %collective-permute-start.1) | collective-permute-done | bytes 688160 | tf_op jit(solution)/shard_map/ppermute | solution.py:430
  28.0 5.2 %attention.2 = bf16[2,96,896]{2,1,0:T(8,128)(2,1)} custom-call(s32[7]{0:T(128)S(1)} %pad_add_fusion.where_ref, bf16[2,3,96,896]{3,2,1,0:T(8,128)(2,1)S(1)} %bitcast.18, bf16[2,2,96,896]{3,2,1,0:T(8,128)(2,1)S(1)} %collective-permute-done.right_ref, bf16[2,2,96,896]{3,2,1,0:T(8,128)(2,1)S(1)} %collective-permute-done.1.left_ref), custom_call_target="tpu_custom_call" | custom-call | tf_op jit(solution)/shard_map/attention/pallas_call | solution.py:129
  33.2 2.0 %collective-permute-start.2 = (bf16[1,192,896]{2,1,0:T(8,128)(2,1)}, bf16[1,192,896]{2,1,0:T(8,128)(2,1)}, u32[]{:S(2)}, u32[]{:S(2)}) collective-permute-start(bf16[1,192,896]{2,1,0:T(8,128)(2,1)} %bitcast.8), channel_id=1, source_target_pairs={{0,1},{1,0},{2,3},{3,2},{4,5},{5,4},{6,7},{7,6},{8,9},{9,8},{10,11... | collective-permute-start | bytes 1032200 | tf_op jit(solution)/shard_map/ppermute | solution.py:370
  38.7 4.5 %attention.3 = bf16[2,96,896]{2,1,0:T(8,128)(2,1)S(1)} custom-call(s32[7]{0:T(128)S(1)} %copy-done.8, bf16[2,3,96,896]{3,2,1,0:T(8,128)(2,1)S(1)} %add_convert_fusion.own_ref, bf16[2,2,96,896]{3,2,1,0:T(8,128)(2,1)S(1)} %collective-permute-done.right_ref, bf16[2,2,96,896]{3,2,1,0:T(8,128)(2,1)S(1)} %copy-done.5), custom_call_target="tpu_custom_call" | custom-call | tf_op jit(solution)/shard_map/attention/pallas_call | solution.py:129
  43.2 1.6 %collective-permute-start.8 = (bf16[1,192,896]{2,1,0:T(8,128)(2,1)S(1)}, bf16[1,192,896]{2,1,0:T(8,128)(2,1)S(1)}, u32[]{:S(2)}, u32[]{:S(2)}) collective-permute-start(bf16[1,192,896]{2,1,0:T(8,128)(2,1)S(1)} %bitcast.22), channel_id=1, source_target_pairs={{0,4},{2,6},{4,0},{6,2},{1,5},{3,7},{5,1},{7,3},{8,12},{10,14},{12... | collective-permute-start | bytes 1032200 | tf_op jit(solution)/shard_map/ppermute | solution.py:370
  48.0 2.5 %collective-permute-done.8 = bf16[1,192,896]{2,1,0:T(8,128)(2,1)S(1)} collective-permute-done((bf16[1,192,896]{2,1,0:T(8,128)(2,1)S(1)}, bf16[1,192,896]{2,1,0:T(8,128)(2,1)S(1)}, u32[]{:S(2)}, u32[]{:S(2)}) %collective-permute-start.8) | collective-permute-done | bytes 344096 | tf_op jit(solution)/shard_map/ppermute | solution.py:370
  51.6 1.5 %collective-permute-start.5 = (bf16[2,192,896]{2,1,0:T(8,128)(2,1)S(1)}, bf16[2,192,896]{2,1,0:T(8,128)(2,1)S(1)}, u32[]{:S(2)}, u32[]{:S(2)}) collective-permute-start(bf16[2,192,896]{2,1,0:T(8,128)(2,1)S(1)} %pad_maximum_fusion.refs_0_), channel_id=1, source_target_pairs={{0,4},{2,6},{4,0},{6,2},{1,5},{3,7},{5,1},{7,3},{8,12},{10,14},{12... | collective-permute-start | bytes 2064392 | tf_op jit(solution)/shard_map/ppermute | solution.py:370
  53.1 13.2 %collective-permute-done.10.refs_5_ = bf16[2,192,896]{2,1,0:T(8,128)(2,1)S(1)} collective-permute-done((bf16[2,192,896]{2,1,0:T(8,128)(2,1)S(1)}, bf16[2,192,896]{2,1,0:T(8,128)(2,1)S(1)}, u32[]{:S(2)}, u32[]{:S(2)}) %collective-permute-start.10) | collective-permute-done | bytes 688160 | tf_op jit(solution)/shard_map/ppermute | solution.py:370
  68.1 5.1 %collective-permute-start.15 = (bf16[320,896]{1,0:T(8,128)(2,1)S(1)}, bf16[320,896]{1,0:T(8,128)(2,1)S(1)}, u32[]{:S(2)}, u32[]{:S(2)}) collective-permute-start(bf16[320,896]{1,0:T(8,128)(2,1)S(1)} %slice.32), channel_id=1, source_target_pairs={{0,24},{24,0},{1,25},{25,1},{2,26},{26,2},{3,27},{27,3},{4,28},{28... | collective-permute-start | bytes 1720328 | tf_op jit(solution)/shard_map/ppermute | solution.py:449
  73.2 6.8 %project.2.refs_9_ = f32[2,384,512]{2,1,0:T(8,128)S(1)} custom-call(s32[7]{0:T(128)S(1)} %copy-done.8, bf16[2,192,896]{2,1,0:T(8,128)(2,1)S(1)} %pad_maximum_fusion.refs_0_, bf16[2,192,896]{2,1,0:T(8,128)(2,1)S(1)} %collective-permute-done.5.refs_1_, bf16[2,192,896]{2,1,0:T(8,128)(2,1)S(1)} %collective-permute-done.6.refs_2_, ...), custom_call_target="tpu_custom_call" | custom-call | tf_op jit(solution)/shard_map/project/pallas_call | solution.py:259
  80.0 6.7 %collective-permute-done.15.refs_8_ = bf16[320,896]{1,0:T(8,128)(2,1)S(1)} collective-permute-done((bf16[320,896]{1,0:T(8,128)(2,1)S(1)}, bf16[320,896]{1,0:T(8,128)(2,1)S(1)}, u32[]{:S(2)}, u32[]{:S(2)}) %collective-permute-start.15) | collective-permute-done | bytes 573472 | tf_op jit(solution)/shard_map/ppermute | solution.py:449
  86.7 2.6 %project.3 = (f32[2,384,512]{2,1,0:T(8,128)S(1)}, f32[8,1,768]{2,1,0:T(1,128)S(1)}) custom-call(s32[7]{0:T(128)S(1)} %copy-done.8, bf16[2,192,896]{2,1,0:T(8,128)(2,1)S(1)} %pad_maximum_fusion.refs_0_, bf16[2,192,896]{2,1,0:T(8,128)(2,1)S(1)} %collective-permute-done.5.refs_1_, ...), custom_call_target="tpu_custom_call", output_to_operand_aliasing={{0}: (10, {})} | custom-call | tf_op jit(solution)/shard_map/project/pallas_call | solution.py:259
  89.3 7.9 %all_to_all.10.squares_ref = f32[8,1,768]{2,1,0:T(1,128)S(1)} all-to-all(f32[8,1,768]{2,1,0:T(1,128)S(1)} %get-tuple-element.44), channel_id=1, replica_groups=mesh['frames'=4,'mp'=4,'dp'=2] {'mp','dp'}, dimensions={0} | all-to-all | bytes 49152 | tf_op jit(solution)/shard_map/all_to_all | solution.py:393
  99.3 4.7 %all-to-all-start.1 = ((f32[32,1,512]{2,1,0:T(1,128)}), f32[32,1,512]{2,1,0:T(1,128)S(1)}, u32[]{:S(2)}, u32[]{:S(2)}) async-start(f32[32,1,512]{2,1,0:T(1,128)} %get-tuple-element.46), calls=%async_computation.1 | async-start | bytes 131072 | tf_op jit(solution)/shard_map/all_to_all | solution.py:393
  104.0 1.5 %collective-permute-done.16 = bf16[2,96,448]{2,1,0:T(8,128)(2,1)S(1)} collective-permute-done((bf16[2,96,448]{2,1,0:T(8,128)(2,1)S(1)}, bf16[2,96,448]{2,1,0:T(8,128)(2,1)S(1)}, u32[]{:S(2)}, u32[]{:S(2)}) %collective-permute-start.16) | collective-permute-done | bytes 172064 | tf_op jit(solution)/shard_map/ppermute | solution.py:370
  106.5 5.2 %all-to-all-done.1.rows_ref = f32[32,1,512]{2,1,0:T(1,128)S(1)} async-done(((f32[32,1,512]{2,1,0:T(1,128)}), f32[32,1,512]{2,1,0:T(1,128)S(1)}, u32[]{:S(2)}, u32[]{:S(2)}) %all-to-all-start.1) | async-done | bytes 65568 | tf_op jit(solution)/shard_map/all_to_all | solution.py:393
  112.3 1.7 %conclude.1 = (f32[1]{0:T(128)}, f32[896]{0:T(1024)}) custom-call(s32[7]{0:T(128)} %copy-done.7, f32[32,1,512]{2,1,0:T(1,128)} %copy-done.9, f32[1,896]{1,0:T(1,128)} %broadcast_in_dim.10.gain_ref), custom_call_target="tpu_custom_call" | custom-call | tf_op jit(solution)/shard_map/conclude/pallas_call | solution.py:352
  (58 shorter events, 18.1 us)
Async XLA Ops:
  0.6 11.3 %copy-start.11 = (s32[1,8]{1,0:T(1,128)S(1)}, s32[1,8]{1,0:T(1,128)}, u32[]{:S(2)}) copy-start(s32[1,8]{1,0:T(1,128)} %param.9) | copy-start | bytes 100
  4.8 23.1 %copy-start.1 = (bf16[1,2,96,3,896]{4,2,3,1,0:T(8,128)(2,1)S(1)}, bf16[1,2,96,3,896]{4,2,3,1,0:T(8,128)(2,1)}, u32[]{:S(2)}) copy-start(bf16[1,2,96,3,896]{4,2,3,1,0:T(8,128)(2,1)} %param.5) | copy-start | bytes 3096580
  4.9 21.5 %collective-permute-start = (bf16[2,2,96,896]{3,2,1,0:T(8,128)(2,1)}, bf16[2,2,96,896]{3,2,1,0:T(8,128)(2,1)S(1)}, u32[]{:S(2)}, u32[]{:S(2)}) collective-permute-start(bf16[2,2,96,896]{3,2,1,0:T(8,128)(2,1)} %get-tuple-element.31), channel_id=1, source_target_pairs={{8,0},{16,8},{24,16},{9,1},{17,9},{25,17},{10,2},{18,10},{26,18},{... | collective-permute-start | bytes 2064392 | tf_op jit(solution)/shard_map/ppermute | solution.py:429
  6.3 21.7 %collective-permute-start.1 = (bf16[2,2,96,896]{3,2,1,0:T(8,128)(2,1)}, bf16[2,2,96,896]{3,2,1,0:T(8,128)(2,1)S(1)}, u32[]{:S(2)}, u32[]{:S(2)}) collective-permute-start(bf16[2,2,96,896]{3,2,1,0:T(8,128)(2,1)} %get-tuple-element.32), channel_id=1, source_target_pairs={{0,8},{8,16},{16,24},{1,9},{9,17},{17,25},{2,10},{10,18},{18,26},{... | collective-permute-start | bytes 2064392 | tf_op jit(solution)/shard_map/ppermute | solution.py:430
  13.5 19.7 %copy-start.7 = (s32[7]{0:T(128)}, s32[7]{0:T(128)S(1)}, u32[]{:S(2)}) copy-start(s32[7]{0:T(128)S(1)} %pad_add_fusion.where_ref) | copy-start | bytes 88
  14.3 20.9 %copy-start.3 = (bf16[1,2,96,3,896]{4,2,3,1,0:T(8,128)(2,1)S(1)}, bf16[1,2,96,3,896]{4,2,3,1,0:T(8,128)(2,1)}, u32[]{:S(2)}) copy-start(bf16[1,2,96,3,896]{4,2,3,1,0:T(8,128)(2,1)} %param.6) | copy-start | bytes 3096580
  14.3 31.7 %collective-permute-start.3 = (bf16[448,896]{1,0:T(8,128)(2,1)S(1)}, bf16[448,896]{1,0:T(8,128)(2,1)}, u32[]{:S(2)}, u32[]{:S(2)}) collective-permute-start(bf16[448,896]{1,0:T(8,128)(2,1)S(1)} %prepare_weight.1.refs_8_), channel_id=1, source_target_pairs={{8,0},{16,8},{24,16},{9,1},{17,9},{25,17},{10,2},{18,10},{26,18},{... | collective-permute-start | bytes 2408456 | tf_op jit(solution)/shard_map/ppermute | solution.py:447
  15.8 30.2 %collective-permute-start.4 = (bf16[448,896]{1,0:T(8,128)(2,1)S(1)}, bf16[448,896]{1,0:T(8,128)(2,1)}, u32[]{:S(2)}, u32[]{:S(2)}) collective-permute-start(bf16[448,896]{1,0:T(8,128)(2,1)S(1)} %prepare_weight.1.refs_8_), channel_id=1, source_target_pairs={{0,8},{8,16},{16,24},{1,9},{9,17},{17,25},{2,10},{10,18},{18,26},{... | collective-permute-start | bytes 2408456 | tf_op jit(solution)/shard_map/ppermute | solution.py:447
  22.0 28.6 %collective-permute-start.9 = (bf16[128,896]{1,0:T(8,128)(2,1)}, bf16[128,896]{1,0:T(8,128)(2,1)}, u32[]{:S(2)}, u32[]{:S(2)}) collective-permute-start(bf16[128,896]{1,0:T(8,128)(2,1)} %slice.31), channel_id=1, source_target_pairs={{0,24},{24,0},{1,25},{25,1},{2,26},{26,2},{3,27},{27,3},{4,28},{28... | collective-permute-start | bytes 688136 | tf_op jit(solution)/shard_map/ppermute | solution.py:449
  28.0 5.2 %copy-start.4 = (bf16[2,2,96,896]{3,2,1,0:T(8,128)(2,1)}, bf16[2,2,96,896]{3,2,1,0:T(8,128)(2,1)S(1)}, u32[]{:S(2)}) copy-start(bf16[2,2,96,896]{3,2,1,0:T(8,128)(2,1)S(1)} %collective-permute-done.1.left_ref) | copy-start | bytes 2064388
  33.2 11.6 %collective-permute-start.2 = (bf16[1,192,896]{2,1,0:T(8,128)(2,1)}, bf16[1,192,896]{2,1,0:T(8,128)(2,1)}, u32[]{:S(2)}, u32[]{:S(2)}) collective-permute-start(bf16[1,192,896]{2,1,0:T(8,128)(2,1)} %bitcast.8), channel_id=1, source_target_pairs={{0,1},{1,0},{2,3},{3,2},{4,5},{5,4},{6,7},{7,6},{8,9},{9,8},{10,11... | collective-permute-start | bytes 1032200 | tf_op jit(solution)/shard_map/ppermute | solution.py:370
  35.6 9.2 %copy-start.10 = (f32[896]{0:T(1024)S(1)}, f32[896]{0:T(1024)}, u32[]{:S(2)}) copy-start(f32[896]{0:T(1024)} %param.8) | copy-start | bytes 10756
  43.2 7.3 %collective-permute-start.8 = (bf16[1,192,896]{2,1,0:T(8,128)(2,1)S(1)}, bf16[1,192,896]{2,1,0:T(8,128)(2,1)S(1)}, u32[]{:S(2)}, u32[]{:S(2)}) collective-permute-start(bf16[1,192,896]{2,1,0:T(8,128)(2,1)S(1)} %bitcast.22), channel_id=1, source_target_pairs={{0,4},{2,6},{4,0},{6,2},{1,5},{3,7},{5,1},{7,3},{8,12},{10,14},{12... | collective-permute-start | bytes 1032200 | tf_op jit(solution)/shard_map/ppermute | solution.py:370
  46.0 21.5 %collective-permute-start.12 = (bf16[448,896]{1,0:T(8,128)(2,1)}, bf16[448,896]{1,0:T(8,128)(2,1)S(1)}, u32[]{:S(2)}, u32[]{:S(2)}) collective-permute-start(bf16[448,896]{1,0:T(8,128)(2,1)} %collective-permute-done.3.refs_9_), channel_id=1, source_target_pairs={{8,0},{16,8},{9,1},{17,9},{10,2},{18,10},{11,3},{19,11},{12,4},{20... | collective-permute-start | bytes 2408456 | tf_op jit(solution)/shard_map/ppermute | solution.py:460
  47.3 20.2 %collective-permute-start.13 = (bf16[448,896]{1,0:T(8,128)(2,1)}, bf16[448,896]{1,0:T(8,128)(2,1)S(1)}, u32[]{:S(2)}, u32[]{:S(2)}) collective-permute-start(bf16[448,896]{1,0:T(8,128)(2,1)} %collective-permute-done.4.refs_10_), channel_id=1, source_target_pairs={{8,16},{16,24},{9,17},{17,25},{10,18},{18,26},{11,19},{19,27},{12,... | collective-permute-start | bytes 2408456 | tf_op jit(solution)/shard_map/ppermute | solution.py:461
  50.6 15.7 %collective-permute-start.10 = (bf16[2,192,896]{2,1,0:T(8,128)(2,1)S(1)}, bf16[2,192,896]{2,1,0:T(8,128)(2,1)S(1)}, u32[]{:S(2)}, u32[]{:S(2)}) collective-permute-start(bf16[2,192,896]{2,1,0:T(8,128)(2,1)S(1)} %pad_maximum_fusion.1.refs_4_), channel_id=1, source_target_pairs={{0,1},{1,0},{2,3},{3,2},{4,5},{5,4},{6,7},{7,6},{8,9},{9,8},{10,11... | collective-permute-start | bytes 2064392 | tf_op jit(solution)/shard_map/ppermute | solution.py:370
  51.6 15.9 %collective-permute-start.5 = (bf16[2,192,896]{2,1,0:T(8,128)(2,1)S(1)}, bf16[2,192,896]{2,1,0:T(8,128)(2,1)S(1)}, u32[]{:S(2)}, u32[]{:S(2)}) collective-permute-start(bf16[2,192,896]{2,1,0:T(8,128)(2,1)S(1)} %pad_maximum_fusion.refs_0_), channel_id=1, source_target_pairs={{0,4},{2,6},{4,0},{6,2},{1,5},{3,7},{5,1},{7,3},{8,12},{10,14},{12... | collective-permute-start | bytes 2064392 | tf_op jit(solution)/shard_map/ppermute | solution.py:370
  53.1 20.1 %collective-permute-start.11 = (bf16[2,192,896]{2,1,0:T(8,128)(2,1)S(1)}, bf16[2,192,896]{2,1,0:T(8,128)(2,1)S(1)}, u32[]{:S(2)}, u32[]{:S(2)}) collective-permute-start(bf16[2,192,896]{2,1,0:T(8,128)(2,1)S(1)} %pad_maximum_fusion.1.refs_4_), channel_id=1, source_target_pairs={{0,2},{2,0},{4,6},{6,4},{1,3},{3,1},{5,7},{7,5},{8,10},{10,8},{12,... | collective-permute-start | bytes 2064392 | tf_op jit(solution)/shard_map/ppermute | solution.py:370
  66.3 6.9 %collective-permute-start.6 = (bf16[2,192,896]{2,1,0:T(8,128)(2,1)S(1)}, bf16[2,192,896]{2,1,0:T(8,128)(2,1)S(1)}, u32[]{:S(2)}, u32[]{:S(2)}) collective-permute-start(bf16[2,192,896]{2,1,0:T(8,128)(2,1)S(1)} %pad_maximum_fusion.refs_0_), channel_id=1, source_target_pairs={{0,2},{2,0},{4,6},{6,4},{1,3},{3,1},{5,7},{7,5},{8,10},{10,8},{12,... | collective-permute-start | bytes 2064392 | tf_op jit(solution)/shard_map/ppermute | solution.py:370
  67.5 5.7 %collective-permute-start.7 = (bf16[2,192,896]{2,1,0:T(8,128)(2,1)S(1)}, bf16[2,192,896]{2,1,0:T(8,128)(2,1)S(1)}, u32[]{:S(2)}, u32[]{:S(2)}) collective-permute-start(bf16[2,192,896]{2,1,0:T(8,128)(2,1)S(1)} %collective-permute-done.5.refs_1_), channel_id=1, source_target_pairs={{0,2},{2,0},{4,6},{6,4},{1,3},{3,1},{5,7},{7,5},{8,10},{10,8},{12,... | collective-permute-start | bytes 2064392 | tf_op jit(solution)/shard_map/ppermute | solution.py:370
  67.5 5.7 %collective-permute-start.14 = (bf16[2,192,896]{2,1,0:T(8,128)(2,1)S(1)}, bf16[2,192,896]{2,1,0:T(8,128)(2,1)S(1)}, u32[]{:S(2)}, u32[]{:S(2)}) collective-permute-start(bf16[2,192,896]{2,1,0:T(8,128)(2,1)S(1)} %collective-permute-done.10.refs_5_), channel_id=1, source_target_pairs={{0,2},{2,0},{4,6},{6,4},{1,3},{3,1},{5,7},{7,5},{8,10},{10,8},{12,... | collective-permute-start | bytes 2064392 | tf_op jit(solution)/shard_map/ppermute | solution.py:370
  68.1 18.6 %collective-permute-start.15 = (bf16[320,896]{1,0:T(8,128)(2,1)S(1)}, bf16[320,896]{1,0:T(8,128)(2,1)S(1)}, u32[]{:S(2)}, u32[]{:S(2)}) collective-permute-start(bf16[320,896]{1,0:T(8,128)(2,1)S(1)} %slice.32), channel_id=1, source_target_pairs={{0,24},{24,0},{1,25},{25,1},{2,26},{26,2},{3,27},{27,3},{4,28},{28... | collective-permute-start | bytes 1720328 | tf_op jit(solution)/shard_map/ppermute | solution.py:449
  98.6 7.0 %collective-permute-start.16 = (bf16[2,96,448]{2,1,0:T(8,128)(2,1)S(1)}, bf16[2,96,448]{2,1,0:T(8,128)(2,1)S(1)}, u32[]{:S(2)}, u32[]{:S(2)}) collective-permute-start(bf16[2,96,448]{2,1,0:T(8,128)(2,1)S(1)} %bitcast.26), channel_id=1, source_target_pairs={{0,1},{1,0},{2,3},{3,2},{4,5},{5,4},{6,7},{7,6},{8,9},{9,8},{10,11... | collective-permute-start | bytes 516104 | tf_op jit(solution)/shard_map/ppermute | solution.py:370
  99.3 12.3 %all-to-all-start.1 = ((f32[32,1,512]{2,1,0:T(1,128)}), f32[32,1,512]{2,1,0:T(1,128)S(1)}, u32[]{:S(2)}, u32[]{:S(2)}) async-start(f32[32,1,512]{2,1,0:T(1,128)} %get-tuple-element.46), calls=%async_computation.1 | async-start | bytes 131072 | tf_op jit(solution)/shard_map/all_to_all | solution.py:393
  (6 other events, 6.3 us)

commit v4 on v3

--- a/solution.py
+++ b/solution.py
@@ -24,43 +24,53 @@
     _, _, tile_len, width = clean.shape
 
     def kernel(clean_ref, noise_ref, *refs):
-        out_refs, (keep, add, sems) = refs[: len(slots)], refs[len(slots) :]
-        copies = []
-        for n, slot in enumerate(slots):
+        out_refs, (keep, add, in_sems, out_sems) = refs[: len(slots)], refs[len(slots) :]
+        pieces = [(n, slot, part) for n, slot in enumerate(slots) for part in range(2)]
+        loads, stores = [], []
+        for n, slot, part in pieces:
             for m, (source, target) in enumerate(((clean_ref, keep), (noise_ref, add))):
-                copies.append(
+                loads.append(
                     pltpu.make_async_copy(
-                        source.at[slot, pl.ds(1, 2)], target.at[n], sems.at[n, m]
+                        source.at[slot, 1 + part], target.at[n, part], in_sems.at[n, part, m]
                     )
                 )
-                copies[-1].start()
-        for n in range(len(slots)):
-            copies[2 * n].wait()
-            copies[2 * n + 1].wait()
-            out_refs[n][0] = keep[n]
-            out_refs[n][1] = perturb(keep[n], add[n])
-
-    block = (2, 2, tile_len, width)
+                loads[-1].start()
+        for at, (n, slot, part) in enumerate(pieces):
+            loads[2 * at].wait()
+            loads[2 * at + 1].wait()
+            add[n, part] = perturb(keep[n, part], add[n, part])
+            for m, source in enumerate((keep, add)):
+                stores.append(
+                    pltpu.make_async_copy(
+                        source.at[n, part], out_refs[n].at[m, part], out_sems.at[n, part, m]
+                    )
+                )
+                stores[-1].start()
+        for store in stores:
+            store.wait()
+
+    scratch = pltpu.VMEM((len(slots), 2, tile_len, width), jnp.bfloat16)
     return pl.pallas_call(
         kernel,
         in_specs=[pl.BlockSpec(memory_space=pl.ANY)] * 2,
-        out_specs=[pl.BlockSpec(memory_space=pltpu.VMEM)] * len(slots),
-        out_shape=[jax.ShapeDtypeStruct(block, jnp.bfloat16)] * len(slots),
+        out_specs=[pl.BlockSpec(memory_space=pl.ANY)] * len(slots),
+        out_shape=[jax.ShapeDtypeStruct((2, 2, tile_len, width), jnp.bfloat16)] * len(slots),
         scratch_shapes=[
-            pltpu.VMEM((len(slots), 2, tile_len, width), jnp.bfloat16),
-            pltpu.VMEM((len(slots), 2, tile_len, width), jnp.bfloat16),
-            pltpu.SemaphoreType.DMA((len(slots), 2)),
-        ],
-        compiler_params=pltpu.CompilerParams(vmem_limit_bytes=16 * 1024 * 1024),
+            scratch,
+            scratch,
+            pltpu.SemaphoreType.DMA((len(slots), 2, 2)),
+            pltpu.SemaphoreType.DMA((len(slots), 2, 2)),
+        ],
+        compiler_params=pltpu.CompilerParams(vmem_limit_bytes=60 * 1024 * 1024),
         name="prepare_halo",
     )(clean, noise)
 
 
-def prepare_weight(where, weight, clip_count):
+def prepare_weight(where, weight, clip_count, cut):
     depth, width = weight.shape
     half = width // clip_count
 
-    def kernel(where_ref, weight_ref, out_ref):
+    def kernel(where_ref, weight_ref, whole_ref, early_ref, late_ref):
         for clip in range(clip_count):
 
             @pl.when(where_ref[2] == clip)
@@ -69,7 +79,10 @@
                 for first in range(begin // LANES * LANES, end, LANES):
                     low, high = max(first, begin), min(first + LANES, end)
                     turned = weight_ref[:, pl.ds(first, LANES)].T
-                    out_ref[pl.ds(low - begin, high - low)] = turned[low - first : high - first]
+                    whole_ref[pl.ds(low - begin, high - low)] = turned[low - first : high - first]
+
+        early_ref[...] = whole_ref[:cut]
+        late_ref[...] = whole_ref[cut:]
 
     return pl.pallas_call(
         kernel,
@@ -77,9 +90,11 @@
             pl.BlockSpec(memory_space=pltpu.SMEM),
             pl.BlockSpec(memory_space=pltpu.VMEM),
         ],
-        out_specs=pl.BlockSpec(memory_space=pltpu.VMEM),
-        out_shape=jax.ShapeDtypeStruct((half, depth), weight.dtype),
-        compiler_params=pltpu.CompilerParams(vmem_limit_bytes=16 * 1024 * 1024),
+        out_specs=[pl.BlockSpec(memory_space=pltpu.VMEM)] * 3,
+        out_shape=[
+            jax.ShapeDtypeStruct((rows, depth), weight.dtype) for rows in (half, cut, half - cut)
+        ],
+        compiler_params=pltpu.CompilerParams(vmem_limit_bytes=60 * 1024 * 1024),
         name="prepare_weight",
     )(where, weight)
 
@@ -278,55 +293,59 @@
     )(where, *operands)
 
 
+def row_scales(squares_ref, clip, row_count, model_width):
+    diagonal = on_diagonal()
+    scales = []
+    for first in range(0, row_count, LANES):
+        at = pl.ds(pl.multiple_of(clip * row_count + first, LANES), LANES)
+        mean = jnp.sum(squares_ref[:, :, at], axis=0) / model_width
+        scale = jnp.broadcast_to(lax.rsqrt(mean + epsilon), (LANES, LANES))
+        scales.append(jnp.sum(jnp.where(diagonal, scale, 0.0), axis=1, keepdims=True))
+    return jnp.concatenate(scales, axis=0)
+
+
 def finish(total, squares, gain, columns, model_width, devices):
     clip_count, row_count, lanes = total.shape
     near_rows = row_count // 2
 
-    def kernel(total_ref, squares_ref, gain_ref, features_ref, row_ref):
-        clip = pl.program_id(0)
-        diagonal = on_diagonal()
-        scales = []
-        for first in range(0, row_count, LANES):
-            at = pl.ds(pl.multiple_of(clip * row_count + first, LANES), LANES)
-            mean = jnp.sum(squares_ref[:, :, at], axis=0) / model_width
-            scale = jnp.broadcast_to(lax.rsqrt(mean + epsilon), (LANES, LANES))
-            scales.append(jnp.sum(jnp.where(diagonal, scale, 0.0), axis=1, keepdims=True))
-        scale = jnp.concatenate(scales, axis=0)
-        clean = total_ref[0, :near_rows] * scale[:near_rows]
-        features_ref[0] = (clean * gain_ref[...]).astype(jnp.bfloat16)
-        difference = total_ref[0, near_rows:] * scale[near_rows:] - clean
-        sums = jnp.sum(difference * difference, axis=0, keepdims=True)
-        penalty = jnp.sum(sums * gain_ref[...] * gain_ref[...], axis=1, keepdims=True)
+    def kernel(total_ref, squares_ref, gain_ref, row_ref):
         lane = lax.broadcasted_iota(jnp.int32, (1, lanes), 1)
-        sums = sums + jnp.where(lane == columns + clip, penalty, 0.0)
-        sums = jnp.broadcast_to(sums[None], row_ref.shape)
-
-        @pl.when(clip == 0)
-        def _():
-            row_ref[...] = sums
-
-        @pl.when(clip > 0)
-        def _():
-            row_ref[...] += sums
+        row = jnp.zeros((1, lanes), jnp.float32)
+        for clip in range(clip_count):
+            scale = row_scales(squares_ref, clip, row_count, model_width)
+            clean = total_ref[clip, :near_rows] * scale[:near_rows]
+            difference = total_ref[clip, near_rows:] * scale[near_rows:] - clean
+            sums = jnp.sum(difference * difference, axis=0, keepdims=True)
+            penalty = jnp.sum(sums * gain_ref[...] * gain_ref[...], axis=1, keepdims=True)
+            row = row + sums + jnp.where(lane == columns + clip, penalty, 0.0)
+        row_ref[...] = jnp.broadcast_to(row[None], row_ref.shape)
 
     return pl.pallas_call(
         kernel,
-        grid=(clip_count,),
-        in_specs=[
-            pl.BlockSpec((1, row_count, lanes), lambda c: (c, 0, 0)),
-            pl.BlockSpec(squares.shape, lambda c: (0, 0, 0)),
-            pl.BlockSpec((1, lanes), lambda c: (0, 0)),
-        ],
-        out_specs=[
-            pl.BlockSpec((1, near_rows, lanes), lambda c: (c, 0, 0)),
-            pl.BlockSpec((devices, 1, lanes), lambda c: (0, 0, 0)),
-        ],
-        out_shape=[
-            jax.ShapeDtypeStruct((clip_count, near_rows, lanes), jnp.bfloat16),
-            jax.ShapeDtypeStruct((devices, 1, lanes), jnp.float32),
-        ],
+        out_shape=jax.ShapeDtypeStruct((devices, 1, lanes), jnp.float32),
         compiler_params=pltpu.CompilerParams(vmem_limit_bytes=16 * 1024 * 1024),
         name="finish",
+    )(total, squares, gain)
+
+
+def make_features(total, squares, gain, model_width):
+    clip_count, row_count, lanes = total.shape
+    near_rows = row_count // 2
+
+    def kernel(total_ref, squares_ref, gain_ref, features_ref):
+        for clip in range(clip_count):
+            scale = row_scales(squares_ref, clip, row_count, model_width)
+            clean = total_ref[clip, :near_rows] * scale[:near_rows]
+            features_ref[clip] = (clean * gain_ref[...]).astype(jnp.bfloat16)
+
+    return pl.pallas_call(
+        kernel,
+        out_shape=jax.ShapeDtypeStruct((clip_count, near_rows, lanes), jnp.bfloat16),
+        compiler_params=pltpu.CompilerParams(vmem_limit_bytes=16 * 1024 * 1024),
+        cost_estimate=pl.CostEstimate(
+            flops=10**10, bytes_accessed=0, transcendentals=0
+        ),
+        name="make_features",
     )(total, squares, gain)
 
 
@@ -361,6 +380,7 @@
             jax.ShapeDtypeStruct((1,), jnp.float32),
             jax.ShapeDtypeStruct((gain.shape[1],), jnp.float32),
         ],
+        compiler_params=pltpu.CompilerParams(vmem_limit_bytes=60 * 1024 * 1024),
         name="conclude",
     )(where, rows, gain)
 
@@ -437,17 +457,16 @@
     gain_row = jnp.pad(own_columns(norm_gain), (0, whole_lanes(half) - half))[None]
     gain_all = norm_gain[None]
 
-    own_weight = prepare_weight(where, out_weight, clip_count)
+    cut = min(LANES, half // 2)
+    own_weight, *parts = prepare_weight(where, out_weight, clip_count, cut)
     line = slab_count == model_count and slab_count == 4
     last = slab_count - 1
-    cut = min(LANES, half)
     near, passed, across = [], [], []
 
     if line:
         near = [lax.ppermute(own_weight, "frames", pairs) for pairs in (down, up)]
         across = [
-            lax.ppermute(block, "frames", [(0, last), (last, 0)])
-            for block in (own_weight[:cut], own_weight[cut:])
+            lax.ppermute(block, "frames", [(0, last), (last, 0)]) for block in parts
         ]
 
     def before_step(stream, step, part, value):
@@ -506,9 +525,10 @@
         total, squares = project(where, gathered, shards, None, half, peers)
 
     squares = collect(squares, ("mp", "dp"))
-    features, sums = finish(
+    sums = finish(
         total, squares, gain_row, half, model_width, slab_count * model_count * clip_count
     )
+    features = make_features(total, squares, gain_row, model_width)
     sums = collect(sums, ("frames", "mp", "dp"))
 
     features = features[..., :half].reshape(clip_count, slots, tile_len, half)

time: 115 us -> 112 us (0.974)
  local copies, waits for them, and re-layouts: 8.44 us -> 1.33 us
  Pallas kernels: 24.7 us -> 27.5 us
    unnamed x24 -> x16, local copies, waits for them, and re-layouts: 6.27 us -> 0.67 us
    ppermute x9, waiting for transfers between devices: 18.4 us -> 15.6 us  [swap(): return lax.ppermute(array, axis, [(i, i ^ distance) for i in range(count)])]
    pallas_call x1, Pallas kernels: 0.82 us -> 2.88 us  [prepare_weight(): pl.pallas_call(kernel, in_specs=[pl.BlockSpec(memory_space=pltpu.SMEM), p...]
    ppermute x2, waiting for transfers between devices: 6.73 us -> 8.7 us  [local(): lax.ppermute(block, 'frames', [(0, last), (last, 0)])]
    ppermute x2, waiting for transfers between devices: 0.01 us -> 1.72 us  [local(): near = [lax.ppermute(own_weight, 'frames', pairs) for pairs in (down, up)]]
    ppermute x2, starting transfers between devices: 8.76 us -> 10.1 us  [local(): lax.ppermute(block, 'frames', [(0, last), (last, 0)])]
    all_to_all x1, waiting for transfers between devices: 5.19 us -> 6.37 us  [collect(): return lax.all_to_all(rows, axes, split_axis=0, concat_axis=0, tiled=True)]
  transfers between devices with their start and end apart: 18 -> 18, of which waited for: 8 -> 9; matrix products, arithmetic and copies ran while one was open for 4% -> 3% of each run, Pallas kernels for 15% -> 18%
where the time goes in v4:
time: 112 us
  starting transfers between devices  37.7 us (34%)
  waiting for transfers between devices  33.5 us (30%)
  Pallas kernels  27.5 us (25%)
  blocking collectives  7.87 us (7%)
  other arithmetic  3.21 us (3%)
  local copies, waits for them, and re-layouts  1.33 us (1%)
    ppermute x9, waiting for transfers between devices, swap(): return lax.ppermute(array, axis, [(i, i ^ distance) for i in range(count)])  15.6 us
    ppermute x2, starting transfers between devices, local(): lax.ppermute(block, 'frames', [(0, last), (last, 0)])  10.1 us
    pallas_call x2, Pallas kernels, attention(): pl.pallas_call(attend_kernel, grid_spec=pltpu.PrefetchScalarGridSpec(num_...  9.75 us
    pallas_call x2, Pallas kernels, project(): pl.pallas_call(kernel, in_specs=[pl.BlockSpec(memory_space=pltpu.SMEM)] +...  9.37 us
    ppermute x2, waiting for transfers between devices, local(): lax.ppermute(block, 'frames', [(0, last), (last, 0)])  8.7 us
    all_to_all x1, blocking collectives, collect(): return lax.all_to_all(rows, axes, split_axis=0, concat_axis=0, tiled=True)  7.87 us
    ppermute x9, starting transfers between devices, swap(): return lax.ppermute(array, axis, [(i, i ^ distance) for i in range(count)])  7.8 us
    all_to_all x1, waiting for transfers between devices, collect(): return lax.all_to_all(rows, axes, split_axis=0, concat_axis=0, tiled=True)  6.37 us
  transfers between devices with their start and end apart: 18, of which 9 were waited for; matrix products, arithmetic and copies ran while one was open for 3% of the time, Pallas kernels for 18%

profile of v4, /device:TPU:0, one launch (start us, length us, event | category | flops | bytes accessed | tf_op | source)
XLA Modules:
  0.0 112.0 jit_solution(14145014675533977290)
XLA Ops:
  0.6 2.4 %prepare_halo.1 = (bf16[2,2,96,896]{3,2,1,0:T(8,128)(2,1)}, bf16[2,2,96,896]{3,2,1,0:T(8,128)(2,1)}) custom-call(bf16[2,3,96,896]{3,2,1,0:T(8,128)(2,1)} %bitcast.17, bf16[2,3,96,896]{3,2,1,0:T(8,128)(2,1)} %bitcast.24), custom_call_target="tpu_custom_call" | custom-call | tf_op jit(solution)/shard_map/prepare_halo/pallas_call | solution.py:53
  3.0 1.3 %collective-permute-start = (bf16[2,2,96,896]{3,2,1,0:T(8,128)(2,1)}, bf16[2,2,96,896]{3,2,1,0:T(8,128)(2,1)S(1)}, u32[]{:S(2)}, u32[]{:S(2)}) collective-permute-start(bf16[2,2,96,896]{3,2,1,0:T(8,128)(2,1)} %get-tuple-element.32), channel_id=1, source_target_pairs={{8,0},{16,8},{24,16},{9,1},{17,9},{25,17},{10,2},{18,10},{26,18},{... | collective-permute-start | bytes 2064392 | tf_op jit(solution)/shard_map/ppermute | solution.py:449
  4.3 5.6 %collective-permute-start.1 = (bf16[2,2,96,896]{3,2,1,0:T(8,128)(2,1)}, bf16[2,2,96,896]{3,2,1,0:T(8,128)(2,1)S(1)}, u32[]{:S(2)}, u32[]{:S(2)}) collective-permute-start(bf16[2,2,96,896]{3,2,1,0:T(8,128)(2,1)} %get-tuple-element.33), channel_id=1, source_target_pairs={{0,8},{8,16},{16,24},{1,9},{9,17},{17,25},{2,10},{10,18},{18,26},{... | collective-permute-start | bytes 2064392 | tf_op jit(solution)/shard_map/ppermute | solution.py:450
  10.7 2.9 %prepare_weight.1 = (bf16[448,896]{1,0:T(8,128)(2,1)}, bf16[128,896]{1,0:T(8,128)(2,1)}, bf16[320,896]{1,0:T(8,128)(2,1)}) custom-call(s32[7]{0:T(128)} %pad_add_fusion.where_ref, bf16[896,896]{1,0:T(8,128)(2,1)} %weight_ref), custom_call_target="tpu_custom_call" | custom-call | tf_op jit(solution)/shard_map/prepare_weight/pallas_call | solution.py:87
  13.6 4.9 %collective-permute-start.4 = (bf16[448,896]{1,0:T(8,128)(2,1)}, bf16[448,896]{1,0:T(8,128)(2,1)}, u32[]{:S(2)}, u32[]{:S(2)}) collective-permute-start(bf16[448,896]{1,0:T(8,128)(2,1)} %get-tuple-element.35.refs_8_), channel_id=1, source_target_pairs={{0,8},{8,16},{16,24},{1,9},{9,17},{17,25},{2,10},{10,18},{18,26},{... | collective-permute-start | bytes 2408456 | tf_op jit(solution)/shard_map/ppermute | solution.py:467
  19.8 5.1 %collective-permute-start.9 = (bf16[128,896]{1,0:T(8,128)(2,1)}, bf16[128,896]{1,0:T(8,128)(2,1)}, u32[]{:S(2)}, u32[]{:S(2)}) collective-permute-start(bf16[128,896]{1,0:T(8,128)(2,1)} %get-tuple-element.38), channel_id=1, source_target_pairs={{0,24},{24,0},{1,25},{25,1},{2,26},{26,2},{3,27},{27,3},{4,28},{28... | collective-permute-start | bytes 688136 | tf_op jit(solution)/shard_map/ppermute | solution.py:469
  26.0 5.2 %attention.2 = bf16[2,96,896]{2,1,0:T(8,128)(2,1)} custom-call(s32[7]{0:T(128)S(1)} %copy-done.2, bf16[2,3,96,896]{3,2,1,0:T(8,128)(2,1)S(1)} %bitcast.18, bf16[2,2,96,896]{3,2,1,0:T(8,128)(2,1)S(1)} %collective-permute-done.right_ref, bf16[2,2,96,896]{3,2,1,0:T(8,128)(2,1)S(1)} %collective-permute-done.1.left_ref), custom_call_target="tpu_custom_call" | custom-call | tf_op jit(solution)/shard_map/attention/pallas_call | solution.py:144
  31.3 2.0 %collective-permute-start.2 = (bf16[1,192,896]{2,1,0:T(8,128)(2,1)}, bf16[1,192,896]{2,1,0:T(8,128)(2,1)}, u32[]{:S(2)}, u32[]{:S(2)}) collective-permute-start(bf16[1,192,896]{2,1,0:T(8,128)(2,1)} %bitcast.8), channel_id=1, source_target_pairs={{0,1},{1,0},{2,3},{3,2},{4,5},{5,4},{6,7},{7,6},{8,9},{9,8},{10,11... | collective-permute-start | bytes 1032200 | tf_op jit(solution)/shard_map/ppermute | solution.py:390
  34.2 4.5 %attention.3 = bf16[2,96,896]{2,1,0:T(8,128)(2,1)S(1)} custom-call(s32[7]{0:T(128)S(1)} %copy-done.2, bf16[2,3,96,896]{3,2,1,0:T(8,128)(2,1)S(1)} %add_convert_fusion.own_ref, bf16[2,2,96,896]{3,2,1,0:T(8,128)(2,1)S(1)} %collective-permute-done.right_ref, bf16[2,2,96,896]{3,2,1,0:T(8,128)(2,1)S(1)} %collective-permute-done.1.left_ref), custom_call_target="tpu_custom_call" | custom-call | tf_op jit(solution)/shard_map/attention/pallas_call | solution.py:144
  38.7 1.6 %collective-permute-start.8 = (bf16[1,192,896]{2,1,0:T(8,128)(2,1)S(1)}, bf16[1,192,896]{2,1,0:T(8,128)(2,1)S(1)}, u32[]{:S(2)}, u32[]{:S(2)}) collective-permute-start(bf16[1,192,896]{2,1,0:T(8,128)(2,1)S(1)} %bitcast.20), channel_id=1, source_target_pairs={{0,4},{2,6},{4,0},{6,2},{1,5},{3,7},{5,1},{7,3},{8,12},{10,14},{12... | collective-permute-start | bytes 1032200 | tf_op jit(solution)/shard_map/ppermute | solution.py:390
  41.5 1.7 %collective-permute-done.4.refs_10_ = bf16[448,896]{1,0:T(8,128)(2,1)} collective-permute-done((bf16[448,896]{1,0:T(8,128)(2,1)}, bf16[448,896]{1,0:T(8,128)(2,1)}, u32[]{:S(2)}, u32[]{:S(2)}) %collective-permute-start.4) | collective-permute-done | bytes 802848 | tf_op jit(solution)/shard_map/ppermute | solution.py:467
  43.2 1.3 %collective-permute-start.12 = (bf16[448,896]{1,0:T(8,128)(2,1)}, bf16[448,896]{1,0:T(8,128)(2,1)S(1)}, u32[]{:S(2)}, u32[]{:S(2)}) collective-permute-start(bf16[448,896]{1,0:T(8,128)(2,1)} %collective-permute-done.3.refs_9_), channel_id=1, source_target_pairs={{8,0},{16,8},{9,1},{17,9},{10,2},{18,10},{11,3},{19,11},{12,4},{20... | collective-permute-start | bytes 2408456 | tf_op jit(solution)/shard_map/ppermute | solution.py:479
  46.1 2.0 %collective-permute-done.9.refs_13_ = bf16[128,896]{1,0:T(8,128)(2,1)} collective-permute-done((bf16[128,896]{1,0:T(8,128)(2,1)}, bf16[128,896]{1,0:T(8,128)(2,1)}, u32[]{:S(2)}, u32[]{:S(2)}) %collective-permute-start.9) | collective-permute-done | bytes 229408 | tf_op jit(solution)/shard_map/ppermute | solution.py:469
  48.1 1.5 %collective-permute-start.10 = (bf16[2,192,896]{2,1,0:T(8,128)(2,1)S(1)}, bf16[2,192,896]{2,1,0:T(8,128)(2,1)S(1)}, u32[]{:S(2)}, u32[]{:S(2)}) collective-permute-start(bf16[2,192,896]{2,1,0:T(8,128)(2,1)S(1)} %pad_maximum_fusion.1.refs_4_), channel_id=1, source_target_pairs={{0,1},{1,0},{2,3},{3,2},{4,5},{5,4},{6,7},{7,6},{8,9},{9,8},{10,11... | collective-permute-start | bytes 2064392 | tf_op jit(solution)/shard_map/ppermute | solution.py:390
  49.6 1.5 %collective-permute-start.5 = (bf16[2,192,896]{2,1,0:T(8,128)(2,1)S(1)}, bf16[2,192,896]{2,1,0:T(8,128)(2,1)S(1)}, u32[]{:S(2)}, u32[]{:S(2)}) collective-permute-start(bf16[2,192,896]{2,1,0:T(8,128)(2,1)S(1)} %pad_maximum_fusion.refs_0_), channel_id=1, source_target_pairs={{0,4},{2,6},{4,0},{6,2},{1,5},{3,7},{5,1},{7,3},{8,12},{10,14},{12... | collective-permute-start | bytes 2064392 | tf_op jit(solution)/shard_map/ppermute | solution.py:390
  51.1 13.2 %collective-permute-done.10.refs_5_ = bf16[2,192,896]{2,1,0:T(8,128)(2,1)S(1)} collective-permute-done((bf16[2,192,896]{2,1,0:T(8,128)(2,1)S(1)}, bf16[2,192,896]{2,1,0:T(8,128)(2,1)S(1)}, u32[]{:S(2)}, u32[]{:S(2)}) %collective-permute-start.10) | collective-permute-done | bytes 688160 | tf_op jit(solution)/shard_map/ppermute | solution.py:390
  66.1 5.1 %collective-permute-start.15 = (bf16[320,896]{1,0:T(8,128)(2,1)S(1)}, bf16[320,896]{1,0:T(8,128)(2,1)S(1)}, u32[]{:S(2)}, u32[]{:S(2)}) collective-permute-start(bf16[320,896]{1,0:T(8,128)(2,1)S(1)} %copy-done.6), channel_id=1, source_target_pairs={{0,24},{24,0},{1,25},{25,1},{2,26},{26,2},{3,27},{27,3},{4,28},{28... | collective-permute-start | bytes 1720328 | tf_op jit(solution)/shard_map/ppermute | solution.py:469
  71.2 6.8 %project.2.refs_9_ = f32[2,384,512]{2,1,0:T(8,128)S(1)} custom-call(s32[7]{0:T(128)S(1)} %copy-done.2, bf16[2,192,896]{2,1,0:T(8,128)(2,1)S(1)} %pad_maximum_fusion.refs_0_, bf16[2,192,896]{2,1,0:T(8,128)(2,1)S(1)} %collective-permute-done.5.refs_1_, bf16[2,192,896]{2,1,0:T(8,128)(2,1)S(1)} %collective-permute-done.6.refs_2_, ...), custom_call_target="tpu_custom_call" | custom-call | tf_op jit(solution)/shard_map/project/pallas_call | solution.py:274
  78.0 6.7 %collective-permute-done.15.refs_8_ = bf16[320,896]{1,0:T(8,128)(2,1)S(1)} collective-permute-done((bf16[320,896]{1,0:T(8,128)(2,1)S(1)}, bf16[320,896]{1,0:T(8,128)(2,1)S(1)}, u32[]{:S(2)}, u32[]{:S(2)}) %collective-permute-start.15) | collective-permute-done | bytes 573472 | tf_op jit(solution)/shard_map/ppermute | solution.py:469
  84.7 2.6 %project.3 = (f32[2,384,512]{2,1,0:T(8,128)S(1)}, f32[8,1,768]{2,1,0:T(1,128)S(1)}) custom-call(s32[7]{0:T(128)S(1)} %copy-done.2, bf16[2,192,896]{2,1,0:T(8,128)(2,1)S(1)} %pad_maximum_fusion.refs_0_, bf16[2,192,896]{2,1,0:T(8,128)(2,1)S(1)} %collective-permute-done.5.refs_1_, ...), custom_call_target="tpu_custom_call", output_to_operand_aliasing={{0}: (10, {})} | custom-call | tf_op jit(solution)/shard_map/project/pallas_call | solution.py:274
  87.3 7.9 %all_to_all.10.squares_ref = f32[8,1,768]{2,1,0:T(1,128)S(1)} all-to-all(f32[8,1,768]{2,1,0:T(1,128)S(1)} %get-tuple-element.48), channel_id=1, replica_groups=mesh['frames'=4,'mp'=4,'dp'=2] {'mp','dp'}, dimensions={0} | all-to-all | bytes 49152 | tf_op jit(solution)/shard_map/all_to_all | solution.py:413
  97.3 4.7 %all-to-all-start.1 = ((f32[32,1,512]{2,1,0:T(1,128)}), f32[32,1,512]{2,1,0:T(1,128)S(1)}, u32[]{:S(2)}, u32[]{:S(2)}) async-start(f32[32,1,512]{2,1,0:T(1,128)} %finish.1), calls=%async_computation.1 | async-start | bytes 131072 | tf_op jit(solution)/shard_map/all_to_all | solution.py:413
  103.3 6.4 %all-to-all-done.1.rows_ref = f32[32,1,512]{2,1,0:T(1,128)S(1)} async-done(((f32[32,1,512]{2,1,0:T(1,128)}), f32[32,1,512]{2,1,0:T(1,128)S(1)}, u32[]{:S(2)}, u32[]{:S(2)}) %all-to-all-start.1) | async-done | bytes 65568 | tf_op jit(solution)/shard_map/all_to_all | solution.py:413
  110.3 1.7 %conclude.1 = (f32[1]{0:T(128)}, f32[896]{0:T(1024)}) custom-call(s32[7]{0:T(128)} %pad_add_fusion.where_ref, f32[32,1,512]{2,1,0:T(1,128)} %copy-done.4, f32[1,896]{1,0:T(1,128)} %broadcast_in_dim.10.gain_ref), custom_call_target="tpu_custom_call" | custom-call | tf_op jit(solution)/shard_map/conclude/pallas_call | solution.py:371
  (49 shorter events, 12.7 us)
Async XLA Ops:
  0.6 9.3 %copy-start.7 = (s32[1,8]{1,0:T(1,128)S(1)}, s32[1,8]{1,0:T(1,128)}, u32[]{:S(2)}) copy-start(s32[1,8]{1,0:T(1,128)} %param.9) | copy-start | bytes 100
  0.6 25.4 %copy-start = (bf16[1,2,96,3,896]{4,2,3,1,0:T(8,128)(2,1)S(1)}, bf16[1,2,96,3,896]{4,2,3,1,0:T(8,128)(2,1)}, u32[]{:S(2)}) copy-start(bf16[1,2,96,3,896]{4,2,3,1,0:T(8,128)(2,1)} %param.5) | copy-start | bytes 3096580
  3.0 21.9 %collective-permute-start = (bf16[2,2,96,896]{3,2,1,0:T(8,128)(2,1)}, bf16[2,2,96,896]{3,2,1,0:T(8,128)(2,1)S(1)}, u32[]{:S(2)}, u32[]{:S(2)}) collective-permute-start(bf16[2,2,96,896]{3,2,1,0:T(8,128)(2,1)} %get-tuple-element.32), channel_id=1, source_target_pairs={{8,0},{16,8},{24,16},{9,1},{17,9},{25,17},{10,2},{18,10},{26,18},{... | collective-permute-start | bytes 2064392 | tf_op jit(solution)/shard_map/ppermute | solution.py:449
  4.3 21.7 %collective-permute-start.1 = (bf16[2,2,96,896]{3,2,1,0:T(8,128)(2,1)}, bf16[2,2,96,896]{3,2,1,0:T(8,128)(2,1)S(1)}, u32[]{:S(2)}, u32[]{:S(2)}) collective-permute-start(bf16[2,2,96,896]{3,2,1,0:T(8,128)(2,1)} %get-tuple-element.33), channel_id=1, source_target_pairs={{0,8},{8,16},{16,24},{1,9},{9,17},{17,25},{2,10},{10,18},{18,26},{... | collective-permute-start | bytes 2064392 | tf_op jit(solution)/shard_map/ppermute | solution.py:450
  10.7 15.3 %copy-start.2 = (s32[7]{0:T(128)S(1)}, s32[7]{0:T(128)}, u32[]{:S(2)}) copy-start(s32[7]{0:T(128)} %pad_add_fusion.where_ref) | copy-start | bytes 88
  13.6 19.7 %copy-start.3 = (bf16[1,2,96,3,896]{4,2,3,1,0:T(8,128)(2,1)S(1)}, bf16[1,2,96,3,896]{4,2,3,1,0:T(8,128)(2,1)}, u32[]{:S(2)}) copy-start(bf16[1,2,96,3,896]{4,2,3,1,0:T(8,128)(2,1)} %param.6) | copy-start | bytes 3096580
  13.6 29.6 %collective-permute-start.4 = (bf16[448,896]{1,0:T(8,128)(2,1)}, bf16[448,896]{1,0:T(8,128)(2,1)}, u32[]{:S(2)}, u32[]{:S(2)}) collective-permute-start(bf16[448,896]{1,0:T(8,128)(2,1)} %get-tuple-element.35.refs_8_), channel_id=1, source_target_pairs={{0,8},{8,16},{16,24},{1,9},{9,17},{17,25},{2,10},{10,18},{18,26},{... | collective-permute-start | bytes 2408456 | tf_op jit(solution)/shard_map/ppermute | solution.py:467
  18.5 24.7 %collective-permute-start.3 = (bf16[448,896]{1,0:T(8,128)(2,1)}, bf16[448,896]{1,0:T(8,128)(2,1)}, u32[]{:S(2)}, u32[]{:S(2)}) collective-permute-start(bf16[448,896]{1,0:T(8,128)(2,1)} %get-tuple-element.35.refs_8_), channel_id=1, source_target_pairs={{8,0},{16,8},{24,16},{9,1},{17,9},{25,17},{10,2},{18,10},{26,18},{... | collective-permute-start | bytes 2408456 | tf_op jit(solution)/shard_map/ppermute | solution.py:467
  19.8 28.3 %collective-permute-start.9 = (bf16[128,896]{1,0:T(8,128)(2,1)}, bf16[128,896]{1,0:T(8,128)(2,1)}, u32[]{:S(2)}, u32[]{:S(2)}) collective-permute-start(bf16[128,896]{1,0:T(8,128)(2,1)} %get-tuple-element.38), channel_id=1, source_target_pairs={{0,24},{24,0},{1,25},{25,1},{2,26},{26,2},{3,27},{27,3},{4,28},{28... | collective-permute-start | bytes 688136 | tf_op jit(solution)/shard_map/ppermute | solution.py:469
  31.3 9.1 %collective-permute-start.2 = (bf16[1,192,896]{2,1,0:T(8,128)(2,1)}, bf16[1,192,896]{2,1,0:T(8,128)(2,1)}, u32[]{:S(2)}, u32[]{:S(2)}) collective-permute-start(bf16[1,192,896]{2,1,0:T(8,128)(2,1)} %bitcast.8), channel_id=1, source_target_pairs={{0,1},{1,0},{2,3},{3,2},{4,5},{5,4},{6,7},{7,6},{8,9},{9,8},{10,11... | collective-permute-start | bytes 1032200 | tf_op jit(solution)/shard_map/ppermute | solution.py:390
  38.7 27.4 %copy-start.6 = (bf16[320,896]{1,0:T(8,128)(2,1)S(1)}, bf16[320,896]{1,0:T(8,128)(2,1)}, u32[]{:S(2)}) copy-start(bf16[320,896]{1,0:T(8,128)(2,1)} %get-tuple-element.43) | copy-start | bytes 1720324
  38.7 32.5 %copy-start.1 = (bf16[448,896]{1,0:T(8,128)(2,1)S(1)}, bf16[448,896]{1,0:T(8,128)(2,1)}, u32[]{:S(2)}) copy-start(bf16[448,896]{1,0:T(8,128)(2,1)} %get-tuple-element.35.refs_8_) | copy-start | bytes 2408452
  38.7 7.3 %collective-permute-start.8 = (bf16[1,192,896]{2,1,0:T(8,128)(2,1)S(1)}, bf16[1,192,896]{2,1,0:T(8,128)(2,1)S(1)}, u32[]{:S(2)}, u32[]{:S(2)}) collective-permute-start(bf16[1,192,896]{2,1,0:T(8,128)(2,1)S(1)} %bitcast.20), channel_id=1, source_target_pairs={{0,4},{2,6},{4,0},{6,2},{1,5},{3,7},{5,1},{7,3},{8,12},{10,14},{12... | collective-permute-start | bytes 1032200 | tf_op jit(solution)/shard_map/ppermute | solution.py:390
  43.2 22.3 %collective-permute-start.12 = (bf16[448,896]{1,0:T(8,128)(2,1)}, bf16[448,896]{1,0:T(8,128)(2,1)S(1)}, u32[]{:S(2)}, u32[]{:S(2)}) collective-permute-start(bf16[448,896]{1,0:T(8,128)(2,1)} %collective-permute-done.3.refs_9_), channel_id=1, source_target_pairs={{8,0},{16,8},{9,1},{17,9},{10,2},{18,10},{11,3},{19,11},{12,4},{20... | collective-permute-start | bytes 2408456 | tf_op jit(solution)/shard_map/ppermute | solution.py:479
  44.5 21.0 %collective-permute-start.13 = (bf16[448,896]{1,0:T(8,128)(2,1)}, bf16[448,896]{1,0:T(8,128)(2,1)S(1)}, u32[]{:S(2)}, u32[]{:S(2)}) collective-permute-start(bf16[448,896]{1,0:T(8,128)(2,1)} %collective-permute-done.4.refs_10_), channel_id=1, source_target_pairs={{8,16},{16,24},{9,17},{17,25},{10,18},{18,26},{11,19},{19,27},{12,... | collective-permute-start | bytes 2408456 | tf_op jit(solution)/shard_map/ppermute | solution.py:480
  48.1 16.2 %collective-permute-start.10 = (bf16[2,192,896]{2,1,0:T(8,128)(2,1)S(1)}, bf16[2,192,896]{2,1,0:T(8,128)(2,1)S(1)}, u32[]{:S(2)}, u32[]{:S(2)}) collective-permute-start(bf16[2,192,896]{2,1,0:T(8,128)(2,1)S(1)} %pad_maximum_fusion.1.refs_4_), channel_id=1, source_target_pairs={{0,1},{1,0},{2,3},{3,2},{4,5},{5,4},{6,7},{7,6},{8,9},{9,8},{10,11... | collective-permute-start | bytes 2064392 | tf_op jit(solution)/shard_map/ppermute | solution.py:390
  49.6 15.9 %collective-permute-start.5 = (bf16[2,192,896]{2,1,0:T(8,128)(2,1)S(1)}, bf16[2,192,896]{2,1,0:T(8,128)(2,1)S(1)}, u32[]{:S(2)}, u32[]{:S(2)}) collective-permute-start(bf16[2,192,896]{2,1,0:T(8,128)(2,1)S(1)} %pad_maximum_fusion.refs_0_), channel_id=1, source_target_pairs={{0,4},{2,6},{4,0},{6,2},{1,5},{3,7},{5,1},{7,3},{8,12},{10,14},{12... | collective-permute-start | bytes 2064392 | tf_op jit(solution)/shard_map/ppermute | solution.py:390
  51.1 20.0 %collective-permute-start.6 = (bf16[2,192,896]{2,1,0:T(8,128)(2,1)S(1)}, bf16[2,192,896]{2,1,0:T(8,128)(2,1)S(1)}, u32[]{:S(2)}, u32[]{:S(2)}) collective-permute-start(bf16[2,192,896]{2,1,0:T(8,128)(2,1)S(1)} %pad_maximum_fusion.refs_0_), channel_id=1, source_target_pairs={{0,2},{2,0},{4,6},{6,4},{1,3},{3,1},{5,7},{7,5},{8,10},{10,8},{12,... | collective-permute-start | bytes 2064392 | tf_op jit(solution)/shard_map/ppermute | solution.py:390
  64.3 6.8 %collective-permute-start.11 = (bf16[2,192,896]{2,1,0:T(8,128)(2,1)S(1)}, bf16[2,192,896]{2,1,0:T(8,128)(2,1)S(1)}, u32[]{:S(2)}, u32[]{:S(2)}) collective-permute-start(bf16[2,192,896]{2,1,0:T(8,128)(2,1)S(1)} %pad_maximum_fusion.1.refs_4_), channel_id=1, source_target_pairs={{0,2},{2,0},{4,6},{6,4},{1,3},{3,1},{5,7},{7,5},{8,10},{10,8},{12,... | collective-permute-start | bytes 2064392 | tf_op jit(solution)/shard_map/ppermute | solution.py:390
  65.6 5.6 %collective-permute-start.7 = (bf16[2,192,896]{2,1,0:T(8,128)(2,1)S(1)}, bf16[2,192,896]{2,1,0:T(8,128)(2,1)S(1)}, u32[]{:S(2)}, u32[]{:S(2)}) collective-permute-start(bf16[2,192,896]{2,1,0:T(8,128)(2,1)S(1)} %collective-permute-done.5.refs_1_), channel_id=1, source_target_pairs={{0,2},{2,0},{4,6},{6,4},{1,3},{3,1},{5,7},{7,5},{8,10},{10,8},{12,... | collective-permute-start | bytes 2064392 | tf_op jit(solution)/shard_map/ppermute | solution.py:390
  65.6 5.6 %collective-permute-start.14 = (bf16[2,192,896]{2,1,0:T(8,128)(2,1)S(1)}, bf16[2,192,896]{2,1,0:T(8,128)(2,1)S(1)}, u32[]{:S(2)}, u32[]{:S(2)}) collective-permute-start(bf16[2,192,896]{2,1,0:T(8,128)(2,1)S(1)} %collective-permute-done.10.refs_5_), channel_id=1, source_target_pairs={{0,2},{2,0},{4,6},{6,4},{1,3},{3,1},{5,7},{7,5},{8,10},{10,8},{12,... | collective-permute-start | bytes 2064392 | tf_op jit(solution)/shard_map/ppermute | solution.py:390
  66.1 18.6 %collective-permute-start.15 = (bf16[320,896]{1,0:T(8,128)(2,1)S(1)}, bf16[320,896]{1,0:T(8,128)(2,1)S(1)}, u32[]{:S(2)}, u32[]{:S(2)}) collective-permute-start(bf16[320,896]{1,0:T(8,128)(2,1)S(1)} %copy-done.6), channel_id=1, source_target_pairs={{0,24},{24,0},{1,25},{25,1},{2,26},{26,2},{3,27},{27,3},{4,28},{28... | collective-permute-start | bytes 1720328 | tf_op jit(solution)/shard_map/ppermute | solution.py:469
  95.4 7.0 %collective-permute-start.16 = (bf16[2,96,448]{2,1,0:T(8,128)(2,1)S(1)}, bf16[2,96,448]{2,1,0:T(8,128)(2,1)S(1)}, u32[]{:S(2)}, u32[]{:S(2)}) collective-permute-start(bf16[2,96,448]{2,1,0:T(8,128)(2,1)S(1)} %bitcast.27), channel_id=1, source_target_pairs={{0,1},{1,0},{2,3},{3,2},{4,5},{5,4},{6,7},{7,6},{8,9},{9,8},{10,11... | collective-permute-start | bytes 516104 | tf_op jit(solution)/shard_map/ppermute | solution.py:390
  97.3 12.3 %all-to-all-start.1 = ((f32[32,1,512]{2,1,0:T(1,128)}), f32[32,1,512]{2,1,0:T(1,128)S(1)}, u32[]{:S(2)}, u32[]{:S(2)}) async-start(f32[32,1,512]{2,1,0:T(1,128)} %finish.1), calls=%async_computation.1 | async-start | bytes 131072 | tf_op jit(solution)/shard_map/all_to_all | solution.py:413
  (2 other events, 3.0 us)

commit v5 on v4

--- a/solution.py
+++ b/solution.py
@@ -457,7 +457,7 @@
     gain_row = jnp.pad(own_columns(norm_gain), (0, whole_lanes(half) - half))[None]
     gain_all = norm_gain[None]
 
-    cut = min(LANES, half // 2)
+    cut = whole_lanes(half) // 2
     own_weight, *parts = prepare_weight(where, out_weight, clip_count, cut)
     line = slab_count == model_count and slab_count == 4
     last = slab_count - 1
@@ -481,8 +481,8 @@
             ]
         if line and stream == 1 and step == 1:
             value, across[0] = lax.optimization_barrier((value, across[0]))
-        if line and stream == 1 and step == 2 and part == 1:
-            value, passed = lax.optimization_barrier((value, passed))
+        if line and step == 2:
+            value, across[1] = lax.optimization_barrier((value, across[1]))
         return value
 
     gathered = []
@@ -502,15 +502,17 @@
             (0, own_weight, lambda slab: slab, lambda slab: slab >= 0),
             (0, near[0], lambda slab: jnp.minimum(slab + 1, last), lambda slab: slab < last),
             (0, near[1], lambda slab: jnp.maximum(slab - 1, 0), lambda slab: slab > 0),
-            (0, passed[0], lambda slab: jnp.minimum(slab + 2, last), lambda slab: slab < 2),
-            (0, passed[1], lambda slab: jnp.maximum(slab - 2, 0), lambda slab: slab >= 2),
         ]
         for first, block in zip((0, cut), across):
             shards.append(
                 (first, block, lambda slab: last - slab, lambda slab: (slab == 0) | (slab == last))
             )
-        (total,) = project(where, gathered, shards[:-1], None, half, 0)
-        total, squares = project(where, gathered, shards[-1:], total, half, peers)
+        shards += [
+            (0, passed[0], lambda slab: jnp.minimum(slab + 2, last), lambda slab: slab < 2),
+            (0, passed[1], lambda slab: jnp.maximum(slab - 2, 0), lambda slab: slab >= 2),
+        ]
+        (total,) = project(where, gathered, shards[:-2], None, half, 0)
+        total, squares = project(where, gathered, shards[-2:], total, half, peers)
     else:
         weight = lax.all_gather(own_weight, "frames", axis=1, tiled=True)
         shards = [

time: 112 us -> 115 us (1.027)
  waiting for transfers between devices: 33.5 us -> 39.7 us
  starting transfers between devices: 37.7 us -> 33.8 us
  Pallas kernels: 27.5 us -> 26.3 us
    ppermute x9, waiting for transfers between devices: 15.6 us -> 24.2 us  [swap(): return lax.ppermute(array, axis, [(i, i ^ distance) for i in range(count)])]
    ppermute x2, waiting for transfers between devices: 8.7 us -> 2.14 us  [local(): lax.ppermute(block, 'frames', [(0, last), (last, 0)])]
    ppermute x1, waiting for transfers between devices: 0.01 us -> 5.69 us  [local(): right = lax.ppermute(head, 'frames', down)]
    ppermute x2, starting transfers between devices: 10.1 us -> 8.26 us  [local(): lax.ppermute(block, 'frames', [(0, last), (last, 0)])]
    ppermute x2, waiting for transfers between devices: 1.72 us -> 0.01 us  [local(): near = [lax.ppermute(own_weight, 'frames', pairs) for pairs in (down, up)]]
    convert_element_type x1, other arithmetic: 0.32 us -> 1.54 us  [perturb(): (clean.astype(jnp.float32) + sigma_noise * noise.astype(jnp.float32)).ast...]
  transfers between devices with their start and end apart: 18 -> 18, of which waited for: 9 -> 11; matrix products, arithmetic and copies ran while one was open for 3% -> 4% of each run, Pallas kernels for 18% -> 17%
where the time goes in v5:
time: 115 us; the launch traced here: 114 us
  waiting for transfers between devices  39.7 us (35%)
  starting transfers between devices  33.8 us (29%)
  Pallas kernels  26.3 us (23%)
  blocking collectives  8.23 us (7%)
  other arithmetic  4.26 us (4%)
  local copies, waits for them, and re-layouts  1.32 us (1%)
    ppermute x9, waiting for transfers between devices, swap(): return lax.ppermute(array, axis, [(i, i ^ distance) for i in range(count)])  24.2 us
    pallas_call x2, Pallas kernels, attention(): pl.pallas_call(attend_kernel, grid_spec=pltpu.PrefetchScalarGridSpec(num_...  9.04 us
    pallas_call x2, Pallas kernels, project(): pl.pallas_call(kernel, in_specs=[pl.BlockSpec(memory_space=pltpu.SMEM)] +...  8.98 us
    ppermute x2, starting transfers between devices, local(): lax.ppermute(block, 'frames', [(0, last), (last, 0)])  8.26 us
    all_to_all x1, blocking collectives, collect(): return lax.all_to_all(rows, axes, split_axis=0, concat_axis=0, tiled=True)  8.23 us
    ppermute x9, starting transfers between devices, swap(): return lax.ppermute(array, axis, [(i, i ^ distance) for i in range(count)])  6.97 us
    all_to_all x1, waiting for transfers between devices, collect(): return lax.all_to_all(rows, axes, split_axis=0, concat_axis=0, tiled=True)  6.06 us
    ppermute x1, waiting for transfers between devices, local(): right = lax.ppermute(head, 'frames', down)  5.69 us
  transfers between devices with their start and end apart: 18, of which 11 were waited for; matrix products, arithmetic and copies ran while one was open for 4% of the time, Pallas kernels for 17%

profile of v5, /device:TPU:0, one launch (start us, length us, event | category | flops | bytes accessed | tf_op | source)
XLA Modules:
  0.0 114.5 jit_solution(890020849244287905)
XLA Ops:
  0.6 2.4 %prepare_halo.1 = (bf16[2,2,96,896]{3,2,1,0:T(8,128)(2,1)}, bf16[2,2,96,896]{3,2,1,0:T(8,128)(2,1)}) custom-call(bf16[2,3,96,896]{3,2,1,0:T(8,128)(2,1)} %bitcast.17, bf16[2,3,96,896]{3,2,1,0:T(8,128)(2,1)} %bitcast.26), custom_call_target="tpu_custom_call" | custom-call | tf_op jit(solution)/shard_map/prepare_halo/pallas_call | solution.py:53
  4.3 5.6 %collective-permute-start.1 = (bf16[2,2,96,896]{3,2,1,0:T(8,128)(2,1)}, bf16[2,2,96,896]{3,2,1,0:T(8,128)(2,1)S(1)}, u32[]{:S(2)}, u32[]{:S(2)}) collective-permute-start(bf16[2,2,96,896]{3,2,1,0:T(8,128)(2,1)} %get-tuple-element.38), channel_id=1, source_target_pairs={{0,8},{8,16},{16,24},{1,9},{9,17},{17,25},{2,10},{10,18},{18,26},{... | collective-permute-start | bytes 2064392 | tf_op jit(solution)/shard_map/ppermute | solution.py:450
  10.7 2.9 %prepare_weight.1 = (bf16[448,896]{1,0:T(8,128)(2,1)}, bf16[256,896]{1,0:T(8,128)(2,1)}, bf16[192,896]{1,0:T(8,128)(2,1)}) custom-call(s32[7]{0:T(128)} %pad_add_fusion.where_ref, bf16[896,896]{1,0:T(8,128)(2,1)} %weight_ref), custom_call_target="tpu_custom_call" | custom-call | tf_op jit(solution)/shard_map/prepare_weight/pallas_call | solution.py:87
  13.5 3.9 %collective-permute-start.4 = (bf16[448,896]{1,0:T(8,128)(2,1)}, bf16[448,896]{1,0:T(8,128)(2,1)S(1)}, u32[]{:S(2)}, u32[]{:S(2)}) collective-permute-start(bf16[448,896]{1,0:T(8,128)(2,1)} %get-tuple-element.40.refs_8_), channel_id=1, source_target_pairs={{0,8},{8,16},{16,24},{1,9},{9,17},{17,25},{2,10},{10,18},{18,26},{... | collective-permute-start | bytes 2408456 | tf_op jit(solution)/shard_map/ppermute | solution.py:467
  18.7 5.7 %collective-permute-done.right_ref = bf16[2,2,96,896]{3,2,1,0:T(8,128)(2,1)S(1)} collective-permute-done((bf16[2,2,96,896]{3,2,1,0:T(8,128)(2,1)}, bf16[2,2,96,896]{3,2,1,0:T(8,128)(2,1)S(1)}, u32[]{:S(2)}, u32[]{:S(2)}) %collective-permute-start) | collective-permute-done | bytes 688160 | tf_op jit(solution)/shard_map/ppermute | solution.py:449
  24.4 1.6 %collective-permute-done.1.left_ref = bf16[2,2,96,896]{3,2,1,0:T(8,128)(2,1)S(1)} collective-permute-done((bf16[2,2,96,896]{3,2,1,0:T(8,128)(2,1)}, bf16[2,2,96,896]{3,2,1,0:T(8,128)(2,1)S(1)}, u32[]{:S(2)}, u32[]{:S(2)}) %collective-permute-start.1) | collective-permute-done | bytes 688160 | tf_op jit(solution)/shard_map/ppermute | solution.py:450
  26.0 4.5 %attention.2 = bf16[2,96,896]{2,1,0:T(8,128)(2,1)S(1)} custom-call(s32[7]{0:T(128)S(1)} %copy-done.2, bf16[2,3,96,896]{3,2,1,0:T(8,128)(2,1)S(1)} %bitcast.18, bf16[2,2,96,896]{3,2,1,0:T(8,128)(2,1)S(1)} %collective-permute-done.right_ref, bf16[2,2,96,896]{3,2,1,0:T(8,128)(2,1)S(1)} %collective-permute-done.1.left_ref), custom_call_target="tpu_custom_call" | custom-call | tf_op jit(solution)/shard_map/attention/pallas_call | solution.py:144
  30.6 2.1 %collective-permute-start.2 = (bf16[1,192,896]{2,1,0:T(8,128)(2,1)S(1)}, bf16[1,192,896]{2,1,0:T(8,128)(2,1)}, u32[]{:S(2)}, u32[]{:S(2)}) collective-permute-start(bf16[1,192,896]{2,1,0:T(8,128)(2,1)S(1)} %bitcast.20), channel_id=1, source_target_pairs={{0,1},{1,0},{2,3},{3,2},{4,5},{5,4},{6,7},{7,6},{8,9},{9,8},{10,11... | collective-permute-start | bytes 1032200 | tf_op jit(solution)/shard_map/ppermute | solution.py:390
  32.6 6.3 %collective-permute-start.6 = (bf16[192,896]{1,0:T(8,128)(2,1)}, bf16[192,896]{1,0:T(8,128)(2,1)}, u32[]{:S(2)}, u32[]{:S(2)}) collective-permute-start(bf16[192,896]{1,0:T(8,128)(2,1)} %get-tuple-element.42), channel_id=1, source_target_pairs={{0,24},{24,0},{1,25},{25,1},{2,26},{26,2},{3,27},{27,3},{4,28},{28... | collective-permute-start | bytes 1032200 | tf_op jit(solution)/shard_map/ppermute | solution.py:469
  39.0 1.9 %collective-permute-start.10 = (bf16[256,896]{1,0:T(8,128)(2,1)}, bf16[256,896]{1,0:T(8,128)(2,1)}, u32[]{:S(2)}, u32[]{:S(2)}) collective-permute-start(bf16[256,896]{1,0:T(8,128)(2,1)} %get-tuple-element.47), channel_id=1, source_target_pairs={{0,24},{24,0},{1,25},{25,1},{2,26},{26,2},{3,27},{27,3},{4,28},{28... | collective-permute-start | bytes 1376264 | tf_op jit(solution)/shard_map/ppermute | solution.py:469
  40.9 1.5 %add_convert_fusion.own_ref = bf16[2,3,96,896]{3,2,1,0:T(8,128)(2,1)S(1)} fusion(bf16[2,3,96,896]{3,2,1,0:T(8,128)(2,1)} %bitcast.27, bf16[2,3,96,896]{3,2,1,0:T(8,128)(2,1)S(1)} %bitcast.19), kind=kLoop, calls=%fused_computation | loop fusion | flops 2580480 | bytes 3096576 | tf_op jit(solution)/shard_map/convert_element_type | solution.py:20
  42.5 4.5 %attention.3 = bf16[2,96,896]{2,1,0:T(8,128)(2,1)S(1)} custom-call(s32[7]{0:T(128)S(1)} %copy-done.3, bf16[2,3,96,896]{3,2,1,0:T(8,128)(2,1)S(1)} %add_convert_fusion.own_ref, bf16[2,2,96,896]{3,2,1,0:T(8,128)(2,1)S(1)} %collective-permute-done.right_ref, bf16[2,2,96,896]{3,2,1,0:T(8,128)(2,1)S(1)} %collective-permute-done.1.left_ref), custom_call_target="tpu_custom_call" | custom-call | tf_op jit(solution)/shard_map/attention/pallas_call | solution.py:144
  47.0 1.6 %collective-permute-start.9 = (bf16[1,192,896]{2,1,0:T(8,128)(2,1)S(1)}, bf16[1,192,896]{2,1,0:T(8,128)(2,1)S(1)}, u32[]{:S(2)}, u32[]{:S(2)}) collective-permute-start(bf16[1,192,896]{2,1,0:T(8,128)(2,1)S(1)} %bitcast.22), channel_id=1, source_target_pairs={{0,4},{2,6},{4,0},{6,2},{1,5},{3,7},{5,1},{7,3},{8,12},{10,14},{12... | collective-permute-start | bytes 1032200 | tf_op jit(solution)/shard_map/ppermute | solution.py:390
  50.9 7.2 %collective-permute-done.9 = bf16[1,192,896]{2,1,0:T(8,128)(2,1)S(1)} collective-permute-done((bf16[1,192,896]{2,1,0:T(8,128)(2,1)S(1)}, bf16[1,192,896]{2,1,0:T(8,128)(2,1)S(1)}, u32[]{:S(2)}, u32[]{:S(2)}) %collective-permute-start.9) | collective-permute-done | bytes 344096 | tf_op jit(solution)/shard_map/ppermute | solution.py:390
  58.2 2.1 %collective-permute-done.10.refs_11_ = bf16[256,896]{1,0:T(8,128)(2,1)} collective-permute-done((bf16[256,896]{1,0:T(8,128)(2,1)}, bf16[256,896]{1,0:T(8,128)(2,1)}, u32[]{:S(2)}, u32[]{:S(2)}) %collective-permute-start.10) | collective-permute-done | bytes 458784 | tf_op jit(solution)/shard_map/ppermute | solution.py:469
  63.8 4.6 %collective-permute-done.5.refs_1_ = bf16[2,192,896]{2,1,0:T(8,128)(2,1)S(1)} collective-permute-done((bf16[2,192,896]{2,1,0:T(8,128)(2,1)S(1)}, bf16[2,192,896]{2,1,0:T(8,128)(2,1)S(1)}, u32[]{:S(2)}, u32[]{:S(2)}) %collective-permute-start.5) | collective-permute-done | bytes 688160 | tf_op jit(solution)/shard_map/ppermute | solution.py:390
  68.4 8.2 %collective-permute-done.11.refs_5_ = bf16[2,192,896]{2,1,0:T(8,128)(2,1)S(1)} collective-permute-done((bf16[2,192,896]{2,1,0:T(8,128)(2,1)S(1)}, bf16[2,192,896]{2,1,0:T(8,128)(2,1)S(1)}, u32[]{:S(2)}, u32[]{:S(2)}) %collective-permute-start.11) | collective-permute-done | bytes 688160 | tf_op jit(solution)/shard_map/ppermute | solution.py:390
  77.1 1.6 %collective-permute-done.13.refs_7_ = bf16[2,192,896]{2,1,0:T(8,128)(2,1)S(1)} collective-permute-done((bf16[2,192,896]{2,1,0:T(8,128)(2,1)S(1)}, bf16[2,192,896]{2,1,0:T(8,128)(2,1)S(1)}, u32[]{:S(2)}, u32[]{:S(2)}) %collective-permute-start.13) | collective-permute-done | bytes 688160 | tf_op jit(solution)/shard_map/ppermute | solution.py:390
  80.7 6.3 %project.2.refs_10_ = f32[2,384,512]{2,1,0:T(8,128)S(1)} custom-call(s32[7]{0:T(128)S(1)} %copy-done.3, bf16[2,192,896]{2,1,0:T(8,128)(2,1)S(1)} %pad_maximum_fusion.refs_0_, bf16[2,192,896]{2,1,0:T(8,128)(2,1)S(1)} %collective-permute-done.5.refs_1_, bf16[2,192,896]{2,1,0:T(8,128)(2,1)S(1)} %collective-permute-done.7.refs_2_, ...), custom_call_target="tpu_custom_call" | custom-call | tf_op jit(solution)/shard_map/project/pallas_call | solution.py:274
  87.1 2.7 %project.3 = (f32[2,384,512]{2,1,0:T(8,128)S(1)}, f32[8,1,768]{2,1,0:T(1,128)S(1)}) custom-call(s32[7]{0:T(128)S(1)} %copy-done.3, bf16[2,192,896]{2,1,0:T(8,128)(2,1)S(1)} %pad_maximum_fusion.refs_0_, bf16[2,192,896]{2,1,0:T(8,128)(2,1)S(1)} %collective-permute-done.5.refs_1_, ...), custom_call_target="tpu_custom_call", output_to_operand_aliasing={{0}: (11, {})} | custom-call | tf_op jit(solution)/shard_map/project/pallas_call | solution.py:274
  89.7 8.2 %all_to_all.10.squares_ref = f32[8,1,768]{2,1,0:T(1,128)S(1)} all-to-all(f32[8,1,768]{2,1,0:T(1,128)S(1)} %get-tuple-element.58), channel_id=1, replica_groups=mesh['frames'=4,'mp'=4,'dp'=2] {'mp','dp'}, dimensions={0} | all-to-all | bytes 49152 | tf_op jit(solution)/shard_map/all_to_all | solution.py:413
  100.1 4.4 %all-to-all-start.1 = ((f32[32,1,512]{2,1,0:T(1,128)}), f32[32,1,512]{2,1,0:T(1,128)S(1)}, u32[]{:S(2)}, u32[]{:S(2)}) async-start(f32[32,1,512]{2,1,0:T(1,128)} %finish.1), calls=%async_computation.1 | async-start | bytes 131072 | tf_op jit(solution)/shard_map/all_to_all | solution.py:413
  106.1 6.1 %all-to-all-done.1.rows_ref = f32[32,1,512]{2,1,0:T(1,128)S(1)} async-done(((f32[32,1,512]{2,1,0:T(1,128)}), f32[32,1,512]{2,1,0:T(1,128)S(1)}, u32[]{:S(2)}, u32[]{:S(2)}) %all-to-all-start.1) | async-done | bytes 65568 | tf_op jit(solution)/shard_map/all_to_all | solution.py:413
  112.8 1.7 %conclude.1 = (f32[1]{0:T(128)}, f32[896]{0:T(1024)}) custom-call(s32[7]{0:T(128)} %pad_add_fusion.where_ref, f32[32,1,512]{2,1,0:T(1,128)} %copy-done.4, f32[1,896]{1,0:T(1,128)} %broadcast_in_dim.10.gain_ref), custom_call_target="tpu_custom_call" | custom-call | tf_op jit(solution)/shard_map/conclude/pallas_call | solution.py:371
  (47 shorter events, 16.0 us)
Async XLA Ops:
  0.6 9.3 %copy-start.6 = (s32[1,8]{1,0:T(1,128)S(1)}, s32[1,8]{1,0:T(1,128)}, u32[]{:S(2)}) copy-start(s32[1,8]{1,0:T(1,128)} %param.9) | copy-start | bytes 100
  0.6 25.4 %copy-start = (bf16[1,2,96,3,896]{4,2,3,1,0:T(8,128)(2,1)S(1)}, bf16[1,2,96,3,896]{4,2,3,1,0:T(8,128)(2,1)}, u32[]{:S(2)}) copy-start(bf16[1,2,96,3,896]{4,2,3,1,0:T(8,128)(2,1)} %param.5) | copy-start | bytes 3096580
  3.0 21.4 %collective-permute-start = (bf16[2,2,96,896]{3,2,1,0:T(8,128)(2,1)}, bf16[2,2,96,896]{3,2,1,0:T(8,128)(2,1)S(1)}, u32[]{:S(2)}, u32[]{:S(2)}) collective-permute-start(bf16[2,2,96,896]{3,2,1,0:T(8,128)(2,1)} %get-tuple-element.37), channel_id=1, source_target_pairs={{8,0},{16,8},{24,16},{9,1},{17,9},{25,17},{10,2},{18,10},{26,18},{... | collective-permute-start | bytes 2064392 | tf_op jit(solution)/shard_map/ppermute | solution.py:449
  4.3 21.7 %collective-permute-start.1 = (bf16[2,2,96,896]{3,2,1,0:T(8,128)(2,1)}, bf16[2,2,96,896]{3,2,1,0:T(8,128)(2,1)S(1)}, u32[]{:S(2)}, u32[]{:S(2)}) collective-permute-start(bf16[2,2,96,896]{3,2,1,0:T(8,128)(2,1)} %get-tuple-element.38), channel_id=1, source_target_pairs={{0,8},{8,16},{16,24},{1,9},{9,17},{17,25},{2,10},{10,18},{18,26},{... | collective-permute-start | bytes 2064392 | tf_op jit(solution)/shard_map/ppermute | solution.py:450
  10.7 15.4 %copy-start.2 = (s32[7]{0:T(128)S(1)}, s32[7]{0:T(128)}, u32[]{:S(2)}) copy-start(s32[7]{0:T(128)} %pad_add_fusion.where_ref) | copy-start | bytes 88
  13.5 36.8 %collective-permute-start.4 = (bf16[448,896]{1,0:T(8,128)(2,1)}, bf16[448,896]{1,0:T(8,128)(2,1)S(1)}, u32[]{:S(2)}, u32[]{:S(2)}) collective-permute-start(bf16[448,896]{1,0:T(8,128)(2,1)} %get-tuple-element.40.refs_8_), channel_id=1, source_target_pairs={{0,8},{8,16},{16,24},{1,9},{9,17},{17,25},{2,10},{10,18},{18,26},{... | collective-permute-start | bytes 2408456 | tf_op jit(solution)/shard_map/ppermute | solution.py:467
  17.4 32.9 %collective-permute-start.3 = (bf16[448,896]{1,0:T(8,128)(2,1)}, bf16[448,896]{1,0:T(8,128)(2,1)}, u32[]{:S(2)}, u32[]{:S(2)}) collective-permute-start(bf16[448,896]{1,0:T(8,128)(2,1)} %get-tuple-element.40.refs_8_), channel_id=1, source_target_pairs={{8,0},{16,8},{24,16},{9,1},{17,9},{25,17},{10,2},{18,10},{26,18},{... | collective-permute-start | bytes 2408456 | tf_op jit(solution)/shard_map/ppermute | solution.py:467
  30.6 16.4 %collective-permute-start.2 = (bf16[1,192,896]{2,1,0:T(8,128)(2,1)S(1)}, bf16[1,192,896]{2,1,0:T(8,128)(2,1)}, u32[]{:S(2)}, u32[]{:S(2)}) collective-permute-start(bf16[1,192,896]{2,1,0:T(8,128)(2,1)S(1)} %bitcast.20), channel_id=1, source_target_pairs={{0,1},{1,0},{2,3},{3,2},{4,5},{5,4},{6,7},{7,6},{8,9},{9,8},{10,11... | collective-permute-start | bytes 1032200 | tf_op jit(solution)/shard_map/ppermute | solution.py:390
  32.6 29.2 %collective-permute-start.6 = (bf16[192,896]{1,0:T(8,128)(2,1)}, bf16[192,896]{1,0:T(8,128)(2,1)}, u32[]{:S(2)}, u32[]{:S(2)}) collective-permute-start(bf16[192,896]{1,0:T(8,128)(2,1)} %get-tuple-element.42), channel_id=1, source_target_pairs={{0,24},{24,0},{1,25},{25,1},{2,26},{26,2},{3,27},{27,3},{4,28},{28... | collective-permute-start | bytes 1032200 | tf_op jit(solution)/shard_map/ppermute | solution.py:469
  39.0 21.3 %collective-permute-start.10 = (bf16[256,896]{1,0:T(8,128)(2,1)}, bf16[256,896]{1,0:T(8,128)(2,1)}, u32[]{:S(2)}, u32[]{:S(2)}) collective-permute-start(bf16[256,896]{1,0:T(8,128)(2,1)} %get-tuple-element.47), channel_id=1, source_target_pairs={{0,24},{24,0},{1,25},{25,1},{2,26},{26,2},{3,27},{27,3},{4,28},{28... | collective-permute-start | bytes 1376264 | tf_op jit(solution)/shard_map/ppermute | solution.py:469
  40.9 1.6 %copy-start.3 = (s32[7]{0:T(128)S(1)}, s32[7]{0:T(128)}, u32[]{:S(2)}) copy-start(s32[7]{0:T(128)} %pad_add_fusion.where_ref) | copy-start | bytes 88
  42.5 6.1 %copy-start.5 = (f32[896]{0:T(1024)S(1)}, f32[896]{0:T(1024)}, u32[]{:S(2)}) copy-start(f32[896]{0:T(1024)} %param.8) | copy-start | bytes 10756
  47.0 33.7 %copy-start.1 = (bf16[448,896]{1,0:T(8,128)(2,1)S(1)}, bf16[448,896]{1,0:T(8,128)(2,1)}, u32[]{:S(2)}) copy-start(bf16[448,896]{1,0:T(8,128)(2,1)} %get-tuple-element.40.refs_8_) | copy-start | bytes 2408452
  47.0 11.1 %collective-permute-start.9 = (bf16[1,192,896]{2,1,0:T(8,128)(2,1)S(1)}, bf16[1,192,896]{2,1,0:T(8,128)(2,1)S(1)}, u32[]{:S(2)}, u32[]{:S(2)}) collective-permute-start(bf16[1,192,896]{2,1,0:T(8,128)(2,1)S(1)} %bitcast.22), channel_id=1, source_target_pairs={{0,4},{2,6},{4,0},{6,2},{1,5},{3,7},{5,1},{7,3},{8,12},{10,14},{12... | collective-permute-start | bytes 1032200 | tf_op jit(solution)/shard_map/ppermute | solution.py:390
  50.3 18.1 %collective-permute-start.5 = (bf16[2,192,896]{2,1,0:T(8,128)(2,1)S(1)}, bf16[2,192,896]{2,1,0:T(8,128)(2,1)S(1)}, u32[]{:S(2)}, u32[]{:S(2)}) collective-permute-start(bf16[2,192,896]{2,1,0:T(8,128)(2,1)S(1)} %pad_maximum_fusion.refs_0_), channel_id=1, source_target_pairs={{0,4},{2,6},{4,0},{6,2},{1,5},{3,7},{5,1},{7,3},{8,12},{10,14},{12... | collective-permute-start | bytes 2064392 | tf_op jit(solution)/shard_map/ppermute | solution.py:390
  60.3 16.3 %collective-permute-start.11 = (bf16[2,192,896]{2,1,0:T(8,128)(2,1)S(1)}, bf16[2,192,896]{2,1,0:T(8,128)(2,1)S(1)}, u32[]{:S(2)}, u32[]{:S(2)}) collective-permute-start(bf16[2,192,896]{2,1,0:T(8,128)(2,1)S(1)} %pad_maximum_fusion.1.refs_4_), channel_id=1, source_target_pairs={{0,1},{1,0},{2,3},{3,2},{4,5},{5,4},{6,7},{7,6},{8,9},{9,8},{10,11... | collective-permute-start | bytes 2064392 | tf_op jit(solution)/shard_map/ppermute | solution.py:390
  61.8 15.3 %collective-permute-start.7 = (bf16[2,192,896]{2,1,0:T(8,128)(2,1)S(1)}, bf16[2,192,896]{2,1,0:T(8,128)(2,1)S(1)}, u32[]{:S(2)}, u32[]{:S(2)}) collective-permute-start(bf16[2,192,896]{2,1,0:T(8,128)(2,1)S(1)} %pad_maximum_fusion.refs_0_), channel_id=1, source_target_pairs={{0,2},{2,0},{4,6},{6,4},{1,3},{3,1},{5,7},{7,5},{8,10},{10,8},{12,... | collective-permute-start | bytes 2064392 | tf_op jit(solution)/shard_map/ppermute | solution.py:390
  61.8 25.2 %collective-permute-start.14 = (bf16[448,896]{1,0:T(8,128)(2,1)}, bf16[448,896]{1,0:T(8,128)(2,1)S(1)}, u32[]{:S(2)}, u32[]{:S(2)}) collective-permute-start(bf16[448,896]{1,0:T(8,128)(2,1)} %collective-permute-done.3.refs_9_), channel_id=1, source_target_pairs={{8,0},{16,8},{9,1},{17,9},{10,2},{18,10},{11,3},{19,11},{12,4},{20... | collective-permute-start | bytes 2408456 | tf_op jit(solution)/shard_map/ppermute | solution.py:479
  63.1 23.9 %collective-permute-start.15 = (bf16[448,896]{1,0:T(8,128)(2,1)S(1)}, bf16[448,896]{1,0:T(8,128)(2,1)S(1)}, u32[]{:S(2)}, u32[]{:S(2)}) collective-permute-start(bf16[448,896]{1,0:T(8,128)(2,1)S(1)} %collective-permute-done.4.refs_10_), channel_id=1, source_target_pairs={{8,16},{16,24},{9,17},{17,25},{10,18},{18,26},{11,19},{19,27},{12,... | collective-permute-start | bytes 2408456 | tf_op jit(solution)/shard_map/ppermute | solution.py:480
  76.6 2.1 %collective-permute-start.13 = (bf16[2,192,896]{2,1,0:T(8,128)(2,1)S(1)}, bf16[2,192,896]{2,1,0:T(8,128)(2,1)S(1)}, u32[]{:S(2)}, u32[]{:S(2)}) collective-permute-start(bf16[2,192,896]{2,1,0:T(8,128)(2,1)S(1)} %collective-permute-done.11.refs_5_), channel_id=1, source_target_pairs={{0,2},{2,0},{4,6},{6,4},{1,3},{3,1},{5,7},{7,5},{8,10},{10,8},{12,... | collective-permute-start | bytes 2064392 | tf_op jit(solution)/shard_map/ppermute | solution.py:390
  76.6 3.1 %collective-permute-start.12 = (bf16[2,192,896]{2,1,0:T(8,128)(2,1)S(1)}, bf16[2,192,896]{2,1,0:T(8,128)(2,1)S(1)}, u32[]{:S(2)}, u32[]{:S(2)}) collective-permute-start(bf16[2,192,896]{2,1,0:T(8,128)(2,1)S(1)} %pad_maximum_fusion.1.refs_4_), channel_id=1, source_target_pairs={{0,2},{2,0},{4,6},{6,4},{1,3},{3,1},{5,7},{7,5},{8,10},{10,8},{12,... | collective-permute-start | bytes 2064392 | tf_op jit(solution)/shard_map/ppermute | solution.py:390
  77.1 3.6 %collective-permute-start.8 = (bf16[2,192,896]{2,1,0:T(8,128)(2,1)S(1)}, bf16[2,192,896]{2,1,0:T(8,128)(2,1)S(1)}, u32[]{:S(2)}, u32[]{:S(2)}) collective-permute-start(bf16[2,192,896]{2,1,0:T(8,128)(2,1)S(1)} %collective-permute-done.5.refs_1_), channel_id=1, source_target_pairs={{0,2},{2,0},{4,6},{6,4},{1,3},{3,1},{5,7},{7,5},{8,10},{10,8},{12,... | collective-permute-start | bytes 2064392 | tf_op jit(solution)/shard_map/ppermute | solution.py:390
  98.2 7.0 %collective-permute-start.16 = (bf16[2,96,448]{2,1,0:T(8,128)(2,1)S(1)}, bf16[2,96,448]{2,1,0:T(8,128)(2,1)S(1)}, u32[]{:S(2)}, u32[]{:S(2)}) collective-permute-start(bf16[2,96,448]{2,1,0:T(8,128)(2,1)S(1)} %bitcast.29), channel_id=1, source_target_pairs={{0,1},{1,0},{2,3},{3,2},{4,5},{5,4},{6,7},{7,6},{8,9},{9,8},{10,11... | collective-permute-start | bytes 516104 | tf_op jit(solution)/shard_map/ppermute | solution.py:390
  100.1 12.0 %all-to-all-start.1 = ((f32[32,1,512]{2,1,0:T(1,128)}), f32[32,1,512]{2,1,0:T(1,128)S(1)}, u32[]{:S(2)}, u32[]{:S(2)}) async-start(f32[32,1,512]{2,1,0:T(1,128)} %finish.1), calls=%async_computation.1 | async-start | bytes 131072 | tf_op jit(solution)/shard_map/all_to_all | solution.py:413
  (1 other events, 0.6 us)

commit v6 on v5

--- a/solution.py
+++ b/solution.py
@@ -461,7 +461,7 @@
     own_weight, *parts = prepare_weight(where, out_weight, clip_count, cut)
     line = slab_count == model_count and slab_count == 4
     last = slab_count - 1
-    near, passed, across = [], [], []
+    near, passed, across = [], None, []
 
     if line:
         near = [lax.ppermute(own_weight, "frames", pairs) for pairs in (down, up)]
@@ -475,14 +475,11 @@
             value, near, gain_row, gain_all = lax.optimization_barrier(
                 (value, near, gain_row, gain_all)
             )
-            passed = [
-                lax.ppermute(near[0], "frames", down[:2]),
-                lax.ppermute(near[1], "frames", up[1:]),
-            ]
+            options = [own_weight, near[0], near[1], own_weight]
+            sent = lax.select_n(slab_index, *options)
+            passed = lax.ppermute(sent, "frames", [(0, 2), (1, 0), (2, last), (last, 1)])
         if line and stream == 1 and step == 1:
             value, across[0] = lax.optimization_barrier((value, across[0]))
-        if line and step == 2:
-            value, across[1] = lax.optimization_barrier((value, across[1]))
         return value
 
     gathered = []
@@ -507,12 +504,10 @@
             shards.append(
                 (first, block, lambda slab: last - slab, lambda slab: (slab == 0) | (slab == last))
             )
-        shards += [
-            (0, passed[0], lambda slab: jnp.minimum(slab + 2, last), lambda slab: slab < 2),
-            (0, passed[1], lambda slab: jnp.maximum(slab - 2, 0), lambda slab: slab >= 2),
-        ]
-        (total,) = project(where, gathered, shards[:-2], None, half, 0)
-        total, squares = project(where, gathered, shards[-2:], total, half, peers)
+        shards.append((0, passed, lambda slab: (slab + 2) % slab_count, lambda slab: slab >= 0))
+        (total,) = project(where, gathered, shards[:4], None, half, 0)
+        (total,) = project(where, gathered, shards[5:], total, half, 0)
+        total, squares = project(where, gathered, shards[4:5], total, half, peers)
     else:
         weight = lax.all_gather(own_weight, "frames", axis=1, tiled=True)
         shards = [

time: 115 us -> 114 us (level)
  waiting for transfers between devices: 39.7 us -> 32.2 us
  starting transfers between devices: 33.8 us -> 39.4 us
  Pallas kernels: 26.3 us -> 27.9 us
  blocking collectives: 8.23 us -> 7.06 us
    ppermute x9, waiting for transfers between devices: 24.2 us -> 11.8 us  [swap(): return lax.ppermute(array, axis, [(i, i ^ distance) for i in range(count)])]
    ppermute x2, waiting for transfers between devices: 2.14 us -> 8.49 us  [local(): lax.ppermute(block, 'frames', [(0, last), (last, 0)])]
    ppermute x2, starting transfers between devices: 8.26 us -> 11.4 us  [local(): lax.ppermute(block, 'frames', [(0, last), (last, 0)])]
    ppermute x1, waiting for transfers between devices: 5.69 us -> 3.64 us  [local(): right = lax.ppermute(head, 'frames', down)]
    ppermute x2, starting transfers between devices: 5.21 us -> 6.89 us  [local(): near = [lax.ppermute(own_weight, 'frames', pairs) for pairs in (down, up)]]
    select_n x0 -> x1, other arithmetic: none -> 1.32 us  [before_step(): sent = lax.select_n(slab_index, *options)]
    convert_element_type x1, other arithmetic: 1.54 us -> 0.32 us  [perturb(): (clean.astype(jnp.float32) + sigma_noise * noise.astype(jnp.float32)).ast...]
    all_to_all x1, blocking collectives: 8.23 us -> 7.06 us  [collect(): return lax.all_to_all(rows, axes, split_axis=0, concat_axis=0, tiled=True)]
  transfers between devices with their start and end apart: 18 -> 17, of which waited for: 11 -> 7; matrix products, arithmetic and copies ran while one was open for 4% -> 5% of each run, Pallas kernels for 17% -> 19%
where the time goes in v6:
time: 114 us
  starting transfers between devices  39.4 us (35%)
  waiting for transfers between devices  32.2 us (28%)
  Pallas kernels  27.9 us (24%)
  blocking collectives  7.06 us (6%)
  other arithmetic  4.41 us (4%)
  local copies, waits for them, and re-layouts  1.92 us (2%)
    ppermute x9, waiting for transfers between devices, swap(): return lax.ppermute(array, axis, [(i, i ^ distance) for i in range(count)])  11.8 us
    ppermute x2, starting transfers between devices, local(): lax.ppermute(block, 'frames', [(0, last), (last, 0)])  11.4 us
    pallas_call x3, Pallas kernels, project(): pl.pallas_call(kernel, in_specs=[pl.BlockSpec(memory_space=pltpu.SMEM)] +...  9.81 us
    pallas_call x2, Pallas kernels, attention(): pl.pallas_call(attend_kernel, grid_spec=pltpu.PrefetchScalarGridSpec(num_...  9.75 us
    ppermute x2, waiting for transfers between devices, local(): lax.ppermute(block, 'frames', [(0, last), (last, 0)])  8.49 us
    ppermute x9, starting transfers between devices, swap(): return lax.ppermute(array, axis, [(i, i ^ distance) for i in range(count)])  7.55 us
    all_to_all x1, blocking collectives, collect(): return lax.all_to_all(rows, axes, split_axis=0, concat_axis=0, tiled=True)  7.06 us
    ppermute x2, starting transfers between devices, local(): near = [lax.ppermute(own_weight, 'frames', pairs) for pairs in (down, up)]  6.89 us
  transfers between devices with their start and end apart: 17, of which 7 were waited for; matrix products, arithmetic and copies ran while one was open for 5% of the time, Pallas kernels for 19%

profile of v6, /device:TPU:0, one launch (start us, length us, event | category | flops | bytes accessed | tf_op | source)
XLA Modules:
  0.0 113.8 jit_solution(5046395301475421330)
XLA Ops:
  0.7 2.4 %prepare_halo.1 = (bf16[2,2,96,896]{3,2,1,0:T(8,128)(2,1)}, bf16[2,2,96,896]{3,2,1,0:T(8,128)(2,1)}) custom-call(bf16[2,3,96,896]{3,2,1,0:T(8,128)(2,1)} %bitcast.17, bf16[2,3,96,896]{3,2,1,0:T(8,128)(2,1)} %bitcast.24), custom_call_target="tpu_custom_call" | custom-call | tf_op jit(solution)/shard_map/prepare_halo/pallas_call | solution.py:53
  4.4 5.6 %collective-permute-start.1 = (bf16[2,2,96,896]{3,2,1,0:T(8,128)(2,1)}, bf16[2,2,96,896]{3,2,1,0:T(8,128)(2,1)S(1)}, u32[]{:S(2)}, u32[]{:S(2)}) collective-permute-start(bf16[2,2,96,896]{3,2,1,0:T(8,128)(2,1)} %get-tuple-element.30), channel_id=1, source_target_pairs={{0,8},{8,16},{16,24},{1,9},{9,17},{17,25},{2,10},{10,18},{18,26},{... | collective-permute-start | bytes 2064392 | tf_op jit(solution)/shard_map/ppermute | solution.py:450
  10.8 2.9 %prepare_weight.1 = (bf16[448,896]{1,0:T(8,128)(2,1)}, bf16[256,896]{1,0:T(8,128)(2,1)}, bf16[192,896]{1,0:T(8,128)(2,1)}) custom-call(s32[7]{0:T(128)} %pad_add_fusion.where_ref, bf16[896,896]{1,0:T(8,128)(2,1)} %weight_ref), custom_call_target="tpu_custom_call" | custom-call | tf_op jit(solution)/shard_map/prepare_weight/pallas_call | solution.py:87
  15.0 5.5 %collective-permute-start.4 = (bf16[448,896]{1,0:T(8,128)(2,1)}, bf16[448,896]{1,0:T(8,128)(2,1)}, u32[]{:S(2)}, u32[]{:S(2)}) collective-permute-start(bf16[448,896]{1,0:T(8,128)(2,1)} %get-tuple-element.32.refs_8_), channel_id=1, source_target_pairs={{0,8},{8,16},{16,24},{1,9},{9,17},{17,25},{2,10},{10,18},{18,26},{... | collective-permute-start | bytes 2408456 | tf_op jit(solution)/shard_map/ppermute | solution.py:467
  20.9 3.6 %collective-permute-done.right_ref = bf16[2,2,96,896]{3,2,1,0:T(8,128)(2,1)S(1)} collective-permute-done((bf16[2,2,96,896]{3,2,1,0:T(8,128)(2,1)}, bf16[2,2,96,896]{3,2,1,0:T(8,128)(2,1)S(1)}, u32[]{:S(2)}, u32[]{:S(2)}) %collective-permute-start) | collective-permute-done | bytes 688160 | tf_op jit(solution)/shard_map/ppermute | solution.py:449
  24.5 1.6 %collective-permute-done.1.left_ref = bf16[2,2,96,896]{3,2,1,0:T(8,128)(2,1)S(1)} collective-permute-done((bf16[2,2,96,896]{3,2,1,0:T(8,128)(2,1)}, bf16[2,2,96,896]{3,2,1,0:T(8,128)(2,1)S(1)}, u32[]{:S(2)}, u32[]{:S(2)}) %collective-permute-start.1) | collective-permute-done | bytes 688160 | tf_op jit(solution)/shard_map/ppermute | solution.py:450
  26.1 5.2 %attention.3 = bf16[2,96,896]{2,1,0:T(8,128)(2,1)} custom-call(s32[7]{0:T(128)S(1)} %copy-done.2, bf16[2,3,96,896]{3,2,1,0:T(8,128)(2,1)S(1)} %add_convert_fusion.own_ref, bf16[2,2,96,896]{3,2,1,0:T(8,128)(2,1)S(1)} %collective-permute-done.right_ref, bf16[2,2,96,896]{3,2,1,0:T(8,128)(2,1)S(1)} %collective-permute-done.1.left_ref), custom_call_target="tpu_custom_call" | custom-call | tf_op jit(solution)/shard_map/attention/pallas_call | solution.py:144
  31.3 2.0 %collective-permute-start.8 = (bf16[1,192,896]{2,1,0:T(8,128)(2,1)}, bf16[1,192,896]{2,1,0:T(8,128)(2,1)S(1)}, u32[]{:S(2)}, u32[]{:S(2)}) collective-permute-start(bf16[1,192,896]{2,1,0:T(8,128)(2,1)} %bitcast.10), channel_id=1, source_target_pairs={{0,4},{2,6},{4,0},{6,2},{1,5},{3,7},{5,1},{7,3},{8,12},{10,14},{12... | collective-permute-start | bytes 1032200 | tf_op jit(solution)/shard_map/ppermute | solution.py:390
  33.3 6.3 %collective-permute-start.9 = (bf16[256,896]{1,0:T(8,128)(2,1)}, bf16[256,896]{1,0:T(8,128)(2,1)}, u32[]{:S(2)}, u32[]{:S(2)}) collective-permute-start(bf16[256,896]{1,0:T(8,128)(2,1)} %get-tuple-element.35), channel_id=1, source_target_pairs={{0,24},{24,0},{1,25},{25,1},{2,26},{26,2},{3,27},{27,3},{4,28},{28... | collective-permute-start | bytes 1376264 | tf_op jit(solution)/shard_map/ppermute | solution.py:469
  40.3 4.5 %attention.2 = bf16[2,96,896]{2,1,0:T(8,128)(2,1)S(1)} custom-call(s32[7]{0:T(128)S(1)} %copy-done.2, bf16[2,3,96,896]{3,2,1,0:T(8,128)(2,1)S(1)} %bitcast.19, bf16[2,2,96,896]{3,2,1,0:T(8,128)(2,1)S(1)} %collective-permute-done.right_ref, bf16[2,2,96,896]{3,2,1,0:T(8,128)(2,1)S(1)} %collective-permute-done.1.left_ref), custom_call_target="tpu_custom_call" | custom-call | tf_op jit(solution)/shard_map/attention/pallas_call | solution.py:144
  44.8 1.6 %collective-permute-start.2 = (bf16[1,192,896]{2,1,0:T(8,128)(2,1)S(1)}, bf16[1,192,896]{2,1,0:T(8,128)(2,1)S(1)}, u32[]{:S(2)}, u32[]{:S(2)}) collective-permute-start(bf16[1,192,896]{2,1,0:T(8,128)(2,1)S(1)} %bitcast.20), channel_id=1, source_target_pairs={{0,1},{1,0},{2,3},{3,2},{4,5},{5,4},{6,7},{7,6},{8,9},{9,8},{10,11... | collective-permute-start | bytes 1032200 | tf_op jit(solution)/shard_map/ppermute | solution.py:390
  48.1 4.9 %collective-permute-done.9.refs_11_ = bf16[256,896]{1,0:T(8,128)(2,1)} collective-permute-done((bf16[256,896]{1,0:T(8,128)(2,1)}, bf16[256,896]{1,0:T(8,128)(2,1)}, u32[]{:S(2)}, u32[]{:S(2)}) %collective-permute-start.9) | collective-permute-done | bytes 458784 | tf_op jit(solution)/shard_map/ppermute | solution.py:469
  53.0 1.5 %collective-permute-start.10 = (bf16[2,192,896]{2,1,0:T(8,128)(2,1)S(1)}, bf16[2,192,896]{2,1,0:T(8,128)(2,1)S(1)}, u32[]{:S(2)}, u32[]{:S(2)}) collective-permute-start(bf16[2,192,896]{2,1,0:T(8,128)(2,1)S(1)} %pad_maximum_fusion.1.refs_4_), channel_id=1, source_target_pairs={{0,1},{1,0},{2,3},{3,2},{4,5},{5,4},{6,7},{7,6},{8,9},{9,8},{10,11... | collective-permute-start | bytes 2064392 | tf_op jit(solution)/shard_map/ppermute | solution.py:390
  54.6 1.6 %collective-permute-start.5 = (bf16[2,192,896]{2,1,0:T(8,128)(2,1)S(1)}, bf16[2,192,896]{2,1,0:T(8,128)(2,1)S(1)}, u32[]{:S(2)}, u32[]{:S(2)}) collective-permute-start(bf16[2,192,896]{2,1,0:T(8,128)(2,1)S(1)} %pad_maximum_fusion.refs_0_), channel_id=1, source_target_pairs={{0,4},{2,6},{4,0},{6,2},{1,5},{3,7},{5,1},{7,3},{8,12},{10,14},{12... | collective-permute-start | bytes 2064392 | tf_op jit(solution)/shard_map/ppermute | solution.py:390
  58.9 10.4 %collective-permute-done.10.refs_5_ = bf16[2,192,896]{2,1,0:T(8,128)(2,1)S(1)} collective-permute-done((bf16[2,192,896]{2,1,0:T(8,128)(2,1)S(1)}, bf16[2,192,896]{2,1,0:T(8,128)(2,1)S(1)}, u32[]{:S(2)}, u32[]{:S(2)}) %collective-permute-start.10) | collective-permute-done | bytes 688160 | tf_op jit(solution)/shard_map/ppermute | solution.py:390
  70.7 5.1 %collective-permute-start.13 = (bf16[192,896]{1,0:T(8,128)(2,1)S(1)}, bf16[192,896]{1,0:T(8,128)(2,1)S(1)}, u32[]{:S(2)}, u32[]{:S(2)}) collective-permute-start(bf16[192,896]{1,0:T(8,128)(2,1)S(1)} %copy-done.8), channel_id=1, source_target_pairs={{0,24},{24,0},{1,25},{25,1},{2,26},{26,2},{3,27},{27,3},{4,28},{28... | collective-permute-start | bytes 1032200 | tf_op jit(solution)/shard_map/ppermute | solution.py:469
  75.8 5.1 %project.3.refs_9_ = f32[2,384,512]{2,1,0:T(8,128)S(1)} custom-call(s32[7]{0:T(128)S(1)} %copy-done.3, bf16[2,192,896]{2,1,0:T(8,128)(2,1)S(1)} %pad_maximum_fusion.refs_0_, bf16[2,192,896]{2,1,0:T(8,128)(2,1)S(1)} %collective-permute-done.5.refs_1_, bf16[2,192,896]{2,1,0:T(8,128)(2,1)S(1)} %collective-permute-done.6.refs_2_, ...), custom_call_target="tpu_custom_call" | custom-call | tf_op jit(solution)/shard_map/project/pallas_call | solution.py:274
  81.0 2.4 %project.4.refs_9_ = f32[2,384,512]{2,1,0:T(8,128)S(1)} custom-call(s32[7]{0:T(128)S(1)} %copy-done.3, bf16[2,192,896]{2,1,0:T(8,128)(2,1)S(1)} %pad_maximum_fusion.refs_0_, bf16[2,192,896]{2,1,0:T(8,128)(2,1)S(1)} %collective-permute-done.5.refs_1_, bf16[2,192,896]{2,1,0:T(8,128)(2,1)S(1)} %collective-permute-done.6.refs_2_, ...), custom_call_target="tpu_custom_call", output_to_operand_aliasing={{}: (10, {})} | custom-call | tf_op jit(solution)/shard_map/project/pallas_call | solution.py:274
  83.4 3.6 %collective-permute-done.13.refs_8_ = bf16[192,896]{1,0:T(8,128)(2,1)S(1)} collective-permute-done((bf16[192,896]{1,0:T(8,128)(2,1)S(1)}, bf16[192,896]{1,0:T(8,128)(2,1)S(1)}, u32[]{:S(2)}, u32[]{:S(2)}) %collective-permute-start.13) | collective-permute-done | bytes 344096 | tf_op jit(solution)/shard_map/ppermute | solution.py:469
  87.0 2.2 %project.5 = (f32[2,384,512]{2,1,0:T(8,128)S(1)}, f32[8,1,768]{2,1,0:T(1,128)S(1)}) custom-call(s32[7]{0:T(128)S(1)} %copy-done.3, bf16[2,192,896]{2,1,0:T(8,128)(2,1)S(1)} %pad_maximum_fusion.refs_0_, bf16[2,192,896]{2,1,0:T(8,128)(2,1)S(1)} %collective-permute-done.5.refs_1_, ...), custom_call_target="tpu_custom_call", output_to_operand_aliasing={{0}: (10, {})} | custom-call | tf_op jit(solution)/shard_map/project/pallas_call | solution.py:274
  89.3 7.1 %all_to_all.10.squares_ref = f32[8,1,768]{2,1,0:T(1,128)S(1)} all-to-all(f32[8,1,768]{2,1,0:T(1,128)S(1)} %get-tuple-element.42), channel_id=1, replica_groups=mesh['frames'=4,'mp'=4,'dp'=2] {'mp','dp'}, dimensions={0} | all-to-all | bytes 49152 | tf_op jit(solution)/shard_map/all_to_all | solution.py:413
  98.5 5.4 %all-to-all-start.1 = ((f32[32,1,512]{2,1,0:T(1,128)}), f32[32,1,512]{2,1,0:T(1,128)S(1)}, u32[]{:S(2)}, u32[]{:S(2)}) async-start(f32[32,1,512]{2,1,0:T(1,128)} %finish.1), calls=%async_computation.1 | async-start | bytes 131072 | tf_op jit(solution)/shard_map/all_to_all | solution.py:413
  104.8 6.7 %all-to-all-done.1.rows_ref = f32[32,1,512]{2,1,0:T(1,128)S(1)} async-done(((f32[32,1,512]{2,1,0:T(1,128)}), f32[32,1,512]{2,1,0:T(1,128)S(1)}, u32[]{:S(2)}, u32[]{:S(2)}) %all-to-all-start.1) | async-done | bytes 65568 | tf_op jit(solution)/shard_map/all_to_all | solution.py:413
  112.1 1.7 %conclude.1 = (f32[1]{0:T(128)}, f32[896]{0:T(1024)}) custom-call(s32[7]{0:T(128)} %pad_add_fusion.where_ref, f32[32,1,512]{2,1,0:T(1,128)} %copy-done.6, f32[1,896]{1,0:T(1,128)} %broadcast_in_dim.10.gain_ref), custom_call_target="tpu_custom_call" | custom-call | tf_op jit(solution)/shard_map/conclude/pallas_call | solution.py:371
  (53 shorter events, 14.0 us)
Async XLA Ops:
  0.6 19.9 %copy-start = (bf16[1,2,96,3,896]{4,2,3,1,0:T(8,128)(2,1)S(1)}, bf16[1,2,96,3,896]{4,2,3,1,0:T(8,128)(2,1)}, u32[]{:S(2)}) copy-start(bf16[1,2,96,3,896]{4,2,3,1,0:T(8,128)(2,1)} %param.5) | copy-start | bytes 3096580
  0.7 19.9 %copy-start.5 = (bf16[1,2,96,3,896]{4,2,3,1,0:T(8,128)(2,1)S(1)}, bf16[1,2,96,3,896]{4,2,3,1,0:T(8,128)(2,1)}, u32[]{:S(2)}) copy-start(bf16[1,2,96,3,896]{4,2,3,1,0:T(8,128)(2,1)} %param.6) | copy-start | bytes 3096580
  3.1 21.4 %collective-permute-start = (bf16[2,2,96,896]{3,2,1,0:T(8,128)(2,1)}, bf16[2,2,96,896]{3,2,1,0:T(8,128)(2,1)S(1)}, u32[]{:S(2)}, u32[]{:S(2)}) collective-permute-start(bf16[2,2,96,896]{3,2,1,0:T(8,128)(2,1)} %get-tuple-element.29), channel_id=1, source_target_pairs={{8,0},{16,8},{24,16},{9,1},{17,9},{25,17},{10,2},{18,10},{26,18},{... | collective-permute-start | bytes 2064392 | tf_op jit(solution)/shard_map/ppermute | solution.py:449
  4.4 21.7 %collective-permute-start.1 = (bf16[2,2,96,896]{3,2,1,0:T(8,128)(2,1)}, bf16[2,2,96,896]{3,2,1,0:T(8,128)(2,1)S(1)}, u32[]{:S(2)}, u32[]{:S(2)}) collective-permute-start(bf16[2,2,96,896]{3,2,1,0:T(8,128)(2,1)} %get-tuple-element.30), channel_id=1, source_target_pairs={{0,8},{8,16},{16,24},{1,9},{9,17},{17,25},{2,10},{10,18},{18,26},{... | collective-permute-start | bytes 2064392 | tf_op jit(solution)/shard_map/ppermute | solution.py:450
  13.6 12.5 %copy-start.2 = (s32[7]{0:T(128)S(1)}, s32[7]{0:T(128)}, u32[]{:S(2)}) copy-start(s32[7]{0:T(128)} %pad_add_fusion.where_ref) | copy-start | bytes 88
  13.6 41.0 %collective-permute-start.3 = (bf16[448,896]{1,0:T(8,128)(2,1)}, bf16[448,896]{1,0:T(8,128)(2,1)}, u32[]{:S(2)}, u32[]{:S(2)}) collective-permute-start(bf16[448,896]{1,0:T(8,128)(2,1)} %get-tuple-element.32.refs_8_), channel_id=1, source_target_pairs={{8,0},{16,8},{24,16},{9,1},{17,9},{25,17},{10,2},{18,10},{26,18},{... | collective-permute-start | bytes 2408456 | tf_op jit(solution)/shard_map/ppermute | solution.py:467
  15.0 39.6 %collective-permute-start.4 = (bf16[448,896]{1,0:T(8,128)(2,1)}, bf16[448,896]{1,0:T(8,128)(2,1)}, u32[]{:S(2)}, u32[]{:S(2)}) collective-permute-start(bf16[448,896]{1,0:T(8,128)(2,1)} %get-tuple-element.32.refs_8_), channel_id=1, source_target_pairs={{0,8},{8,16},{16,24},{1,9},{9,17},{17,25},{2,10},{10,18},{18,26},{... | collective-permute-start | bytes 2408456 | tf_op jit(solution)/shard_map/ppermute | solution.py:467
  20.8 18.8 %copy-start.7 = (f32[896]{0:T(1024)S(1)}, f32[896]{0:T(1024)}, u32[]{:S(2)}) copy-start(f32[896]{0:T(1024)} %param.8) | copy-start | bytes 10756
  31.3 15.7 %collective-permute-start.8 = (bf16[1,192,896]{2,1,0:T(8,128)(2,1)}, bf16[1,192,896]{2,1,0:T(8,128)(2,1)S(1)}, u32[]{:S(2)}, u32[]{:S(2)}) collective-permute-start(bf16[1,192,896]{2,1,0:T(8,128)(2,1)} %bitcast.10), channel_id=1, source_target_pairs={{0,4},{2,6},{4,0},{6,2},{1,5},{3,7},{5,1},{7,3},{8,12},{10,14},{12... | collective-permute-start | bytes 1032200 | tf_op jit(solution)/shard_map/ppermute | solution.py:390
  33.3 19.7 %collective-permute-start.9 = (bf16[256,896]{1,0:T(8,128)(2,1)}, bf16[256,896]{1,0:T(8,128)(2,1)}, u32[]{:S(2)}, u32[]{:S(2)}) collective-permute-start(bf16[256,896]{1,0:T(8,128)(2,1)} %get-tuple-element.35), channel_id=1, source_target_pairs={{0,24},{24,0},{1,25},{25,1},{2,26},{26,2},{3,27},{27,3},{4,28},{28... | collective-permute-start | bytes 1376264 | tf_op jit(solution)/shard_map/ppermute | solution.py:469
  44.8 9.7 %collective-permute-start.2 = (bf16[1,192,896]{2,1,0:T(8,128)(2,1)S(1)}, bf16[1,192,896]{2,1,0:T(8,128)(2,1)S(1)}, u32[]{:S(2)}, u32[]{:S(2)}) collective-permute-start(bf16[1,192,896]{2,1,0:T(8,128)(2,1)S(1)} %bitcast.20), channel_id=1, source_target_pairs={{0,1},{1,0},{2,3},{3,2},{4,5},{5,4},{6,7},{7,6},{8,9},{9,8},{10,11... | collective-permute-start | bytes 1032200 | tf_op jit(solution)/shard_map/ppermute | solution.py:390
  53.0 16.3 %collective-permute-start.10 = (bf16[2,192,896]{2,1,0:T(8,128)(2,1)S(1)}, bf16[2,192,896]{2,1,0:T(8,128)(2,1)S(1)}, u32[]{:S(2)}, u32[]{:S(2)}) collective-permute-start(bf16[2,192,896]{2,1,0:T(8,128)(2,1)S(1)} %pad_maximum_fusion.1.refs_4_), channel_id=1, source_target_pairs={{0,1},{1,0},{2,3},{3,2},{4,5},{5,4},{6,7},{7,6},{8,9},{9,8},{10,11... | collective-permute-start | bytes 2064392 | tf_op jit(solution)/shard_map/ppermute | solution.py:390
  54.6 16.1 %collective-permute-start.5 = (bf16[2,192,896]{2,1,0:T(8,128)(2,1)S(1)}, bf16[2,192,896]{2,1,0:T(8,128)(2,1)S(1)}, u32[]{:S(2)}, u32[]{:S(2)}) collective-permute-start(bf16[2,192,896]{2,1,0:T(8,128)(2,1)S(1)} %pad_maximum_fusion.refs_0_), channel_id=1, source_target_pairs={{0,4},{2,6},{4,0},{6,2},{1,5},{3,7},{5,1},{7,3},{8,12},{10,14},{12... | collective-permute-start | bytes 2064392 | tf_op jit(solution)/shard_map/ppermute | solution.py:390
  56.2 14.5 %copy-start.8 = (bf16[192,896]{1,0:T(8,128)(2,1)S(1)}, bf16[192,896]{1,0:T(8,128)(2,1)}, u32[]{:S(2)}) copy-start(bf16[192,896]{1,0:T(8,128)(2,1)} %get-tuple-element.37) | copy-start | bytes 1032196
  56.2 19.7 %copy-start.3 = (s32[7]{0:T(128)S(1)}, s32[7]{0:T(128)}, u32[]{:S(2)}) copy-start(s32[7]{0:T(128)} %pad_add_fusion.where_ref) | copy-start | bytes 88
  56.2 14.5 %collective-permute-start.11 = (bf16[2,192,896]{2,1,0:T(8,128)(2,1)S(1)}, bf16[2,192,896]{2,1,0:T(8,128)(2,1)S(1)}, u32[]{:S(2)}, u32[]{:S(2)}) collective-permute-start(bf16[2,192,896]{2,1,0:T(8,128)(2,1)S(1)} %pad_maximum_fusion.1.refs_4_), channel_id=1, source_target_pairs={{0,2},{2,0},{4,6},{6,4},{1,3},{3,1},{5,7},{7,5},{8,10},{10,8},{12,... | collective-permute-start | bytes 2064392 | tf_op jit(solution)/shard_map/ppermute | solution.py:390
  57.5 23.5 %collective-permute-start.14 = (bf16[448,896]{1,0:T(8,128)(2,1)S(1)}, bf16[448,896]{1,0:T(8,128)(2,1)S(1)}, u32[]{:S(2)}, u32[]{:S(2)}) collective-permute-start(bf16[448,896]{1,0:T(8,128)(2,1)S(1)} %select_select_fusion), channel_id=1, source_target_pairs={{0,16},{8,0},{16,24},{24,8},{1,17},{9,1},{17,25},{25,9},{2,18},{10... | collective-permute-start | bytes 2408456 | tf_op jit(solution)/shard_map/ppermute | solution.py:480
  58.8 17.0 %collective-permute-start.6 = (bf16[2,192,896]{2,1,0:T(8,128)(2,1)S(1)}, bf16[2,192,896]{2,1,0:T(8,128)(2,1)S(1)}, u32[]{:S(2)}, u32[]{:S(2)}) collective-permute-start(bf16[2,192,896]{2,1,0:T(8,128)(2,1)S(1)} %pad_maximum_fusion.refs_0_), channel_id=1, source_target_pairs={{0,2},{2,0},{4,6},{6,4},{1,3},{3,1},{5,7},{7,5},{8,10},{10,8},{12,... | collective-permute-start | bytes 2064392 | tf_op jit(solution)/shard_map/ppermute | solution.py:390
  69.3 6.5 %collective-permute-start.12 = (bf16[2,192,896]{2,1,0:T(8,128)(2,1)S(1)}, bf16[2,192,896]{2,1,0:T(8,128)(2,1)S(1)}, u32[]{:S(2)}, u32[]{:S(2)}) collective-permute-start(bf16[2,192,896]{2,1,0:T(8,128)(2,1)S(1)} %collective-permute-done.10.refs_5_), channel_id=1, source_target_pairs={{0,2},{2,0},{4,6},{6,4},{1,3},{3,1},{5,7},{7,5},{8,10},{10,8},{12,... | collective-permute-start | bytes 2064392 | tf_op jit(solution)/shard_map/ppermute | solution.py:390
  70.7 5.1 %collective-permute-start.7 = (bf16[2,192,896]{2,1,0:T(8,128)(2,1)S(1)}, bf16[2,192,896]{2,1,0:T(8,128)(2,1)S(1)}, u32[]{:S(2)}, u32[]{:S(2)}) collective-permute-start(bf16[2,192,896]{2,1,0:T(8,128)(2,1)S(1)} %collective-permute-done.5.refs_1_), channel_id=1, source_target_pairs={{0,2},{2,0},{4,6},{6,4},{1,3},{3,1},{5,7},{7,5},{8,10},{10,8},{12,... | collective-permute-start | bytes 2064392 | tf_op jit(solution)/shard_map/ppermute | solution.py:390
  70.7 16.3 %collective-permute-start.13 = (bf16[192,896]{1,0:T(8,128)(2,1)S(1)}, bf16[192,896]{1,0:T(8,128)(2,1)S(1)}, u32[]{:S(2)}, u32[]{:S(2)}) collective-permute-start(bf16[192,896]{1,0:T(8,128)(2,1)S(1)} %copy-done.8), channel_id=1, source_target_pairs={{0,24},{24,0},{1,25},{25,1},{2,26},{26,2},{3,27},{27,3},{4,28},{28... | collective-permute-start | bytes 1032200 | tf_op jit(solution)/shard_map/ppermute | solution.py:469
  83.4 12.9 %copy-start.4 = (f32[512]{0:T(512)S(1)}, f32[512]{0:T(512)}, u32[]{:S(2)}) copy-start(f32[512]{0:T(512)} %pad.9) | copy-start | bytes 6148
  96.6 7.3 %collective-permute-start.15 = (bf16[2,96,448]{2,1,0:T(8,128)(2,1)S(1)}, bf16[2,96,448]{2,1,0:T(8,128)(2,1)S(1)}, u32[]{:S(2)}, u32[]{:S(2)}) collective-permute-start(bf16[2,96,448]{2,1,0:T(8,128)(2,1)S(1)} %bitcast.27), channel_id=1, source_target_pairs={{0,1},{1,0},{2,3},{3,2},{4,5},{5,4},{6,7},{7,6},{8,9},{9,8},{10,11... | collective-permute-start | bytes 516104 | tf_op jit(solution)/shard_map/ppermute | solution.py:390
  98.5 13.0 %all-to-all-start.1 = ((f32[32,1,512]{2,1,0:T(1,128)}), f32[32,1,512]{2,1,0:T(1,128)S(1)}, u32[]{:S(2)}, u32[]{:S(2)}) async-start(f32[32,1,512]{2,1,0:T(1,128)} %finish.1), calls=%async_computation.1 | async-start | bytes 131072 | tf_op jit(solution)/shard_map/all_to_all | solution.py:413
  (3 other events, 21.4 us)

commit v7 on v4

--- a/solution.py
+++ b/solution.py
@@ -242,24 +242,22 @@
                 wide = whole_lanes(size)
                 if wide > size:
                     held[shard, size:wide] = jnp.zeros((wide - size, depth), held.dtype)
-                for clip in range(clip_count):
-                    out_ref[clip, :, pl.ds(first, wide)] += lax.dot_general(
-                        rows[shard, pl.ds(clip * row_count, row_count)],
-                        held[shard, pl.ds(0, wide)],
-                        (((1,), (1,)), ((), ())),
-                        preferred_element_type=jnp.float32,
-                    )
+                out_ref[:, pl.ds(first, wide)] += lax.dot_general(
+                    rows[shard],
+                    held[shard, pl.ds(0, wide)],
+                    (((1,), (1,)), ((), ())),
+                    preferred_element_type=jnp.float32,
+                )
 
         if peers:
             diagonal = on_diagonal()
-            for clip in range(clip_count):
-                for first in range(0, row_count, LANES):
-                    piece = out_ref[clip, pl.ds(first, LANES)]
-                    sums = jnp.sum(piece * piece, axis=1, keepdims=True)
-                    sums = jnp.sum(jnp.where(diagonal, sums, 0.0), axis=0, keepdims=True)
-                    squares_ref[:, :, pl.ds(clip * row_count + first, LANES)] = jnp.broadcast_to(
-                        sums[None], (peers, 1, LANES)
-                    )
+            for first in range(0, clip_count * row_count, LANES):
+                piece = out_ref[pl.ds(first, LANES)]
+                sums = jnp.sum(piece * piece, axis=1, keepdims=True)
+                sums = jnp.sum(jnp.where(diagonal, sums, 0.0), axis=0, keepdims=True)
+                squares_ref[:, :, pl.ds(first, LANES)] = jnp.broadcast_to(
+                    sums[None], (peers, 1, LANES)
+                )
 
     operands = [*flat, *(array for _, array, _, _ in shards)]
     in_specs = [pl.BlockSpec(memory_space=pl.ANY) for _ in operands]
@@ -268,7 +266,7 @@
         operands.append(total)
         in_specs.append(pl.BlockSpec(memory_space=pltpu.VMEM))
         aliases = {len(operands): 0}
-    out_shape = [jax.ShapeDtypeStruct((clip_count, row_count, lanes), jnp.float32)]
+    out_shape = [jax.ShapeDtypeStruct((clip_count * row_count, lanes), jnp.float32)]
     if peers:
         out_shape.append(jax.ShapeDtypeStruct((peers, 1, clip_count * row_count), jnp.float32))
     return pl.pallas_call(
@@ -297,15 +295,16 @@
     diagonal = on_diagonal()
     scales = []
     for first in range(0, row_count, LANES):
-        at = pl.ds(pl.multiple_of(clip * row_count + first, LANES), LANES)
+        at = pl.ds(clip * row_count + first, LANES)
         mean = jnp.sum(squares_ref[:, :, at], axis=0) / model_width
         scale = jnp.broadcast_to(lax.rsqrt(mean + epsilon), (LANES, LANES))
         scales.append(jnp.sum(jnp.where(diagonal, scale, 0.0), axis=1, keepdims=True))
     return jnp.concatenate(scales, axis=0)
 
 
-def finish(total, squares, gain, columns, model_width, devices):
-    clip_count, row_count, lanes = total.shape
+def finish(total, squares, gain, clip_count, columns, model_width, devices):
+    rows, lanes = total.shape
+    row_count = rows // clip_count
     near_rows = row_count // 2
 
     def kernel(total_ref, squares_ref, gain_ref, row_ref):
@@ -313,8 +312,8 @@
         row = jnp.zeros((1, lanes), jnp.float32)
         for clip in range(clip_count):
             scale = row_scales(squares_ref, clip, row_count, model_width)
-            clean = total_ref[clip, :near_rows] * scale[:near_rows]
-            difference = total_ref[clip, near_rows:] * scale[near_rows:] - clean
+            clean = total_ref[pl.ds(clip * row_count, near_rows)] * scale[:near_rows]
+            difference = total_ref[pl.ds(clip * row_count + near_rows, near_rows)] * scale[near_rows:] - clean
             sums = jnp.sum(difference * difference, axis=0, keepdims=True)
             penalty = jnp.sum(sums * gain_ref[...] * gain_ref[...], axis=1, keepdims=True)
             row = row + sums + jnp.where(lane == columns + clip, penalty, 0.0)
@@ -328,14 +327,15 @@
     )(total, squares, gain)
 
 
-def make_features(total, squares, gain, model_width):
-    clip_count, row_count, lanes = total.shape
+def make_features(total, squares, gain, clip_count, model_width):
+    rows, lanes = total.shape
+    row_count = rows // clip_count
     near_rows = row_count // 2
 
     def kernel(total_ref, squares_ref, gain_ref, features_ref):
         for clip in range(clip_count):
             scale = row_scales(squares_ref, clip, row_count, model_width)
-            clean = total_ref[clip, :near_rows] * scale[:near_rows]
+            clean = total_ref[pl.ds(clip * row_count, near_rows)] * scale[:near_rows]
             features_ref[clip] = (clean * gain_ref[...]).astype(jnp.bfloat16)
 
     return pl.pallas_call(
@@ -380,7 +380,7 @@
             jax.ShapeDtypeStruct((1,), jnp.float32),
             jax.ShapeDtypeStruct((gain.shape[1],), jnp.float32),
         ],
-        compiler_params=pltpu.CompilerParams(vmem_limit_bytes=60 * 1024 * 1024),
+        compiler_params=pltpu.CompilerParams(vmem_limit_bytes=4 * 1024 * 1024),
         name="conclude",
     )(where, rows, gain)
 
@@ -526,9 +526,15 @@
 
     squares = collect(squares, ("mp", "dp"))
     sums = finish(
-        total, squares, gain_row, half, model_width, slab_count * model_count * clip_count
-    )
-    features = make_features(total, squares, gain_row, model_width)
+        total,
+        squares,
+        gain_row,
+        clip_count,
+        half,
+        model_width,
+        slab_count * model_count * clip_count,
+    )
+    features = make_features(total, squares, gain_row, clip_count, model_width)
     sums = collect(sums, ("frames", "mp", "dp"))
 
     features = features[..., :half].reshape(clip_count, slots, tile_len, half)

time: 112 us -> 111 us (level)
  local copies, waits for them, and re-layouts: 1.33 us -> 0.12 us
  transfers between devices with their start and end apart: 18 -> 18, of which waited for: 9 -> 9; matrix products, arithmetic and copies ran while one was open for 3% -> 3% of each run, Pallas kernels for 18% -> 19%
where the time goes in v7:
time: 111 us
  starting transfers between devices  37.7 us (34%)
  waiting for transfers between devices  34.1 us (31%)
  Pallas kernels  27.1 us (24%)
  blocking collectives  7.87 us (7%)
  other arithmetic  3.13 us (3%)
    ppermute x9, waiting for transfers between devices, swap(): return lax.ppermute(array, axis, [(i, i ^ distance) for i in range(count)])  15 us
    ppermute x2, starting transfers between devices, local(): lax.ppermute(block, 'frames', [(0, last), (last, 0)])  10.1 us
    pallas_call x2, Pallas kernels, attention(): pl.pallas_call(attend_kernel, grid_spec=pltpu.PrefetchScalarGridSpec(num_...  9.76 us
    pallas_call x2, Pallas kernels, project(): pl.pallas_call(kernel, in_specs=[pl.BlockSpec(memory_space=pltpu.SMEM)] +...  9.34 us
    ppermute x2, waiting for transfers between devices, local(): lax.ppermute(block, 'frames', [(0, last), (last, 0)])  9.28 us
    all_to_all x1, blocking collectives, collect(): return lax.all_to_all(rows, axes, split_axis=0, concat_axis=0, tiled=True)  7.87 us
    ppermute x9, starting transfers between devices, swap(): return lax.ppermute(array, axis, [(i, i ^ distance) for i in range(count)])  7.8 us
    all_to_all x1, waiting for transfers between devices, collect(): return lax.all_to_all(rows, axes, split_axis=0, concat_axis=0, tiled=True)  6.35 us
  transfers between devices with their start and end apart: 18, of which 9 were waited for; matrix products, arithmetic and copies ran while one was open for 3% of the time, Pallas kernels for 19%

profile of v7, /device:TPU:0, one launch (start us, length us, event | category | flops | bytes accessed | tf_op | source)
XLA Modules:
  0.0 111.0 jit_solution(7757272214840849671)
XLA Ops:
  0.6 2.4 %prepare_halo.1 = (bf16[2,2,96,896]{3,2,1,0:T(8,128)(2,1)}, bf16[2,2,96,896]{3,2,1,0:T(8,128)(2,1)}) custom-call(bf16[2,3,96,896]{3,2,1,0:T(8,128)(2,1)} %bitcast.17, bf16[2,3,96,896]{3,2,1,0:T(8,128)(2,1)} %bitcast.24), custom_call_target="tpu_custom_call" | custom-call | tf_op jit(solution)/shard_map/prepare_halo/pallas_call | solution.py:53
  3.0 1.3 %collective-permute-start = (bf16[2,2,96,896]{3,2,1,0:T(8,128)(2,1)}, bf16[2,2,96,896]{3,2,1,0:T(8,128)(2,1)S(1)}, u32[]{:S(2)}, u32[]{:S(2)}) collective-permute-start(bf16[2,2,96,896]{3,2,1,0:T(8,128)(2,1)} %get-tuple-element.32), channel_id=1, source_target_pairs={{8,0},{16,8},{24,16},{9,1},{17,9},{25,17},{10,2},{18,10},{26,18},{... | collective-permute-start | bytes 2064392 | tf_op jit(solution)/shard_map/ppermute | solution.py:449
  4.3 5.6 %collective-permute-start.1 = (bf16[2,2,96,896]{3,2,1,0:T(8,128)(2,1)}, bf16[2,2,96,896]{3,2,1,0:T(8,128)(2,1)S(1)}, u32[]{:S(2)}, u32[]{:S(2)}) collective-permute-start(bf16[2,2,96,896]{3,2,1,0:T(8,128)(2,1)} %get-tuple-element.33), channel_id=1, source_target_pairs={{0,8},{8,16},{16,24},{1,9},{9,17},{17,25},{2,10},{10,18},{18,26},{... | collective-permute-start | bytes 2064392 | tf_op jit(solution)/shard_map/ppermute | solution.py:450
  10.6 2.9 %prepare_weight.1 = (bf16[448,896]{1,0:T(8,128)(2,1)}, bf16[128,896]{1,0:T(8,128)(2,1)}, bf16[320,896]{1,0:T(8,128)(2,1)}) custom-call(s32[7]{0:T(128)} %pad_add_fusion.where_ref, bf16[896,896]{1,0:T(8,128)(2,1)} %weight_ref), custom_call_target="tpu_custom_call" | custom-call | tf_op jit(solution)/shard_map/prepare_weight/pallas_call | solution.py:87
  13.5 4.9 %collective-permute-start.4 = (bf16[448,896]{1,0:T(8,128)(2,1)}, bf16[448,896]{1,0:T(8,128)(2,1)}, u32[]{:S(2)}, u32[]{:S(2)}) collective-permute-start(bf16[448,896]{1,0:T(8,128)(2,1)} %get-tuple-element.35.refs_8_), channel_id=1, source_target_pairs={{0,8},{8,16},{16,24},{1,9},{9,17},{17,25},{2,10},{10,18},{18,26},{... | collective-permute-start | bytes 2408456 | tf_op jit(solution)/shard_map/ppermute | solution.py:467
  19.7 5.1 %collective-permute-start.9 = (bf16[128,896]{1,0:T(8,128)(2,1)}, bf16[128,896]{1,0:T(8,128)(2,1)}, u32[]{:S(2)}, u32[]{:S(2)}) collective-permute-start(bf16[128,896]{1,0:T(8,128)(2,1)} %get-tuple-element.38), channel_id=1, source_target_pairs={{0,24},{24,0},{1,25},{25,1},{2,26},{26,2},{3,27},{27,3},{4,28},{28... | collective-permute-start | bytes 688136 | tf_op jit(solution)/shard_map/ppermute | solution.py:469
  26.1 5.2 %attention.2 = bf16[2,96,896]{2,1,0:T(8,128)(2,1)} custom-call(s32[7]{0:T(128)S(1)} %copy-done.2, bf16[2,3,96,896]{3,2,1,0:T(8,128)(2,1)S(1)} %bitcast.18, bf16[2,2,96,896]{3,2,1,0:T(8,128)(2,1)S(1)} %collective-permute-done.right_ref, bf16[2,2,96,896]{3,2,1,0:T(8,128)(2,1)S(1)} %collective-permute-done.1.left_ref), custom_call_target="tpu_custom_call" | custom-call | tf_op jit(solution)/shard_map/attention/pallas_call | solution.py:144
  31.3 2.0 %collective-permute-start.2 = (bf16[1,192,896]{2,1,0:T(8,128)(2,1)}, bf16[1,192,896]{2,1,0:T(8,128)(2,1)}, u32[]{:S(2)}, u32[]{:S(2)}) collective-permute-start(bf16[1,192,896]{2,1,0:T(8,128)(2,1)} %bitcast.8), channel_id=1, source_target_pairs={{0,1},{1,0},{2,3},{3,2},{4,5},{5,4},{6,7},{7,6},{8,9},{9,8},{10,11... | collective-permute-start | bytes 1032200 | tf_op jit(solution)/shard_map/ppermute | solution.py:390
  33.6 4.5 %attention.3 = bf16[2,96,896]{2,1,0:T(8,128)(2,1)S(1)} custom-call(s32[7]{0:T(128)S(1)} %copy-done.2, bf16[2,3,96,896]{3,2,1,0:T(8,128)(2,1)S(1)} %add_convert_fusion.own_ref, bf16[2,2,96,896]{3,2,1,0:T(8,128)(2,1)S(1)} %collective-permute-done.right_ref, bf16[2,2,96,896]{3,2,1,0:T(8,128)(2,1)S(1)} %collective-permute-done.1.left_ref), custom_call_target="tpu_custom_call" | custom-call | tf_op jit(solution)/shard_map/attention/pallas_call | solution.py:144
  38.2 1.6 %collective-permute-start.8 = (bf16[1,192,896]{2,1,0:T(8,128)(2,1)S(1)}, bf16[1,192,896]{2,1,0:T(8,128)(2,1)S(1)}, u32[]{:S(2)}, u32[]{:S(2)}) collective-permute-start(bf16[1,192,896]{2,1,0:T(8,128)(2,1)S(1)} %bitcast.20), channel_id=1, source_target_pairs={{0,4},{2,6},{4,0},{6,2},{1,5},{3,7},{5,1},{7,3},{8,12},{10,14},{12... | collective-permute-start | bytes 1032200 | tf_op jit(solution)/shard_map/ppermute | solution.py:390
  41.0 2.3 %collective-permute-done.4.refs_10_ = bf16[448,896]{1,0:T(8,128)(2,1)} collective-permute-done((bf16[448,896]{1,0:T(8,128)(2,1)}, bf16[448,896]{1,0:T(8,128)(2,1)}, u32[]{:S(2)}, u32[]{:S(2)}) %collective-permute-start.4) | collective-permute-done | bytes 802848 | tf_op jit(solution)/shard_map/ppermute | solution.py:467
  43.3 1.3 %collective-permute-start.12 = (bf16[448,896]{1,0:T(8,128)(2,1)}, bf16[448,896]{1,0:T(8,128)(2,1)S(1)}, u32[]{:S(2)}, u32[]{:S(2)}) collective-permute-start(bf16[448,896]{1,0:T(8,128)(2,1)} %collective-permute-done.3.refs_9_), channel_id=1, source_target_pairs={{8,0},{16,8},{9,1},{17,9},{10,2},{18,10},{11,3},{19,11},{12,4},{20... | collective-permute-start | bytes 2408456 | tf_op jit(solution)/shard_map/ppermute | solution.py:479
  45.6 2.6 %collective-permute-done.9.refs_13_ = bf16[128,896]{1,0:T(8,128)(2,1)} collective-permute-done((bf16[128,896]{1,0:T(8,128)(2,1)}, bf16[128,896]{1,0:T(8,128)(2,1)}, u32[]{:S(2)}, u32[]{:S(2)}) %collective-permute-start.9) | collective-permute-done | bytes 229408 | tf_op jit(solution)/shard_map/ppermute | solution.py:469
  48.1 1.5 %collective-permute-start.10 = (bf16[2,192,896]{2,1,0:T(8,128)(2,1)S(1)}, bf16[2,192,896]{2,1,0:T(8,128)(2,1)S(1)}, u32[]{:S(2)}, u32[]{:S(2)}) collective-permute-start(bf16[2,192,896]{2,1,0:T(8,128)(2,1)S(1)} %pad_maximum_fusion.1.refs_4_), channel_id=1, source_target_pairs={{0,1},{1,0},{2,3},{3,2},{4,5},{5,4},{6,7},{7,6},{8,9},{9,8},{10,11... | collective-permute-start | bytes 2064392 | tf_op jit(solution)/shard_map/ppermute | solution.py:390
  49.6 1.5 %collective-permute-start.5 = (bf16[2,192,896]{2,1,0:T(8,128)(2,1)S(1)}, bf16[2,192,896]{2,1,0:T(8,128)(2,1)S(1)}, u32[]{:S(2)}, u32[]{:S(2)}) collective-permute-start(bf16[2,192,896]{2,1,0:T(8,128)(2,1)S(1)} %pad_maximum_fusion.refs_0_), channel_id=1, source_target_pairs={{0,4},{2,6},{4,0},{6,2},{1,5},{3,7},{5,1},{7,3},{8,12},{10,14},{12... | collective-permute-start | bytes 2064392 | tf_op jit(solution)/shard_map/ppermute | solution.py:390
  51.1 13.2 %collective-permute-done.10.refs_5_ = bf16[2,192,896]{2,1,0:T(8,128)(2,1)S(1)} collective-permute-done((bf16[2,192,896]{2,1,0:T(8,128)(2,1)S(1)}, bf16[2,192,896]{2,1,0:T(8,128)(2,1)S(1)}, u32[]{:S(2)}, u32[]{:S(2)}) %collective-permute-start.10) | collective-permute-done | bytes 688160 | tf_op jit(solution)/shard_map/ppermute | solution.py:390
  66.1 5.1 %collective-permute-start.15 = (bf16[320,896]{1,0:T(8,128)(2,1)S(1)}, bf16[320,896]{1,0:T(8,128)(2,1)S(1)}, u32[]{:S(2)}, u32[]{:S(2)}) collective-permute-start(bf16[320,896]{1,0:T(8,128)(2,1)S(1)} %copy-done.5), channel_id=1, source_target_pairs={{0,24},{24,0},{1,25},{25,1},{2,26},{26,2},{3,27},{27,3},{4,28},{28... | collective-permute-start | bytes 1720328 | tf_op jit(solution)/shard_map/ppermute | solution.py:469
  71.2 6.8 %project.2.refs_9_ = f32[768,512]{1,0:T(8,128)S(1)} custom-call(s32[7]{0:T(128)S(1)} %copy-done.2, bf16[2,192,896]{2,1,0:T(8,128)(2,1)S(1)} %pad_maximum_fusion.refs_0_, bf16[2,192,896]{2,1,0:T(8,128)(2,1)S(1)} %collective-permute-done.5.refs_1_, bf16[2,192,896]{2,1,0:T(8,128)(2,1)S(1)} %collective-permute-done.6.refs_2_, ...), custom_call_target="tpu_custom_call" | custom-call | tf_op jit(solution)/shard_map/project/pallas_call | solution.py:272
  78.0 6.7 %collective-permute-done.15.refs_8_ = bf16[320,896]{1,0:T(8,128)(2,1)S(1)} collective-permute-done((bf16[320,896]{1,0:T(8,128)(2,1)S(1)}, bf16[320,896]{1,0:T(8,128)(2,1)S(1)}, u32[]{:S(2)}, u32[]{:S(2)}) %collective-permute-start.15) | collective-permute-done | bytes 573472 | tf_op jit(solution)/shard_map/ppermute | solution.py:469
  84.7 2.6 %project.3 = (f32[768,512]{1,0:T(8,128)S(1)}, f32[8,1,768]{2,1,0:T(1,128)S(1)}) custom-call(s32[7]{0:T(128)S(1)} %copy-done.2, bf16[2,192,896]{2,1,0:T(8,128)(2,1)S(1)} %pad_maximum_fusion.refs_0_, bf16[2,192,896]{2,1,0:T(8,128)(2,1)S(1)} %collective-permute-done.5.refs_1_, ...), custom_call_target="tpu_custom_call", output_to_operand_aliasing={{0}: (10, {})} | custom-call | tf_op jit(solution)/shard_map/project/pallas_call | solution.py:272
  87.3 7.9 %all_to_all.10.squares_ref = f32[8,1,768]{2,1,0:T(1,128)S(1)} all-to-all(f32[8,1,768]{2,1,0:T(1,128)S(1)} %get-tuple-element.48), channel_id=1, replica_groups=mesh['frames'=4,'mp'=4,'dp'=2] {'mp','dp'}, dimensions={0} | all-to-all | bytes 49152 | tf_op jit(solution)/shard_map/all_to_all | solution.py:413
  97.3 4.7 %all-to-all-start.1 = ((f32[32,1,512]{2,1,0:T(1,128)}), f32[32,1,512]{2,1,0:T(1,128)S(1)}, u32[]{:S(2)}, u32[]{:S(2)}) async-start(f32[32,1,512]{2,1,0:T(1,128)} %finish.1), calls=%async_computation.1 | async-start | bytes 131072 | tf_op jit(solution)/shard_map/all_to_all | solution.py:413
  103.3 6.3 %all-to-all-done.1.rows_ref = f32[32,1,512]{2,1,0:T(1,128)S(1)} async-done(((f32[32,1,512]{2,1,0:T(1,128)}), f32[32,1,512]{2,1,0:T(1,128)S(1)}, u32[]{:S(2)}, u32[]{:S(2)}) %all-to-all-start.1) | async-done | bytes 65568 | tf_op jit(solution)/shard_map/all_to_all | solution.py:413
  109.7 1.4 %conclude.1 = (f32[1]{0:T(128)}, f32[896]{0:T(1024)}) custom-call(s32[7]{0:T(128)S(1)} %copy-done.2, f32[32,1,512]{2,1,0:T(1,128)S(1)} %all-to-all-done.1.rows_ref, f32[1,896]{1,0:T(1,128)S(1)} %broadcast_in_dim.10.gain_ref), custom_call_target="tpu_custom_call" | custom-call | tf_op jit(solution)/shard_map/conclude/pallas_call | solution.py:371
  (47 shorter events, 10.9 us)
Async XLA Ops:
  0.6 9.3 %copy-start.6 = (s32[1,8]{1,0:T(1,128)S(1)}, s32[1,8]{1,0:T(1,128)}, u32[]{:S(2)}) copy-start(s32[1,8]{1,0:T(1,128)} %param.9) | copy-start | bytes 100
  0.6 25.4 %copy-start = (bf16[1,2,96,3,896]{4,2,3,1,0:T(8,128)(2,1)S(1)}, bf16[1,2,96,3,896]{4,2,3,1,0:T(8,128)(2,1)}, u32[]{:S(2)}) copy-start(bf16[1,2,96,3,896]{4,2,3,1,0:T(8,128)(2,1)} %param.5) | copy-start | bytes 3096580
  3.0 21.8 %collective-permute-start = (bf16[2,2,96,896]{3,2,1,0:T(8,128)(2,1)}, bf16[2,2,96,896]{3,2,1,0:T(8,128)(2,1)S(1)}, u32[]{:S(2)}, u32[]{:S(2)}) collective-permute-start(bf16[2,2,96,896]{3,2,1,0:T(8,128)(2,1)} %get-tuple-element.32), channel_id=1, source_target_pairs={{8,0},{16,8},{24,16},{9,1},{17,9},{25,17},{10,2},{18,10},{26,18},{... | collective-permute-start | bytes 2064392 | tf_op jit(solution)/shard_map/ppermute | solution.py:449
  4.3 21.7 %collective-permute-start.1 = (bf16[2,2,96,896]{3,2,1,0:T(8,128)(2,1)}, bf16[2,2,96,896]{3,2,1,0:T(8,128)(2,1)S(1)}, u32[]{:S(2)}, u32[]{:S(2)}) collective-permute-start(bf16[2,2,96,896]{3,2,1,0:T(8,128)(2,1)} %get-tuple-element.33), channel_id=1, source_target_pairs={{0,8},{8,16},{16,24},{1,9},{9,17},{17,25},{2,10},{10,18},{18,26},{... | collective-permute-start | bytes 2064392 | tf_op jit(solution)/shard_map/ppermute | solution.py:450
  10.6 15.4 %copy-start.2 = (s32[7]{0:T(128)S(1)}, s32[7]{0:T(128)}, u32[]{:S(2)}) copy-start(s32[7]{0:T(128)} %pad_add_fusion.where_ref) | copy-start | bytes 88
  13.5 19.7 %copy-start.3 = (bf16[1,2,96,3,896]{4,2,3,1,0:T(8,128)(2,1)S(1)}, bf16[1,2,96,3,896]{4,2,3,1,0:T(8,128)(2,1)}, u32[]{:S(2)}) copy-start(bf16[1,2,96,3,896]{4,2,3,1,0:T(8,128)(2,1)} %param.6) | copy-start | bytes 3096580
  13.5 29.7 %collective-permute-start.4 = (bf16[448,896]{1,0:T(8,128)(2,1)}, bf16[448,896]{1,0:T(8,128)(2,1)}, u32[]{:S(2)}, u32[]{:S(2)}) collective-permute-start(bf16[448,896]{1,0:T(8,128)(2,1)} %get-tuple-element.35.refs_8_), channel_id=1, source_target_pairs={{0,8},{8,16},{16,24},{1,9},{9,17},{17,25},{2,10},{10,18},{18,26},{... | collective-permute-start | bytes 2408456 | tf_op jit(solution)/shard_map/ppermute | solution.py:467
  18.5 24.8 %collective-permute-start.3 = (bf16[448,896]{1,0:T(8,128)(2,1)}, bf16[448,896]{1,0:T(8,128)(2,1)}, u32[]{:S(2)}, u32[]{:S(2)}) collective-permute-start(bf16[448,896]{1,0:T(8,128)(2,1)} %get-tuple-element.35.refs_8_), channel_id=1, source_target_pairs={{8,0},{16,8},{24,16},{9,1},{17,9},{25,17},{10,2},{18,10},{26,18},{... | collective-permute-start | bytes 2408456 | tf_op jit(solution)/shard_map/ppermute | solution.py:467
  19.7 28.4 %collective-permute-start.9 = (bf16[128,896]{1,0:T(8,128)(2,1)}, bf16[128,896]{1,0:T(8,128)(2,1)}, u32[]{:S(2)}, u32[]{:S(2)}) collective-permute-start(bf16[128,896]{1,0:T(8,128)(2,1)} %get-tuple-element.38), channel_id=1, source_target_pairs={{0,24},{24,0},{1,25},{25,1},{2,26},{26,2},{3,27},{27,3},{4,28},{28... | collective-permute-start | bytes 688136 | tf_op jit(solution)/shard_map/ppermute | solution.py:469
  31.3 8.5 %collective-permute-start.2 = (bf16[1,192,896]{2,1,0:T(8,128)(2,1)}, bf16[1,192,896]{2,1,0:T(8,128)(2,1)}, u32[]{:S(2)}, u32[]{:S(2)}) collective-permute-start(bf16[1,192,896]{2,1,0:T(8,128)(2,1)} %bitcast.8), channel_id=1, source_target_pairs={{0,1},{1,0},{2,3},{3,2},{4,5},{5,4},{6,7},{7,6},{8,9},{9,8},{10,11... | collective-permute-start | bytes 1032200 | tf_op jit(solution)/shard_map/ppermute | solution.py:390
  38.2 27.9 %copy-start.5 = (bf16[320,896]{1,0:T(8,128)(2,1)S(1)}, bf16[320,896]{1,0:T(8,128)(2,1)}, u32[]{:S(2)}) copy-start(bf16[320,896]{1,0:T(8,128)(2,1)} %get-tuple-element.43) | copy-start | bytes 1720324
  38.2 33.0 %copy-start.1 = (bf16[448,896]{1,0:T(8,128)(2,1)S(1)}, bf16[448,896]{1,0:T(8,128)(2,1)}, u32[]{:S(2)}) copy-start(bf16[448,896]{1,0:T(8,128)(2,1)} %get-tuple-element.35.refs_8_) | copy-start | bytes 2408452
  38.2 7.3 %collective-permute-start.8 = (bf16[1,192,896]{2,1,0:T(8,128)(2,1)S(1)}, bf16[1,192,896]{2,1,0:T(8,128)(2,1)S(1)}, u32[]{:S(2)}, u32[]{:S(2)}) collective-permute-start(bf16[1,192,896]{2,1,0:T(8,128)(2,1)S(1)} %bitcast.20), channel_id=1, source_target_pairs={{0,4},{2,6},{4,0},{6,2},{1,5},{3,7},{5,1},{7,3},{8,12},{10,14},{12... | collective-permute-start | bytes 1032200 | tf_op jit(solution)/shard_map/ppermute | solution.py:390
  43.3 22.3 %collective-permute-start.12 = (bf16[448,896]{1,0:T(8,128)(2,1)}, bf16[448,896]{1,0:T(8,128)(2,1)S(1)}, u32[]{:S(2)}, u32[]{:S(2)}) collective-permute-start(bf16[448,896]{1,0:T(8,128)(2,1)} %collective-permute-done.3.refs_9_), channel_id=1, source_target_pairs={{8,0},{16,8},{9,1},{17,9},{10,2},{18,10},{11,3},{19,11},{12,4},{20... | collective-permute-start | bytes 2408456 | tf_op jit(solution)/shard_map/ppermute | solution.py:479
  44.5 21.0 %collective-permute-start.13 = (bf16[448,896]{1,0:T(8,128)(2,1)}, bf16[448,896]{1,0:T(8,128)(2,1)S(1)}, u32[]{:S(2)}, u32[]{:S(2)}) collective-permute-start(bf16[448,896]{1,0:T(8,128)(2,1)} %collective-permute-done.4.refs_10_), channel_id=1, source_target_pairs={{8,16},{16,24},{9,17},{17,25},{10,18},{18,26},{11,19},{19,27},{12,... | collective-permute-start | bytes 2408456 | tf_op jit(solution)/shard_map/ppermute | solution.py:480
  48.1 16.2 %collective-permute-start.10 = (bf16[2,192,896]{2,1,0:T(8,128)(2,1)S(1)}, bf16[2,192,896]{2,1,0:T(8,128)(2,1)S(1)}, u32[]{:S(2)}, u32[]{:S(2)}) collective-permute-start(bf16[2,192,896]{2,1,0:T(8,128)(2,1)S(1)} %pad_maximum_fusion.1.refs_4_), channel_id=1, source_target_pairs={{0,1},{1,0},{2,3},{3,2},{4,5},{5,4},{6,7},{7,6},{8,9},{9,8},{10,11... | collective-permute-start | bytes 2064392 | tf_op jit(solution)/shard_map/ppermute | solution.py:390
  49.6 15.9 %collective-permute-start.5 = (bf16[2,192,896]{2,1,0:T(8,128)(2,1)S(1)}, bf16[2,192,896]{2,1,0:T(8,128)(2,1)S(1)}, u32[]{:S(2)}, u32[]{:S(2)}) collective-permute-start(bf16[2,192,896]{2,1,0:T(8,128)(2,1)S(1)} %pad_maximum_fusion.refs_0_), channel_id=1, source_target_pairs={{0,4},{2,6},{4,0},{6,2},{1,5},{3,7},{5,1},{7,3},{8,12},{10,14},{12... | collective-permute-start | bytes 2064392 | tf_op jit(solution)/shard_map/ppermute | solution.py:390
  51.1 20.0 %collective-permute-start.6 = (bf16[2,192,896]{2,1,0:T(8,128)(2,1)S(1)}, bf16[2,192,896]{2,1,0:T(8,128)(2,1)S(1)}, u32[]{:S(2)}, u32[]{:S(2)}) collective-permute-start(bf16[2,192,896]{2,1,0:T(8,128)(2,1)S(1)} %pad_maximum_fusion.refs_0_), channel_id=1, source_target_pairs={{0,2},{2,0},{4,6},{6,4},{1,3},{3,1},{5,7},{7,5},{8,10},{10,8},{12,... | collective-permute-start | bytes 2064392 | tf_op jit(solution)/shard_map/ppermute | solution.py:390
  64.3 6.8 %collective-permute-start.11 = (bf16[2,192,896]{2,1,0:T(8,128)(2,1)S(1)}, bf16[2,192,896]{2,1,0:T(8,128)(2,1)S(1)}, u32[]{:S(2)}, u32[]{:S(2)}) collective-permute-start(bf16[2,192,896]{2,1,0:T(8,128)(2,1)S(1)} %pad_maximum_fusion.1.refs_4_), channel_id=1, source_target_pairs={{0,2},{2,0},{4,6},{6,4},{1,3},{3,1},{5,7},{7,5},{8,10},{10,8},{12,... | collective-permute-start | bytes 2064392 | tf_op jit(solution)/shard_map/ppermute | solution.py:390
  65.6 5.6 %collective-permute-start.7 = (bf16[2,192,896]{2,1,0:T(8,128)(2,1)S(1)}, bf16[2,192,896]{2,1,0:T(8,128)(2,1)S(1)}, u32[]{:S(2)}, u32[]{:S(2)}) collective-permute-start(bf16[2,192,896]{2,1,0:T(8,128)(2,1)S(1)} %collective-permute-done.5.refs_1_), channel_id=1, source_target_pairs={{0,2},{2,0},{4,6},{6,4},{1,3},{3,1},{5,7},{7,5},{8,10},{10,8},{12,... | collective-permute-start | bytes 2064392 | tf_op jit(solution)/shard_map/ppermute | solution.py:390
  65.6 5.6 %collective-permute-start.14 = (bf16[2,192,896]{2,1,0:T(8,128)(2,1)S(1)}, bf16[2,192,896]{2,1,0:T(8,128)(2,1)S(1)}, u32[]{:S(2)}, u32[]{:S(2)}) collective-permute-start(bf16[2,192,896]{2,1,0:T(8,128)(2,1)S(1)} %collective-permute-done.10.refs_5_), channel_id=1, source_target_pairs={{0,2},{2,0},{4,6},{6,4},{1,3},{3,1},{5,7},{7,5},{8,10},{10,8},{12,... | collective-permute-start | bytes 2064392 | tf_op jit(solution)/shard_map/ppermute | solution.py:390
  66.1 18.6 %collective-permute-start.15 = (bf16[320,896]{1,0:T(8,128)(2,1)S(1)}, bf16[320,896]{1,0:T(8,128)(2,1)S(1)}, u32[]{:S(2)}, u32[]{:S(2)}) collective-permute-start(bf16[320,896]{1,0:T(8,128)(2,1)S(1)} %copy-done.5), channel_id=1, source_target_pairs={{0,24},{24,0},{1,25},{25,1},{2,26},{26,2},{3,27},{27,3},{4,28},{28... | collective-permute-start | bytes 1720328 | tf_op jit(solution)/shard_map/ppermute | solution.py:469
  95.4 7.0 %collective-permute-start.16 = (bf16[2,96,448]{2,1,0:T(8,128)(2,1)S(1)}, bf16[2,96,448]{2,1,0:T(8,128)(2,1)S(1)}, u32[]{:S(2)}, u32[]{:S(2)}) collective-permute-start(bf16[2,96,448]{2,1,0:T(8,128)(2,1)S(1)} %bitcast.27), channel_id=1, source_target_pairs={{0,1},{1,0},{2,3},{3,2},{4,5},{5,4},{6,7},{7,6},{8,9},{9,8},{10,11... | collective-permute-start | bytes 516104 | tf_op jit(solution)/shard_map/ppermute | solution.py:390
  97.3 12.3 %all-to-all-start.1 = ((f32[32,1,512]{2,1,0:T(1,128)}), f32[32,1,512]{2,1,0:T(1,128)S(1)}, u32[]{:S(2)}, u32[]{:S(2)}) async-start(f32[32,1,512]{2,1,0:T(1,128)} %finish.1), calls=%async_computation.1 | async-start | bytes 131072 | tf_op jit(solution)/shard_map/all_to_all | solution.py:413
  (1 other events, 2.3 us)

commit v8 on v7

--- a/solution.py
+++ b/solution.py
@@ -189,62 +189,34 @@
         block_refs = refs[: len(flat)]
         weight_refs = refs[len(flat) : len(flat) + shard_total]
         total_ref = refs[len(flat) + shard_total] if total is not None else None
-        rows, held, row_sem, weight_sem = refs[-4:]
+        rows = refs[-1]
         out_ref = refs[len(operands)]
         squares_ref = refs[len(operands) + 1]
-
-        def weight_copy(shard):
-            size = shards[shard][1].shape[0]
-            return pltpu.make_async_copy(
-                weight_refs[shard], held.at[shard, pl.ds(0, size)], weight_sem.at[shard]
-            )
-
-        def row_copy(place, shard, clip, stream):
-            stack, at = home[stream][place, clip]
-            source = block_refs[base[stream] + stack].at[at]
-            first = pl.multiple_of(
-                (clip ^ own_clip) * row_count + stream * block_rows, 16
-            )
-            return pltpu.make_async_copy(
-                source,
-                rows.at[shard, pl.ds(first, block_rows)],
-                row_sem.at[shard, clip, stream],
-            )
-
-        for shard in range(shard_total):
-
-            @pl.when(shards[shard][3](slab))
-            def _():
-                weight_copy(shard).start()
-                for place in range(place_count):
-
-                    @pl.when((shards[shard][2](slab) ^ model) == place)
-                    def _():
-                        for clip in range(clip_count):
-                            for stream in range(stream_count):
-                                row_copy(place, shard, clip, stream).start()
-
         if total is None:
             out_ref[...] = jnp.zeros_like(out_ref)
         else:
             out_ref[...] = total_ref[...]
 
-        for shard in range(shard_total):
-
-            @pl.when(shards[shard][3](slab))
+        for shard, (first, array, place_of, exists) in enumerate(shards):
+
+            @pl.when(exists(slab))
             def _():
-                weight_copy(shard).wait()
-                for clip in range(clip_count):
-                    for stream in range(stream_count):
-                        row_copy(0, shard, clip, stream).wait()
-                first, array = shards[shard][:2]
-                size = array.shape[0]
-                wide = whole_lanes(size)
-                if wide > size:
-                    held[shard, size:wide] = jnp.zeros((wide - size, depth), held.dtype)
-                out_ref[:, pl.ds(first, wide)] += lax.dot_general(
-                    rows[shard],
-                    held[shard, pl.ds(0, wide)],
+                held = rows.at[shard % 2]
+                for place in range(place_count):
+
+                    @pl.when((place_of(slab) ^ model) == place)
+                    def _():
+                        for clip in range(clip_count):
+                            for stream in range(stream_count):
+                                stack, at = home[stream][place, clip]
+                                begin = (clip ^ own_clip) * row_count + stream * block_rows
+                                held[pl.ds(pl.multiple_of(begin, 16), block_rows)] = block_refs[
+                                    base[stream] + stack
+                                ][at]
+
+                out_ref[:, pl.ds(first, array.shape[0])] += lax.dot_general(
+                    held[...],
+                    weight_refs[shard][...],
                     (((1,), (1,)), ((), ())),
                     preferred_element_type=jnp.float32,
                 )
@@ -260,12 +232,11 @@
                 )
 
     operands = [*flat, *(array for _, array, _, _ in shards)]
-    in_specs = [pl.BlockSpec(memory_space=pl.ANY) for _ in operands]
     aliases = {}
     if total is not None:
         operands.append(total)
-        in_specs.append(pl.BlockSpec(memory_space=pltpu.VMEM))
         aliases = {len(operands): 0}
+    in_specs = [pl.BlockSpec(memory_space=pltpu.VMEM) for _ in operands]
     out_shape = [jax.ShapeDtypeStruct((clip_count * row_count, lanes), jnp.float32)]
     if peers:
         out_shape.append(jax.ShapeDtypeStruct((peers, 1, clip_count * row_count), jnp.float32))
@@ -274,14 +245,9 @@
         in_specs=[pl.BlockSpec(memory_space=pltpu.SMEM)] + in_specs,
         out_specs=[pl.BlockSpec(memory_space=pltpu.VMEM)] * len(out_shape),
         out_shape=out_shape,
-        scratch_shapes=[
-            pltpu.VMEM((shard_total, clip_count * row_count, depth), jnp.bfloat16),
-            pltpu.VMEM((shard_total, lanes, depth), jnp.bfloat16),
-            pltpu.SemaphoreType.DMA((shard_total, clip_count, stream_count)),
-            pltpu.SemaphoreType.DMA((shard_total,)),
-        ],
+        scratch_shapes=[pltpu.VMEM((2, clip_count * row_count, depth), jnp.bfloat16)],
         input_output_aliases=aliases,
-        compiler_params=pltpu.CompilerParams(vmem_limit_bytes=(8 + 4 * shard_total) * 1024 * 1024),
+        compiler_params=pltpu.CompilerParams(vmem_limit_bytes=(16 + shard_total) * 1024 * 1024),
         cost_estimate=pl.CostEstimate(
             flops=0,
             bytes_accessed=0,

time: 111 us -> 111 us (level)
  Pallas kernels: 27.1 us -> 25.4 us
  waiting for transfers between devices: 34.1 us -> 35.4 us
    pallas_call x2, Pallas kernels: 9.34 us -> 7.57 us  [project(): pl.pallas_call(kernel, in_specs=[pl.BlockSpec(memory_space=pltpu.SMEM)] +...]
    ppermute x2, waiting for transfers between devices: 9.28 us -> 10.5 us  [local(): lax.ppermute(block, 'frames', [(0, last), (last, 0)])]
  transfers between devices with their start and end apart: 18 -> 18, of which waited for: 9 -> 9; matrix products, arithmetic and copies ran while one was open for 3% -> 3% of each run, Pallas kernels for 19% -> 18%
where the time goes in v8:
time: 111 us; the launch traced here: 110 us
  starting transfers between devices  37.7 us (34%)
  waiting for transfers between devices  35.4 us (32%)
  Pallas kernels  25.4 us (23%)
  blocking collectives  7.86 us (7%)
  other arithmetic  3.13 us (3%)
    ppermute x9, waiting for transfers between devices, swap(): return lax.ppermute(array, axis, [(i, i ^ distance) for i in range(count)])  15 us
    ppermute x2, waiting for transfers between devices, local(): lax.ppermute(block, 'frames', [(0, last), (last, 0)])  10.5 us
    ppermute x2, starting transfers between devices, local(): lax.ppermute(block, 'frames', [(0, last), (last, 0)])  10.1 us
    pallas_call x2, Pallas kernels, attention(): pl.pallas_call(attend_kernel, grid_spec=pltpu.PrefetchScalarGridSpec(num_...  9.76 us
    all_to_all x1, blocking collectives, collect(): return lax.all_to_all(rows, axes, split_axis=0, concat_axis=0, tiled=True)  7.86 us
    ppermute x9, starting transfers between devices, swap(): return lax.ppermute(array, axis, [(i, i ^ distance) for i in range(count)])  7.8 us
    pallas_call x2, Pallas kernels, project(): pl.pallas_call(kernel, in_specs=[pl.BlockSpec(memory_space=pltpu.SMEM)] +...  7.57 us
    all_to_all x1, waiting for transfers between devices, collect(): return lax.all_to_all(rows, axes, split_axis=0, concat_axis=0, tiled=True)  6.35 us
  transfers between devices with their start and end apart: 18, of which 9 were waited for; matrix products, arithmetic and copies ran while one was open for 3% of the time, Pallas kernels for 18%

profile of v8, /device:TPU:0, one launch (start us, length us, event | category | flops | bytes accessed | tf_op | source)
XLA Modules:
  0.0 110.5 jit_solution(14922423716664060789)
XLA Ops:
  0.6 2.4 %prepare_halo.1 = (bf16[2,2,96,896]{3,2,1,0:T(8,128)(2,1)}, bf16[2,2,96,896]{3,2,1,0:T(8,128)(2,1)}) custom-call(bf16[2,3,96,896]{3,2,1,0:T(8,128)(2,1)} %bitcast.17, bf16[2,3,96,896]{3,2,1,0:T(8,128)(2,1)} %bitcast.24), custom_call_target="tpu_custom_call" | custom-call | tf_op jit(solution)/shard_map/prepare_halo/pallas_call | solution.py:53
  3.0 1.3 %collective-permute-start = (bf16[2,2,96,896]{3,2,1,0:T(8,128)(2,1)}, bf16[2,2,96,896]{3,2,1,0:T(8,128)(2,1)S(1)}, u32[]{:S(2)}, u32[]{:S(2)}) collective-permute-start(bf16[2,2,96,896]{3,2,1,0:T(8,128)(2,1)} %get-tuple-element.32), channel_id=1, source_target_pairs={{8,0},{16,8},{24,16},{9,1},{17,9},{25,17},{10,2},{18,10},{26,18},{... | collective-permute-start | bytes 2064392 | tf_op jit(solution)/shard_map/ppermute | solution.py:415
  4.3 5.6 %collective-permute-start.1 = (bf16[2,2,96,896]{3,2,1,0:T(8,128)(2,1)}, bf16[2,2,96,896]{3,2,1,0:T(8,128)(2,1)S(1)}, u32[]{:S(2)}, u32[]{:S(2)}) collective-permute-start(bf16[2,2,96,896]{3,2,1,0:T(8,128)(2,1)} %get-tuple-element.33), channel_id=1, source_target_pairs={{0,8},{8,16},{16,24},{1,9},{9,17},{17,25},{2,10},{10,18},{18,26},{... | collective-permute-start | bytes 2064392 | tf_op jit(solution)/shard_map/ppermute | solution.py:416
  10.6 2.9 %prepare_weight.1 = (bf16[448,896]{1,0:T(8,128)(2,1)}, bf16[128,896]{1,0:T(8,128)(2,1)}, bf16[320,896]{1,0:T(8,128)(2,1)}) custom-call(s32[7]{0:T(128)} %pad_add_fusion.where_ref, bf16[896,896]{1,0:T(8,128)(2,1)} %weight_ref), custom_call_target="tpu_custom_call" | custom-call | tf_op jit(solution)/shard_map/prepare_weight/pallas_call | solution.py:87
  13.5 4.9 %collective-permute-start.4 = (bf16[448,896]{1,0:T(8,128)(2,1)}, bf16[448,896]{1,0:T(8,128)(2,1)}, u32[]{:S(2)}, u32[]{:S(2)}) collective-permute-start(bf16[448,896]{1,0:T(8,128)(2,1)} %get-tuple-element.35.refs_8_), channel_id=1, source_target_pairs={{0,8},{8,16},{16,24},{1,9},{9,17},{17,25},{2,10},{10,18},{18,26},{... | collective-permute-start | bytes 2408456 | tf_op jit(solution)/shard_map/ppermute | solution.py:433
  19.7 5.1 %collective-permute-start.9 = (bf16[128,896]{1,0:T(8,128)(2,1)}, bf16[128,896]{1,0:T(8,128)(2,1)}, u32[]{:S(2)}, u32[]{:S(2)}) collective-permute-start(bf16[128,896]{1,0:T(8,128)(2,1)} %get-tuple-element.38), channel_id=1, source_target_pairs={{0,24},{24,0},{1,25},{25,1},{2,26},{26,2},{3,27},{27,3},{4,28},{28... | collective-permute-start | bytes 688136 | tf_op jit(solution)/shard_map/ppermute | solution.py:435
  26.1 5.2 %attention.2 = bf16[2,96,896]{2,1,0:T(8,128)(2,1)} custom-call(s32[7]{0:T(128)S(1)} %copy-done.2, bf16[2,3,96,896]{3,2,1,0:T(8,128)(2,1)S(1)} %bitcast.18, bf16[2,2,96,896]{3,2,1,0:T(8,128)(2,1)S(1)} %collective-permute-done.right_ref, bf16[2,2,96,896]{3,2,1,0:T(8,128)(2,1)S(1)} %collective-permute-done.1.left_ref), custom_call_target="tpu_custom_call" | custom-call | tf_op jit(solution)/shard_map/attention/pallas_call | solution.py:144
  31.3 2.0 %collective-permute-start.2 = (bf16[1,192,896]{2,1,0:T(8,128)(2,1)}, bf16[1,192,896]{2,1,0:T(8,128)(2,1)}, u32[]{:S(2)}, u32[]{:S(2)}) collective-permute-start(bf16[1,192,896]{2,1,0:T(8,128)(2,1)} %bitcast.8), channel_id=1, source_target_pairs={{0,1},{1,0},{2,3},{3,2},{4,5},{5,4},{6,7},{7,6},{8,9},{9,8},{10,11... | collective-permute-start | bytes 1032200 | tf_op jit(solution)/shard_map/ppermute | solution.py:356
  33.6 4.5 %attention.3 = bf16[2,96,896]{2,1,0:T(8,128)(2,1)S(1)} custom-call(s32[7]{0:T(128)S(1)} %copy-done.2, bf16[2,3,96,896]{3,2,1,0:T(8,128)(2,1)S(1)} %add_convert_fusion.own_ref, bf16[2,2,96,896]{3,2,1,0:T(8,128)(2,1)S(1)} %collective-permute-done.right_ref, bf16[2,2,96,896]{3,2,1,0:T(8,128)(2,1)S(1)} %collective-permute-done.1.left_ref), custom_call_target="tpu_custom_call" | custom-call | tf_op jit(solution)/shard_map/attention/pallas_call | solution.py:144
  38.2 1.6 %collective-permute-start.8 = (bf16[1,192,896]{2,1,0:T(8,128)(2,1)S(1)}, bf16[1,192,896]{2,1,0:T(8,128)(2,1)S(1)}, u32[]{:S(2)}, u32[]{:S(2)}) collective-permute-start(bf16[1,192,896]{2,1,0:T(8,128)(2,1)S(1)} %bitcast.20), channel_id=1, source_target_pairs={{0,4},{2,6},{4,0},{6,2},{1,5},{3,7},{5,1},{7,3},{8,12},{10,14},{12... | collective-permute-start | bytes 1032200 | tf_op jit(solution)/shard_map/ppermute | solution.py:356
  41.0 2.3 %collective-permute-done.4.refs_10_ = bf16[448,896]{1,0:T(8,128)(2,1)} collective-permute-done((bf16[448,896]{1,0:T(8,128)(2,1)}, bf16[448,896]{1,0:T(8,128)(2,1)}, u32[]{:S(2)}, u32[]{:S(2)}) %collective-permute-start.4) | collective-permute-done | bytes 802848 | tf_op jit(solution)/shard_map/ppermute | solution.py:433
  43.3 1.3 %collective-permute-start.12 = (bf16[448,896]{1,0:T(8,128)(2,1)}, bf16[448,896]{1,0:T(8,128)(2,1)S(1)}, u32[]{:S(2)}, u32[]{:S(2)}) collective-permute-start(bf16[448,896]{1,0:T(8,128)(2,1)} %collective-permute-done.3.refs_9_), channel_id=1, source_target_pairs={{8,0},{16,8},{9,1},{17,9},{10,2},{18,10},{11,3},{19,11},{12,4},{20... | collective-permute-start | bytes 2408456 | tf_op jit(solution)/shard_map/ppermute | solution.py:445
  45.6 2.6 %collective-permute-done.9.refs_13_ = bf16[128,896]{1,0:T(8,128)(2,1)} collective-permute-done((bf16[128,896]{1,0:T(8,128)(2,1)}, bf16[128,896]{1,0:T(8,128)(2,1)}, u32[]{:S(2)}, u32[]{:S(2)}) %collective-permute-start.9) | collective-permute-done | bytes 229408 | tf_op jit(solution)/shard_map/ppermute | solution.py:435
  48.1 1.5 %collective-permute-start.10 = (bf16[2,192,896]{2,1,0:T(8,128)(2,1)S(1)}, bf16[2,192,896]{2,1,0:T(8,128)(2,1)S(1)}, u32[]{:S(2)}, u32[]{:S(2)}) collective-permute-start(bf16[2,192,896]{2,1,0:T(8,128)(2,1)S(1)} %pad_maximum_fusion.1.refs_4_), channel_id=1, source_target_pairs={{0,1},{1,0},{2,3},{3,2},{4,5},{5,4},{6,7},{7,6},{8,9},{9,8},{10,11... | collective-permute-start | bytes 2064392 | tf_op jit(solution)/shard_map/ppermute | solution.py:356
  49.6 1.5 %collective-permute-start.5 = (bf16[2,192,896]{2,1,0:T(8,128)(2,1)S(1)}, bf16[2,192,896]{2,1,0:T(8,128)(2,1)S(1)}, u32[]{:S(2)}, u32[]{:S(2)}) collective-permute-start(bf16[2,192,896]{2,1,0:T(8,128)(2,1)S(1)} %pad_maximum_fusion.refs_0_), channel_id=1, source_target_pairs={{0,4},{2,6},{4,0},{6,2},{1,5},{3,7},{5,1},{7,3},{8,12},{10,14},{12... | collective-permute-start | bytes 2064392 | tf_op jit(solution)/shard_map/ppermute | solution.py:356
  51.1 13.2 %collective-permute-done.10.refs_5_ = bf16[2,192,896]{2,1,0:T(8,128)(2,1)S(1)} collective-permute-done((bf16[2,192,896]{2,1,0:T(8,128)(2,1)S(1)}, bf16[2,192,896]{2,1,0:T(8,128)(2,1)S(1)}, u32[]{:S(2)}, u32[]{:S(2)}) %collective-permute-start.10) | collective-permute-done | bytes 688160 | tf_op jit(solution)/shard_map/ppermute | solution.py:356
  66.1 5.1 %collective-permute-start.15 = (bf16[320,896]{1,0:T(8,128)(2,1)S(1)}, bf16[320,896]{1,0:T(8,128)(2,1)S(1)}, u32[]{:S(2)}, u32[]{:S(2)}) collective-permute-start(bf16[320,896]{1,0:T(8,128)(2,1)S(1)} %copy-done.5), channel_id=1, source_target_pairs={{0,24},{24,0},{1,25},{25,1},{2,26},{26,2},{3,27},{27,3},{4,28},{28... | collective-permute-start | bytes 1720328 | tf_op jit(solution)/shard_map/ppermute | solution.py:435
  71.2 5.6 %project.2.refs_9_ = f32[768,512]{1,0:T(8,128)S(1)} custom-call(s32[7]{0:T(128)S(1)} %copy-done.2, bf16[2,192,896]{2,1,0:T(8,128)(2,1)S(1)} %pad_maximum_fusion.refs_0_, bf16[2,192,896]{2,1,0:T(8,128)(2,1)S(1)} %collective-permute-done.5.refs_1_, bf16[2,192,896]{2,1,0:T(8,128)(2,1)S(1)} %collective-permute-done.6.refs_2_, ...), custom_call_target="tpu_custom_call" | custom-call | tf_op jit(solution)/shard_map/project/pallas_call | solution.py:243
  76.8 7.9 %collective-permute-done.15.refs_8_ = bf16[320,896]{1,0:T(8,128)(2,1)S(1)} collective-permute-done((bf16[320,896]{1,0:T(8,128)(2,1)S(1)}, bf16[320,896]{1,0:T(8,128)(2,1)S(1)}, u32[]{:S(2)}, u32[]{:S(2)}) %collective-permute-start.15) | collective-permute-done | bytes 573472 | tf_op jit(solution)/shard_map/ppermute | solution.py:435
  84.7 2.0 %project.3 = (f32[768,512]{1,0:T(8,128)S(1)}, f32[8,1,768]{2,1,0:T(1,128)S(1)}) custom-call(s32[7]{0:T(128)S(1)} %copy-done.2, bf16[2,192,896]{2,1,0:T(8,128)(2,1)S(1)} %pad_maximum_fusion.refs_0_, bf16[2,192,896]{2,1,0:T(8,128)(2,1)S(1)} %collective-permute-done.5.refs_1_, ...), custom_call_target="tpu_custom_call", output_to_operand_aliasing={{0}: (10, {})} | custom-call | tf_op jit(solution)/shard_map/project/pallas_call | solution.py:243
  86.7 7.9 %all_to_all.10.squares_ref = f32[8,1,768]{2,1,0:T(1,128)S(1)} all-to-all(f32[8,1,768]{2,1,0:T(1,128)S(1)} %get-tuple-element.48), channel_id=1, replica_groups=mesh['frames'=4,'mp'=4,'dp'=2] {'mp','dp'}, dimensions={0} | all-to-all | bytes 49152 | tf_op jit(solution)/shard_map/all_to_all | solution.py:379
  96.8 4.7 %all-to-all-start.1 = ((f32[32,1,512]{2,1,0:T(1,128)}), f32[32,1,512]{2,1,0:T(1,128)S(1)}, u32[]{:S(2)}, u32[]{:S(2)}) async-start(f32[32,1,512]{2,1,0:T(1,128)} %finish.1), calls=%async_computation.1 | async-start | bytes 131072 | tf_op jit(solution)/shard_map/all_to_all | solution.py:379
  102.8 6.4 %all-to-all-done.1.rows_ref = f32[32,1,512]{2,1,0:T(1,128)S(1)} async-done(((f32[32,1,512]{2,1,0:T(1,128)}), f32[32,1,512]{2,1,0:T(1,128)S(1)}, u32[]{:S(2)}, u32[]{:S(2)}) %all-to-all-start.1) | async-done | bytes 65568 | tf_op jit(solution)/shard_map/all_to_all | solution.py:379
  109.1 1.4 %conclude.1 = (f32[1]{0:T(128)}, f32[896]{0:T(1024)}) custom-call(s32[7]{0:T(128)S(1)} %copy-done.2, f32[32,1,512]{2,1,0:T(1,128)S(1)} %all-to-all-done.1.rows_ref, f32[1,896]{1,0:T(1,128)S(1)} %broadcast_in_dim.10.gain_ref), custom_call_target="tpu_custom_call" | custom-call | tf_op jit(solution)/shard_map/conclude/pallas_call | solution.py:337
  (47 shorter events, 10.9 us)
Async XLA Ops:
  0.6 9.3 %copy-start.6 = (s32[1,8]{1,0:T(1,128)S(1)}, s32[1,8]{1,0:T(1,128)}, u32[]{:S(2)}) copy-start(s32[1,8]{1,0:T(1,128)} %param.9) | copy-start | bytes 100
  0.6 25.4 %copy-start = (bf16[1,2,96,3,896]{4,2,3,1,0:T(8,128)(2,1)S(1)}, bf16[1,2,96,3,896]{4,2,3,1,0:T(8,128)(2,1)}, u32[]{:S(2)}) copy-start(bf16[1,2,96,3,896]{4,2,3,1,0:T(8,128)(2,1)} %param.5) | copy-start | bytes 3096580
  3.0 21.8 %collective-permute-start = (bf16[2,2,96,896]{3,2,1,0:T(8,128)(2,1)}, bf16[2,2,96,896]{3,2,1,0:T(8,128)(2,1)S(1)}, u32[]{:S(2)}, u32[]{:S(2)}) collective-permute-start(bf16[2,2,96,896]{3,2,1,0:T(8,128)(2,1)} %get-tuple-element.32), channel_id=1, source_target_pairs={{8,0},{16,8},{24,16},{9,1},{17,9},{25,17},{10,2},{18,10},{26,18},{... | collective-permute-start | bytes 2064392 | tf_op jit(solution)/shard_map/ppermute | solution.py:415
  4.3 21.7 %collective-permute-start.1 = (bf16[2,2,96,896]{3,2,1,0:T(8,128)(2,1)}, bf16[2,2,96,896]{3,2,1,0:T(8,128)(2,1)S(1)}, u32[]{:S(2)}, u32[]{:S(2)}) collective-permute-start(bf16[2,2,96,896]{3,2,1,0:T(8,128)(2,1)} %get-tuple-element.33), channel_id=1, source_target_pairs={{0,8},{8,16},{16,24},{1,9},{9,17},{17,25},{2,10},{10,18},{18,26},{... | collective-permute-start | bytes 2064392 | tf_op jit(solution)/shard_map/ppermute | solution.py:416
  10.6 15.4 %copy-start.2 = (s32[7]{0:T(128)S(1)}, s32[7]{0:T(128)}, u32[]{:S(2)}) copy-start(s32[7]{0:T(128)} %pad_add_fusion.where_ref) | copy-start | bytes 88
  13.5 19.7 %copy-start.3 = (bf16[1,2,96,3,896]{4,2,3,1,0:T(8,128)(2,1)S(1)}, bf16[1,2,96,3,896]{4,2,3,1,0:T(8,128)(2,1)}, u32[]{:S(2)}) copy-start(bf16[1,2,96,3,896]{4,2,3,1,0:T(8,128)(2,1)} %param.6) | copy-start | bytes 3096580
  13.5 29.7 %collective-permute-start.4 = (bf16[448,896]{1,0:T(8,128)(2,1)}, bf16[448,896]{1,0:T(8,128)(2,1)}, u32[]{:S(2)}, u32[]{:S(2)}) collective-permute-start(bf16[448,896]{1,0:T(8,128)(2,1)} %get-tuple-element.35.refs_8_), channel_id=1, source_target_pairs={{0,8},{8,16},{16,24},{1,9},{9,17},{17,25},{2,10},{10,18},{18,26},{... | collective-permute-start | bytes 2408456 | tf_op jit(solution)/shard_map/ppermute | solution.py:433
  18.5 24.8 %collective-permute-start.3 = (bf16[448,896]{1,0:T(8,128)(2,1)}, bf16[448,896]{1,0:T(8,128)(2,1)}, u32[]{:S(2)}, u32[]{:S(2)}) collective-permute-start(bf16[448,896]{1,0:T(8,128)(2,1)} %get-tuple-element.35.refs_8_), channel_id=1, source_target_pairs={{8,0},{16,8},{24,16},{9,1},{17,9},{25,17},{10,2},{18,10},{26,18},{... | collective-permute-start | bytes 2408456 | tf_op jit(solution)/shard_map/ppermute | solution.py:433
  19.7 28.4 %collective-permute-start.9 = (bf16[128,896]{1,0:T(8,128)(2,1)}, bf16[128,896]{1,0:T(8,128)(2,1)}, u32[]{:S(2)}, u32[]{:S(2)}) collective-permute-start(bf16[128,896]{1,0:T(8,128)(2,1)} %get-tuple-element.38), channel_id=1, source_target_pairs={{0,24},{24,0},{1,25},{25,1},{2,26},{26,2},{3,27},{27,3},{4,28},{28... | collective-permute-start | bytes 688136 | tf_op jit(solution)/shard_map/ppermute | solution.py:435
  31.3 8.5 %collective-permute-start.2 = (bf16[1,192,896]{2,1,0:T(8,128)(2,1)}, bf16[1,192,896]{2,1,0:T(8,128)(2,1)}, u32[]{:S(2)}, u32[]{:S(2)}) collective-permute-start(bf16[1,192,896]{2,1,0:T(8,128)(2,1)} %bitcast.8), channel_id=1, source_target_pairs={{0,1},{1,0},{2,3},{3,2},{4,5},{5,4},{6,7},{7,6},{8,9},{9,8},{10,11... | collective-permute-start | bytes 1032200 | tf_op jit(solution)/shard_map/ppermute | solution.py:356
  38.2 27.9 %copy-start.5 = (bf16[320,896]{1,0:T(8,128)(2,1)S(1)}, bf16[320,896]{1,0:T(8,128)(2,1)}, u32[]{:S(2)}) copy-start(bf16[320,896]{1,0:T(8,128)(2,1)} %get-tuple-element.43) | copy-start | bytes 1720324
  38.2 33.0 %copy-start.1 = (bf16[448,896]{1,0:T(8,128)(2,1)S(1)}, bf16[448,896]{1,0:T(8,128)(2,1)}, u32[]{:S(2)}) copy-start(bf16[448,896]{1,0:T(8,128)(2,1)} %get-tuple-element.35.refs_8_) | copy-start | bytes 2408452
  38.2 7.3 %collective-permute-start.8 = (bf16[1,192,896]{2,1,0:T(8,128)(2,1)S(1)}, bf16[1,192,896]{2,1,0:T(8,128)(2,1)S(1)}, u32[]{:S(2)}, u32[]{:S(2)}) collective-permute-start(bf16[1,192,896]{2,1,0:T(8,128)(2,1)S(1)} %bitcast.20), channel_id=1, source_target_pairs={{0,4},{2,6},{4,0},{6,2},{1,5},{3,7},{5,1},{7,3},{8,12},{10,14},{12... | collective-permute-start | bytes 1032200 | tf_op jit(solution)/shard_map/ppermute | solution.py:356
  43.3 22.3 %collective-permute-start.12 = (bf16[448,896]{1,0:T(8,128)(2,1)}, bf16[448,896]{1,0:T(8,128)(2,1)S(1)}, u32[]{:S(2)}, u32[]{:S(2)}) collective-permute-start(bf16[448,896]{1,0:T(8,128)(2,1)} %collective-permute-done.3.refs_9_), channel_id=1, source_target_pairs={{8,0},{16,8},{9,1},{17,9},{10,2},{18,10},{11,3},{19,11},{12,4},{20... | collective-permute-start | bytes 2408456 | tf_op jit(solution)/shard_map/ppermute | solution.py:445
  44.5 21.0 %collective-permute-start.13 = (bf16[448,896]{1,0:T(8,128)(2,1)}, bf16[448,896]{1,0:T(8,128)(2,1)S(1)}, u32[]{:S(2)}, u32[]{:S(2)}) collective-permute-start(bf16[448,896]{1,0:T(8,128)(2,1)} %collective-permute-done.4.refs_10_), channel_id=1, source_target_pairs={{8,16},{16,24},{9,17},{17,25},{10,18},{18,26},{11,19},{19,27},{12,... | collective-permute-start | bytes 2408456 | tf_op jit(solution)/shard_map/ppermute | solution.py:446
  48.1 16.2 %collective-permute-start.10 = (bf16[2,192,896]{2,1,0:T(8,128)(2,1)S(1)}, bf16[2,192,896]{2,1,0:T(8,128)(2,1)S(1)}, u32[]{:S(2)}, u32[]{:S(2)}) collective-permute-start(bf16[2,192,896]{2,1,0:T(8,128)(2,1)S(1)} %pad_maximum_fusion.1.refs_4_), channel_id=1, source_target_pairs={{0,1},{1,0},{2,3},{3,2},{4,5},{5,4},{6,7},{7,6},{8,9},{9,8},{10,11... | collective-permute-start | bytes 2064392 | tf_op jit(solution)/shard_map/ppermute | solution.py:356
  49.6 15.9 %collective-permute-start.5 = (bf16[2,192,896]{2,1,0:T(8,128)(2,1)S(1)}, bf16[2,192,896]{2,1,0:T(8,128)(2,1)S(1)}, u32[]{:S(2)}, u32[]{:S(2)}) collective-permute-start(bf16[2,192,896]{2,1,0:T(8,128)(2,1)S(1)} %pad_maximum_fusion.refs_0_), channel_id=1, source_target_pairs={{0,4},{2,6},{4,0},{6,2},{1,5},{3,7},{5,1},{7,3},{8,12},{10,14},{12... | collective-permute-start | bytes 2064392 | tf_op jit(solution)/shard_map/ppermute | solution.py:356
  51.1 20.0 %collective-permute-start.6 = (bf16[2,192,896]{2,1,0:T(8,128)(2,1)S(1)}, bf16[2,192,896]{2,1,0:T(8,128)(2,1)S(1)}, u32[]{:S(2)}, u32[]{:S(2)}) collective-permute-start(bf16[2,192,896]{2,1,0:T(8,128)(2,1)S(1)} %pad_maximum_fusion.refs_0_), channel_id=1, source_target_pairs={{0,2},{2,0},{4,6},{6,4},{1,3},{3,1},{5,7},{7,5},{8,10},{10,8},{12,... | collective-permute-start | bytes 2064392 | tf_op jit(solution)/shard_map/ppermute | solution.py:356
  64.3 6.8 %collective-permute-start.11 = (bf16[2,192,896]{2,1,0:T(8,128)(2,1)S(1)}, bf16[2,192,896]{2,1,0:T(8,128)(2,1)S(1)}, u32[]{:S(2)}, u32[]{:S(2)}) collective-permute-start(bf16[2,192,896]{2,1,0:T(8,128)(2,1)S(1)} %pad_maximum_fusion.1.refs_4_), channel_id=1, source_target_pairs={{0,2},{2,0},{4,6},{6,4},{1,3},{3,1},{5,7},{7,5},{8,10},{10,8},{12,... | collective-permute-start | bytes 2064392 | tf_op jit(solution)/shard_map/ppermute | solution.py:356
  65.6 5.6 %collective-permute-start.7 = (bf16[2,192,896]{2,1,0:T(8,128)(2,1)S(1)}, bf16[2,192,896]{2,1,0:T(8,128)(2,1)S(1)}, u32[]{:S(2)}, u32[]{:S(2)}) collective-permute-start(bf16[2,192,896]{2,1,0:T(8,128)(2,1)S(1)} %collective-permute-done.5.refs_1_), channel_id=1, source_target_pairs={{0,2},{2,0},{4,6},{6,4},{1,3},{3,1},{5,7},{7,5},{8,10},{10,8},{12,... | collective-permute-start | bytes 2064392 | tf_op jit(solution)/shard_map/ppermute | solution.py:356
  65.6 5.6 %collective-permute-start.14 = (bf16[2,192,896]{2,1,0:T(8,128)(2,1)S(1)}, bf16[2,192,896]{2,1,0:T(8,128)(2,1)S(1)}, u32[]{:S(2)}, u32[]{:S(2)}) collective-permute-start(bf16[2,192,896]{2,1,0:T(8,128)(2,1)S(1)} %collective-permute-done.10.refs_5_), channel_id=1, source_target_pairs={{0,2},{2,0},{4,6},{6,4},{1,3},{3,1},{5,7},{7,5},{8,10},{10,8},{12,... | collective-permute-start | bytes 2064392 | tf_op jit(solution)/shard_map/ppermute | solution.py:356
  66.1 18.6 %collective-permute-start.15 = (bf16[320,896]{1,0:T(8,128)(2,1)S(1)}, bf16[320,896]{1,0:T(8,128)(2,1)S(1)}, u32[]{:S(2)}, u32[]{:S(2)}) collective-permute-start(bf16[320,896]{1,0:T(8,128)(2,1)S(1)} %copy-done.5), channel_id=1, source_target_pairs={{0,24},{24,0},{1,25},{25,1},{2,26},{26,2},{3,27},{27,3},{4,28},{28... | collective-permute-start | bytes 1720328 | tf_op jit(solution)/shard_map/ppermute | solution.py:435
  94.9 7.0 %collective-permute-start.16 = (bf16[2,96,448]{2,1,0:T(8,128)(2,1)S(1)}, bf16[2,96,448]{2,1,0:T(8,128)(2,1)S(1)}, u32[]{:S(2)}, u32[]{:S(2)}) collective-permute-start(bf16[2,96,448]{2,1,0:T(8,128)(2,1)S(1)} %bitcast.27), channel_id=1, source_target_pairs={{0,1},{1,0},{2,3},{3,2},{4,5},{5,4},{6,7},{7,6},{8,9},{9,8},{10,11... | collective-permute-start | bytes 516104 | tf_op jit(solution)/shard_map/ppermute | solution.py:356
  96.8 12.3 %all-to-all-start.1 = ((f32[32,1,512]{2,1,0:T(1,128)}), f32[32,1,512]{2,1,0:T(1,128)S(1)}, u32[]{:S(2)}, u32[]{:S(2)}) async-start(f32[32,1,512]{2,1,0:T(1,128)} %finish.1), calls=%async_computation.1 | async-start | bytes 131072 | tf_op jit(solution)/shard_map/all_to_all | solution.py:379
  (1 other events, 2.3 us)

commit v9 on v8

--- a/solution.py
+++ b/solution.py
@@ -169,7 +169,7 @@
     return row == lax.broadcasted_iota(jnp.int32, (LANES, LANES), 1)
 
 
-def project(where, gathered, shards, total, columns, peers):
+def project(where, gathered, shards, columns, peers, ahead=None):
     stream_count = len(gathered)
     home = [
         {key: (n, at) for n, (keys, _) in enumerate(stacks) for at, key in enumerate(keys)}
@@ -180,40 +180,35 @@
     _, block_rows, depth = gathered[0][0][1].shape
     lanes = whole_lanes(columns)
     row_count = stream_count * block_rows
-    shard_total = len(shards)
     flat = [array for stacks in gathered for _, array in stacks]
     base = [sum(len(stacks) for stacks in gathered[:n]) for n in range(stream_count)]
 
     def kernel(where_ref, *refs):
         slab, model, own_clip = where_ref[0], where_ref[1], where_ref[2]
         block_refs = refs[: len(flat)]
-        weight_refs = refs[len(flat) : len(flat) + shard_total]
-        total_ref = refs[len(flat) + shard_total] if total is not None else None
-        rows = refs[-1]
-        out_ref = refs[len(operands)]
-        squares_ref = refs[len(operands) + 1]
-        if total is None:
-            out_ref[...] = jnp.zeros_like(out_ref)
-        else:
-            out_ref[...] = total_ref[...]
+        weight_refs = refs[len(flat) : len(operands)]
+        out_ref, other_ref, rows = refs[len(operands) :]
+        out_ref[...] = jnp.zeros_like(out_ref)
+
+        def gather_rows(wanted, held):
+            for place in range(place_count):
+
+                @pl.when((wanted ^ model) == place)
+                def _():
+                    for clip in range(clip_count):
+                        for stream in range(stream_count):
+                            stack, at = home[stream][place, clip]
+                            begin = (clip ^ own_clip) * row_count + stream * block_rows
+                            held[pl.ds(pl.multiple_of(begin, 16), block_rows)] = block_refs[
+                                base[stream] + stack
+                            ][at]
 
         for shard, (first, array, place_of, exists) in enumerate(shards):
 
             @pl.when(exists(slab))
             def _():
                 held = rows.at[shard % 2]
-                for place in range(place_count):
-
-                    @pl.when((place_of(slab) ^ model) == place)
-                    def _():
-                        for clip in range(clip_count):
-                            for stream in range(stream_count):
-                                stack, at = home[stream][place, clip]
-                                begin = (clip ^ own_clip) * row_count + stream * block_rows
-                                held[pl.ds(pl.multiple_of(begin, 16), block_rows)] = block_refs[
-                                    base[stream] + stack
-                                ][at]
-
+                gather_rows(place_of(slab), held)
                 out_ref[:, pl.ds(first, array.shape[0])] += lax.dot_general(
                     held[...],
                     weight_refs[shard][...],
@@ -221,40 +216,78 @@
                     preferred_element_type=jnp.float32,
                 )
 
-        if peers:
-            diagonal = on_diagonal()
-            for first in range(0, clip_count * row_count, LANES):
-                piece = out_ref[pl.ds(first, LANES)]
-                sums = jnp.sum(piece * piece, axis=1, keepdims=True)
-                sums = jnp.sum(jnp.where(diagonal, sums, 0.0), axis=0, keepdims=True)
-                squares_ref[:, :, pl.ds(first, LANES)] = jnp.broadcast_to(
-                    sums[None], (peers, 1, LANES)
-                )
+        if ahead is None:
+            put_squares(out_ref, other_ref)
+        else:
+            gather_rows(ahead(slab), other_ref)
 
     operands = [*flat, *(array for _, array, _, _ in shards)]
-    aliases = {}
-    if total is not None:
-        operands.append(total)
-        aliases = {len(operands): 0}
-    in_specs = [pl.BlockSpec(memory_space=pltpu.VMEM) for _ in operands]
-    out_shape = [jax.ShapeDtypeStruct((clip_count * row_count, lanes), jnp.float32)]
-    if peers:
-        out_shape.append(jax.ShapeDtypeStruct((peers, 1, clip_count * row_count), jnp.float32))
-    return pl.pallas_call(
-        kernel,
-        in_specs=[pl.BlockSpec(memory_space=pltpu.SMEM)] + in_specs,
-        out_specs=[pl.BlockSpec(memory_space=pltpu.VMEM)] * len(out_shape),
-        out_shape=out_shape,
-        scratch_shapes=[pltpu.VMEM((2, clip_count * row_count, depth), jnp.bfloat16)],
-        input_output_aliases=aliases,
-        compiler_params=pltpu.CompilerParams(vmem_limit_bytes=(16 + shard_total) * 1024 * 1024),
-        cost_estimate=pl.CostEstimate(
-            flops=0,
-            bytes_accessed=0,
-            transcendentals=0,
-        ),
+    total_shape = (clip_count * row_count, lanes)
+    if ahead is None:
+        other = jax.ShapeDtypeStruct((peers, 1, total_shape[0]), jnp.float32)
+    else:
+        other = jax.ShapeDtypeStruct((total_shape[0], depth), jnp.bfloat16)
+    return pl.pallas_call(
+        kernel,
+        in_specs=[pl.BlockSpec(memory_space=pltpu.SMEM)]
+        + [pl.BlockSpec(memory_space=pltpu.VMEM) for _ in operands],
+        out_specs=[pl.BlockSpec(memory_space=pltpu.VMEM)] * 2,
+        out_shape=[jax.ShapeDtypeStruct(total_shape, jnp.float32), other],
+        scratch_shapes=[pltpu.VMEM((2, total_shape[0], depth), jnp.bfloat16)],
+        compiler_params=pltpu.CompilerParams(vmem_limit_bytes=24 * 1024 * 1024),
+        cost_estimate=pl.CostEstimate(flops=0, bytes_accessed=0, transcendentals=0),
         name="project",
     )(where, *operands)
+
+
+def put_squares(total_ref, squares_ref):
+    diagonal = on_diagonal()
+    for first in range(0, total_ref.shape[0], LANES):
+        piece = total_ref[pl.ds(first, LANES)]
+        sums = jnp.sum(piece * piece, axis=1, keepdims=True)
+        sums = jnp.sum(jnp.where(diagonal, sums, 0.0), axis=0, keepdims=True)
+        squares_ref[:, :, pl.ds(first, LANES)] = jnp.broadcast_to(
+            sums[None], (squares_ref.shape[0], 1, LANES)
+        )
+
+
+def project_last(where, rows, first, weight, exists, total, peers):
+    size = weight.shape[0]
+
+    def kernel(where_ref, rows_ref, weight_ref, total_ref, out_ref, squares_ref):
+        present = exists(where_ref[0])
+
+        @pl.when(present)
+        def _():
+            out_ref[:, :first] = total_ref[:, :first]
+            out_ref[:, first + size :] = total_ref[:, first + size :]
+            out_ref[:, pl.ds(first, size)] = total_ref[:, pl.ds(first, size)] + lax.dot_general(
+                rows_ref[...],
+                weight_ref[...],
+                (((1,), (1,)), ((), ())),
+                preferred_element_type=jnp.float32,
+            )
+
+        @pl.when(jnp.logical_not(present))
+        def _():
+            out_ref[...] = total_ref[...]
+
+        put_squares(out_ref, squares_ref)
+
+    return pl.pallas_call(
+        kernel,
+        in_specs=[pl.BlockSpec(memory_space=pltpu.SMEM)]
+        + [pl.BlockSpec(memory_space=pltpu.VMEM)] * 3,
+        out_specs=[pl.BlockSpec(memory_space=pltpu.VMEM)] * 2,
+        out_shape=[
+            jax.ShapeDtypeStruct(total.shape, jnp.float32),
+            jax.ShapeDtypeStruct((peers, 1, total.shape[0]), jnp.float32),
+        ],
+        input_output_aliases={3: 0},
+        compiler_params=pltpu.CompilerParams(vmem_limit_bytes=12 * 1024 * 1024),
+        cost_estimate=pl.CostEstimate(flops=0, bytes_accessed=0, transcendentals=0),
+        name="project_last",
+    )(where, rows, weight, total)
 
 
 def row_scales(squares_ref, clip, row_count, model_width):
@@ -293,12 +326,12 @@
     )(total, squares, gain)
 
 
-def make_features(total, squares, gain, clip_count, model_width):
+def make_features(total, squares, gain, after, clip_count, model_width):
     rows, lanes = total.shape
     row_count = rows // clip_count
     near_rows = row_count // 2
 
-    def kernel(total_ref, squares_ref, gain_ref, features_ref):
+    def kernel(total_ref, squares_ref, gain_ref, after_ref, features_ref):
         for clip in range(clip_count):
             scale = row_scales(squares_ref, clip, row_count, model_width)
             clean = total_ref[pl.ds(clip * row_count, near_rows)] * scale[:near_rows]
@@ -306,13 +339,12 @@
 
     return pl.pallas_call(
         kernel,
+        in_specs=[pl.BlockSpec(memory_space=pltpu.VMEM)] * 3 + [pl.BlockSpec(memory_space=pl.ANY)],
         out_shape=jax.ShapeDtypeStruct((clip_count, near_rows, lanes), jnp.bfloat16),
         compiler_params=pltpu.CompilerParams(vmem_limit_bytes=16 * 1024 * 1024),
-        cost_estimate=pl.CostEstimate(
-            flops=10**10, bytes_accessed=0, transcendentals=0
-        ),
+        cost_estimate=pl.CostEstimate(flops=0, bytes_accessed=0, transcendentals=0),
         name="make_features",
-    )(total, squares, gain)
+    )(total, squares, gain, after)
 
 
 def conclude(rows, where, gain, model_count, clip_count, tokens):
@@ -475,8 +507,9 @@
             shards.append(
                 (first, block, lambda slab: last - slab, lambda slab: (slab == 0) | (slab == last))
             )
-        (total,) = project(where, gathered, shards[:-1], None, half, 0)
-        total, squares = project(where, gathered, shards[-1:], total, half, peers)
+        first, block, place_of, exists = shards.pop()
+        total, rows = project(where, gathered, shards, half, peers, ahead=place_of)
+        total, squares = project_last(where, rows, first, block, exists, total, peers)
     else:
         weight = lax.all_gather(own_weight, "frames", axis=1, tiled=True)
         shards = [
@@ -488,7 +521,7 @@
             )
             for m in range(model_count)
         ]
-        total, squares = project(where, gathered, shards, None, half, peers)
+        total, squares = project(where, gathered, shards, half, peers)
 
     squares = collect(squares, ("mp", "dp"))
     sums = finish(
@@ -500,14 +533,16 @@
         model_width,
         slab_count * model_count * clip_count,
     )
-    features = make_features(total, squares, gain_row, clip_count, model_width)
+    features = make_features(total, squares, gain_row, sums, clip_count, model_width)
     sums = collect(sums, ("frames", "mp", "dp"))
 
     features = features[..., :half].reshape(clip_count, slots, tile_len, half)
     columns = [pick([features[d] for d in range(clip_count)], clip_index)]
     for distance in range(1, clip_count):
         sent = pick([features[d ^ distance] for d in range(clip_count)], clip_index)
-        columns.append(swap(sent, "dp", distance))
+        parts = jnp.split(sent.reshape(near_rows, half), 4)
+        parts = [swap(part, "dp", distance) for part in parts]
+        columns.append(jnp.concatenate(parts).reshape(sent.shape))
     features = jnp.concatenate(
         [
             pick([columns[n ^ d] for d in range(clip_count)], clip_index)

time: 111 us -> 114 us (1.027)
  starting transfers between devices: 37.7 us -> 40.4 us
    ppermute x9 -> x12, starting transfers between devices: 7.8 us -> 11.2 us  [swap(): return lax.ppermute(array, axis, [(i, i ^ distance) for i in range(count)])]
    pallas_call x1 -> x2, Pallas kernels: 0.23 us -> 2.2 us  [the longest x1 1.97 us: project_last(): pl.pallas_call(kernel, in_specs=[pl.BlockSpec(memory_space=pltpu.SMEM)] +...]
    pallas_call x2 -> x1, Pallas kernels: 7.57 us -> 5.68 us  [project(): pl.pallas_call(kernel, in_specs=[pl.BlockSpec(memory_space=pltpu.SMEM)] +...]
    ppermute x9 -> x12, waiting for transfers between devices: 15 us -> 14.7 us  [swap(): return lax.ppermute(array, axis, [(i, i ^ distance) for i in range(count)])]
  transfers between devices with their start and end apart: 18 -> 21, of which waited for: 9 -> 8; matrix products, arithmetic and copies ran while one was open for 3% -> 3% of each run, Pallas kernels for 18% -> 16%
where the time goes in v9:
time: 114 us; the launch traced here: 113 us
  starting transfers between devices  40.4 us (35%)
  waiting for transfers between devices  35.1 us (31%)
  Pallas kernels  25.4 us (22%)
  blocking collectives  7.87 us (7%)
  other arithmetic  3.22 us (3%)
    ppermute x12, waiting for transfers between devices, swap(): return lax.ppermute(array, axis, [(i, i ^ distance) for i in range(count)])  14.7 us
    ppermute x12, starting transfers between devices, swap(): return lax.ppermute(array, axis, [(i, i ^ distance) for i in range(count)])  11.2 us
    ppermute x2, waiting for transfers between devices, local(): lax.ppermute(block, 'frames', [(0, last), (last, 0)])  10.4 us
    ppermute x2, starting transfers between devices, local(): lax.ppermute(block, 'frames', [(0, last), (last, 0)])  10.2 us
    pallas_call x2, Pallas kernels, attention(): pl.pallas_call(attend_kernel, grid_spec=pltpu.PrefetchScalarGridSpec(num_...  9.75 us
    all_to_all x1, blocking collectives, collect(): return lax.all_to_all(rows, axes, split_axis=0, concat_axis=0, tiled=True)  7.87 us
    all_to_all x1, waiting for transfers between devices, collect(): return lax.all_to_all(rows, axes, split_axis=0, concat_axis=0, tiled=True)  6.63 us
    ppermute x2, starting transfers between devices, local(): near = [lax.ppermute(own_weight, 'frames', pairs) for pairs in (down, up)]  6.17 us
  transfers between devices with their start and end apart: 21, of which 8 were waited for; matrix products, arithmetic and copies ran while one was open for 3% of the time, Pallas kernels for 16%

profile of v9, /device:TPU:0, one launch (start us, length us, event | category | flops | bytes accessed | tf_op | source)
XLA Modules:
  0.0 113.1 jit_solution(17707396843056351583)
XLA Ops:
  0.6 2.4 %prepare_halo.1 = (bf16[2,2,96,896]{3,2,1,0:T(8,128)(2,1)}, bf16[2,2,96,896]{3,2,1,0:T(8,128)(2,1)}) custom-call(bf16[2,3,96,896]{3,2,1,0:T(8,128)(2,1)} %bitcast.25, bf16[2,3,96,896]{3,2,1,0:T(8,128)(2,1)} %bitcast.32), custom_call_target="tpu_custom_call" | custom-call | tf_op jit(solution)/shard_map/prepare_halo/pallas_call | solution.py:53
  4.4 5.6 %collective-permute-start.1 = (bf16[2,2,96,896]{3,2,1,0:T(8,128)(2,1)}, bf16[2,2,96,896]{3,2,1,0:T(8,128)(2,1)S(1)}, u32[]{:S(2)}, u32[]{:S(2)}) collective-permute-start(bf16[2,2,96,896]{3,2,1,0:T(8,128)(2,1)} %get-tuple-element.35), channel_id=1, source_target_pairs={{0,8},{8,16},{16,24},{1,9},{9,17},{17,25},{2,10},{10,18},{18,26},{... | collective-permute-start | bytes 2064392 | tf_op jit(solution)/shard_map/ppermute | solution.py:448
  10.7 2.9 %prepare_weight.1 = (bf16[448,896]{1,0:T(8,128)(2,1)}, bf16[128,896]{1,0:T(8,128)(2,1)}, bf16[320,896]{1,0:T(8,128)(2,1)}) custom-call(s32[7]{0:T(128)} %pad_add_fusion.where_ref, bf16[896,896]{1,0:T(8,128)(2,1)} %weight_ref), custom_call_target="tpu_custom_call" | custom-call | tf_op jit(solution)/shard_map/prepare_weight/pallas_call | solution.py:87
  13.6 4.9 %collective-permute-start.4 = (bf16[448,896]{1,0:T(8,128)(2,1)}, bf16[448,896]{1,0:T(8,128)(2,1)}, u32[]{:S(2)}, u32[]{:S(2)}) collective-permute-start(bf16[448,896]{1,0:T(8,128)(2,1)} %get-tuple-element.37.refs_8_), channel_id=1, source_target_pairs={{0,8},{8,16},{16,24},{1,9},{9,17},{17,25},{2,10},{10,18},{18,26},{... | collective-permute-start | bytes 2408456 | tf_op jit(solution)/shard_map/ppermute | solution.py:465
  19.8 5.1 %collective-permute-start.9 = (bf16[128,896]{1,0:T(8,128)(2,1)}, bf16[128,896]{1,0:T(8,128)(2,1)}, u32[]{:S(2)}, u32[]{:S(2)}) collective-permute-start(bf16[128,896]{1,0:T(8,128)(2,1)} %get-tuple-element.40), channel_id=1, source_target_pairs={{0,24},{24,0},{1,25},{25,1},{2,26},{26,2},{3,27},{27,3},{4,28},{28... | collective-permute-start | bytes 688136 | tf_op jit(solution)/shard_map/ppermute | solution.py:467
  26.1 5.2 %attention.2 = bf16[2,96,896]{2,1,0:T(8,128)(2,1)} custom-call(s32[7]{0:T(128)S(1)} %copy-done.2, bf16[2,3,96,896]{3,2,1,0:T(8,128)(2,1)S(1)} %bitcast.26, bf16[2,2,96,896]{3,2,1,0:T(8,128)(2,1)S(1)} %collective-permute-done.right_ref, bf16[2,2,96,896]{3,2,1,0:T(8,128)(2,1)S(1)} %collective-permute-done.1.left_ref), custom_call_target="tpu_custom_call" | custom-call | tf_op jit(solution)/shard_map/attention/pallas_call | solution.py:144
  31.3 2.0 %collective-permute-start.2 = (bf16[1,192,896]{2,1,0:T(8,128)(2,1)}, bf16[1,192,896]{2,1,0:T(8,128)(2,1)}, u32[]{:S(2)}, u32[]{:S(2)}) collective-permute-start(bf16[1,192,896]{2,1,0:T(8,128)(2,1)} %bitcast.8), channel_id=1, source_target_pairs={{0,1},{1,0},{2,3},{3,2},{4,5},{5,4},{6,7},{7,6},{8,9},{9,8},{10,11... | collective-permute-start | bytes 1032200 | tf_op jit(solution)/shard_map/ppermute | solution.py:388
  33.6 4.5 %attention.3 = bf16[2,96,896]{2,1,0:T(8,128)(2,1)S(1)} custom-call(s32[7]{0:T(128)S(1)} %copy-done.2, bf16[2,3,96,896]{3,2,1,0:T(8,128)(2,1)S(1)} %add_convert_fusion.own_ref, bf16[2,2,96,896]{3,2,1,0:T(8,128)(2,1)S(1)} %collective-permute-done.right_ref, bf16[2,2,96,896]{3,2,1,0:T(8,128)(2,1)S(1)} %collective-permute-done.1.left_ref), custom_call_target="tpu_custom_call" | custom-call | tf_op jit(solution)/shard_map/attention/pallas_call | solution.py:144
  38.2 1.6 %collective-permute-start.8 = (bf16[1,192,896]{2,1,0:T(8,128)(2,1)S(1)}, bf16[1,192,896]{2,1,0:T(8,128)(2,1)S(1)}, u32[]{:S(2)}, u32[]{:S(2)}) collective-permute-start(bf16[1,192,896]{2,1,0:T(8,128)(2,1)S(1)} %bitcast.28), channel_id=1, source_target_pairs={{0,4},{2,6},{4,0},{6,2},{1,5},{3,7},{5,1},{7,3},{8,12},{10,14},{12... | collective-permute-start | bytes 1032200 | tf_op jit(solution)/shard_map/ppermute | solution.py:388
  41.0 2.3 %collective-permute-done.4.refs_10_ = bf16[448,896]{1,0:T(8,128)(2,1)} collective-permute-done((bf16[448,896]{1,0:T(8,128)(2,1)}, bf16[448,896]{1,0:T(8,128)(2,1)}, u32[]{:S(2)}, u32[]{:S(2)}) %collective-permute-start.4) | collective-permute-done | bytes 802848 | tf_op jit(solution)/shard_map/ppermute | solution.py:465
  45.6 2.6 %collective-permute-done.9.refs_13_ = bf16[128,896]{1,0:T(8,128)(2,1)} collective-permute-done((bf16[128,896]{1,0:T(8,128)(2,1)}, bf16[128,896]{1,0:T(8,128)(2,1)}, u32[]{:S(2)}, u32[]{:S(2)}) %collective-permute-start.9) | collective-permute-done | bytes 229408 | tf_op jit(solution)/shard_map/ppermute | solution.py:467
  48.1 1.5 %collective-permute-start.10 = (bf16[2,192,896]{2,1,0:T(8,128)(2,1)S(1)}, bf16[2,192,896]{2,1,0:T(8,128)(2,1)S(1)}, u32[]{:S(2)}, u32[]{:S(2)}) collective-permute-start(bf16[2,192,896]{2,1,0:T(8,128)(2,1)S(1)} %pad_maximum_fusion.1.refs_4_), channel_id=1, source_target_pairs={{0,1},{1,0},{2,3},{3,2},{4,5},{5,4},{6,7},{7,6},{8,9},{9,8},{10,11... | collective-permute-start | bytes 2064392 | tf_op jit(solution)/shard_map/ppermute | solution.py:388
  49.7 1.5 %collective-permute-start.5 = (bf16[2,192,896]{2,1,0:T(8,128)(2,1)S(1)}, bf16[2,192,896]{2,1,0:T(8,128)(2,1)S(1)}, u32[]{:S(2)}, u32[]{:S(2)}) collective-permute-start(bf16[2,192,896]{2,1,0:T(8,128)(2,1)S(1)} %pad_maximum_fusion.refs_0_), channel_id=1, source_target_pairs={{0,4},{2,6},{4,0},{6,2},{1,5},{3,7},{5,1},{7,3},{8,12},{10,14},{12... | collective-permute-start | bytes 2064392 | tf_op jit(solution)/shard_map/ppermute | solution.py:388
  51.2 13.2 %collective-permute-done.10.refs_5_ = bf16[2,192,896]{2,1,0:T(8,128)(2,1)S(1)} collective-permute-done((bf16[2,192,896]{2,1,0:T(8,128)(2,1)S(1)}, bf16[2,192,896]{2,1,0:T(8,128)(2,1)S(1)}, u32[]{:S(2)}, u32[]{:S(2)}) %collective-permute-start.10) | collective-permute-done | bytes 688160 | tf_op jit(solution)/shard_map/ppermute | solution.py:388
  66.1 5.1 %collective-permute-start.15 = (bf16[320,896]{1,0:T(8,128)(2,1)S(1)}, bf16[320,896]{1,0:T(8,128)(2,1)S(1)}, u32[]{:S(2)}, u32[]{:S(2)}) collective-permute-start(bf16[320,896]{1,0:T(8,128)(2,1)S(1)} %copy-done.5), channel_id=1, source_target_pairs={{0,24},{24,0},{1,25},{25,1},{2,26},{26,2},{3,27},{27,3},{4,28},{28... | collective-permute-start | bytes 1720328 | tf_op jit(solution)/shard_map/ppermute | solution.py:467
  71.2 5.7 %project.1 = (f32[768,512]{1,0:T(8,128)S(1)}, bf16[768,896]{1,0:T(8,128)(2,1)S(1)}) custom-call(s32[7]{0:T(128)S(1)} %copy-done.2, bf16[2,192,896]{2,1,0:T(8,128)(2,1)S(1)} %pad_maximum_fusion.refs_0_, bf16[2,192,896]{2,1,0:T(8,128)(2,1)S(1)} %collective-permute-done.5.refs_1_, bf16[2,192,896]{2,1,0:T(8,128)(2,1)S(1)} %collective-permute-done.6.refs_2_, ...), custom_call_target="tpu_custom_call" | custom-call | tf_op jit(solution)/shard_map/project/pallas_call | solution.py:230
  76.9 7.8 %collective-permute-done.15.weight_ref = bf16[320,896]{1,0:T(8,128)(2,1)S(1)} collective-permute-done((bf16[320,896]{1,0:T(8,128)(2,1)S(1)}, bf16[320,896]{1,0:T(8,128)(2,1)S(1)}, u32[]{:S(2)}, u32[]{:S(2)}) %collective-permute-start.15) | collective-permute-done | bytes 573472 | tf_op jit(solution)/shard_map/ppermute | solution.py:467
  84.7 2.0 %project_last.1 = (f32[768,512]{1,0:T(8,128)S(1)}, f32[8,1,768]{2,1,0:T(1,128)S(1)}) custom-call(s32[7]{0:T(128)S(1)} %copy-done.2, bf16[768,896]{1,0:T(8,128)(2,1)S(1)} %get-tuple-element.48.rows_ref, bf16[320,896]{1,0:T(8,128)(2,1)S(1)} %collective-permute-done.15.weight_ref, ...), custom_call_target="tpu_custom_call", output_to_operand_aliasing={{0}: (3, {})} | custom-call | tf_op jit(solution)/shard_map/project_last/pallas_call | solution.py:277
  86.7 7.9 %all_to_all.10.squares_ref = f32[8,1,768]{2,1,0:T(1,128)S(1)} all-to-all(f32[8,1,768]{2,1,0:T(1,128)S(1)} %get-tuple-element.52), channel_id=1, replica_groups=mesh['frames'=4,'mp'=4,'dp'=2] {'mp','dp'}, dimensions={0} | all-to-all | bytes 49152 | tf_op jit(solution)/shard_map/all_to_all | solution.py:411
  96.8 1.4 %collective-permute-start.19 = (bf16[48,448]{1,0:T(8,128)(2,1)S(1)}, bf16[48,448]{1,0:T(8,128)(2,1)S(1)}, u32[]{:S(2)}, u32[]{:S(2)}) collective-permute-start(bf16[48,448]{1,0:T(8,128)(2,1)S(1)} %get-tuple-element.64), channel_id=1, source_target_pairs={{0,1},{1,0},{2,3},{3,2},{4,5},{5,4},{6,7},{7,6},{8,9},{9,8},{10,11... | collective-permute-start | bytes 129032 | tf_op jit(solution)/shard_map/ppermute | solution.py:388
  98.8 1.4 %collective-permute-start.17 = (bf16[48,448]{1,0:T(8,128)(2,1)S(1)}, bf16[48,448]{1,0:T(8,128)(2,1)S(1)}, u32[]{:S(2)}, u32[]{:S(2)}) collective-permute-start(bf16[48,448]{1,0:T(8,128)(2,1)S(1)} %get-tuple-element.66), channel_id=1, source_target_pairs={{0,1},{1,0},{2,3},{3,2},{4,5},{5,4},{6,7},{7,6},{8,9},{9,8},{10,11... | collective-permute-start | bytes 129032 | tf_op jit(solution)/shard_map/ppermute | solution.py:388
  100.2 4.0 %all-to-all-start.1 = ((f32[32,1,512]{2,1,0:T(1,128)}), f32[32,1,512]{2,1,0:T(1,128)S(1)}, u32[]{:S(2)}, u32[]{:S(2)}) async-start(f32[32,1,512]{2,1,0:T(1,128)} %finish.1.after_ref), calls=%async_computation.1 | async-start | bytes 131072 | tf_op jit(solution)/shard_map/all_to_all | solution.py:411
  105.2 6.6 %all-to-all-done.1.rows_ref = f32[32,1,512]{2,1,0:T(1,128)S(1)} async-done(((f32[32,1,512]{2,1,0:T(1,128)}), f32[32,1,512]{2,1,0:T(1,128)S(1)}, u32[]{:S(2)}, u32[]{:S(2)}) %all-to-all-start.1) | async-done | bytes 65568 | tf_op jit(solution)/shard_map/all_to_all | solution.py:411
  111.8 1.4 %conclude.1 = (f32[1]{0:T(128)}, f32[896]{0:T(1024)}) custom-call(s32[7]{0:T(128)S(1)} %copy-done.2, f32[32,1,512]{2,1,0:T(1,128)S(1)} %all-to-all-done.1.rows_ref, f32[1,896]{1,0:T(1,128)S(1)} %broadcast_in_dim.10.gain_ref), custom_call_target="tpu_custom_call" | custom-call | tf_op jit(solution)/shard_map/conclude/pallas_call | solution.py:369
  (55 shorter events, 13.9 us)
Async XLA Ops:
  0.6 25.4 %copy-start = (bf16[1,2,96,3,896]{4,2,3,1,0:T(8,128)(2,1)S(1)}, bf16[1,2,96,3,896]{4,2,3,1,0:T(8,128)(2,1)}, u32[]{:S(2)}) copy-start(bf16[1,2,96,3,896]{4,2,3,1,0:T(8,128)(2,1)} %param.5) | copy-start | bytes 3096580
  3.1 21.8 %collective-permute-start = (bf16[2,2,96,896]{3,2,1,0:T(8,128)(2,1)}, bf16[2,2,96,896]{3,2,1,0:T(8,128)(2,1)S(1)}, u32[]{:S(2)}, u32[]{:S(2)}) collective-permute-start(bf16[2,2,96,896]{3,2,1,0:T(8,128)(2,1)} %get-tuple-element.34), channel_id=1, source_target_pairs={{8,0},{16,8},{24,16},{9,1},{17,9},{25,17},{10,2},{18,10},{26,18},{... | collective-permute-start | bytes 2064392 | tf_op jit(solution)/shard_map/ppermute | solution.py:447
  4.4 21.7 %collective-permute-start.1 = (bf16[2,2,96,896]{3,2,1,0:T(8,128)(2,1)}, bf16[2,2,96,896]{3,2,1,0:T(8,128)(2,1)S(1)}, u32[]{:S(2)}, u32[]{:S(2)}) collective-permute-start(bf16[2,2,96,896]{3,2,1,0:T(8,128)(2,1)} %get-tuple-element.35), channel_id=1, source_target_pairs={{0,8},{8,16},{16,24},{1,9},{9,17},{17,25},{2,10},{10,18},{18,26},{... | collective-permute-start | bytes 2064392 | tf_op jit(solution)/shard_map/ppermute | solution.py:448
  13.6 29.7 %collective-permute-start.4 = (bf16[448,896]{1,0:T(8,128)(2,1)}, bf16[448,896]{1,0:T(8,128)(2,1)}, u32[]{:S(2)}, u32[]{:S(2)}) collective-permute-start(bf16[448,896]{1,0:T(8,128)(2,1)} %get-tuple-element.37.refs_8_), channel_id=1, source_target_pairs={{0,8},{8,16},{16,24},{1,9},{9,17},{17,25},{2,10},{10,18},{18,26},{... | collective-permute-start | bytes 2408456 | tf_op jit(solution)/shard_map/ppermute | solution.py:465
  18.5 24.8 %collective-permute-start.3 = (bf16[448,896]{1,0:T(8,128)(2,1)}, bf16[448,896]{1,0:T(8,128)(2,1)}, u32[]{:S(2)}, u32[]{:S(2)}) collective-permute-start(bf16[448,896]{1,0:T(8,128)(2,1)} %get-tuple-element.37.refs_8_), channel_id=1, source_target_pairs={{8,0},{16,8},{24,16},{9,1},{17,9},{25,17},{10,2},{18,10},{26,18},{... | collective-permute-start | bytes 2408456 | tf_op jit(solution)/shard_map/ppermute | solution.py:465
  19.8 28.4 %collective-permute-start.9 = (bf16[128,896]{1,0:T(8,128)(2,1)}, bf16[128,896]{1,0:T(8,128)(2,1)}, u32[]{:S(2)}, u32[]{:S(2)}) collective-permute-start(bf16[128,896]{1,0:T(8,128)(2,1)} %get-tuple-element.40), channel_id=1, source_target_pairs={{0,24},{24,0},{1,25},{25,1},{2,26},{26,2},{3,27},{27,3},{4,28},{28... | collective-permute-start | bytes 688136 | tf_op jit(solution)/shard_map/ppermute | solution.py:467
  31.3 8.5 %collective-permute-start.2 = (bf16[1,192,896]{2,1,0:T(8,128)(2,1)}, bf16[1,192,896]{2,1,0:T(8,128)(2,1)}, u32[]{:S(2)}, u32[]{:S(2)}) collective-permute-start(bf16[1,192,896]{2,1,0:T(8,128)(2,1)} %bitcast.8), channel_id=1, source_target_pairs={{0,1},{1,0},{2,3},{3,2},{4,5},{5,4},{6,7},{7,6},{8,9},{9,8},{10,11... | collective-permute-start | bytes 1032200 | tf_op jit(solution)/shard_map/ppermute | solution.py:388
  38.2 27.9 %copy-start.5 = (bf16[320,896]{1,0:T(8,128)(2,1)S(1)}, bf16[320,896]{1,0:T(8,128)(2,1)}, u32[]{:S(2)}) copy-start(bf16[320,896]{1,0:T(8,128)(2,1)} %get-tuple-element.49) | copy-start | bytes 1720324
  38.2 33.0 %copy-start.1 = (bf16[448,896]{1,0:T(8,128)(2,1)S(1)}, bf16[448,896]{1,0:T(8,128)(2,1)}, u32[]{:S(2)}) copy-start(bf16[448,896]{1,0:T(8,128)(2,1)} %get-tuple-element.37.refs_8_) | copy-start | bytes 2408452
  38.2 7.3 %collective-permute-start.8 = (bf16[1,192,896]{2,1,0:T(8,128)(2,1)S(1)}, bf16[1,192,896]{2,1,0:T(8,128)(2,1)S(1)}, u32[]{:S(2)}, u32[]{:S(2)}) collective-permute-start(bf16[1,192,896]{2,1,0:T(8,128)(2,1)S(1)} %bitcast.28), channel_id=1, source_target_pairs={{0,4},{2,6},{4,0},{6,2},{1,5},{3,7},{5,1},{7,3},{8,12},{10,14},{12... | collective-permute-start | bytes 1032200 | tf_op jit(solution)/shard_map/ppermute | solution.py:388
  43.3 22.3 %collective-permute-start.12 = (bf16[448,896]{1,0:T(8,128)(2,1)}, bf16[448,896]{1,0:T(8,128)(2,1)S(1)}, u32[]{:S(2)}, u32[]{:S(2)}) collective-permute-start(bf16[448,896]{1,0:T(8,128)(2,1)} %collective-permute-done.3.refs_9_), channel_id=1, source_target_pairs={{8,0},{16,8},{9,1},{17,9},{10,2},{18,10},{11,3},{19,11},{12,4},{20... | collective-permute-start | bytes 2408456 | tf_op jit(solution)/shard_map/ppermute | solution.py:477
  44.6 21.0 %collective-permute-start.13 = (bf16[448,896]{1,0:T(8,128)(2,1)}, bf16[448,896]{1,0:T(8,128)(2,1)S(1)}, u32[]{:S(2)}, u32[]{:S(2)}) collective-permute-start(bf16[448,896]{1,0:T(8,128)(2,1)} %collective-permute-done.4.refs_10_), channel_id=1, source_target_pairs={{8,16},{16,24},{9,17},{17,25},{10,18},{18,26},{11,19},{19,27},{12,... | collective-permute-start | bytes 2408456 | tf_op jit(solution)/shard_map/ppermute | solution.py:478
  48.1 16.2 %collective-permute-start.10 = (bf16[2,192,896]{2,1,0:T(8,128)(2,1)S(1)}, bf16[2,192,896]{2,1,0:T(8,128)(2,1)S(1)}, u32[]{:S(2)}, u32[]{:S(2)}) collective-permute-start(bf16[2,192,896]{2,1,0:T(8,128)(2,1)S(1)} %pad_maximum_fusion.1.refs_4_), channel_id=1, source_target_pairs={{0,1},{1,0},{2,3},{3,2},{4,5},{5,4},{6,7},{7,6},{8,9},{9,8},{10,11... | collective-permute-start | bytes 2064392 | tf_op jit(solution)/shard_map/ppermute | solution.py:388
  49.7 15.9 %collective-permute-start.5 = (bf16[2,192,896]{2,1,0:T(8,128)(2,1)S(1)}, bf16[2,192,896]{2,1,0:T(8,128)(2,1)S(1)}, u32[]{:S(2)}, u32[]{:S(2)}) collective-permute-start(bf16[2,192,896]{2,1,0:T(8,128)(2,1)S(1)} %pad_maximum_fusion.refs_0_), channel_id=1, source_target_pairs={{0,4},{2,6},{4,0},{6,2},{1,5},{3,7},{5,1},{7,3},{8,12},{10,14},{12... | collective-permute-start | bytes 2064392 | tf_op jit(solution)/shard_map/ppermute | solution.py:388
  51.2 20.0 %collective-permute-start.6 = (bf16[2,192,896]{2,1,0:T(8,128)(2,1)S(1)}, bf16[2,192,896]{2,1,0:T(8,128)(2,1)S(1)}, u32[]{:S(2)}, u32[]{:S(2)}) collective-permute-start(bf16[2,192,896]{2,1,0:T(8,128)(2,1)S(1)} %pad_maximum_fusion.refs_0_), channel_id=1, source_target_pairs={{0,2},{2,0},{4,6},{6,4},{1,3},{3,1},{5,7},{7,5},{8,10},{10,8},{12,... | collective-permute-start | bytes 2064392 | tf_op jit(solution)/shard_map/ppermute | solution.py:388
  64.3 6.8 %collective-permute-start.11 = (bf16[2,192,896]{2,1,0:T(8,128)(2,1)S(1)}, bf16[2,192,896]{2,1,0:T(8,128)(2,1)S(1)}, u32[]{:S(2)}, u32[]{:S(2)}) collective-permute-start(bf16[2,192,896]{2,1,0:T(8,128)(2,1)S(1)} %pad_maximum_fusion.1.refs_4_), channel_id=1, source_target_pairs={{0,2},{2,0},{4,6},{6,4},{1,3},{3,1},{5,7},{7,5},{8,10},{10,8},{12,... | collective-permute-start | bytes 2064392 | tf_op jit(solution)/shard_map/ppermute | solution.py:388
  65.6 5.6 %collective-permute-start.7 = (bf16[2,192,896]{2,1,0:T(8,128)(2,1)S(1)}, bf16[2,192,896]{2,1,0:T(8,128)(2,1)S(1)}, u32[]{:S(2)}, u32[]{:S(2)}) collective-permute-start(bf16[2,192,896]{2,1,0:T(8,128)(2,1)S(1)} %collective-permute-done.5.refs_1_), channel_id=1, source_target_pairs={{0,2},{2,0},{4,6},{6,4},{1,3},{3,1},{5,7},{7,5},{8,10},{10,8},{12,... | collective-permute-start | bytes 2064392 | tf_op jit(solution)/shard_map/ppermute | solution.py:388
  65.6 5.6 %collective-permute-start.14 = (bf16[2,192,896]{2,1,0:T(8,128)(2,1)S(1)}, bf16[2,192,896]{2,1,0:T(8,128)(2,1)S(1)}, u32[]{:S(2)}, u32[]{:S(2)}) collective-permute-start(bf16[2,192,896]{2,1,0:T(8,128)(2,1)S(1)} %collective-permute-done.10.refs_5_), channel_id=1, source_target_pairs={{0,2},{2,0},{4,6},{6,4},{1,3},{3,1},{5,7},{7,5},{8,10},{10,8},{12,... | collective-permute-start | bytes 2064392 | tf_op jit(solution)/shard_map/ppermute | solution.py:388
  66.1 18.6 %collective-permute-start.15 = (bf16[320,896]{1,0:T(8,128)(2,1)S(1)}, bf16[320,896]{1,0:T(8,128)(2,1)S(1)}, u32[]{:S(2)}, u32[]{:S(2)}) collective-permute-start(bf16[320,896]{1,0:T(8,128)(2,1)S(1)} %copy-done.5), channel_id=1, source_target_pairs={{0,24},{24,0},{1,25},{25,1},{2,26},{26,2},{3,27},{27,3},{4,28},{28... | collective-permute-start | bytes 1720328 | tf_op jit(solution)/shard_map/ppermute | solution.py:467
  96.1 8.1 %collective-permute-start.16 = (bf16[48,448]{1,0:T(8,128)(2,1)S(1)}, bf16[48,448]{1,0:T(8,128)(2,1)S(1)}, u32[]{:S(2)}, u32[]{:S(2)}) collective-permute-start(bf16[48,448]{1,0:T(8,128)(2,1)S(1)} %get-tuple-element.63), channel_id=1, source_target_pairs={{0,1},{1,0},{2,3},{3,2},{4,5},{5,4},{6,7},{7,6},{8,9},{9,8},{10,11... | collective-permute-start | bytes 129032 | tf_op jit(solution)/shard_map/ppermute | solution.py:388
  96.8 7.4 %collective-permute-start.19 = (bf16[48,448]{1,0:T(8,128)(2,1)S(1)}, bf16[48,448]{1,0:T(8,128)(2,1)S(1)}, u32[]{:S(2)}, u32[]{:S(2)}) collective-permute-start(bf16[48,448]{1,0:T(8,128)(2,1)S(1)} %get-tuple-element.64), channel_id=1, source_target_pairs={{0,1},{1,0},{2,3},{3,2},{4,5},{5,4},{6,7},{7,6},{8,9},{9,8},{10,11... | collective-permute-start | bytes 129032 | tf_op jit(solution)/shard_map/ppermute | solution.py:388
  98.1 6.1 %collective-permute-start.18 = (bf16[48,448]{1,0:T(8,128)(2,1)S(1)}, bf16[48,448]{1,0:T(8,128)(2,1)S(1)}, u32[]{:S(2)}, u32[]{:S(2)}) collective-permute-start(bf16[48,448]{1,0:T(8,128)(2,1)S(1)} %get-tuple-element.65), channel_id=1, source_target_pairs={{0,1},{1,0},{2,3},{3,2},{4,5},{5,4},{6,7},{7,6},{8,9},{9,8},{10,11... | collective-permute-start | bytes 129032 | tf_op jit(solution)/shard_map/ppermute | solution.py:388
  98.8 5.4 %collective-permute-start.17 = (bf16[48,448]{1,0:T(8,128)(2,1)S(1)}, bf16[48,448]{1,0:T(8,128)(2,1)S(1)}, u32[]{:S(2)}, u32[]{:S(2)}) collective-permute-start(bf16[48,448]{1,0:T(8,128)(2,1)S(1)} %get-tuple-element.66), channel_id=1, source_target_pairs={{0,1},{1,0},{2,3},{3,2},{4,5},{5,4},{6,7},{7,6},{8,9},{9,8},{10,11... | collective-permute-start | bytes 129032 | tf_op jit(solution)/shard_map/ppermute | solution.py:388
  100.2 11.6 %all-to-all-start.1 = ((f32[32,1,512]{2,1,0:T(1,128)}), f32[32,1,512]{2,1,0:T(1,128)S(1)}, u32[]{:S(2)}, u32[]{:S(2)}) async-start(f32[32,1,512]{2,1,0:T(1,128)} %finish.1.after_ref), calls=%async_computation.1 | async-start | bytes 131072 | tf_op jit(solution)/shard_map/all_to_all | solution.py:411
  (4 other events, 46.7 us)

commit v10 on v8

--- a/solution.py
+++ b/solution.py
@@ -99,7 +99,7 @@
     )(where, weight)
 
 
-def attend_kernel(where_ref, own_ref, right_ref, left_ref, out_ref):
+def attend_kernel(where_ref, own_ref, left_ref, right_ref, out_ref):
     slots, _, tile_len, width = own_ref.shape
     key_pos = lax.broadcasted_iota(jnp.int32, (1, 2 * tile_len), 1)
     live = []
@@ -157,7 +157,7 @@
             transcendentals=0,
         ),
         name="attention",
-    )(where, own, right, left)
+    )(where, own, left, right)
 
 
 def whole_lanes(columns):

time: 111 us -> 112 us (level)
  waiting for transfers between devices: 35.4 us -> 40.2 us
  starting transfers between devices: 37.7 us -> 33.7 us
    ppermute x2, waiting for transfers between devices: 10.5 us -> 14.4 us  [local(): lax.ppermute(block, 'frames', [(0, last), (last, 0)])]
    ppermute x9, waiting for transfers between devices: 15 us -> 18.2 us  [swap(): return lax.ppermute(array, axis, [(i, i ^ distance) for i in range(count)])]
    all_to_all x1, waiting for transfers between devices: 6.35 us -> 4.19 us  [collect(): return lax.all_to_all(rows, axes, split_axis=0, concat_axis=0, tiled=True)]
    all_to_all x1, starting transfers between devices: 4.73 us -> 2.57 us  [collect(): return lax.all_to_all(rows, axes, split_axis=0, concat_axis=0, tiled=True)]
    ppermute x1, waiting for transfers between devices: 0.01 us -> 2.08 us  [local(): right = lax.ppermute(head, 'frames', down)]
    ppermute x2, starting transfers between devices: 10.1 us -> 8.71 us  [local(): lax.ppermute(block, 'frames', [(0, last), (last, 0)])]
    ppermute x1, waiting for transfers between devices: 1.2 us -> 0.01 us  [local(): left = lax.ppermute(tail, 'frames', up)]
  transfers between devices with their start and end apart: 18 -> 18, of which waited for: 9 -> 10; matrix products, arithmetic and copies ran while one was open for 3% -> 3% of each run, Pallas kernels for 18% -> 17%
where the time goes in v10:
time: 112 us; the launch traced here: 111 us
  waiting for transfers between devices  40.2 us (36%)
  starting transfers between devices  33.7 us (30%)
  Pallas kernels  25.3 us (23%)
  blocking collectives  7.92 us (7%)
  other arithmetic  3.13 us (3%)
    ppermute x9, waiting for transfers between devices, swap(): return lax.ppermute(array, axis, [(i, i ^ distance) for i in range(count)])  18.2 us
    ppermute x2, waiting for transfers between devices, local(): lax.ppermute(block, 'frames', [(0, last), (last, 0)])  14.4 us
    pallas_call x2, Pallas kernels, attention(): pl.pallas_call(attend_kernel, grid_spec=pltpu.PrefetchScalarGridSpec(num_...  9.76 us
    ppermute x2, starting transfers between devices, local(): lax.ppermute(block, 'frames', [(0, last), (last, 0)])  8.71 us
    all_to_all x1, blocking collectives, collect(): return lax.all_to_all(rows, axes, split_axis=0, concat_axis=0, tiled=True)  7.92 us
    pallas_call x2, Pallas kernels, project(): pl.pallas_call(kernel, in_specs=[pl.BlockSpec(memory_space=pltpu.SMEM)] +...  7.56 us
    ppermute x9, starting transfers between devices, swap(): return lax.ppermute(array, axis, [(i, i ^ distance) for i in range(count)])  7.32 us
    ppermute x2, starting transfers between devices, local(): near = [lax.ppermute(own_weight, 'frames', pairs) for pairs in (down, up)]  6.86 us
  transfers between devices with their start and end apart: 18, of which 10 were waited for; matrix products, arithmetic and copies ran while one was open for 3% of the time, Pallas kernels for 17%

profile of v10, /device:TPU:0, one launch (start us, length us, event | category | flops | bytes accessed | tf_op | source)
XLA Modules:
  0.0 111.3 jit_solution(17002473339676847201)
XLA Ops:
  0.6 2.4 %prepare_halo.1 = (bf16[2,2,96,896]{3,2,1,0:T(8,128)(2,1)}, bf16[2,2,96,896]{3,2,1,0:T(8,128)(2,1)}) custom-call(bf16[2,3,96,896]{3,2,1,0:T(8,128)(2,1)} %bitcast.17, bf16[2,3,96,896]{3,2,1,0:T(8,128)(2,1)} %bitcast.24), custom_call_target="tpu_custom_call" | custom-call | tf_op jit(solution)/shard_map/prepare_halo/pallas_call | solution.py:53
  3.0 5.0 %collective-permute-start = (bf16[2,2,96,896]{3,2,1,0:T(8,128)(2,1)}, bf16[2,2,96,896]{3,2,1,0:T(8,128)(2,1)S(1)}, u32[]{:S(2)}, u32[]{:S(2)}) collective-permute-start(bf16[2,2,96,896]{3,2,1,0:T(8,128)(2,1)} %get-tuple-element.32), channel_id=1, source_target_pairs={{0,8},{8,16},{16,24},{1,9},{9,17},{17,25},{2,10},{10,18},{18,26},{... | collective-permute-start | bytes 2064392 | tf_op jit(solution)/shard_map/ppermute | solution.py:416
  10.0 2.9 %prepare_weight.1 = (bf16[448,896]{1,0:T(8,128)(2,1)}, bf16[128,896]{1,0:T(8,128)(2,1)}, bf16[320,896]{1,0:T(8,128)(2,1)}) custom-call(s32[7]{0:T(128)} %pad_add_fusion.where_ref, bf16[896,896]{1,0:T(8,128)(2,1)} %weight_ref), custom_call_target="tpu_custom_call" | custom-call | tf_op jit(solution)/shard_map/prepare_weight/pallas_call | solution.py:87
  12.9 5.6 %collective-permute-start.4 = (bf16[448,896]{1,0:T(8,128)(2,1)}, bf16[448,896]{1,0:T(8,128)(2,1)}, u32[]{:S(2)}, u32[]{:S(2)}) collective-permute-start(bf16[448,896]{1,0:T(8,128)(2,1)} %get-tuple-element.35.refs_8_), channel_id=1, source_target_pairs={{0,8},{8,16},{16,24},{1,9},{9,17},{17,25},{2,10},{10,18},{18,26},{... | collective-permute-start | bytes 2408456 | tf_op jit(solution)/shard_map/ppermute | solution.py:433
  19.8 6.6 %collective-permute-start.9 = (bf16[128,896]{1,0:T(8,128)(2,1)}, bf16[128,896]{1,0:T(8,128)(2,1)}, u32[]{:S(2)}, u32[]{:S(2)}) collective-permute-start(bf16[128,896]{1,0:T(8,128)(2,1)} %get-tuple-element.38), channel_id=1, source_target_pairs={{0,24},{24,0},{1,25},{25,1},{2,26},{26,2},{3,27},{27,3},{4,28},{28... | collective-permute-start | bytes 688136 | tf_op jit(solution)/shard_map/ppermute | solution.py:435
  26.4 2.1 %collective-permute-done.1.right_ref = bf16[2,2,96,896]{3,2,1,0:T(8,128)(2,1)S(1)} collective-permute-done((bf16[2,2,96,896]{3,2,1,0:T(8,128)(2,1)}, bf16[2,2,96,896]{3,2,1,0:T(8,128)(2,1)S(1)}, u32[]{:S(2)}, u32[]{:S(2)}) %collective-permute-start.1) | collective-permute-done | bytes 688160 | tf_op jit(solution)/shard_map/ppermute | solution.py:415
  28.5 5.2 %attention.2 = bf16[2,96,896]{2,1,0:T(8,128)(2,1)} custom-call(s32[7]{0:T(128)S(1)} %copy-done.2, bf16[2,3,96,896]{3,2,1,0:T(8,128)(2,1)S(1)} %bitcast.18, bf16[2,2,96,896]{3,2,1,0:T(8,128)(2,1)S(1)} %collective-permute-done.left_ref, bf16[2,2,96,896]{3,2,1,0:T(8,128)(2,1)S(1)} %collective-permute-done.1.right_ref), custom_call_target="tpu_custom_call" | custom-call | tf_op jit(solution)/shard_map/attention/pallas_call | solution.py:144
  33.7 1.5 %collective-permute-start.2 = (bf16[1,192,896]{2,1,0:T(8,128)(2,1)}, bf16[1,192,896]{2,1,0:T(8,128)(2,1)}, u32[]{:S(2)}, u32[]{:S(2)}) collective-permute-start(bf16[1,192,896]{2,1,0:T(8,128)(2,1)} %bitcast.8), channel_id=1, source_target_pairs={{0,1},{1,0},{2,3},{3,2},{4,5},{5,4},{6,7},{7,6},{8,9},{9,8},{10,11... | collective-permute-start | bytes 1032200 | tf_op jit(solution)/shard_map/ppermute | solution.py:356
  35.6 4.5 %attention.3 = bf16[2,96,896]{2,1,0:T(8,128)(2,1)S(1)} custom-call(s32[7]{0:T(128)S(1)} %copy-done.2, bf16[2,3,96,896]{3,2,1,0:T(8,128)(2,1)S(1)} %add_convert_fusion.own_ref, bf16[2,2,96,896]{3,2,1,0:T(8,128)(2,1)S(1)} %collective-permute-done.left_ref, bf16[2,2,96,896]{3,2,1,0:T(8,128)(2,1)S(1)} %collective-permute-done.1.right_ref), custom_call_target="tpu_custom_call" | custom-call | tf_op jit(solution)/shard_map/attention/pallas_call | solution.py:144
  40.2 1.5 %collective-permute-start.8 = (bf16[1,192,896]{2,1,0:T(8,128)(2,1)S(1)}, bf16[1,192,896]{2,1,0:T(8,128)(2,1)S(1)}, u32[]{:S(2)}, u32[]{:S(2)}) collective-permute-start(bf16[1,192,896]{2,1,0:T(8,128)(2,1)S(1)} %bitcast.20), channel_id=1, source_target_pairs={{0,4},{2,6},{4,0},{6,2},{1,5},{3,7},{5,1},{7,3},{8,12},{10,14},{12... | collective-permute-start | bytes 1032200 | tf_op jit(solution)/shard_map/ppermute | solution.py:356
  42.9 1.4 %collective-permute-done.3.refs_9_ = bf16[448,896]{1,0:T(8,128)(2,1)} collective-permute-done((bf16[448,896]{1,0:T(8,128)(2,1)}, bf16[448,896]{1,0:T(8,128)(2,1)}, u32[]{:S(2)}, u32[]{:S(2)}) %collective-permute-start.3) | collective-permute-done | bytes 802848 | tf_op jit(solution)/shard_map/ppermute | solution.py:433
  47.5 3.9 %collective-permute-done.9.refs_13_ = bf16[128,896]{1,0:T(8,128)(2,1)} collective-permute-done((bf16[128,896]{1,0:T(8,128)(2,1)}, bf16[128,896]{1,0:T(8,128)(2,1)}, u32[]{:S(2)}, u32[]{:S(2)}) %collective-permute-start.9) | collective-permute-done | bytes 229408 | tf_op jit(solution)/shard_map/ppermute | solution.py:435
  51.4 1.5 %collective-permute-start.10 = (bf16[2,192,896]{2,1,0:T(8,128)(2,1)S(1)}, bf16[2,192,896]{2,1,0:T(8,128)(2,1)S(1)}, u32[]{:S(2)}, u32[]{:S(2)}) collective-permute-start(bf16[2,192,896]{2,1,0:T(8,128)(2,1)S(1)} %pad_maximum_fusion.1.refs_4_), channel_id=1, source_target_pairs={{0,1},{1,0},{2,3},{3,2},{4,5},{5,4},{6,7},{7,6},{8,9},{9,8},{10,11... | collective-permute-start | bytes 2064392 | tf_op jit(solution)/shard_map/ppermute | solution.py:356
  53.0 1.5 %collective-permute-start.5 = (bf16[2,192,896]{2,1,0:T(8,128)(2,1)S(1)}, bf16[2,192,896]{2,1,0:T(8,128)(2,1)S(1)}, u32[]{:S(2)}, u32[]{:S(2)}) collective-permute-start(bf16[2,192,896]{2,1,0:T(8,128)(2,1)S(1)} %pad_maximum_fusion.refs_0_), channel_id=1, source_target_pairs={{0,4},{2,6},{4,0},{6,2},{1,5},{3,7},{5,1},{7,3},{8,12},{10,14},{12... | collective-permute-start | bytes 2064392 | tf_op jit(solution)/shard_map/ppermute | solution.py:356
  54.5 12.9 %collective-permute-done.10.refs_5_ = bf16[2,192,896]{2,1,0:T(8,128)(2,1)S(1)} collective-permute-done((bf16[2,192,896]{2,1,0:T(8,128)(2,1)S(1)}, bf16[2,192,896]{2,1,0:T(8,128)(2,1)S(1)}, u32[]{:S(2)}, u32[]{:S(2)}) %collective-permute-start.10) | collective-permute-done | bytes 688160 | tf_op jit(solution)/shard_map/ppermute | solution.py:356
  69.1 2.1 %collective-permute-start.15 = (bf16[320,896]{1,0:T(8,128)(2,1)S(1)}, bf16[320,896]{1,0:T(8,128)(2,1)S(1)}, u32[]{:S(2)}, u32[]{:S(2)}) collective-permute-start(bf16[320,896]{1,0:T(8,128)(2,1)S(1)} %copy-done.5), channel_id=1, source_target_pairs={{0,24},{24,0},{1,25},{25,1},{2,26},{26,2},{3,27},{27,3},{4,28},{28... | collective-permute-start | bytes 1720328 | tf_op jit(solution)/shard_map/ppermute | solution.py:435
  71.7 5.6 %project.2.refs_9_ = f32[768,512]{1,0:T(8,128)S(1)} custom-call(s32[7]{0:T(128)S(1)} %copy-done.2, bf16[2,192,896]{2,1,0:T(8,128)(2,1)S(1)} %pad_maximum_fusion.refs_0_, bf16[2,192,896]{2,1,0:T(8,128)(2,1)S(1)} %collective-permute-done.5.refs_1_, bf16[2,192,896]{2,1,0:T(8,128)(2,1)S(1)} %collective-permute-done.6.refs_2_, ...), custom_call_target="tpu_custom_call" | custom-call | tf_op jit(solution)/shard_map/project/pallas_call | solution.py:243
  77.2 10.5 %collective-permute-done.15.refs_8_ = bf16[320,896]{1,0:T(8,128)(2,1)S(1)} collective-permute-done((bf16[320,896]{1,0:T(8,128)(2,1)S(1)}, bf16[320,896]{1,0:T(8,128)(2,1)S(1)}, u32[]{:S(2)}, u32[]{:S(2)}) %collective-permute-start.15) | collective-permute-done | bytes 573472 | tf_op jit(solution)/shard_map/ppermute | solution.py:435
  87.7 2.0 %project.3 = (f32[768,512]{1,0:T(8,128)S(1)}, f32[8,1,768]{2,1,0:T(1,128)S(1)}) custom-call(s32[7]{0:T(128)S(1)} %copy-done.2, bf16[2,192,896]{2,1,0:T(8,128)(2,1)S(1)} %pad_maximum_fusion.refs_0_, bf16[2,192,896]{2,1,0:T(8,128)(2,1)S(1)} %collective-permute-done.5.refs_1_, ...), custom_call_target="tpu_custom_call", output_to_operand_aliasing={{0}: (10, {})} | custom-call | tf_op jit(solution)/shard_map/project/pallas_call | solution.py:243
  89.7 7.9 %all_to_all.10.squares_ref = f32[8,1,768]{2,1,0:T(1,128)S(1)} all-to-all(f32[8,1,768]{2,1,0:T(1,128)S(1)} %get-tuple-element.48), channel_id=1, replica_groups=mesh['frames'=4,'mp'=4,'dp'=2] {'mp','dp'}, dimensions={0} | all-to-all | bytes 49152 | tf_op jit(solution)/shard_map/all_to_all | solution.py:379
  99.8 2.6 %all-to-all-start.1 = ((f32[32,1,512]{2,1,0:T(1,128)}), f32[32,1,512]{2,1,0:T(1,128)S(1)}, u32[]{:S(2)}, u32[]{:S(2)}) async-start(f32[32,1,512]{2,1,0:T(1,128)} %finish.1), calls=%async_computation.1 | async-start | bytes 131072 | tf_op jit(solution)/shard_map/all_to_all | solution.py:379
  102.4 2.5 %collective-permute-done.16 = bf16[2,96,448]{2,1,0:T(8,128)(2,1)S(1)} collective-permute-done((bf16[2,96,448]{2,1,0:T(8,128)(2,1)S(1)}, bf16[2,96,448]{2,1,0:T(8,128)(2,1)S(1)}, u32[]{:S(2)}, u32[]{:S(2)}) %collective-permute-start.16) | collective-permute-done | bytes 172064 | tf_op jit(solution)/shard_map/ppermute | solution.py:356
  105.8 4.2 %all-to-all-done.1.rows_ref = f32[32,1,512]{2,1,0:T(1,128)S(1)} async-done(((f32[32,1,512]{2,1,0:T(1,128)}), f32[32,1,512]{2,1,0:T(1,128)S(1)}, u32[]{:S(2)}, u32[]{:S(2)}) %all-to-all-start.1) | async-done | bytes 65568 | tf_op jit(solution)/shard_map/all_to_all | solution.py:379
  110.0 1.4 %conclude.1 = (f32[1]{0:T(128)}, f32[896]{0:T(1024)}) custom-call(s32[7]{0:T(128)S(1)} %copy-done.2, f32[32,1,512]{2,1,0:T(1,128)S(1)} %all-to-all-done.1.rows_ref, f32[1,896]{1,0:T(1,128)S(1)} %broadcast_in_dim.10.gain_ref), custom_call_target="tpu_custom_call" | custom-call | tf_op jit(solution)/shard_map/conclude/pallas_call | solution.py:337
  (47 shorter events, 13.3 us)
Async XLA Ops:
  0.6 8.7 %copy-start.6 = (s32[1,8]{1,0:T(1,128)S(1)}, s32[1,8]{1,0:T(1,128)}, u32[]{:S(2)}) copy-start(s32[1,8]{1,0:T(1,128)} %param.9) | copy-start | bytes 100
  0.6 27.8 %copy-start = (bf16[1,2,96,3,896]{4,2,3,1,0:T(8,128)(2,1)S(1)}, bf16[1,2,96,3,896]{4,2,3,1,0:T(8,128)(2,1)}, u32[]{:S(2)}) copy-start(bf16[1,2,96,3,896]{4,2,3,1,0:T(8,128)(2,1)} %param.5) | copy-start | bytes 3096580
  3.0 23.4 %collective-permute-start = (bf16[2,2,96,896]{3,2,1,0:T(8,128)(2,1)}, bf16[2,2,96,896]{3,2,1,0:T(8,128)(2,1)S(1)}, u32[]{:S(2)}, u32[]{:S(2)}) collective-permute-start(bf16[2,2,96,896]{3,2,1,0:T(8,128)(2,1)} %get-tuple-element.32), channel_id=1, source_target_pairs={{0,8},{8,16},{16,24},{1,9},{9,17},{17,25},{2,10},{10,18},{18,26},{... | collective-permute-start | bytes 2064392 | tf_op jit(solution)/shard_map/ppermute | solution.py:416
  8.0 20.5 %collective-permute-start.1 = (bf16[2,2,96,896]{3,2,1,0:T(8,128)(2,1)}, bf16[2,2,96,896]{3,2,1,0:T(8,128)(2,1)S(1)}, u32[]{:S(2)}, u32[]{:S(2)}) collective-permute-start(bf16[2,2,96,896]{3,2,1,0:T(8,128)(2,1)} %get-tuple-element.33), channel_id=1, source_target_pairs={{8,0},{16,8},{24,16},{9,1},{17,9},{25,17},{10,2},{18,10},{26,18},{... | collective-permute-start | bytes 2064392 | tf_op jit(solution)/shard_map/ppermute | solution.py:415
  10.0 18.5 %copy-start.2 = (s32[7]{0:T(128)S(1)}, s32[7]{0:T(128)}, u32[]{:S(2)}) copy-start(s32[7]{0:T(128)} %pad_add_fusion.where_ref) | copy-start | bytes 88
  12.9 22.3 %copy-start.3 = (bf16[1,2,96,3,896]{4,2,3,1,0:T(8,128)(2,1)S(1)}, bf16[1,2,96,3,896]{4,2,3,1,0:T(8,128)(2,1)}, u32[]{:S(2)}) copy-start(bf16[1,2,96,3,896]{4,2,3,1,0:T(8,128)(2,1)} %param.6) | copy-start | bytes 3096580
  12.9 30.0 %collective-permute-start.4 = (bf16[448,896]{1,0:T(8,128)(2,1)}, bf16[448,896]{1,0:T(8,128)(2,1)}, u32[]{:S(2)}, u32[]{:S(2)}) collective-permute-start(bf16[448,896]{1,0:T(8,128)(2,1)} %get-tuple-element.35.refs_8_), channel_id=1, source_target_pairs={{0,8},{8,16},{16,24},{1,9},{9,17},{17,25},{2,10},{10,18},{18,26},{... | collective-permute-start | bytes 2408456 | tf_op jit(solution)/shard_map/ppermute | solution.py:433
  18.5 25.8 %collective-permute-start.3 = (bf16[448,896]{1,0:T(8,128)(2,1)}, bf16[448,896]{1,0:T(8,128)(2,1)}, u32[]{:S(2)}, u32[]{:S(2)}) collective-permute-start(bf16[448,896]{1,0:T(8,128)(2,1)} %get-tuple-element.35.refs_8_), channel_id=1, source_target_pairs={{8,0},{16,8},{24,16},{9,1},{17,9},{25,17},{10,2},{18,10},{26,18},{... | collective-permute-start | bytes 2408456 | tf_op jit(solution)/shard_map/ppermute | solution.py:433
  19.8 31.7 %collective-permute-start.9 = (bf16[128,896]{1,0:T(8,128)(2,1)}, bf16[128,896]{1,0:T(8,128)(2,1)}, u32[]{:S(2)}, u32[]{:S(2)}) collective-permute-start(bf16[128,896]{1,0:T(8,128)(2,1)} %get-tuple-element.38), channel_id=1, source_target_pairs={{0,24},{24,0},{1,25},{25,1},{2,26},{26,2},{3,27},{27,3},{4,28},{28... | collective-permute-start | bytes 688136 | tf_op jit(solution)/shard_map/ppermute | solution.py:435
  33.7 8.1 %collective-permute-start.2 = (bf16[1,192,896]{2,1,0:T(8,128)(2,1)}, bf16[1,192,896]{2,1,0:T(8,128)(2,1)}, u32[]{:S(2)}, u32[]{:S(2)}) collective-permute-start(bf16[1,192,896]{2,1,0:T(8,128)(2,1)} %bitcast.8), channel_id=1, source_target_pairs={{0,1},{1,0},{2,3},{3,2},{4,5},{5,4},{6,7},{7,6},{8,9},{9,8},{10,11... | collective-permute-start | bytes 1032200 | tf_op jit(solution)/shard_map/ppermute | solution.py:356
  40.1 28.9 %copy-start.5 = (bf16[320,896]{1,0:T(8,128)(2,1)S(1)}, bf16[320,896]{1,0:T(8,128)(2,1)}, u32[]{:S(2)}) copy-start(bf16[320,896]{1,0:T(8,128)(2,1)} %get-tuple-element.43) | copy-start | bytes 1720324
  40.1 31.5 %copy-start.1 = (bf16[448,896]{1,0:T(8,128)(2,1)S(1)}, bf16[448,896]{1,0:T(8,128)(2,1)}, u32[]{:S(2)}) copy-start(bf16[448,896]{1,0:T(8,128)(2,1)} %get-tuple-element.35.refs_8_) | copy-start | bytes 2408452
  40.2 7.3 %collective-permute-start.8 = (bf16[1,192,896]{2,1,0:T(8,128)(2,1)S(1)}, bf16[1,192,896]{2,1,0:T(8,128)(2,1)S(1)}, u32[]{:S(2)}, u32[]{:S(2)}) collective-permute-start(bf16[1,192,896]{2,1,0:T(8,128)(2,1)S(1)} %bitcast.20), channel_id=1, source_target_pairs={{0,4},{2,6},{4,0},{6,2},{1,5},{3,7},{5,1},{7,3},{8,12},{10,14},{12... | collective-permute-start | bytes 1032200 | tf_op jit(solution)/shard_map/ppermute | solution.py:356
  44.3 24.2 %collective-permute-start.12 = (bf16[448,896]{1,0:T(8,128)(2,1)}, bf16[448,896]{1,0:T(8,128)(2,1)S(1)}, u32[]{:S(2)}, u32[]{:S(2)}) collective-permute-start(bf16[448,896]{1,0:T(8,128)(2,1)} %collective-permute-done.3.refs_9_), channel_id=1, source_target_pairs={{8,0},{16,8},{9,1},{17,9},{10,2},{18,10},{11,3},{19,11},{12,4},{20... | collective-permute-start | bytes 2408456 | tf_op jit(solution)/shard_map/ppermute | solution.py:445
  45.6 22.9 %collective-permute-start.13 = (bf16[448,896]{1,0:T(8,128)(2,1)}, bf16[448,896]{1,0:T(8,128)(2,1)S(1)}, u32[]{:S(2)}, u32[]{:S(2)}) collective-permute-start(bf16[448,896]{1,0:T(8,128)(2,1)} %collective-permute-done.4.refs_10_), channel_id=1, source_target_pairs={{8,16},{16,24},{9,17},{17,25},{10,18},{18,26},{11,19},{19,27},{12,... | collective-permute-start | bytes 2408456 | tf_op jit(solution)/shard_map/ppermute | solution.py:446
  51.4 15.9 %collective-permute-start.10 = (bf16[2,192,896]{2,1,0:T(8,128)(2,1)S(1)}, bf16[2,192,896]{2,1,0:T(8,128)(2,1)S(1)}, u32[]{:S(2)}, u32[]{:S(2)}) collective-permute-start(bf16[2,192,896]{2,1,0:T(8,128)(2,1)S(1)} %pad_maximum_fusion.1.refs_4_), channel_id=1, source_target_pairs={{0,1},{1,0},{2,3},{3,2},{4,5},{5,4},{6,7},{7,6},{8,9},{9,8},{10,11... | collective-permute-start | bytes 2064392 | tf_op jit(solution)/shard_map/ppermute | solution.py:356
  53.0 15.6 %collective-permute-start.5 = (bf16[2,192,896]{2,1,0:T(8,128)(2,1)S(1)}, bf16[2,192,896]{2,1,0:T(8,128)(2,1)S(1)}, u32[]{:S(2)}, u32[]{:S(2)}) collective-permute-start(bf16[2,192,896]{2,1,0:T(8,128)(2,1)S(1)} %pad_maximum_fusion.refs_0_), channel_id=1, source_target_pairs={{0,4},{2,6},{4,0},{6,2},{1,5},{3,7},{5,1},{7,3},{8,12},{10,14},{12... | collective-permute-start | bytes 2064392 | tf_op jit(solution)/shard_map/ppermute | solution.py:356
  54.4 16.7 %collective-permute-start.6 = (bf16[2,192,896]{2,1,0:T(8,128)(2,1)S(1)}, bf16[2,192,896]{2,1,0:T(8,128)(2,1)S(1)}, u32[]{:S(2)}, u32[]{:S(2)}) collective-permute-start(bf16[2,192,896]{2,1,0:T(8,128)(2,1)S(1)} %pad_maximum_fusion.refs_0_), channel_id=1, source_target_pairs={{0,2},{2,0},{4,6},{6,4},{1,3},{3,1},{5,7},{7,5},{8,10},{10,8},{12,... | collective-permute-start | bytes 2064392 | tf_op jit(solution)/shard_map/ppermute | solution.py:356
  67.3 3.9 %collective-permute-start.11 = (bf16[2,192,896]{2,1,0:T(8,128)(2,1)S(1)}, bf16[2,192,896]{2,1,0:T(8,128)(2,1)S(1)}, u32[]{:S(2)}, u32[]{:S(2)}) collective-permute-start(bf16[2,192,896]{2,1,0:T(8,128)(2,1)S(1)} %pad_maximum_fusion.1.refs_4_), channel_id=1, source_target_pairs={{0,2},{2,0},{4,6},{6,4},{1,3},{3,1},{5,7},{7,5},{8,10},{10,8},{12,... | collective-permute-start | bytes 2064392 | tf_op jit(solution)/shard_map/ppermute | solution.py:356
  68.6 2.7 %collective-permute-start.7 = (bf16[2,192,896]{2,1,0:T(8,128)(2,1)S(1)}, bf16[2,192,896]{2,1,0:T(8,128)(2,1)S(1)}, u32[]{:S(2)}, u32[]{:S(2)}) collective-permute-start(bf16[2,192,896]{2,1,0:T(8,128)(2,1)S(1)} %collective-permute-done.5.refs_1_), channel_id=1, source_target_pairs={{0,2},{2,0},{4,6},{6,4},{1,3},{3,1},{5,7},{7,5},{8,10},{10,8},{12,... | collective-permute-start | bytes 2064392 | tf_op jit(solution)/shard_map/ppermute | solution.py:356
  68.6 3.1 %collective-permute-start.14 = (bf16[2,192,896]{2,1,0:T(8,128)(2,1)S(1)}, bf16[2,192,896]{2,1,0:T(8,128)(2,1)S(1)}, u32[]{:S(2)}, u32[]{:S(2)}) collective-permute-start(bf16[2,192,896]{2,1,0:T(8,128)(2,1)S(1)} %collective-permute-done.10.refs_5_), channel_id=1, source_target_pairs={{0,2},{2,0},{4,6},{6,4},{1,3},{3,1},{5,7},{7,5},{8,10},{10,8},{12,... | collective-permute-start | bytes 2064392 | tf_op jit(solution)/shard_map/ppermute | solution.py:356
  69.1 18.6 %collective-permute-start.15 = (bf16[320,896]{1,0:T(8,128)(2,1)S(1)}, bf16[320,896]{1,0:T(8,128)(2,1)S(1)}, u32[]{:S(2)}, u32[]{:S(2)}) collective-permute-start(bf16[320,896]{1,0:T(8,128)(2,1)S(1)} %copy-done.5), channel_id=1, source_target_pairs={{0,24},{24,0},{1,25},{25,1},{2,26},{26,2},{3,27},{27,3},{4,28},{28... | collective-permute-start | bytes 1720328 | tf_op jit(solution)/shard_map/ppermute | solution.py:435
  97.9 7.0 %collective-permute-start.16 = (bf16[2,96,448]{2,1,0:T(8,128)(2,1)S(1)}, bf16[2,96,448]{2,1,0:T(8,128)(2,1)S(1)}, u32[]{:S(2)}, u32[]{:S(2)}) collective-permute-start(bf16[2,96,448]{2,1,0:T(8,128)(2,1)S(1)} %bitcast.27), channel_id=1, source_target_pairs={{0,1},{1,0},{2,3},{3,2},{4,5},{5,4},{6,7},{7,6},{8,9},{9,8},{10,11... | collective-permute-start | bytes 516104 | tf_op jit(solution)/shard_map/ppermute | solution.py:356
  99.8 10.2 %all-to-all-start.1 = ((f32[32,1,512]{2,1,0:T(1,128)}), f32[32,1,512]{2,1,0:T(1,128)S(1)}, u32[]{:S(2)}, u32[]{:S(2)}) async-start(f32[32,1,512]{2,1,0:T(1,128)} %finish.1), calls=%async_computation.1 | async-start | bytes 131072 | tf_op jit(solution)/shard_map/all_to_all | solution.py:379
  (1 other events, 1.9 us)

commit v11 on v8

--- a/solution.py
+++ b/solution.py
@@ -423,7 +423,7 @@
     gain_row = jnp.pad(own_columns(norm_gain), (0, whole_lanes(half) - half))[None]
     gain_all = norm_gain[None]
 
-    cut = min(LANES, half // 2)
+    cut = whole_lanes(half) // 2
     own_weight, *parts = prepare_weight(where, out_weight, clip_count, cut)
     line = slab_count == model_count and slab_count == 4
     last = slab_count - 1

time: 111 us -> 111 us (level)
  no operation moved by 1% of the time
where the time goes in v11:
time: 111 us; the launch traced here: 110 us
  starting transfers between devices  37.7 us (34%)
  waiting for transfers between devices  35.2 us (32%)
  Pallas kernels  25.1 us (23%)
  blocking collectives  7.82 us (7%)
  other arithmetic  3.2 us (3%)
    ppermute x9, waiting for transfers between devices, swap(): return lax.ppermute(array, axis, [(i, i ^ distance) for i in range(count)])  15 us
    ppermute x2, waiting for transfers between devices, local(): lax.ppermute(block, 'frames', [(0, last), (last, 0)])  10.4 us
    ppermute x2, starting transfers between devices, local(): lax.ppermute(block, 'frames', [(0, last), (last, 0)])  10.1 us
    pallas_call x2, Pallas kernels, attention(): pl.pallas_call(attend_kernel, grid_spec=pltpu.PrefetchScalarGridSpec(num_...  9.76 us
    all_to_all x1, blocking collectives, collect(): return lax.all_to_all(rows, axes, split_axis=0, concat_axis=0, tiled=True)  7.82 us
    ppermute x9, starting transfers between devices, swap(): return lax.ppermute(array, axis, [(i, i ^ distance) for i in range(count)])  7.8 us
    pallas_call x2, Pallas kernels, project(): pl.pallas_call(kernel, in_specs=[pl.BlockSpec(memory_space=pltpu.SMEM)] +...  7.39 us
    all_to_all x1, waiting for transfers between devices, collect(): return lax.all_to_all(rows, axes, split_axis=0, concat_axis=0, tiled=True)  6.35 us
  transfers between devices with their start and end apart: 18, of which 9 were waited for; matrix products, arithmetic and copies ran while one was open for 3% of the time, Pallas kernels for 18%

profile of v11, /device:TPU:0, one launch (start us, length us, event | category | flops | bytes accessed | tf_op | source)
XLA Modules:
  0.0 110.1 jit_solution(329512635017942542)
XLA Ops:
  0.6 2.4 %prepare_halo.1 = (bf16[2,2,96,896]{3,2,1,0:T(8,128)(2,1)}, bf16[2,2,96,896]{3,2,1,0:T(8,128)(2,1)}) custom-call(bf16[2,3,96,896]{3,2,1,0:T(8,128)(2,1)} %bitcast.17, bf16[2,3,96,896]{3,2,1,0:T(8,128)(2,1)} %bitcast.24), custom_call_target="tpu_custom_call" | custom-call | tf_op jit(solution)/shard_map/prepare_halo/pallas_call | solution.py:53
  3.0 1.3 %collective-permute-start = (bf16[2,2,96,896]{3,2,1,0:T(8,128)(2,1)}, bf16[2,2,96,896]{3,2,1,0:T(8,128)(2,1)S(1)}, u32[]{:S(2)}, u32[]{:S(2)}) collective-permute-start(bf16[2,2,96,896]{3,2,1,0:T(8,128)(2,1)} %get-tuple-element.32), channel_id=1, source_target_pairs={{8,0},{16,8},{24,16},{9,1},{17,9},{25,17},{10,2},{18,10},{26,18},{... | collective-permute-start | bytes 2064392 | tf_op jit(solution)/shard_map/ppermute | solution.py:415
  4.3 5.6 %collective-permute-start.1 = (bf16[2,2,96,896]{3,2,1,0:T(8,128)(2,1)}, bf16[2,2,96,896]{3,2,1,0:T(8,128)(2,1)S(1)}, u32[]{:S(2)}, u32[]{:S(2)}) collective-permute-start(bf16[2,2,96,896]{3,2,1,0:T(8,128)(2,1)} %get-tuple-element.33), channel_id=1, source_target_pairs={{0,8},{8,16},{16,24},{1,9},{9,17},{17,25},{2,10},{10,18},{18,26},{... | collective-permute-start | bytes 2064392 | tf_op jit(solution)/shard_map/ppermute | solution.py:416
  10.7 2.9 %prepare_weight.1 = (bf16[448,896]{1,0:T(8,128)(2,1)}, bf16[256,896]{1,0:T(8,128)(2,1)}, bf16[192,896]{1,0:T(8,128)(2,1)}) custom-call(s32[7]{0:T(128)} %pad_add_fusion.where_ref, bf16[896,896]{1,0:T(8,128)(2,1)} %weight_ref), custom_call_target="tpu_custom_call" | custom-call | tf_op jit(solution)/shard_map/prepare_weight/pallas_call | solution.py:87
  13.6 4.9 %collective-permute-start.4 = (bf16[448,896]{1,0:T(8,128)(2,1)}, bf16[448,896]{1,0:T(8,128)(2,1)}, u32[]{:S(2)}, u32[]{:S(2)}) collective-permute-start(bf16[448,896]{1,0:T(8,128)(2,1)} %get-tuple-element.35.refs_8_), channel_id=1, source_target_pairs={{0,8},{8,16},{16,24},{1,9},{9,17},{17,25},{2,10},{10,18},{18,26},{... | collective-permute-start | bytes 2408456 | tf_op jit(solution)/shard_map/ppermute | solution.py:433
  19.8 5.1 %collective-permute-start.9 = (bf16[256,896]{1,0:T(8,128)(2,1)}, bf16[256,896]{1,0:T(8,128)(2,1)}, u32[]{:S(2)}, u32[]{:S(2)}) collective-permute-start(bf16[256,896]{1,0:T(8,128)(2,1)} %get-tuple-element.38), channel_id=1, source_target_pairs={{0,24},{24,0},{1,25},{25,1},{2,26},{26,2},{3,27},{27,3},{4,28},{28... | collective-permute-start | bytes 1376264 | tf_op jit(solution)/shard_map/ppermute | solution.py:435
  26.1 5.2 %attention.2 = bf16[2,96,896]{2,1,0:T(8,128)(2,1)} custom-call(s32[7]{0:T(128)S(1)} %copy-done.2, bf16[2,3,96,896]{3,2,1,0:T(8,128)(2,1)S(1)} %bitcast.18, bf16[2,2,96,896]{3,2,1,0:T(8,128)(2,1)S(1)} %collective-permute-done.right_ref, bf16[2,2,96,896]{3,2,1,0:T(8,128)(2,1)S(1)} %collective-permute-done.1.left_ref), custom_call_target="tpu_custom_call" | custom-call | tf_op jit(solution)/shard_map/attention/pallas_call | solution.py:144
  31.3 2.0 %collective-permute-start.2 = (bf16[1,192,896]{2,1,0:T(8,128)(2,1)}, bf16[1,192,896]{2,1,0:T(8,128)(2,1)}, u32[]{:S(2)}, u32[]{:S(2)}) collective-permute-start(bf16[1,192,896]{2,1,0:T(8,128)(2,1)} %bitcast.8), channel_id=1, source_target_pairs={{0,1},{1,0},{2,3},{3,2},{4,5},{5,4},{6,7},{7,6},{8,9},{9,8},{10,11... | collective-permute-start | bytes 1032200 | tf_op jit(solution)/shard_map/ppermute | solution.py:356
  33.6 4.5 %attention.3 = bf16[2,96,896]{2,1,0:T(8,128)(2,1)S(1)} custom-call(s32[7]{0:T(128)S(1)} %copy-done.2, bf16[2,3,96,896]{3,2,1,0:T(8,128)(2,1)S(1)} %add_convert_fusion.own_ref, bf16[2,2,96,896]{3,2,1,0:T(8,128)(2,1)S(1)} %collective-permute-done.right_ref, bf16[2,2,96,896]{3,2,1,0:T(8,128)(2,1)S(1)} %collective-permute-done.1.left_ref), custom_call_target="tpu_custom_call" | custom-call | tf_op jit(solution)/shard_map/attention/pallas_call | solution.py:144
  38.2 1.6 %collective-permute-start.8 = (bf16[1,192,896]{2,1,0:T(8,128)(2,1)S(1)}, bf16[1,192,896]{2,1,0:T(8,128)(2,1)S(1)}, u32[]{:S(2)}, u32[]{:S(2)}) collective-permute-start(bf16[1,192,896]{2,1,0:T(8,128)(2,1)S(1)} %bitcast.20), channel_id=1, source_target_pairs={{0,4},{2,6},{4,0},{6,2},{1,5},{3,7},{5,1},{7,3},{8,12},{10,14},{12... | collective-permute-start | bytes 1032200 | tf_op jit(solution)/shard_map/ppermute | solution.py:356
  41.0 2.3 %collective-permute-done.4.refs_10_ = bf16[448,896]{1,0:T(8,128)(2,1)} collective-permute-done((bf16[448,896]{1,0:T(8,128)(2,1)}, bf16[448,896]{1,0:T(8,128)(2,1)}, u32[]{:S(2)}, u32[]{:S(2)}) %collective-permute-start.4) | collective-permute-done | bytes 802848 | tf_op jit(solution)/shard_map/ppermute | solution.py:433
  43.3 1.3 %collective-permute-start.12 = (bf16[448,896]{1,0:T(8,128)(2,1)}, bf16[448,896]{1,0:T(8,128)(2,1)S(1)}, u32[]{:S(2)}, u32[]{:S(2)}) collective-permute-start(bf16[448,896]{1,0:T(8,128)(2,1)} %collective-permute-done.3.refs_9_), channel_id=1, source_target_pairs={{8,0},{16,8},{9,1},{17,9},{10,2},{18,10},{11,3},{19,11},{12,4},{20... | collective-permute-start | bytes 2408456 | tf_op jit(solution)/shard_map/ppermute | solution.py:445
  45.6 7.5 %collective-permute-done.9.refs_13_ = bf16[256,896]{1,0:T(8,128)(2,1)} collective-permute-done((bf16[256,896]{1,0:T(8,128)(2,1)}, bf16[256,896]{1,0:T(8,128)(2,1)}, u32[]{:S(2)}, u32[]{:S(2)}) %collective-permute-start.9) | collective-permute-done | bytes 458784 | tf_op jit(solution)/shard_map/ppermute | solution.py:435
  53.1 1.5 %collective-permute-start.10 = (bf16[2,192,896]{2,1,0:T(8,128)(2,1)S(1)}, bf16[2,192,896]{2,1,0:T(8,128)(2,1)S(1)}, u32[]{:S(2)}, u32[]{:S(2)}) collective-permute-start(bf16[2,192,896]{2,1,0:T(8,128)(2,1)S(1)} %pad_maximum_fusion.1.refs_4_), channel_id=1, source_target_pairs={{0,1},{1,0},{2,3},{3,2},{4,5},{5,4},{6,7},{7,6},{8,9},{9,8},{10,11... | collective-permute-start | bytes 2064392 | tf_op jit(solution)/shard_map/ppermute | solution.py:356
  54.6 1.5 %collective-permute-start.5 = (bf16[2,192,896]{2,1,0:T(8,128)(2,1)S(1)}, bf16[2,192,896]{2,1,0:T(8,128)(2,1)S(1)}, u32[]{:S(2)}, u32[]{:S(2)}) collective-permute-start(bf16[2,192,896]{2,1,0:T(8,128)(2,1)S(1)} %pad_maximum_fusion.refs_0_), channel_id=1, source_target_pairs={{0,4},{2,6},{4,0},{6,2},{1,5},{3,7},{5,1},{7,3},{8,12},{10,14},{12... | collective-permute-start | bytes 2064392 | tf_op jit(solution)/shard_map/ppermute | solution.py:356
  56.1 13.2 %collective-permute-done.10.refs_5_ = bf16[2,192,896]{2,1,0:T(8,128)(2,1)S(1)} collective-permute-done((bf16[2,192,896]{2,1,0:T(8,128)(2,1)S(1)}, bf16[2,192,896]{2,1,0:T(8,128)(2,1)S(1)}, u32[]{:S(2)}, u32[]{:S(2)}) %collective-permute-start.10) | collective-permute-done | bytes 688160 | tf_op jit(solution)/shard_map/ppermute | solution.py:356
  71.0 5.0 %collective-permute-start.15 = (bf16[192,896]{1,0:T(8,128)(2,1)S(1)}, bf16[192,896]{1,0:T(8,128)(2,1)S(1)}, u32[]{:S(2)}, u32[]{:S(2)}) collective-permute-start(bf16[192,896]{1,0:T(8,128)(2,1)S(1)} %copy-done.5), channel_id=1, source_target_pairs={{0,24},{24,0},{1,25},{25,1},{2,26},{26,2},{3,27},{27,3},{4,28},{28... | collective-permute-start | bytes 1032200 | tf_op jit(solution)/shard_map/ppermute | solution.py:435
  76.1 5.7 %project.2.refs_9_ = f32[768,512]{1,0:T(8,128)S(1)} custom-call(s32[7]{0:T(128)S(1)} %copy-done.2, bf16[2,192,896]{2,1,0:T(8,128)(2,1)S(1)} %pad_maximum_fusion.refs_0_, bf16[2,192,896]{2,1,0:T(8,128)(2,1)S(1)} %collective-permute-done.5.refs_1_, bf16[2,192,896]{2,1,0:T(8,128)(2,1)S(1)} %collective-permute-done.6.refs_2_, ...), custom_call_target="tpu_custom_call" | custom-call | tf_op jit(solution)/shard_map/project/pallas_call | solution.py:243
  81.9 2.9 %collective-permute-done.15.refs_8_ = bf16[192,896]{1,0:T(8,128)(2,1)S(1)} collective-permute-done((bf16[192,896]{1,0:T(8,128)(2,1)S(1)}, bf16[192,896]{1,0:T(8,128)(2,1)S(1)}, u32[]{:S(2)}, u32[]{:S(2)}) %collective-permute-start.15) | collective-permute-done | bytes 344096 | tf_op jit(solution)/shard_map/ppermute | solution.py:435
  84.8 1.7 %project.3 = (f32[768,512]{1,0:T(8,128)S(1)}, f32[8,1,768]{2,1,0:T(1,128)S(1)}) custom-call(s32[7]{0:T(128)S(1)} %copy-done.2, bf16[2,192,896]{2,1,0:T(8,128)(2,1)S(1)} %pad_maximum_fusion.refs_0_, bf16[2,192,896]{2,1,0:T(8,128)(2,1)S(1)} %collective-permute-done.5.refs_1_, ...), custom_call_target="tpu_custom_call", output_to_operand_aliasing={{0}: (10, {})} | custom-call | tf_op jit(solution)/shard_map/project/pallas_call | solution.py:243
  86.4 7.8 %all_to_all.10.squares_ref = f32[8,1,768]{2,1,0:T(1,128)S(1)} all-to-all(f32[8,1,768]{2,1,0:T(1,128)S(1)} %get-tuple-element.48), channel_id=1, replica_groups=mesh['frames'=4,'mp'=4,'dp'=2] {'mp','dp'}, dimensions={0} | all-to-all | bytes 49152 | tf_op jit(solution)/shard_map/all_to_all | solution.py:379
  96.4 4.7 %all-to-all-start.1 = ((f32[32,1,512]{2,1,0:T(1,128)}), f32[32,1,512]{2,1,0:T(1,128)S(1)}, u32[]{:S(2)}, u32[]{:S(2)}) async-start(f32[32,1,512]{2,1,0:T(1,128)} %finish.1), calls=%async_computation.1 | async-start | bytes 131072 | tf_op jit(solution)/shard_map/all_to_all | solution.py:379
  102.4 6.4 %all-to-all-done.1.rows_ref = f32[32,1,512]{2,1,0:T(1,128)S(1)} async-done(((f32[32,1,512]{2,1,0:T(1,128)}), f32[32,1,512]{2,1,0:T(1,128)S(1)}, u32[]{:S(2)}, u32[]{:S(2)}) %all-to-all-start.1) | async-done | bytes 65568 | tf_op jit(solution)/shard_map/all_to_all | solution.py:379
  108.8 1.4 %conclude.1 = (f32[1]{0:T(128)}, f32[896]{0:T(1024)}) custom-call(s32[7]{0:T(128)S(1)} %copy-done.2, f32[32,1,512]{2,1,0:T(1,128)S(1)} %all-to-all-done.1.rows_ref, f32[1,896]{1,0:T(1,128)S(1)} %broadcast_in_dim.10.gain_ref), custom_call_target="tpu_custom_call" | custom-call | tf_op jit(solution)/shard_map/conclude/pallas_call | solution.py:337
  (47 shorter events, 11.0 us)
Async XLA Ops:
  0.6 9.3 %copy-start.6 = (s32[1,8]{1,0:T(1,128)S(1)}, s32[1,8]{1,0:T(1,128)}, u32[]{:S(2)}) copy-start(s32[1,8]{1,0:T(1,128)} %param.9) | copy-start | bytes 100
  0.6 25.4 %copy-start = (bf16[1,2,96,3,896]{4,2,3,1,0:T(8,128)(2,1)S(1)}, bf16[1,2,96,3,896]{4,2,3,1,0:T(8,128)(2,1)}, u32[]{:S(2)}) copy-start(bf16[1,2,96,3,896]{4,2,3,1,0:T(8,128)(2,1)} %param.5) | copy-start | bytes 3096580
  3.0 21.8 %collective-permute-start = (bf16[2,2,96,896]{3,2,1,0:T(8,128)(2,1)}, bf16[2,2,96,896]{3,2,1,0:T(8,128)(2,1)S(1)}, u32[]{:S(2)}, u32[]{:S(2)}) collective-permute-start(bf16[2,2,96,896]{3,2,1,0:T(8,128)(2,1)} %get-tuple-element.32), channel_id=1, source_target_pairs={{8,0},{16,8},{24,16},{9,1},{17,9},{25,17},{10,2},{18,10},{26,18},{... | collective-permute-start | bytes 2064392 | tf_op jit(solution)/shard_map/ppermute | solution.py:415
  4.3 21.7 %collective-permute-start.1 = (bf16[2,2,96,896]{3,2,1,0:T(8,128)(2,1)}, bf16[2,2,96,896]{3,2,1,0:T(8,128)(2,1)S(1)}, u32[]{:S(2)}, u32[]{:S(2)}) collective-permute-start(bf16[2,2,96,896]{3,2,1,0:T(8,128)(2,1)} %get-tuple-element.33), channel_id=1, source_target_pairs={{0,8},{8,16},{16,24},{1,9},{9,17},{17,25},{2,10},{10,18},{18,26},{... | collective-permute-start | bytes 2064392 | tf_op jit(solution)/shard_map/ppermute | solution.py:416
  10.7 15.3 %copy-start.2 = (s32[7]{0:T(128)S(1)}, s32[7]{0:T(128)}, u32[]{:S(2)}) copy-start(s32[7]{0:T(128)} %pad_add_fusion.where_ref) | copy-start | bytes 88
  13.6 19.7 %copy-start.3 = (bf16[1,2,96,3,896]{4,2,3,1,0:T(8,128)(2,1)S(1)}, bf16[1,2,96,3,896]{4,2,3,1,0:T(8,128)(2,1)}, u32[]{:S(2)}) copy-start(bf16[1,2,96,3,896]{4,2,3,1,0:T(8,128)(2,1)} %param.6) | copy-start | bytes 3096580
  13.6 29.7 %collective-permute-start.4 = (bf16[448,896]{1,0:T(8,128)(2,1)}, bf16[448,896]{1,0:T(8,128)(2,1)}, u32[]{:S(2)}, u32[]{:S(2)}) collective-permute-start(bf16[448,896]{1,0:T(8,128)(2,1)} %get-tuple-element.35.refs_8_), channel_id=1, source_target_pairs={{0,8},{8,16},{16,24},{1,9},{9,17},{17,25},{2,10},{10,18},{18,26},{... | collective-permute-start | bytes 2408456 | tf_op jit(solution)/shard_map/ppermute | solution.py:433
  18.5 24.7 %collective-permute-start.3 = (bf16[448,896]{1,0:T(8,128)(2,1)}, bf16[448,896]{1,0:T(8,128)(2,1)}, u32[]{:S(2)}, u32[]{:S(2)}) collective-permute-start(bf16[448,896]{1,0:T(8,128)(2,1)} %get-tuple-element.35.refs_8_), channel_id=1, source_target_pairs={{8,0},{16,8},{24,16},{9,1},{17,9},{25,17},{10,2},{18,10},{26,18},{... | collective-permute-start | bytes 2408456 | tf_op jit(solution)/shard_map/ppermute | solution.py:433
  19.8 33.3 %collective-permute-start.9 = (bf16[256,896]{1,0:T(8,128)(2,1)}, bf16[256,896]{1,0:T(8,128)(2,1)}, u32[]{:S(2)}, u32[]{:S(2)}) collective-permute-start(bf16[256,896]{1,0:T(8,128)(2,1)} %get-tuple-element.38), channel_id=1, source_target_pairs={{0,24},{24,0},{1,25},{25,1},{2,26},{26,2},{3,27},{27,3},{4,28},{28... | collective-permute-start | bytes 1376264 | tf_op jit(solution)/shard_map/ppermute | solution.py:435
  31.3 8.5 %collective-permute-start.2 = (bf16[1,192,896]{2,1,0:T(8,128)(2,1)}, bf16[1,192,896]{2,1,0:T(8,128)(2,1)}, u32[]{:S(2)}, u32[]{:S(2)}) collective-permute-start(bf16[1,192,896]{2,1,0:T(8,128)(2,1)} %bitcast.8), channel_id=1, source_target_pairs={{0,1},{1,0},{2,3},{3,2},{4,5},{5,4},{6,7},{7,6},{8,9},{9,8},{10,11... | collective-permute-start | bytes 1032200 | tf_op jit(solution)/shard_map/ppermute | solution.py:356
  38.2 32.9 %copy-start.5 = (bf16[192,896]{1,0:T(8,128)(2,1)S(1)}, bf16[192,896]{1,0:T(8,128)(2,1)}, u32[]{:S(2)}) copy-start(bf16[192,896]{1,0:T(8,128)(2,1)} %get-tuple-element.43) | copy-start | bytes 1032196
  38.2 37.9 %copy-start.1 = (bf16[448,896]{1,0:T(8,128)(2,1)S(1)}, bf16[448,896]{1,0:T(8,128)(2,1)}, u32[]{:S(2)}) copy-start(bf16[448,896]{1,0:T(8,128)(2,1)} %get-tuple-element.35.refs_8_) | copy-start | bytes 2408452
  38.2 7.3 %collective-permute-start.8 = (bf16[1,192,896]{2,1,0:T(8,128)(2,1)S(1)}, bf16[1,192,896]{2,1,0:T(8,128)(2,1)S(1)}, u32[]{:S(2)}, u32[]{:S(2)}) collective-permute-start(bf16[1,192,896]{2,1,0:T(8,128)(2,1)S(1)} %bitcast.20), channel_id=1, source_target_pairs={{0,4},{2,6},{4,0},{6,2},{1,5},{3,7},{5,1},{7,3},{8,12},{10,14},{12... | collective-permute-start | bytes 1032200 | tf_op jit(solution)/shard_map/ppermute | solution.py:356
  43.3 27.3 %collective-permute-start.12 = (bf16[448,896]{1,0:T(8,128)(2,1)}, bf16[448,896]{1,0:T(8,128)(2,1)S(1)}, u32[]{:S(2)}, u32[]{:S(2)}) collective-permute-start(bf16[448,896]{1,0:T(8,128)(2,1)} %collective-permute-done.3.refs_9_), channel_id=1, source_target_pairs={{8,0},{16,8},{9,1},{17,9},{10,2},{18,10},{11,3},{19,11},{12,4},{20... | collective-permute-start | bytes 2408456 | tf_op jit(solution)/shard_map/ppermute | solution.py:445
  44.5 26.0 %collective-permute-start.13 = (bf16[448,896]{1,0:T(8,128)(2,1)}, bf16[448,896]{1,0:T(8,128)(2,1)S(1)}, u32[]{:S(2)}, u32[]{:S(2)}) collective-permute-start(bf16[448,896]{1,0:T(8,128)(2,1)} %collective-permute-done.4.refs_10_), channel_id=1, source_target_pairs={{8,16},{16,24},{9,17},{17,25},{10,18},{18,26},{11,19},{19,27},{12,... | collective-permute-start | bytes 2408456 | tf_op jit(solution)/shard_map/ppermute | solution.py:446
  53.1 16.2 %collective-permute-start.10 = (bf16[2,192,896]{2,1,0:T(8,128)(2,1)S(1)}, bf16[2,192,896]{2,1,0:T(8,128)(2,1)S(1)}, u32[]{:S(2)}, u32[]{:S(2)}) collective-permute-start(bf16[2,192,896]{2,1,0:T(8,128)(2,1)S(1)} %pad_maximum_fusion.1.refs_4_), channel_id=1, source_target_pairs={{0,1},{1,0},{2,3},{3,2},{4,5},{5,4},{6,7},{7,6},{8,9},{9,8},{10,11... | collective-permute-start | bytes 2064392 | tf_op jit(solution)/shard_map/ppermute | solution.py:356
  54.6 15.9 %collective-permute-start.5 = (bf16[2,192,896]{2,1,0:T(8,128)(2,1)S(1)}, bf16[2,192,896]{2,1,0:T(8,128)(2,1)S(1)}, u32[]{:S(2)}, u32[]{:S(2)}) collective-permute-start(bf16[2,192,896]{2,1,0:T(8,128)(2,1)S(1)} %pad_maximum_fusion.refs_0_), channel_id=1, source_target_pairs={{0,4},{2,6},{4,0},{6,2},{1,5},{3,7},{5,1},{7,3},{8,12},{10,14},{12... | collective-permute-start | bytes 2064392 | tf_op jit(solution)/shard_map/ppermute | solution.py:356
  56.1 20.0 %collective-permute-start.6 = (bf16[2,192,896]{2,1,0:T(8,128)(2,1)S(1)}, bf16[2,192,896]{2,1,0:T(8,128)(2,1)S(1)}, u32[]{:S(2)}, u32[]{:S(2)}) collective-permute-start(bf16[2,192,896]{2,1,0:T(8,128)(2,1)S(1)} %pad_maximum_fusion.refs_0_), channel_id=1, source_target_pairs={{0,2},{2,0},{4,6},{6,4},{1,3},{3,1},{5,7},{7,5},{8,10},{10,8},{12,... | collective-permute-start | bytes 2064392 | tf_op jit(solution)/shard_map/ppermute | solution.py:356
  69.3 6.8 %collective-permute-start.11 = (bf16[2,192,896]{2,1,0:T(8,128)(2,1)S(1)}, bf16[2,192,896]{2,1,0:T(8,128)(2,1)S(1)}, u32[]{:S(2)}, u32[]{:S(2)}) collective-permute-start(bf16[2,192,896]{2,1,0:T(8,128)(2,1)S(1)} %pad_maximum_fusion.1.refs_4_), channel_id=1, source_target_pairs={{0,2},{2,0},{4,6},{6,4},{1,3},{3,1},{5,7},{7,5},{8,10},{10,8},{12,... | collective-permute-start | bytes 2064392 | tf_op jit(solution)/shard_map/ppermute | solution.py:356
  70.5 5.6 %collective-permute-start.7 = (bf16[2,192,896]{2,1,0:T(8,128)(2,1)S(1)}, bf16[2,192,896]{2,1,0:T(8,128)(2,1)S(1)}, u32[]{:S(2)}, u32[]{:S(2)}) collective-permute-start(bf16[2,192,896]{2,1,0:T(8,128)(2,1)S(1)} %collective-permute-done.5.refs_1_), channel_id=1, source_target_pairs={{0,2},{2,0},{4,6},{6,4},{1,3},{3,1},{5,7},{7,5},{8,10},{10,8},{12,... | collective-permute-start | bytes 2064392 | tf_op jit(solution)/shard_map/ppermute | solution.py:356
  70.5 5.6 %collective-permute-start.14 = (bf16[2,192,896]{2,1,0:T(8,128)(2,1)S(1)}, bf16[2,192,896]{2,1,0:T(8,128)(2,1)S(1)}, u32[]{:S(2)}, u32[]{:S(2)}) collective-permute-start(bf16[2,192,896]{2,1,0:T(8,128)(2,1)S(1)} %collective-permute-done.10.refs_5_), channel_id=1, source_target_pairs={{0,2},{2,0},{4,6},{6,4},{1,3},{3,1},{5,7},{7,5},{8,10},{10,8},{12,... | collective-permute-start | bytes 2064392 | tf_op jit(solution)/shard_map/ppermute | solution.py:356
  71.0 13.7 %collective-permute-start.15 = (bf16[192,896]{1,0:T(8,128)(2,1)S(1)}, bf16[192,896]{1,0:T(8,128)(2,1)S(1)}, u32[]{:S(2)}, u32[]{:S(2)}) collective-permute-start(bf16[192,896]{1,0:T(8,128)(2,1)S(1)} %copy-done.5), channel_id=1, source_target_pairs={{0,24},{24,0},{1,25},{25,1},{2,26},{26,2},{3,27},{27,3},{4,28},{28... | collective-permute-start | bytes 1032200 | tf_op jit(solution)/shard_map/ppermute | solution.py:435
  94.5 7.0 %collective-permute-start.16 = (bf16[2,96,448]{2,1,0:T(8,128)(2,1)S(1)}, bf16[2,96,448]{2,1,0:T(8,128)(2,1)S(1)}, u32[]{:S(2)}, u32[]{:S(2)}) collective-permute-start(bf16[2,96,448]{2,1,0:T(8,128)(2,1)S(1)} %bitcast.27), channel_id=1, source_target_pairs={{0,1},{1,0},{2,3},{3,2},{4,5},{5,4},{6,7},{7,6},{8,9},{9,8},{10,11... | collective-permute-start | bytes 516104 | tf_op jit(solution)/shard_map/ppermute | solution.py:356
  96.4 12.3 %all-to-all-start.1 = ((f32[32,1,512]{2,1,0:T(1,128)}), f32[32,1,512]{2,1,0:T(1,128)S(1)}, u32[]{:S(2)}, u32[]{:S(2)}) async-start(f32[32,1,512]{2,1,0:T(1,128)} %finish.1), calls=%async_computation.1 | async-start | bytes 131072 | tf_op jit(solution)/shard_map/all_to_all | solution.py:379
  (1 other events, 2.3 us)
